TPU v7x, 32 devices: a whole 2x2x4 slice. The times are simulated.
32 devices in a mesh: pipe: 8 (over z, core), dp: 4 (over y, x).
Axes of the slice: x: 2, y: 2, z: 4, core: 2. Of those that a mesh axis runs over, the one named last changes fastest.
Arguments:
- stash_held: bfloat16 [8, 512, 4096], P('pipe', 'dp'), may hold values from -36 to 36
- grad_in: bfloat16 [8, 512, 4096], P('pipe', 'dp'), may hold values from -6 to 6
- w_down: bfloat16 [8, 4096, 128], P('pipe'), may hold values from -0.09375 to 0.09375
- w_up: bfloat16 [8, 128, 4096], P('pipe'), may hold values from -0.5 to 0.5
- gain: float32 [8, 4096], P('pipe'), may hold values from 0.1 to 1.9
Outputs:
- prev_grad: bfloat16 [8, 512, 4096], P('pipe', 'dp')
- grad_down: float32 [8, 4096, 128], P('pipe', 'dp')
- grad_up: float32 [8, 128, 4096], P('pipe', None, 'dp')
All inputs are finite; a program needn't handle non-finite values.
Results may differ from a plain program's by a relative error of at most 0.0055.
Values may be sent and summed in bfloat16 or wider, within the bound.
No kernel may reach another device: no remote copies, remote signals or barrier semaphores. Data moves between devices by JAX's collectives and lax.ppermute only.
A program may use at most 64 MiB of HBM per device.

v0:
```python
import jax
import jax.numpy as jnp
from jax import lax
from jax.sharding import PartitionSpec as P


def swapped(x, axis, stride):
    return lax.ppermute(x, axis, [(i, i ^ 1 << stride) for i in range(lax.axis_size(axis))])


def from_behind(value, axis, steps):
    count = lax.axis_size(axis)
    leading, last = (max(0, -steps), min(count, count - steps))
    return lax.ppermute(value, axis, [(source, source + steps) for source in range(leading, last)])


def per_device(stash_held, grad_in, w_down, w_up, gain):
    sections = lax.axis_size("pipe")
    saved = swapped(stash_held[0], "pipe", sections.bit_length() - 2)
    cot = grad_in[0]
    down = w_down[0]
    upper = w_up[0]
    scale = gain[0]
    xf = saved.astype(jnp.float32)
    rms = jnp.sqrt(jnp.mean(xf * xf, axis=1, keepdims=True) + 1e-05)
    unit = xf / rms
    normed = (unit * scale[None, :]).astype(jnp.bfloat16)
    pre = jnp.dot(normed, down, preferred_element_type=jnp.float32)
    act, pull = jax.vjp(lambda value: jax.nn.gelu(value, approximate=True), pre)
    act_b = act.astype(jnp.bfloat16)
    dact = lax.dot_general(cot, upper, (((1,), (1,)), ((), ())), preferred_element_type=jnp.float32)
    dpre = pull(dact)[0].astype(jnp.bfloat16)
    down_terms = lax.dot_general(
        normed, dpre, (((0,), (0,)), ((), ())), preferred_element_type=jnp.float32
    )
    up_terms = lax.dot_general(
        act_b, cot, (((0,), (0,)), ((), ())), preferred_element_type=jnp.float32
    )
    down_grad, up_grad = (
        lax.psum_scatter(down_terms, "dp", scatter_dimension=0, tiled=True),
        lax.psum_scatter(up_terms, "dp", scatter_dimension=1, tiled=True),
    )
    dnorm = (
        lax.dot_general(dpre, down, (((1,), (1,)), ((), ())), preferred_element_type=jnp.float32)
        * scale[None, :]
    )
    inner = jnp.mean(dnorm * unit, axis=1, keepdims=True)
    dx = (cot.astype(jnp.float32) + (dnorm - unit * inner) / rms).astype(jnp.bfloat16)
    before = from_behind(dx, "pipe", -1)
    return (before[None], down_grad[None], up_grad[None])


def solution(mesh):
    in_specs = (
        P("pipe", "dp", None),
        P("pipe", "dp", None),
        P("pipe", None, None),
        P("pipe", None, None),
        P("pipe", None),
    )
    out_specs = (P("pipe", "dp", None), P("pipe", "dp", None), P("pipe", None, "dp"))
    return jax.shard_map(
        per_device, mesh=mesh, in_specs=in_specs, out_specs=out_specs, check_vma=False
    )
```

profile of v0, /device:TPU:1, one launch (start us, length us, event | category | flops | bytes accessed | tf_op | source)
XLA Modules:
  0.0 144.5 jit_solution(10220265128975432319)
XLA Ops:
  7.2 0.0 copy-start
  7.2 0.0 reduce-scatter.3.cloned.1.call-start
  7.2 3.2 %collective-permute-start = (bf16[128,4096]{1,0:T(8,128)(2,1)}, bf16[128,4096]{1,0:T(8,128)(2,1)S(1)}, u32[]{:S(2)}, u32[]{:S(2)}) collective-permute-start(bf16[128,4096]{1,0:T(8,128)(2,1)} %bitcast.28), channel_id=1, source_target_pairs={{0,16},{4,20},{8,24},{12,28},{16,0},{20,4},{24,8},{28,12},{1,17},{... | collective-permute-start | bytes 3145736 | tf_op jit(solution)/shard_map/ppermute | solution.py:8
  10.4 45.6 %collective-permute-done = bf16[128,4096]{1,0:T(8,128)(2,1)S(1)} collective-permute-done((bf16[128,4096]{1,0:T(8,128)(2,1)}, bf16[128,4096]{1,0:T(8,128)(2,1)S(1)}, u32[]{:S(2)}, u32[]{:S(2)}) %collective-permute-start) | collective-permute-done | bytes 1048608 | tf_op jit(solution)/shard_map/ppermute | solution.py:8
  56.0 0.3 fusion
  56.3 0.0 copy-done
  56.3 0.0 copy-start.1
  56.3 0.0 copy-start.2
  56.3 1.4 fusion.2
  57.7 0.0 copy-done.1
  57.7 0.2 copy-done.2
  57.9 0.0 copy-start.3
  57.9 0.4 fusion.16
  58.3 0.3 copy-done.3
  58.6 1.9 %fusion.9 = f32[4096,128]{1,0:T(8,128)} fusion(bf16[128,128]{1,0:T(8,128)(2,1)S(1)} %fusion.16, f32[4096]{0:T(1024)S(1)} %bitcast.32, bf16[128,4096]{1,0:T(8,128)(2,1)S(1)} %collective-permute-done, f32[128]{0:T(128)S(1)} %add_sqrt_fusion), kind=kOutput, calls=%fused_computation.15 | convolution fusion | flops 136314880 | bytes 3195392 | tf_op jit(solution)/shard_map/dot_general | solution.py:33
  60.5 0.0 reduce-scatter.3.cloned.1.call-update
  60.5 0.0 reduce-scatter.5.cloned.1.call-start
  60.6 1.8 %fusion.6 = f32[128,4096]{1,0:T(8,128)} fusion(bf16[1,128,4096]{2,1,0:T(8,128)(2,1)S(1)} %copy-done.1, f32[128,128]{1,0:T(8,128)S(1)} %fusion.2), kind=kOutput, calls=%fused_computation.12 | convolution fusion | flops 134365184 | bytes 3211264 | tf_op jit(solution)/shard_map/dot_general | solution.py:36
  62.3 0.0 reduce-scatter.5.cloned.1.call-update
  62.4 0.6 multiply_reduce_fusion
  63.0 0.7 add_convert_fusion
  63.7 3.1 %collective-permute-start.1 = (bf16[128,4096]{1,0:T(8,128)(2,1)S(1)}, bf16[128,4096]{1,0:T(8,128)(2,1)S(1)}, u32[]{:S(2)}, u32[]{:S(2)}) collective-permute-start(bf16[128,4096]{1,0:T(8,128)(2,1)S(1)} %add_convert_fusion), channel_id=1, source_target_pairs={{4,0},{8,4},{12,8},{16,12},{20,16},{24,20},{28,24},{5,1},{9,5},{13... | collective-permute-start | bytes 3145736 | tf_op jit(solution)/shard_map/ppermute | solution.py:14
  66.8 13.4 %collective-permute-done.1 = bf16[128,4096]{1,0:T(8,128)(2,1)S(1)} collective-permute-done((bf16[128,4096]{1,0:T(8,128)(2,1)S(1)}, bf16[128,4096]{1,0:T(8,128)(2,1)S(1)}, u32[]{:S(2)}, u32[]{:S(2)}) %collective-permute-start.1) | collective-permute-done | bytes 1048608 | tf_op jit(solution)/shard_map/ppermute | solution.py:14
  80.2 17.4 %reduce-scatter.3.cloned.1.call-done = f32[1024,128]{1,0:T(8,128)} async-done(((f32[4096,128]{1,0:T(8,128)}), f32[1024,128]{1,0:T(8,128)}) %reduce-scatter.3.cloned.1.call-update) | async-done | bytes 524304 | tf_op jit(solution)/shard_map/reduce_scatter | solution.py:40
  97.6 39.0 %reduce-scatter.5.cloned.1.call-done = f32[128,1024]{1,0:T(8,128)} async-done(((f32[128,4096]{1,0:T(8,128)}), f32[128,1024]{1,0:T(8,128)}) %reduce-scatter.5.cloned.1.call-update) | async-done | bytes 524304 | tf_op jit(solution)/shard_map/reduce_scatter | solution.py:41
  136.7 1.0 copy.9
  (2 shorter events, 0.0 us)
Async XLA Ops:
  7.2 49.1 %copy-start = (bf16[1,4096,128]{2,1,0:T(8,128)(2,1)S(1)}, bf16[1,4096,128]{2,1,0:T(8,128)(2,1)}, u32[]{:S(2)}) copy-start(bf16[1,4096,128]{2,1,0:T(8,128)(2,1)} %param.7) | copy-start | bytes 3145732
  7.2 90.4 %reduce-scatter.3.cloned.1.call-start = ((), (), s32[]{:S(2)}) async-start(), calls=%async_computation.2 | async-start | bytes 2621440 | tf_op jit(solution)/shard_map/reduce_scatter | solution.py:40
  7.2 48.8 %collective-permute-start = (bf16[128,4096]{1,0:T(8,128)(2,1)}, bf16[128,4096]{1,0:T(8,128)(2,1)S(1)}, u32[]{:S(2)}, u32[]{:S(2)}) collective-permute-start(bf16[128,4096]{1,0:T(8,128)(2,1)} %bitcast.28), channel_id=1, source_target_pairs={{0,16},{4,20},{8,24},{12,28},{16,0},{20,4},{24,8},{28,12},{1,17},{... | collective-permute-start | bytes 3145736 | tf_op jit(solution)/shard_map/ppermute | solution.py:8
  56.3 1.4 copy-start.1
  56.3 1.6 %copy-start.2 = (bf16[1,128,4096]{2,1,0:T(8,128)(2,1)S(1)}, bf16[1,128,4096]{2,1,0:T(8,128)(2,1)}, u32[]{:S(2)}) copy-start(bf16[1,128,4096]{2,1,0:T(8,128)(2,1)} %param.8) | copy-start | bytes 3145732
  57.9 0.7 copy-start.3
  60.5 76.1 %reduce-scatter.5.cloned.1.call-start = ((), (), s32[]{:S(2)}) async-start(), calls=%async_computation.3 | async-start | bytes 2621440 | tf_op jit(solution)/shard_map/reduce_scatter | solution.py:41
  63.7 16.5 %collective-permute-start.1 = (bf16[128,4096]{1,0:T(8,128)(2,1)S(1)}, bf16[128,4096]{1,0:T(8,128)(2,1)S(1)}, u32[]{:S(2)}, u32[]{:S(2)}) collective-permute-start(bf16[128,4096]{1,0:T(8,128)(2,1)S(1)} %add_convert_fusion), channel_id=1, source_target_pairs={{4,0},{8,4},{12,8},{16,12},{20,16},{24,20},{28,24},{5,1},{9,5},{13... | collective-permute-start | bytes 3145736 | tf_op jit(solution)/shard_map/ppermute | solution.py:14
Sparse Core Ops, SparseCore 0:
  60.6 36.9 reduce-scatter.2
  101.4 35.1 reduce-scatter.4
where the time goes:
time: 145 us; the launch traced here: 144 us
  waiting for transfers between devices  115 us (79%)
  between operations  14.1 us (10%)
  starting transfers between devices  6.43 us (4%)
  matrix products  6.08 us (4%)
    ppermute x1, waiting for transfers between devices, swapped(): lax.ppermute(x, axis, [(i, i ^ 1 << stride) for i in range(lax.axis_size(...  45.6 us
    reduce_scatter x1, waiting for transfers between devices, per_device(): lax.psum_scatter(up_terms, 'dp', scatter_dimension=1, tiled=True)  39 us
    reduce_scatter x1, waiting for transfers between devices, per_device(): lax.psum_scatter(down_terms, 'dp', scatter_dimension=0, tiled=True)  17.4 us
    ppermute x1, waiting for transfers between devices, from_behind(): lax.ppermute(value, axis, [(source, source + steps) for source in range(l...  13.4 us
    ppermute x1, starting transfers between devices, swapped(): lax.ppermute(x, axis, [(i, i ^ 1 << stride) for i in range(lax.axis_size(...  3.2 us
    ppermute x1, starting transfers between devices, from_behind(): lax.ppermute(value, axis, [(source, source + steps) for source in range(l...  3.14 us
  transfers between devices with their start and end apart: 4, of which 4 were waited for; matrix products, arithmetic and copies ran while one was open for 2% of the time, Pallas kernels for 0%

commit v1 on v0

v1 whole, which is shorter than its diff:
```python
import jax
import jax.numpy as jnp
from jax import lax
from jax.sharding import PartitionSpec as P

CHUNKS = 4


def exchanged(x, axis, mask):
    return lax.ppermute(x, axis, [(i, i ^ mask) for i in range(lax.axis_size(axis))])


def to_previous(x, axis):
    return lax.ppermute(x, axis, [(i, i - 1) for i in range(1, lax.axis_size(axis))])


def rows_dot(a, b):
    return lax.dot_general(a, b, (((0,), (0,)), ((), ())), preferred_element_type=jnp.float32)


def last_dot(a, b):
    return lax.dot_general(a, b, (((1,), (1,)), ((), ())), preferred_element_type=jnp.float32)


def per_device(stash_held, grad_in, w_down, w_up, gain):
    sections = lax.axis_size("pipe")
    groups = lax.axis_size("dp")
    me = lax.axis_index("dp")
    stash, cot, down, upper, scale = stash_held[0], grad_in[0], w_down[0], w_up[0], gain
    tokens, features = cot.shape
    rank = down.shape[1]
    rows = tokens // CHUNKS
    width = features // groups

    def block(x, k):
        return lax.dynamic_slice_in_dim(x, (me ^ k) * width, width, axis=1)

    parts = [slice(i * rows, (i + 1) * rows) for i in range(CHUNKS)]
    arrivals = [exchanged(stash[part], "pipe", sections // 2) for part in parts]
    cot_all = [block(cot, 0)] + [exchanged(block(cot, k), "dp", k) for k in range(1, groups)]
    dact = last_dot(cot, upper)

    before = []
    packs = []
    for part, saved in zip(parts, arrivals):
        xf = saved.astype(jnp.float32)
        rms = jnp.sqrt(jnp.mean(xf * xf, axis=1, keepdims=True) + 1e-05)
        unit = xf / rms
        normed = (unit * scale).astype(jnp.bfloat16)
        pre = jnp.dot(normed, down, preferred_element_type=jnp.float32)
        act, pull = jax.vjp(lambda value: jax.nn.gelu(value, approximate=True), pre)
        act = act.astype(jnp.bfloat16)
        dpre = pull(dact[part])[0].astype(jnp.bfloat16)
        inner = jnp.sum(dpre.astype(jnp.float32) * pre, axis=1, keepdims=True) / features
        dnorm = last_dot(dpre, down) * scale
        dx = (cot[part].astype(jnp.float32) + (dnorm - unit * inner) / rms).astype(jnp.bfloat16)
        before.append(to_previous(dx, "pipe"))
        pack = [jnp.concatenate([block(normed, k), dpre, act], axis=1) for k in range(groups)]
        packs.append([pack[0]] + [exchanged(pack[k], "dp", k) for k in range(1, groups)])

    every = jnp.concatenate([packs[i][k] for k in range(groups) for i in range(CHUNKS)], axis=0)
    normed_all = every[:, :width]
    dpre_all = every[:, width : width + rank]
    act_all = every[:, width + rank :]
    down_grad = rows_dot(normed_all, dpre_all)
    up_grad = rows_dot(act_all, jnp.concatenate(cot_all, axis=0))
    return (jnp.concatenate(before, axis=0)[None], down_grad[None], up_grad[None])


def solution(mesh):
    in_specs = (
        P("pipe", "dp", None),
        P("pipe", "dp", None),
        P("pipe", None, None),
        P("pipe", None, None),
        P("pipe", None),
    )
    out_specs = (P("pipe", "dp", None), P("pipe", "dp", None), P("pipe", None, "dp"))
    return jax.shard_map(
        per_device, mesh=mesh, in_specs=in_specs, out_specs=out_specs, check_vma=False
    )
```

time: 145 us -> 129 us (0.89)
  waiting for transfers between devices: 115 us -> 67.8 us
  starting transfers between devices: 6.43 us -> 49.7 us
  between operations: 14.1 us -> 0.91 us
    reduce_scatter x2 -> x0, waiting for transfers between devices: 56.5 us -> none  [the longest x1 39 us: per_device(): lax.psum_scatter(up_terms, 'dp', scatter_dimension=1, tiled=True)]
    ppermute x2 -> x23, starting transfers between devices: 6.35 us -> 49.7 us  [the longest x19 28.9 us: exchanged(): lax.ppermute(x, axis, [(i, i ^ mask) for i in range(lax.axis_size(axis))])]
    ppermute x2 -> x23, waiting for transfers between devices: 58.9 us -> 67.8 us  [the longest x19 63.2 us: exchanged(): lax.ppermute(x, axis, [(i, i ^ mask) for i in range(lax.axis_size(axis))])]
    slice x0 -> x1, local copies, waits for them, and re-layouts: none -> 2.23 us  [per_device(): arrivals = [exchanged(stash[part], 'pipe', sections // 2) for part in parts]]
    dot_general x4 -> x7, matrix products: 4.71 us -> 4.69 us  [the longest x2 2.4 us: rows_dot(): lax.dot_general(a, b, (((0,), (0,)), ((), ())), preferred_element_type=jn...]
  transfers between devices with their start and end apart: 4 -> 23, of which waited for: 4 -> 17; matrix products, arithmetic and copies ran while one was open for 2% -> 6% of each run, Pallas kernels for 0% -> 0%
where the time goes in v1:
time: 129 us
  waiting for transfers between devices  67.8 us (53%)
  starting transfers between devices  49.7 us (39%)
  matrix products  5.99 us (5%)
  local copies, waits for them, and re-layouts  2.51 us (2%)
  other arithmetic  2.21 us (2%)
    ppermute x19, waiting for transfers between devices, exchanged(): lax.ppermute(x, axis, [(i, i ^ mask) for i in range(lax.axis_size(axis))])  63.2 us
    ppermute x19, starting transfers between devices, exchanged(): lax.ppermute(x, axis, [(i, i ^ mask) for i in range(lax.axis_size(axis))])  28.9 us
    ppermute x4, starting transfers between devices, to_previous(): lax.ppermute(x, axis, [(i, i - 1) for i in range(1, lax.axis_size(axis))])  20.8 us
    ppermute x4, waiting for transfers between devices, to_previous(): lax.ppermute(x, axis, [(i, i - 1) for i in range(1, lax.axis_size(axis))])  4.66 us
  transfers between devices with their start and end apart: 23, of which 17 were waited for; matrix products, arithmetic and copies ran while one was open for 6% of the time, Pallas kernels for 0%

profile of v1, /device:TPU:1, one launch (start us, length us, event | category | flops | bytes accessed | tf_op | source)
XLA Modules:
  0.0 129.2 jit_solution(8978797413257722274)
XLA Ops:
  0.7 2.2 %slice_bitcast_fusion.3 = (bf16[32,4096]{1,0:T(8,128)(2,1)}, bf16[32,4096]{1,0:T(8,128)(2,1)}, bf16[32,4096]{1,0:T(8,128)(2,1)S(1)}, bf16[32,4096]{1,0:T(8,128)(2,1)}) fusion(bf16[1,128,4096]{2,1,0:T(8,128)(2,1)} %param.5), kind=kLoop, calls=%fused_computation.61 | loop fusion | bytes 2097152 | tf_op jit(solution)/shard_map/slice | solution.py:39
  2.9 3.1 %collective-permute-start.6 = (bf16[32,4096]{1,0:T(8,128)(2,1)S(1)}, bf16[32,4096]{1,0:T(8,128)(2,1)S(1)}, u32[]{:S(2)}, u32[]{:S(2)}) collective-permute-start(bf16[32,4096]{1,0:T(8,128)(2,1)S(1)} %get-tuple-element.17), channel_id=1, source_target_pairs={{0,16},{4,20},{8,24},{12,28},{16,0},{20,4},{24,8},{28,12},{1,17},{... | collective-permute-start | bytes 786440 | tf_op jit(solution)/shard_map/ppermute | solution.py:10
  6.1 2.3 %collective-permute-start.2 = (bf16[32,4096]{1,0:T(8,128)(2,1)}, bf16[32,4096]{1,0:T(8,128)(2,1)S(1)}, u32[]{:S(2)}, u32[]{:S(2)}) collective-permute-start(bf16[32,4096]{1,0:T(8,128)(2,1)} %get-tuple-element.16), channel_id=1, source_target_pairs={{0,16},{4,20},{8,24},{12,28},{16,0},{20,4},{24,8},{28,12},{1,17},{... | collective-permute-start | bytes 786440 | tf_op jit(solution)/shard_map/ppermute | solution.py:10
  8.5 2.2 %collective-permute-start.22 = (bf16[128,1024]{1,0:T(8,128)(2,1)S(1)}, bf16[128,1024]{1,0:T(8,128)(2,1)S(1)}, u32[]{:S(2)}, u32[]{:S(2)}) collective-permute-start(bf16[128,1024]{1,0:T(8,128)(2,1)S(1)} %get-tuple-element.13), channel_id=1, source_target_pairs={{0,3},{1,2},{2,1},{3,0},{4,7},{5,6},{6,5},{7,4},{8,11},{9,10},{10,... | collective-permute-start | bytes 786440 | tf_op jit(solution)/shard_map/ppermute | solution.py:10
  11.2 28.9 %collective-permute-done = bf16[32,4096]{1,0:T(8,128)(2,1)S(1)} collective-permute-done((bf16[32,4096]{1,0:T(8,128)(2,1)}, bf16[32,4096]{1,0:T(8,128)(2,1)S(1)}, u32[]{:S(2)}, u32[]{:S(2)}) %collective-permute-start) | collective-permute-done | bytes 262176 | tf_op jit(solution)/shard_map/ppermute | solution.py:10
  41.3 4.4 %collective-permute-done.2 = bf16[32,4096]{1,0:T(8,128)(2,1)S(1)} collective-permute-done((bf16[32,4096]{1,0:T(8,128)(2,1)}, bf16[32,4096]{1,0:T(8,128)(2,1)S(1)}, u32[]{:S(2)}, u32[]{:S(2)}) %collective-permute-start.2) | collective-permute-done | bytes 262176 | tf_op jit(solution)/shard_map/ppermute | solution.py:10
  46.9 4.5 %collective-permute-done.4 = bf16[32,4096]{1,0:T(8,128)(2,1)S(1)} collective-permute-done((bf16[32,4096]{1,0:T(8,128)(2,1)}, bf16[32,4096]{1,0:T(8,128)(2,1)S(1)}, u32[]{:S(2)}, u32[]{:S(2)}) %collective-permute-start.4) | collective-permute-done | bytes 262176 | tf_op jit(solution)/shard_map/ppermute | solution.py:10
  54.0 3.1 %collective-permute-start.7 = (bf16[32,4096]{1,0:T(8,128)(2,1)S(1)}, bf16[32,4096]{1,0:T(8,128)(2,1)S(1)}, u32[]{:S(2)}, u32[]{:S(2)}) collective-permute-start(bf16[32,4096]{1,0:T(8,128)(2,1)S(1)} %fusion.27), channel_id=1, source_target_pairs={{4,0},{8,4},{12,8},{16,12},{20,16},{24,20},{28,24},{5,1},{9,5},{13... | collective-permute-start | bytes 786440 | tf_op jit(solution)/shard_map/ppermute | solution.py:14
  57.2 1.3 %collective-permute-start.8 = (bf16[32,1280]{1,0:T(8,128)(2,1)S(1)}, bf16[32,1280]{1,0:T(8,128)(2,1)S(1)}, u32[]{:S(2)}, u32[]{:S(2)}) collective-permute-start(bf16[32,1280]{1,0:T(8,128)(2,1)S(1)} %get-tuple-element.57), channel_id=1, source_target_pairs={{0,1},{1,0},{2,3},{3,2},{4,5},{5,4},{6,7},{7,6},{8,9},{9,8},{10,11... | collective-permute-start | bytes 245768 | tf_op jit(solution)/shard_map/ppermute | solution.py:10
  60.1 1.4 %collective-permute-done.8 = bf16[32,1280]{1,0:T(8,128)(2,1)S(1)} collective-permute-done((bf16[32,1280]{1,0:T(8,128)(2,1)S(1)}, bf16[32,1280]{1,0:T(8,128)(2,1)S(1)}, u32[]{:S(2)}, u32[]{:S(2)}) %collective-permute-start.8) | collective-permute-done | bytes 81952 | tf_op jit(solution)/shard_map/ppermute | solution.py:10
  62.7 2.4 %collective-permute-done.9 = bf16[32,1280]{1,0:T(8,128)(2,1)S(1)} collective-permute-done((bf16[32,1280]{1,0:T(8,128)(2,1)S(1)}, bf16[32,1280]{1,0:T(8,128)(2,1)S(1)}, u32[]{:S(2)}, u32[]{:S(2)}) %collective-permute-start.9) | collective-permute-done | bytes 81952 | tf_op jit(solution)/shard_map/ppermute | solution.py:10
  66.3 2.0 %collective-permute-done.10 = bf16[32,1280]{1,0:T(8,128)(2,1)S(1)} collective-permute-done((bf16[32,1280]{1,0:T(8,128)(2,1)S(1)}, bf16[32,1280]{1,0:T(8,128)(2,1)S(1)}, u32[]{:S(2)}, u32[]{:S(2)}) %collective-permute-start.10) | collective-permute-done | bytes 81952 | tf_op jit(solution)/shard_map/ppermute | solution.py:10
  69.6 2.0 %collective-permute-done.11 = bf16[32,1280]{1,0:T(8,128)(2,1)S(1)} collective-permute-done((bf16[32,1280]{1,0:T(8,128)(2,1)S(1)}, bf16[32,1280]{1,0:T(8,128)(2,1)S(1)}, u32[]{:S(2)}, u32[]{:S(2)}) %collective-permute-start.11) | collective-permute-done | bytes 81952 | tf_op jit(solution)/shard_map/ppermute | solution.py:10
  73.0 2.0 %collective-permute-done.12 = bf16[32,1280]{1,0:T(8,128)(2,1)S(1)} collective-permute-done((bf16[32,1280]{1,0:T(8,128)(2,1)S(1)}, bf16[32,1280]{1,0:T(8,128)(2,1)S(1)}, u32[]{:S(2)}, u32[]{:S(2)}) %collective-permute-start.12) | collective-permute-done | bytes 81952 | tf_op jit(solution)/shard_map/ppermute | solution.py:10
  74.9 1.3 collective-permute-start.13
  76.2 2.5 %collective-permute-done.13 = bf16[32,1280]{1,0:T(8,128)(2,1)S(1)} collective-permute-done((bf16[32,1280]{1,0:T(8,128)(2,1)S(1)}, bf16[32,1280]{1,0:T(8,128)(2,1)S(1)}, u32[]{:S(2)}, u32[]{:S(2)}) %collective-permute-start.13) | collective-permute-done | bytes 81952 | tf_op jit(solution)/shard_map/ppermute | solution.py:10
  78.8 1.3 collective-permute-start.14
  80.1 2.0 %collective-permute-done.14 = bf16[32,1280]{1,0:T(8,128)(2,1)S(1)} collective-permute-done((bf16[32,1280]{1,0:T(8,128)(2,1)S(1)}, bf16[32,1280]{1,0:T(8,128)(2,1)S(1)}, u32[]{:S(2)}, u32[]{:S(2)}) %collective-permute-start.14) | collective-permute-done | bytes 81952 | tf_op jit(solution)/shard_map/ppermute | solution.py:10
  83.3 2.0 %collective-permute-done.15 = bf16[32,1280]{1,0:T(8,128)(2,1)S(1)} collective-permute-done((bf16[32,1280]{1,0:T(8,128)(2,1)S(1)}, bf16[32,1280]{1,0:T(8,128)(2,1)S(1)}, u32[]{:S(2)}, u32[]{:S(2)}) %collective-permute-start.15) | collective-permute-done | bytes 81952 | tf_op jit(solution)/shard_map/ppermute | solution.py:10
  85.3 2.2 %collective-permute-start.16 = (bf16[32,1280]{1,0:T(8,128)(2,1)S(1)}, bf16[32,1280]{1,0:T(8,128)(2,1)S(1)}, u32[]{:S(2)}, u32[]{:S(2)}) collective-permute-start(bf16[32,1280]{1,0:T(8,128)(2,1)S(1)} %get-tuple-element.56), channel_id=1, source_target_pairs={{0,3},{1,2},{2,1},{3,0},{4,7},{5,6},{6,5},{7,4},{8,11},{9,10},{10,... | collective-permute-start | bytes 245768 | tf_op jit(solution)/shard_map/ppermute | solution.py:10
  87.6 2.0 %collective-permute-done.16 = bf16[32,1280]{1,0:T(8,128)(2,1)S(1)} collective-permute-done((bf16[32,1280]{1,0:T(8,128)(2,1)S(1)}, bf16[32,1280]{1,0:T(8,128)(2,1)S(1)}, u32[]{:S(2)}, u32[]{:S(2)}) %collective-permute-start.16) | collective-permute-done | bytes 81952 | tf_op jit(solution)/shard_map/ppermute | solution.py:10
  89.5 2.2 %collective-permute-start.17 = (bf16[32,1280]{1,0:T(8,128)(2,1)S(1)}, bf16[32,1280]{1,0:T(8,128)(2,1)S(1)}, u32[]{:S(2)}, u32[]{:S(2)}) collective-permute-start(bf16[32,1280]{1,0:T(8,128)(2,1)S(1)} %get-tuple-element.52), channel_id=1, source_target_pairs={{0,3},{1,2},{2,1},{3,0},{4,7},{5,6},{6,5},{7,4},{8,11},{9,10},{10,... | collective-permute-start | bytes 245768 | tf_op jit(solution)/shard_map/ppermute | solution.py:10
  91.8 2.0 %collective-permute-done.17 = bf16[32,1280]{1,0:T(8,128)(2,1)S(1)} collective-permute-done((bf16[32,1280]{1,0:T(8,128)(2,1)S(1)}, bf16[32,1280]{1,0:T(8,128)(2,1)S(1)}, u32[]{:S(2)}, u32[]{:S(2)}) %collective-permute-start.17) | collective-permute-done | bytes 81952 | tf_op jit(solution)/shard_map/ppermute | solution.py:10
  93.7 2.2 %collective-permute-start.18 = (bf16[32,1280]{1,0:T(8,128)(2,1)S(1)}, bf16[32,1280]{1,0:T(8,128)(2,1)S(1)}, u32[]{:S(2)}, u32[]{:S(2)}) collective-permute-start(bf16[32,1280]{1,0:T(8,128)(2,1)S(1)} %get-tuple-element.48), channel_id=1, source_target_pairs={{0,3},{1,2},{2,1},{3,0},{4,7},{5,6},{6,5},{7,4},{8,11},{9,10},{10,... | collective-permute-start | bytes 245768 | tf_op jit(solution)/shard_map/ppermute | solution.py:10
  96.0 2.9 %collective-permute-done.18 = bf16[32,1280]{1,0:T(8,128)(2,1)S(1)} collective-permute-done((bf16[32,1280]{1,0:T(8,128)(2,1)S(1)}, bf16[32,1280]{1,0:T(8,128)(2,1)S(1)}, u32[]{:S(2)}, u32[]{:S(2)}) %collective-permute-start.18) | collective-permute-done | bytes 81952 | tf_op jit(solution)/shard_map/ppermute | solution.py:10
  98.8 2.2 %collective-permute-start.19 = (bf16[32,1280]{1,0:T(8,128)(2,1)S(1)}, bf16[32,1280]{1,0:T(8,128)(2,1)S(1)}, u32[]{:S(2)}, u32[]{:S(2)}) collective-permute-start(bf16[32,1280]{1,0:T(8,128)(2,1)S(1)} %get-tuple-element.44), channel_id=1, source_target_pairs={{0,3},{1,2},{2,1},{3,0},{4,7},{5,6},{6,5},{7,4},{8,11},{9,10},{10,... | collective-permute-start | bytes 245768 | tf_op jit(solution)/shard_map/ppermute | solution.py:10
  101.0 2.3 %collective-permute-done.19 = bf16[32,1280]{1,0:T(8,128)(2,1)S(1)} collective-permute-done((bf16[32,1280]{1,0:T(8,128)(2,1)S(1)}, bf16[32,1280]{1,0:T(8,128)(2,1)S(1)}, u32[]{:S(2)}, u32[]{:S(2)}) %collective-permute-start.19) | collective-permute-done | bytes 81952 | tf_op jit(solution)/shard_map/ppermute | solution.py:10
  103.3 13.8 %collective-permute-start.5 = (bf16[32,4096]{1,0:T(8,128)(2,1)S(1)}, bf16[32,4096]{1,0:T(8,128)(2,1)S(1)}, u32[]{:S(2)}, u32[]{:S(2)}) collective-permute-start(bf16[32,4096]{1,0:T(8,128)(2,1)S(1)} %fusion.28), channel_id=1, source_target_pairs={{4,0},{8,4},{12,8},{16,12},{20,16},{24,20},{28,24},{5,1},{9,5},{13... | collective-permute-start | bytes 786440 | tf_op jit(solution)/shard_map/ppermute | solution.py:14
  117.2 1.9 %collective-permute-start.3 = (bf16[32,4096]{1,0:T(8,128)(2,1)S(1)}, bf16[32,4096]{1,0:T(8,128)(2,1)S(1)}, u32[]{:S(2)}, u32[]{:S(2)}) collective-permute-start(bf16[32,4096]{1,0:T(8,128)(2,1)S(1)} %fusion.29), channel_id=1, source_target_pairs={{4,0},{8,4},{12,8},{16,12},{20,16},{24,20},{28,24},{5,1},{9,5},{13... | collective-permute-start | bytes 786440 | tf_op jit(solution)/shard_map/ppermute | solution.py:14
  119.1 1.9 %collective-permute-start.1 = (bf16[32,4096]{1,0:T(8,128)(2,1)S(1)}, bf16[32,4096]{1,0:T(8,128)(2,1)S(1)}, u32[]{:S(2)}, u32[]{:S(2)}) collective-permute-start(bf16[32,4096]{1,0:T(8,128)(2,1)S(1)} %fusion.30), channel_id=1, source_target_pairs={{4,0},{8,4},{12,8},{16,12},{20,16},{24,20},{28,24},{5,1},{9,5},{13... | collective-permute-start | bytes 786440 | tf_op jit(solution)/shard_map/ppermute | solution.py:14
  123.5 1.8 %collective-permute-done.3 = bf16[32,4096]{1,0:T(8,128)(2,1)S(1)} collective-permute-done((bf16[32,4096]{1,0:T(8,128)(2,1)S(1)}, bf16[32,4096]{1,0:T(8,128)(2,1)S(1)}, u32[]{:S(2)}, u32[]{:S(2)}) %collective-permute-start.3) | collective-permute-done | bytes 262176 | tf_op jit(solution)/shard_map/ppermute | solution.py:14
  125.3 2.8 %collective-permute-done.1 = bf16[32,4096]{1,0:T(8,128)(2,1)S(1)} collective-permute-done((bf16[32,4096]{1,0:T(8,128)(2,1)S(1)}, bf16[32,4096]{1,0:T(8,128)(2,1)S(1)}, u32[]{:S(2)}, u32[]{:S(2)}) %collective-permute-start.1) | collective-permute-done | bytes 262176 | tf_op jit(solution)/shard_map/ppermute | solution.py:14
  (67 shorter events, 16.9 us)
Async XLA Ops:
  0.6 51.5 %copy-start = (bf16[1,4096,128]{2,1,0:T(8,128)(2,1)S(1)}, bf16[1,4096,128]{2,1,0:T(8,128)(2,1)}, u32[]{:S(2)}) copy-start(bf16[1,4096,128]{2,1,0:T(8,128)(2,1)} %param.7) | copy-start | bytes 3145732
  0.6 7.8 %copy-start.1 = (bf16[1,128,4096]{2,1,0:T(8,128)(2,1)S(1)}, bf16[1,128,4096]{2,1,0:T(8,128)(2,1)}, u32[]{:S(2)}) copy-start(bf16[1,128,4096]{2,1,0:T(8,128)(2,1)} %param.6) | copy-start | bytes 3145732
  2.9 48.7 %collective-permute-start.6 = (bf16[32,4096]{1,0:T(8,128)(2,1)S(1)}, bf16[32,4096]{1,0:T(8,128)(2,1)S(1)}, u32[]{:S(2)}, u32[]{:S(2)}) collective-permute-start(bf16[32,4096]{1,0:T(8,128)(2,1)S(1)} %get-tuple-element.17), channel_id=1, source_target_pairs={{0,16},{4,20},{8,24},{12,28},{16,0},{20,4},{24,8},{28,12},{1,17},{... | collective-permute-start | bytes 786440 | tf_op jit(solution)/shard_map/ppermute | solution.py:10
  6.0 34.1 %collective-permute-start = (bf16[32,4096]{1,0:T(8,128)(2,1)}, bf16[32,4096]{1,0:T(8,128)(2,1)S(1)}, u32[]{:S(2)}, u32[]{:S(2)}) collective-permute-start(bf16[32,4096]{1,0:T(8,128)(2,1)} %get-tuple-element.15), channel_id=1, source_target_pairs={{0,16},{4,20},{8,24},{12,28},{16,0},{20,4},{24,8},{28,12},{1,17},{... | collective-permute-start | bytes 786440 | tf_op jit(solution)/shard_map/ppermute | solution.py:10
  6.1 39.7 %collective-permute-start.2 = (bf16[32,4096]{1,0:T(8,128)(2,1)}, bf16[32,4096]{1,0:T(8,128)(2,1)S(1)}, u32[]{:S(2)}, u32[]{:S(2)}) collective-permute-start(bf16[32,4096]{1,0:T(8,128)(2,1)} %get-tuple-element.16), channel_id=1, source_target_pairs={{0,16},{4,20},{8,24},{12,28},{16,0},{20,4},{24,8},{28,12},{1,17},{... | collective-permute-start | bytes 786440 | tf_op jit(solution)/shard_map/ppermute | solution.py:10
  8.4 43.0 %collective-permute-start.4 = (bf16[32,4096]{1,0:T(8,128)(2,1)}, bf16[32,4096]{1,0:T(8,128)(2,1)S(1)}, u32[]{:S(2)}, u32[]{:S(2)}) collective-permute-start(bf16[32,4096]{1,0:T(8,128)(2,1)} %get-tuple-element.18), channel_id=1, source_target_pairs={{0,16},{4,20},{8,24},{12,28},{16,0},{20,4},{24,8},{28,12},{1,17},{... | collective-permute-start | bytes 786440 | tf_op jit(solution)/shard_map/ppermute | solution.py:10
  8.4 2.3 %copy-start.2 = (bf16[1,128,4096]{2,1,0:T(8,128)(2,1)S(1)}, bf16[1,128,4096]{2,1,0:T(8,128)(2,1)}, u32[]{:S(2)}) copy-start(bf16[1,128,4096]{2,1,0:T(8,128)(2,1)} %param.8) | copy-start | bytes 3145732
  8.5 43.2 %copy-start.3 = (f32[1,4096]{1,0:T(1,128)S(1)}, f32[1,4096]{1,0:T(1,128)}, u32[]{:S(2)}) copy-start(f32[1,4096]{1,0:T(1,128)} %param.9) | copy-start | bytes 49156
  8.5 108.6 %collective-permute-start.22 = (bf16[128,1024]{1,0:T(8,128)(2,1)S(1)}, bf16[128,1024]{1,0:T(8,128)(2,1)S(1)}, u32[]{:S(2)}, u32[]{:S(2)}) collective-permute-start(bf16[128,1024]{1,0:T(8,128)(2,1)S(1)} %get-tuple-element.13), channel_id=1, source_target_pairs={{0,3},{1,2},{2,1},{3,0},{4,7},{5,6},{6,5},{7,4},{8,11},{9,10},{10,... | collective-permute-start | bytes 786440 | tf_op jit(solution)/shard_map/ppermute | solution.py:10
  40.1 79.0 %collective-permute-start.21 = (bf16[128,1024]{1,0:T(8,128)(2,1)S(1)}, bf16[128,1024]{1,0:T(8,128)(2,1)S(1)}, u32[]{:S(2)}, u32[]{:S(2)}) collective-permute-start(bf16[128,1024]{1,0:T(8,128)(2,1)S(1)} %get-tuple-element.14), channel_id=1, source_target_pairs={{0,2},{1,3},{2,0},{3,1},{4,6},{5,7},{6,4},{7,5},{8,10},{9,11},{10,... | collective-permute-start | bytes 786440 | tf_op jit(solution)/shard_map/ppermute | solution.py:10
  45.8 76.6 %collective-permute-start.20 = (bf16[128,1024]{1,0:T(8,128)(2,1)S(1)}, bf16[128,1024]{1,0:T(8,128)(2,1)S(1)}, u32[]{:S(2)}, u32[]{:S(2)}) collective-permute-start(bf16[128,1024]{1,0:T(8,128)(2,1)S(1)} %get-tuple-element.12), channel_id=1, source_target_pairs={{0,1},{1,0},{2,3},{3,2},{4,5},{5,4},{6,7},{7,6},{8,9},{9,8},{10,11... | collective-permute-start | bytes 786440 | tf_op jit(solution)/shard_map/ppermute | solution.py:10
  54.0 69.4 %collective-permute-start.7 = (bf16[32,4096]{1,0:T(8,128)(2,1)S(1)}, bf16[32,4096]{1,0:T(8,128)(2,1)S(1)}, u32[]{:S(2)}, u32[]{:S(2)}) collective-permute-start(bf16[32,4096]{1,0:T(8,128)(2,1)S(1)} %fusion.27), channel_id=1, source_target_pairs={{4,0},{8,4},{12,8},{16,12},{20,16},{24,20},{28,24},{5,1},{9,5},{13... | collective-permute-start | bytes 786440 | tf_op jit(solution)/shard_map/ppermute | solution.py:14
  57.2 4.2 %collective-permute-start.8 = (bf16[32,1280]{1,0:T(8,128)(2,1)S(1)}, bf16[32,1280]{1,0:T(8,128)(2,1)S(1)}, u32[]{:S(2)}, u32[]{:S(2)}) collective-permute-start(bf16[32,1280]{1,0:T(8,128)(2,1)S(1)} %get-tuple-element.57), channel_id=1, source_target_pairs={{0,1},{1,0},{2,3},{3,2},{4,5},{5,4},{6,7},{7,6},{8,9},{9,8},{10,11... | collective-permute-start | bytes 245768 | tf_op jit(solution)/shard_map/ppermute | solution.py:10
  61.4 3.6 %collective-permute-start.9 = (bf16[32,1280]{1,0:T(8,128)(2,1)S(1)}, bf16[32,1280]{1,0:T(8,128)(2,1)S(1)}, u32[]{:S(2)}, u32[]{:S(2)}) collective-permute-start(bf16[32,1280]{1,0:T(8,128)(2,1)S(1)} %get-tuple-element.53), channel_id=1, source_target_pairs={{0,1},{1,0},{2,3},{3,2},{4,5},{5,4},{6,7},{7,6},{8,9},{9,8},{10,11... | collective-permute-start | bytes 245768 | tf_op jit(solution)/shard_map/ppermute | solution.py:10
  65.1 3.3 %collective-permute-start.10 = (bf16[32,1280]{1,0:T(8,128)(2,1)S(1)}, bf16[32,1280]{1,0:T(8,128)(2,1)S(1)}, u32[]{:S(2)}, u32[]{:S(2)}) collective-permute-start(bf16[32,1280]{1,0:T(8,128)(2,1)S(1)} %get-tuple-element.49), channel_id=1, source_target_pairs={{0,1},{1,0},{2,3},{3,2},{4,5},{5,4},{6,7},{7,6},{8,9},{9,8},{10,11... | collective-permute-start | bytes 245768 | tf_op jit(solution)/shard_map/ppermute | solution.py:10
  68.4 3.3 %collective-permute-start.11 = (bf16[32,1280]{1,0:T(8,128)(2,1)S(1)}, bf16[32,1280]{1,0:T(8,128)(2,1)S(1)}, u32[]{:S(2)}, u32[]{:S(2)}) collective-permute-start(bf16[32,1280]{1,0:T(8,128)(2,1)S(1)} %get-tuple-element.45), channel_id=1, source_target_pairs={{0,1},{1,0},{2,3},{3,2},{4,5},{5,4},{6,7},{7,6},{8,9},{9,8},{10,11... | collective-permute-start | bytes 245768 | tf_op jit(solution)/shard_map/ppermute | solution.py:10
  71.7 3.3 %collective-permute-start.12 = (bf16[32,1280]{1,0:T(8,128)(2,1)S(1)}, bf16[32,1280]{1,0:T(8,128)(2,1)S(1)}, u32[]{:S(2)}, u32[]{:S(2)}) collective-permute-start(bf16[32,1280]{1,0:T(8,128)(2,1)S(1)} %get-tuple-element.58), channel_id=1, source_target_pairs={{0,2},{1,3},{2,0},{3,1},{4,6},{5,7},{6,4},{7,5},{8,10},{9,11},{10,... | collective-permute-start | bytes 245768 | tf_op jit(solution)/shard_map/ppermute | solution.py:10
  74.9 3.8 %collective-permute-start.13 = (bf16[32,1280]{1,0:T(8,128)(2,1)S(1)}, bf16[32,1280]{1,0:T(8,128)(2,1)S(1)}, u32[]{:S(2)}, u32[]{:S(2)}) collective-permute-start(bf16[32,1280]{1,0:T(8,128)(2,1)S(1)} %get-tuple-element.54), channel_id=1, source_target_pairs={{0,2},{1,3},{2,0},{3,1},{4,6},{5,7},{6,4},{7,5},{8,10},{9,11},{10,... | collective-permute-start | bytes 245768 | tf_op jit(solution)/shard_map/ppermute | solution.py:10
  78.8 3.3 %collective-permute-start.14 = (bf16[32,1280]{1,0:T(8,128)(2,1)S(1)}, bf16[32,1280]{1,0:T(8,128)(2,1)S(1)}, u32[]{:S(2)}, u32[]{:S(2)}) collective-permute-start(bf16[32,1280]{1,0:T(8,128)(2,1)S(1)} %get-tuple-element.50), channel_id=1, source_target_pairs={{0,2},{1,3},{2,0},{3,1},{4,6},{5,7},{6,4},{7,5},{8,10},{9,11},{10,... | collective-permute-start | bytes 245768 | tf_op jit(solution)/shard_map/ppermute | solution.py:10
  82.1 3.3 %collective-permute-start.15 = (bf16[32,1280]{1,0:T(8,128)(2,1)S(1)}, bf16[32,1280]{1,0:T(8,128)(2,1)S(1)}, u32[]{:S(2)}, u32[]{:S(2)}) collective-permute-start(bf16[32,1280]{1,0:T(8,128)(2,1)S(1)} %get-tuple-element.46), channel_id=1, source_target_pairs={{0,2},{1,3},{2,0},{3,1},{4,6},{5,7},{6,4},{7,5},{8,10},{9,11},{10,... | collective-permute-start | bytes 245768 | tf_op jit(solution)/shard_map/ppermute | solution.py:10
  85.3 4.2 %collective-permute-start.16 = (bf16[32,1280]{1,0:T(8,128)(2,1)S(1)}, bf16[32,1280]{1,0:T(8,128)(2,1)S(1)}, u32[]{:S(2)}, u32[]{:S(2)}) collective-permute-start(bf16[32,1280]{1,0:T(8,128)(2,1)S(1)} %get-tuple-element.56), channel_id=1, source_target_pairs={{0,3},{1,2},{2,1},{3,0},{4,7},{5,6},{6,5},{7,4},{8,11},{9,10},{10,... | collective-permute-start | bytes 245768 | tf_op jit(solution)/shard_map/ppermute | solution.py:10
  89.5 4.2 %collective-permute-start.17 = (bf16[32,1280]{1,0:T(8,128)(2,1)S(1)}, bf16[32,1280]{1,0:T(8,128)(2,1)S(1)}, u32[]{:S(2)}, u32[]{:S(2)}) collective-permute-start(bf16[32,1280]{1,0:T(8,128)(2,1)S(1)} %get-tuple-element.52), channel_id=1, source_target_pairs={{0,3},{1,2},{2,1},{3,0},{4,7},{5,6},{6,5},{7,4},{8,11},{9,10},{10,... | collective-permute-start | bytes 245768 | tf_op jit(solution)/shard_map/ppermute | solution.py:10
  93.7 5.1 %collective-permute-start.18 = (bf16[32,1280]{1,0:T(8,128)(2,1)S(1)}, bf16[32,1280]{1,0:T(8,128)(2,1)S(1)}, u32[]{:S(2)}, u32[]{:S(2)}) collective-permute-start(bf16[32,1280]{1,0:T(8,128)(2,1)S(1)} %get-tuple-element.48), channel_id=1, source_target_pairs={{0,3},{1,2},{2,1},{3,0},{4,7},{5,6},{6,5},{7,4},{8,11},{9,10},{10,... | collective-permute-start | bytes 245768 | tf_op jit(solution)/shard_map/ppermute | solution.py:10
  98.8 4.5 %collective-permute-start.19 = (bf16[32,1280]{1,0:T(8,128)(2,1)S(1)}, bf16[32,1280]{1,0:T(8,128)(2,1)S(1)}, u32[]{:S(2)}, u32[]{:S(2)}) collective-permute-start(bf16[32,1280]{1,0:T(8,128)(2,1)S(1)} %get-tuple-element.44), channel_id=1, source_target_pairs={{0,3},{1,2},{2,1},{3,0},{4,7},{5,6},{6,5},{7,4},{8,11},{9,10},{10,... | collective-permute-start | bytes 245768 | tf_op jit(solution)/shard_map/ppermute | solution.py:10
  103.3 20.1 %collective-permute-start.5 = (bf16[32,4096]{1,0:T(8,128)(2,1)S(1)}, bf16[32,4096]{1,0:T(8,128)(2,1)S(1)}, u32[]{:S(2)}, u32[]{:S(2)}) collective-permute-start(bf16[32,4096]{1,0:T(8,128)(2,1)S(1)} %fusion.28), channel_id=1, source_target_pairs={{4,0},{8,4},{12,8},{16,12},{20,16},{24,20},{28,24},{5,1},{9,5},{13... | collective-permute-start | bytes 786440 | tf_op jit(solution)/shard_map/ppermute | solution.py:14
  117.2 8.1 %collective-permute-start.3 = (bf16[32,4096]{1,0:T(8,128)(2,1)S(1)}, bf16[32,4096]{1,0:T(8,128)(2,1)S(1)}, u32[]{:S(2)}, u32[]{:S(2)}) collective-permute-start(bf16[32,4096]{1,0:T(8,128)(2,1)S(1)} %fusion.29), channel_id=1, source_target_pairs={{4,0},{8,4},{12,8},{16,12},{20,16},{24,20},{28,24},{5,1},{9,5},{13... | collective-permute-start | bytes 786440 | tf_op jit(solution)/shard_map/ppermute | solution.py:14
  119.1 9.0 %collective-permute-start.1 = (bf16[32,4096]{1,0:T(8,128)(2,1)S(1)}, bf16[32,4096]{1,0:T(8,128)(2,1)S(1)}, u32[]{:S(2)}, u32[]{:S(2)}) collective-permute-start(bf16[32,4096]{1,0:T(8,128)(2,1)S(1)} %fusion.30), channel_id=1, source_target_pairs={{4,0},{8,4},{12,8},{16,12},{20,16},{24,20},{28,24},{5,1},{9,5},{13... | collective-permute-start | bytes 786440 | tf_op jit(solution)/shard_map/ppermute | solution.py:14

commit v2 on v1

v2 whole, which is shorter than its diff:
```python
import functools
import math
import jax
import jax.numpy as jnp
from jax import lax
from jax.experimental import pallas as pl
from jax.experimental.pallas import tpu as pltpu
from jax.sharding import PartitionSpec as P

SHARES = (2, 2, 2, 2)
AHEAD = 2
LANES = 512
VMEM = pl.BlockSpec(memory_space=pltpu.VMEM)
SMEM = pl.BlockSpec(memory_space=pltpu.SMEM)
ANY = pl.BlockSpec(memory_space=pl.ANY)
PARAMS = pltpu.CompilerParams(vmem_limit_bytes=32 * 1024 * 1024)


def exchanged(x, axis, mask):
    return lax.ppermute(x, axis, [(i, i ^ mask) for i in range(lax.axis_size(axis))])


def to_previous(x, axis):
    return lax.ppermute(x, axis, [(i, i - 1) for i in range(1, lax.axis_size(axis))])


def rows_dot(a, b):
    return lax.dot_general(a, b, (((0,), (0,)), ((), ())), preferred_element_type=jnp.float32)


def last_dot(a, b):
    return lax.dot_general(a, b, (((1,), (1,)), ((), ())), preferred_element_type=jnp.float32)


def gelu_and_slope(x):
    c = math.sqrt(2.0 / math.pi)
    th = jnp.tanh(c * (x + 0.044715 * (x * x * x)))
    slope = 0.5 * (1.0 + th) + 0.5 * x * (1.0 - th * th) * (c * (1.0 + 3.0 * 0.044715 * (x * x)))
    return 0.5 * x * (1.0 + th), slope


def chunk_kernel(groups, start, following, waits, me_ref, saved_ref, cot_ref, dact_ref, down_ref, gain_ref, stash_ref, *refs):
    outs = refs[waits:]
    dx_ref, pack_refs = outs[0], outs[1 : 1 + groups]
    rest = outs[1 + groups :]
    normed_ref = rest[-2] if following else rest[-1]
    copy = None
    if following:
        copy = pltpu.make_async_copy(stash_ref.at[pl.ds(*following)], rest[0], rest[-1])
        copy.start()
    rows, features = saved_ref.shape
    width = features // groups
    rank = down_ref.shape[1]
    lanes = [pl.ds(f, LANES) for f in range(0, features, LANES)]
    total = jnp.zeros((rows, 1), jnp.float32)
    for at in lanes:
        xf = saved_ref[:, at].astype(jnp.float32)
        total += jnp.sum(xf * xf, axis=1, keepdims=True)
    inverse = 1.0 / jnp.sqrt(total / features + 1e-05)
    for at in lanes:
        unit = saved_ref[:, at].astype(jnp.float32) * inverse
        normed_ref[:, at] = (unit * gain_ref[:, at]).astype(jnp.bfloat16)
    pre = jnp.dot(normed_ref[...], down_ref[...], preferred_element_type=jnp.float32)
    act, slope = gelu_and_slope(pre)
    act = act.astype(jnp.bfloat16)
    dpre = (dact_ref[pl.ds(start, rows), :] * slope).astype(jnp.bfloat16)
    inner = jnp.sum(dpre.astype(jnp.float32) * pre, axis=1, keepdims=True) / features
    for k in range(groups):
        at = pl.ds(pl.multiple_of((me_ref[0] ^ k) * width, 128), width)
        pack_refs[k][:, :width] = normed_ref[:, at]
        pack_refs[k][:, width : width + rank] = dpre
        pack_refs[k][:, width + rank :] = act
    pull = inner * inverse
    for at in lanes:
        dnorm = last_dot(dpre, down_ref[at, :]) * gain_ref[:, at]
        xf = saved_ref[:, at].astype(jnp.float32)
        held = cot_ref[pl.ds(start, rows), at].astype(jnp.float32)
        dx_ref[:, at] = (held + (dnorm - xf * pull) * inverse).astype(jnp.bfloat16)
    if copy is not None:
        copy.wait()


def run_chunk(me, saved, cot, dact, down, gain, stash, start, following, waits, groups):
    rows, features = saved.shape
    rank = down.shape[1]
    pack = jax.ShapeDtypeStruct((rows, features // groups + 2 * rank), jnp.bfloat16)
    outs = [jax.ShapeDtypeStruct((rows, features), jnp.bfloat16)] + [pack] * groups
    specs = [VMEM] * len(outs)
    scratch = [pltpu.VMEM((rows, features), jnp.bfloat16)]
    if following:
        outs.append(jax.ShapeDtypeStruct((following[1], features), jnp.bfloat16))
        specs.append(ANY)
        scratch.append(pltpu.SemaphoreType.DMA)
    got = pl.pallas_call(
        functools.partial(chunk_kernel, groups, start, following, len(waits)),
        out_shape=outs,
        in_specs=[SMEM] + [VMEM] * 5 + [ANY] * (1 + len(waits)),
        out_specs=specs,
        scratch_shapes=scratch,
        compiler_params=PARAMS,
    )(me, saved, cot, dact, down, gain, stash, *waits)
    return got[0], got[1 : 1 + groups], got[1 + groups :]


def sum_kernel(groups, spans, first, *refs):
    count = groups * len(spans)
    packs, cots = refs[:count], refs[count : count + groups]
    rest = refs[count + groups :]
    olds, rest = ((), rest) if first else (rest[:2], rest[2:])
    down_ref, up_ref, every, held = rest
    width = held.shape[1]
    rank = up_ref.shape[0]
    at = 0
    for k in range(groups):
        for j, (start, rows) in enumerate(spans):
            every[pl.ds(at, rows), :] = packs[k * len(spans) + j][...]
            held[pl.ds(at, rows), :] = cots[k][pl.ds(start, rows), :]
            at += rows
    down = rows_dot(every[:, :width], every[:, width : width + rank])
    up = rows_dot(every[:, width + rank :], held[...])
    down_ref[...] = down if first else down + olds[0][...]
    up_ref[...] = up if first else up + olds[1][...]


def run_sum(packs, cots, spans, olds, rank):
    groups = len(cots)
    width = cots[0].shape[1]
    depth = groups * sum(rows for _, rows in spans)
    args = [packs[j][k] for k in range(groups) for j in range(len(spans))] + list(cots) + list(olds)
    return pl.pallas_call(
        functools.partial(sum_kernel, groups, spans, not olds),
        out_shape=[
            jax.ShapeDtypeStruct((width, rank), jnp.float32),
            jax.ShapeDtypeStruct((rank, width), jnp.float32),
        ],
        in_specs=[VMEM] * len(args),
        out_specs=[VMEM, VMEM],
        scratch_shapes=[
            pltpu.VMEM((depth, width + 2 * rank), jnp.bfloat16),
            pltpu.VMEM((depth, width), jnp.bfloat16),
        ],
        compiler_params=PARAMS,
    )(*args)


def per_device(stash_held, grad_in, w_down, w_up, gain):
    sections = lax.axis_size("pipe")
    groups = lax.axis_size("dp")
    me = lax.axis_index("dp")
    stash, cot, down, upper = stash_held[0], grad_in[0], w_down[0], w_up[0]
    tokens, features = cot.shape
    rank = down.shape[1]
    width = features // groups
    sizes = [tokens * share // sum(SHARES) for share in SHARES]
    spans = [(sum(sizes[:i]), size) for i, size in enumerate(sizes)]
    chunks = len(spans)

    def held(value):
        return exchanged(value, "pipe", sections // 2)

    arrivals = [held(stash[start : start + rows]) for start, rows in spans[:AHEAD]]
    cot_all = []
    for k in range(groups):
        part = lax.dynamic_slice_in_dim(cot, (me ^ k) * width, width, axis=1)
        cot_all.append(exchanged(part, "dp", k) if k else part)
    dact = last_dot(cot, upper)
    index = jnp.reshape(me.astype(jnp.int32), (1,))

    before, packs, partial = [], [], []
    waits = list(cot_all[1:])
    for i, (start, rows) in enumerate(spans):
        following = spans[i + AHEAD] if i + AHEAD < chunks else None
        if i == chunks - 1:
            partial = run_sum(packs, cot_all, spans[:-1], [], rank)
            waits = list(partial) + before[:-1]
        dx, pack, coming = run_chunk(
            index, arrivals[i], cot, dact, down, gain, stash, start, following, waits, groups
        )
        if following:
            arrivals.append(held(coming[0]))
        packs.append([exchanged(pack[k], "dp", k) if k else pack[k] for k in range(groups)])
        before.append(to_previous(dx, "pipe"))
        waits = list(packs[-1][1:]) + before[-1:]
    down_grad, up_grad = run_sum(packs[-1:], cot_all, spans[-1:], partial, rank)
    return (jnp.concatenate(before, axis=0)[None], down_grad[None], up_grad[None])


def solution(mesh):
    in_specs = (
        P("pipe", "dp", None),
        P("pipe", "dp", None),
        P("pipe", None, None),
        P("pipe", None, None),
        P("pipe", None),
    )
    out_specs = (P("pipe", "dp", None), P("pipe", "dp", None), P("pipe", None, "dp"))
    return jax.shard_map(
        per_device, mesh=mesh, in_specs=in_specs, out_specs=out_specs, check_vma=False
    )
```

time: 129 us -> 78.9 us (0.61)
  waiting for transfers between devices: 67.8 us -> 31.6 us
  starting transfers between devices: 49.7 us -> 37.5 us
  matrix products: 5.99 us -> 0.43 us
  Pallas kernels: 0 us -> 5.44 us
    ppermute x19, waiting for transfers between devices: 63.2 us -> 31.6 us  [exchanged(): lax.ppermute(x, axis, [(i, i ^ mask) for i in range(lax.axis_size(axis))])]
    ppermute x19, starting transfers between devices: 28.9 us -> 21.2 us  [exchanged(): lax.ppermute(x, axis, [(i, i ^ mask) for i in range(lax.axis_size(axis))])]
    pallas_call x0 -> x6, Pallas kernels: none -> 5.44 us  [the longest x4 3.6 us: run_chunk(): pl.pallas_call(functools.partial(chunk_kernel, groups, start, following,...]
    ppermute x4, waiting for transfers between devices: 4.66 us -> 0.01 us  [to_previous(): lax.ppermute(x, axis, [(i, i - 1) for i in range(1, lax.axis_size(axis))])]
    ppermute x4, starting transfers between devices: 20.8 us -> 16.3 us  [to_previous(): lax.ppermute(x, axis, [(i, i - 1) for i in range(1, lax.axis_size(axis))])]
    dot_general x6 -> x0, matrix products: 3.69 us -> none  [the longest x2 2.4 us: rows_dot(): lax.dot_general(a, b, (((0,), (0,)), ((), ())), preferred_element_type=jn...]
    dot_general x5 -> x1, matrix products: 2.3 us -> 0.43 us  [last_dot(): lax.dot_general(a, b, (((1,), (1,)), ((), ())), preferred_element_type=jn...]
  transfers between devices with their start and end apart: 23 -> 23, of which waited for: 17 -> 9; matrix products, arithmetic and copies ran while one was open for 6% -> 1% of each run, Pallas kernels for 0% -> 7%
where the time goes in v2:
time: 78.9 us; the launch traced here: 78.2 us
  starting transfers between devices  37.5 us (48%)
  waiting for transfers between devices  31.6 us (40%)
  Pallas kernels  5.44 us (7%)
  local copies, waits for them, and re-layouts  1.32 us (2%)
  other arithmetic  1.05 us (1%)
  between operations  0.81 us (1%)
    ppermute x19, waiting for transfers between devices, exchanged(): lax.ppermute(x, axis, [(i, i ^ mask) for i in range(lax.axis_size(axis))])  31.6 us
    ppermute x19, starting transfers between devices, exchanged(): lax.ppermute(x, axis, [(i, i ^ mask) for i in range(lax.axis_size(axis))])  21.2 us
    ppermute x4, starting transfers between devices, to_previous(): lax.ppermute(x, axis, [(i, i - 1) for i in range(1, lax.axis_size(axis))])  16.3 us
    pallas_call x4, Pallas kernels, run_chunk(): pl.pallas_call(functools.partial(chunk_kernel, groups, start, following,...  3.6 us
    pallas_call x2, Pallas kernels, run_sum(): pl.pallas_call(functools.partial(sum_kernel, groups, spans, not olds), ou...  1.85 us
  transfers between devices with their start and end apart: 23, of which 9 were waited for; matrix products, arithmetic and copies ran while one was open for 1% of the time, Pallas kernels for 7%

profile of v2, /device:TPU:1, one launch (start us, length us, event | category | flops | bytes accessed | tf_op | source)
XLA Modules:
  0.0 78.2 jit_solution(426759971995685770)
XLA Ops:
  0.7 1.2 %slice_bitcast_fusion.1 = (bf16[32,4096]{1,0:T(8,128)(2,1)S(1)}, bf16[32,4096]{1,0:T(8,128)(2,1)S(1)}) fusion(bf16[1,128,4096]{2,1,0:T(8,128)(2,1)} %param.5), kind=kLoop, calls=%fused_computation.8 | loop fusion | bytes 1048576 | tf_op jit(solution)/shard_map/slice | solution.py:161
  1.9 3.2 %collective-permute-start = (bf16[32,4096]{1,0:T(8,128)(2,1)S(1)}, bf16[32,4096]{1,0:T(8,128)(2,1)S(1)}, u32[]{:S(2)}, u32[]{:S(2)}) collective-permute-start(bf16[32,4096]{1,0:T(8,128)(2,1)S(1)} %get-tuple-element.59), channel_id=1, source_target_pairs={{0,16},{4,20},{8,24},{12,28},{16,0},{20,4},{24,8},{28,12},{1,17},{... | collective-permute-start | bytes 786440 | tf_op jit(solution)/shard_map/ppermute | solution.py:20
  5.2 1.3 %collective-permute-start.2 = (bf16[128,1024]{1,0:T(8,128)(2,1)S(1)}, bf16[128,1024]{1,0:T(8,128)(2,1)S(1)}, u32[]{:S(2)}, u32[]{:S(2)}) collective-permute-start(bf16[128,1024]{1,0:T(8,128)(2,1)S(1)} %get-tuple-element.56), channel_id=1, source_target_pairs={{0,2},{1,3},{2,0},{3,1},{4,6},{5,7},{6,4},{7,5},{8,10},{9,11},{10,... | collective-permute-start | bytes 786440 | tf_op jit(solution)/shard_map/ppermute | solution.py:20
  6.6 1.2 %collective-permute-start.1 = (bf16[128,1024]{1,0:T(8,128)(2,1)S(1)}, bf16[128,1024]{1,0:T(8,128)(2,1)S(1)}, u32[]{:S(2)}, u32[]{:S(2)}) collective-permute-start(bf16[128,1024]{1,0:T(8,128)(2,1)S(1)} %get-tuple-element.57), channel_id=1, source_target_pairs={{0,1},{1,0},{2,3},{3,2},{4,5},{5,4},{6,7},{7,6},{8,9},{9,8},{10,11... | collective-permute-start | bytes 786440 | tf_op jit(solution)/shard_map/ppermute | solution.py:20
  8.0 0.4 fusion.dact_ref
  8.4 13.9 %collective-permute-done.saved_ref = bf16[32,4096]{1,0:T(8,128)(2,1)S(1)} collective-permute-done((bf16[32,4096]{1,0:T(8,128)(2,1)S(1)}, bf16[32,4096]{1,0:T(8,128)(2,1)S(1)}, u32[]{:S(2)}, u32[]{:S(2)}) %collective-permute-start) | collective-permute-done | bytes 262176 | tf_op jit(solution)/shard_map/ppermute | solution.py:20
  22.4 0.9 %shard_map.76 = (bf16[32,4096]{1,0:T(8,128)(2,1)S(1)}, bf16[32,1280]{1,0:T(8,128)(2,1)S(1)}, bf16[32,1280]{1,0:T(8,128)(2,1)S(1)}, bf16[32,1280]{1,0:T(8,128)(2,...) custom-call(s32[1]{0:T(128)} %bitcast.me_ref, bf16[32,4096]{1,0:T(8,128)(2,1)S(1)} %collective-permute-done.saved_ref, ...), custom_call_target="tpu_custom_call" | custom-call | tf_op jit(solution)/shard_map/pallas_call | solution.py:94
  23.3 4.0 %collective-permute-start.4 = (bf16[32,4096]{1,0:T(8,128)(2,1)S(1)}, bf16[32,4096]{1,0:T(8,128)(2,1)S(1)}, u32[]{:S(2)}, u32[]{:S(2)}) collective-permute-start(bf16[32,4096]{1,0:T(8,128)(2,1)S(1)} %get-tuple-element.29), channel_id=1, source_target_pairs={{4,0},{8,4},{12,8},{16,12},{20,16},{24,20},{28,24},{5,1},{9,5},{13... | collective-permute-start | bytes 786440 | tf_op jit(solution)/shard_map/ppermute | solution.py:24
  27.3 1.6 %collective-permute-start.6 = (bf16[32,1280]{1,0:T(8,128)(2,1)S(1)}, bf16[32,1280]{1,0:T(8,128)(2,1)S(1)}, u32[]{:S(2)}, u32[]{:S(2)}) collective-permute-start(bf16[32,1280]{1,0:T(8,128)(2,1)S(1)} %get-tuple-element.30), channel_id=1, source_target_pairs={{0,1},{1,0},{2,3},{3,2},{4,5},{5,4},{6,7},{7,6},{8,9},{9,8},{10,11... | collective-permute-start | bytes 245768 | tf_op jit(solution)/shard_map/ppermute | solution.py:20
  28.9 1.2 %collective-permute-start.7 = (bf16[32,1280]{1,0:T(8,128)(2,1)S(1)}, bf16[32,1280]{1,0:T(8,128)(2,1)S(1)}, u32[]{:S(2)}, u32[]{:S(2)}) collective-permute-start(bf16[32,1280]{1,0:T(8,128)(2,1)S(1)} %get-tuple-element.31), channel_id=1, source_target_pairs={{0,2},{1,3},{2,0},{3,1},{4,6},{5,7},{6,4},{7,5},{8,10},{9,11},{10,... | collective-permute-start | bytes 245768 | tf_op jit(solution)/shard_map/ppermute | solution.py:20
  30.2 1.2 %collective-permute-done.6.refs_0_.refs_3_ = bf16[32,1280]{1,0:T(8,128)(2,1)S(1)} collective-permute-done((bf16[32,1280]{1,0:T(8,128)(2,1)S(1)}, bf16[32,1280]{1,0:T(8,128)(2,1)S(1)}, u32[]{:S(2)}, u32[]{:S(2)}) %collective-permute-start.6) | collective-permute-done | bytes 81952 | tf_op jit(solution)/shard_map/ppermute | solution.py:20
  31.4 2.5 %collective-permute-done.7.refs_1_.refs_6_ = bf16[32,1280]{1,0:T(8,128)(2,1)S(1)} collective-permute-done((bf16[32,1280]{1,0:T(8,128)(2,1)S(1)}, bf16[32,1280]{1,0:T(8,128)(2,1)S(1)}, u32[]{:S(2)}, u32[]{:S(2)}) %collective-permute-start.7) | collective-permute-done | bytes 81952 | tf_op jit(solution)/shard_map/ppermute | solution.py:20
  33.9 1.3 %collective-permute-done.8.refs_2_.refs_9_ = bf16[32,1280]{1,0:T(8,128)(2,1)S(1)} collective-permute-done((bf16[32,1280]{1,0:T(8,128)(2,1)S(1)}, bf16[32,1280]{1,0:T(8,128)(2,1)S(1)}, u32[]{:S(2)}, u32[]{:S(2)}) %collective-permute-start.8) | collective-permute-done | bytes 81952 | tf_op jit(solution)/shard_map/ppermute | solution.py:20
  35.2 0.9 %shard_map.77 = (bf16[32,4096]{1,0:T(8,128)(2,1)S(1)}, bf16[32,1280]{1,0:T(8,128)(2,1)S(1)}, bf16[32,1280]{1,0:T(8,128)(2,1)S(1)}, bf16[32,1280]{1,0:T(8,128)(2,...) custom-call(s32[1]{0:T(128)} %bitcast.me_ref, bf16[32,4096]{1,0:T(8,128)(2,1)S(1)} %collective-permute-done.5.saved_ref, ...), custom_call_target="tpu_custom_call" | custom-call | tf_op jit(solution)/shard_map/pallas_call | solution.py:94
  36.1 2.6 %collective-permute-start.9 = (bf16[32,4096]{1,0:T(8,128)(2,1)S(1)}, bf16[32,4096]{1,0:T(8,128)(2,1)S(1)}, u32[]{:S(2)}, u32[]{:S(2)}) collective-permute-start(bf16[32,4096]{1,0:T(8,128)(2,1)S(1)} %get-tuple-element.33), channel_id=1, source_target_pairs={{4,0},{8,4},{12,8},{16,12},{20,16},{24,20},{28,24},{5,1},{9,5},{13... | collective-permute-start | bytes 786440 | tf_op jit(solution)/shard_map/ppermute | solution.py:24
  38.8 0.6 collective-permute-start.15
  39.6 0.5 collective-permute-start.12
  40.0 7.0 %collective-permute-done.10.saved_ref = bf16[32,4096]{1,0:T(8,128)(2,1)S(1)} collective-permute-done((bf16[32,4096]{1,0:T(8,128)(2,1)S(1)}, bf16[32,4096]{1,0:T(8,128)(2,1)S(1)}, u32[]{:S(2)}, u32[]{:S(2)}) %collective-permute-start.10) | collective-permute-done | bytes 262176 | tf_op jit(solution)/shard_map/ppermute | solution.py:20
  47.0 5.7 %collective-permute-start.13 = (bf16[32,1280]{1,0:T(8,128)(2,1)S(1)}, bf16[32,1280]{1,0:T(8,128)(2,1)S(1)}, u32[]{:S(2)}, u32[]{:S(2)}) collective-permute-start(bf16[32,1280]{1,0:T(8,128)(2,1)S(1)} %get-tuple-element.37), channel_id=1, source_target_pairs={{0,3},{1,2},{2,1},{3,0},{4,7},{5,6},{6,5},{7,4},{8,11},{9,10},{10,... | collective-permute-start | bytes 245768 | tf_op jit(solution)/shard_map/ppermute | solution.py:20
  52.7 1.8 %collective-permute-done.13.refs_2_.refs_10_ = bf16[32,1280]{1,0:T(8,128)(2,1)S(1)} collective-permute-done((bf16[32,1280]{1,0:T(8,128)(2,1)S(1)}, bf16[32,1280]{1,0:T(8,128)(2,1)S(1)}, u32[]{:S(2)}, u32[]{:S(2)}) %collective-permute-start.13) | collective-permute-done | bytes 81952 | tf_op jit(solution)/shard_map/ppermute | solution.py:20
  54.5 0.9 %shard_map.78 = (bf16[32,4096]{1,0:T(8,128)(2,1)S(1)}, bf16[32,1280]{1,0:T(8,128)(2,1)S(1)}, bf16[32,1280]{1,0:T(8,128)(2,1)S(1)}, bf16[32,1280]{1,0:T(8,128)(2,1)S(1)}, bf16[32,1280]{1,0:T(8,128)(2,1)S(1)}) custom-call(s32[1]{0:T(128)} %bitcast.me_ref, bf16[32,4096]{1,0:T(8,128)(2,1)S(1)} %collective-permute-done.10.saved_ref, ...), custom_call_target="tpu_custom_call" | custom-call | tf_op jit(solution)/shard_map/pallas_call | solution.py:94
  55.4 1.5 %collective-permute-start.16 = (bf16[32,1280]{1,0:T(8,128)(2,1)S(1)}, bf16[32,1280]{1,0:T(8,128)(2,1)S(1)}, u32[]{:S(2)}, u32[]{:S(2)}) collective-permute-start(bf16[32,1280]{1,0:T(8,128)(2,1)S(1)} %get-tuple-element.43), channel_id=1, source_target_pairs={{0,1},{1,0},{2,3},{3,2},{4,5},{5,4},{6,7},{7,6},{8,9},{9,8},{10,11... | collective-permute-start | bytes 245768 | tf_op jit(solution)/shard_map/ppermute | solution.py:20
  56.9 1.2 %collective-permute-start.17 = (bf16[32,1280]{1,0:T(8,128)(2,1)S(1)}, bf16[32,1280]{1,0:T(8,128)(2,1)S(1)}, u32[]{:S(2)}, u32[]{:S(2)}) collective-permute-start(bf16[32,1280]{1,0:T(8,128)(2,1)S(1)} %get-tuple-element.44), channel_id=1, source_target_pairs={{0,2},{1,3},{2,0},{3,1},{4,6},{5,7},{6,4},{7,5},{8,10},{9,11},{10,... | collective-permute-start | bytes 245768 | tf_op jit(solution)/shard_map/ppermute | solution.py:20
  58.1 4.9 %collective-permute-start.14 = (bf16[32,4096]{1,0:T(8,128)(2,1)S(1)}, bf16[32,4096]{1,0:T(8,128)(2,1)S(1)}, u32[]{:S(2)}, u32[]{:S(2)}) collective-permute-start(bf16[32,4096]{1,0:T(8,128)(2,1)S(1)} %get-tuple-element.38), channel_id=1, source_target_pairs={{4,0},{8,4},{12,8},{16,12},{20,16},{24,20},{28,24},{5,1},{9,5},{13... | collective-permute-start | bytes 786440 | tf_op jit(solution)/shard_map/ppermute | solution.py:24
  63.1 0.5 shard_map.79
  63.7 0.9 %shard_map.80 = (bf16[32,4096]{1,0:T(8,128)(2,1)S(1)}, bf16[32,1280]{1,0:T(8,128)(2,1)S(1)}, bf16[32,1280]{1,0:T(8,128)(2,1)S(1)}, bf16[32,1280]{1,0:T(8,128)(2,1)S(1)}, bf16[32,1280]{1,0:T(8,128)(2,1)S(1)}) custom-call(s32[1]{0:T(128)} %bitcast.me_ref, bf16[32,4096]{1,0:T(8,128)(2,1)S(1)} %collective-permute-done.15.saved_ref, ...), custom_call_target="tpu_custom_call" | custom-call | tf_op jit(solution)/shard_map/pallas_call | solution.py:94
  64.6 4.8 %collective-permute-start.19 = (bf16[32,4096]{1,0:T(8,128)(2,1)S(1)}, bf16[32,4096]{1,0:T(8,128)(2,1)S(1)}, u32[]{:S(2)}, u32[]{:S(2)}) collective-permute-start(bf16[32,4096]{1,0:T(8,128)(2,1)S(1)} %get-tuple-element.48), channel_id=1, source_target_pairs={{4,0},{8,4},{12,8},{16,12},{20,16},{24,20},{28,24},{5,1},{9,5},{13... | collective-permute-start | bytes 786440 | tf_op jit(solution)/shard_map/ppermute | solution.py:24
  69.9 2.2 %collective-permute-start.22 = (bf16[32,1280]{1,0:T(8,128)(2,1)S(1)}, bf16[32,1280]{1,0:T(8,128)(2,1)S(1)}, u32[]{:S(2)}, u32[]{:S(2)}) collective-permute-start(bf16[32,1280]{1,0:T(8,128)(2,1)S(1)} %get-tuple-element.52), channel_id=1, source_target_pairs={{0,3},{1,2},{2,1},{3,0},{4,7},{5,6},{6,5},{7,4},{8,11},{9,10},{10,... | collective-permute-start | bytes 245768 | tf_op jit(solution)/shard_map/ppermute | solution.py:20
  72.1 1.7 %collective-permute-done.20.refs_1_ = bf16[32,1280]{1,0:T(8,128)(2,1)S(1)} collective-permute-done((bf16[32,1280]{1,0:T(8,128)(2,1)S(1)}, bf16[32,1280]{1,0:T(8,128)(2,1)S(1)}, u32[]{:S(2)}, u32[]{:S(2)}) %collective-permute-start.20) | collective-permute-done | bytes 81952 | tf_op jit(solution)/shard_map/ppermute | solution.py:20
  73.8 2.0 %collective-permute-done.21.refs_2_ = bf16[32,1280]{1,0:T(8,128)(2,1)S(1)} collective-permute-done((bf16[32,1280]{1,0:T(8,128)(2,1)S(1)}, bf16[32,1280]{1,0:T(8,128)(2,1)S(1)}, u32[]{:S(2)}, u32[]{:S(2)}) %collective-permute-start.21) | collective-permute-done | bytes 81952 | tf_op jit(solution)/shard_map/ppermute | solution.py:20
  75.8 1.3 %shard_map.81 = (f32[1024,128]{1,0:T(8,128)}, f32[128,1024]{1,0:T(8,128)}) custom-call(bf16[32,1280]{1,0:T(8,128)(2,1)S(1)} %get-tuple-element.49.refs_0_, bf16[32,1280]{1,0:T(8,128)(2,1)S(1)} %collective-permute-done.20.refs_1_, bf16[32,1280]{1,0:T(8,128)(2,1)S(1)} %collective-permute-done.21.refs_2_, bf16[32,1280]{1,0:T(8,128)(2,1)S(1)} %collective-permute-done.22.refs_3_, ...), custom_call_target="tpu_custom_call" | custom-call | tf_op jit(solution)/shard_map/pallas_call | solution.py:130
  77.1 1.1 %maximum_bitcast_fusion = bf16[1,128,4096]{2,1,0:T(8,128)(2,1)} fusion(bf16[32,4096]{1,0:T(8,128)(2,1)S(1)} %collective-permute-done.19, bf16[32,4096]{1,0:T(8,128)(2,1)S(1)} %collective-permute-done.14, bf16[32,4096]{1,0:T(8,128)(2,1)S(1)} %collective-permute-done.9.refs_3_, bf16[32,4096]{1,0:T(8,128)(2,1)S(1)} %collective-permute-done.4.refs_3_.refs_2_), kind=kLoop, calls=%fused_computation | loop fusion | flops 4194304 | bytes 2097152 | tf_op jit(solution)/shard_map/broadcast_in_dim | solution.py:185
  (34 shorter events, 1.3 us)
Async XLA Ops:
  0.6 7.3 %copy-start = (bf16[1,128,4096]{2,1,0:T(8,128)(2,1)S(1)}, bf16[1,128,4096]{2,1,0:T(8,128)(2,1)}, u32[]{:S(2)}) copy-start(bf16[1,128,4096]{2,1,0:T(8,128)(2,1)} %param.8) | copy-start | bytes 3145732
  0.6 4.5 %copy-start.1 = (bf16[1,128,4096]{2,1,0:T(8,128)(2,1)S(1)}, bf16[1,128,4096]{2,1,0:T(8,128)(2,1)}, u32[]{:S(2)}) copy-start(bf16[1,128,4096]{2,1,0:T(8,128)(2,1)} %param.6) | copy-start | bytes 3145732
  1.9 20.5 %collective-permute-start = (bf16[32,4096]{1,0:T(8,128)(2,1)S(1)}, bf16[32,4096]{1,0:T(8,128)(2,1)S(1)}, u32[]{:S(2)}, u32[]{:S(2)}) collective-permute-start(bf16[32,4096]{1,0:T(8,128)(2,1)S(1)} %get-tuple-element.59), channel_id=1, source_target_pairs={{0,16},{4,20},{8,24},{12,28},{16,0},{20,4},{24,8},{28,12},{1,17},{... | collective-permute-start | bytes 786440 | tf_op jit(solution)/shard_map/ppermute | solution.py:20
  5.1 25.1 %collective-permute-start.5 = (bf16[32,4096]{1,0:T(8,128)(2,1)S(1)}, bf16[32,4096]{1,0:T(8,128)(2,1)S(1)}, u32[]{:S(2)}, u32[]{:S(2)}) collective-permute-start(bf16[32,4096]{1,0:T(8,128)(2,1)S(1)} %get-tuple-element.60), channel_id=1, source_target_pairs={{0,16},{4,20},{8,24},{12,28},{16,0},{20,4},{24,8},{28,12},{1,17},{... | collective-permute-start | bytes 786440 | tf_op jit(solution)/shard_map/ppermute | solution.py:20
  5.2 17.1 %collective-permute-start.2 = (bf16[128,1024]{1,0:T(8,128)(2,1)S(1)}, bf16[128,1024]{1,0:T(8,128)(2,1)S(1)}, u32[]{:S(2)}, u32[]{:S(2)}) collective-permute-start(bf16[128,1024]{1,0:T(8,128)(2,1)S(1)} %get-tuple-element.56), channel_id=1, source_target_pairs={{0,2},{1,3},{2,0},{3,1},{4,6},{5,7},{6,4},{7,5},{8,10},{9,11},{10,... | collective-permute-start | bytes 786440 | tf_op jit(solution)/shard_map/ppermute | solution.py:20
  6.6 15.8 %collective-permute-start.1 = (bf16[128,1024]{1,0:T(8,128)(2,1)S(1)}, bf16[128,1024]{1,0:T(8,128)(2,1)S(1)}, u32[]{:S(2)}, u32[]{:S(2)}) collective-permute-start(bf16[128,1024]{1,0:T(8,128)(2,1)S(1)} %get-tuple-element.57), channel_id=1, source_target_pairs={{0,1},{1,0},{2,3},{3,2},{4,5},{5,4},{6,7},{7,6},{8,9},{9,8},{10,11... | collective-permute-start | bytes 786440 | tf_op jit(solution)/shard_map/ppermute | solution.py:20
  7.8 14.6 %copy-start.2 = (bf16[1,128,4096]{2,1,0:T(8,128)(2,1)S(1)}, bf16[1,128,4096]{2,1,0:T(8,128)(2,1)}, u32[]{:S(2)}) copy-start(bf16[1,128,4096]{2,1,0:T(8,128)(2,1)} %param.5) | copy-start | bytes 3145732
  7.8 14.6 %copy-start.3 = (bf16[1,4096,128]{2,1,0:T(8,128)(2,1)S(1)}, bf16[1,4096,128]{2,1,0:T(8,128)(2,1)}, u32[]{:S(2)}) copy-start(bf16[1,4096,128]{2,1,0:T(8,128)(2,1)} %param.7) | copy-start | bytes 3145732
  7.8 14.6 %copy-start.4 = (f32[1,4096]{1,0:T(1,128)S(1)}, f32[1,4096]{1,0:T(1,128)}, u32[]{:S(2)}) copy-start(f32[1,4096]{1,0:T(1,128)} %gain_ref.7) | copy-start | bytes 49156
  7.8 14.6 %collective-permute-start.3 = (bf16[128,1024]{1,0:T(8,128)(2,1)S(1)}, bf16[128,1024]{1,0:T(8,128)(2,1)S(1)}, u32[]{:S(2)}, u32[]{:S(2)}) collective-permute-start(bf16[128,1024]{1,0:T(8,128)(2,1)S(1)} %get-tuple-element.58), channel_id=1, source_target_pairs={{0,3},{1,2},{2,1},{3,0},{4,7},{5,6},{6,5},{7,4},{8,11},{9,10},{10,... | collective-permute-start | bytes 786440 | tf_op jit(solution)/shard_map/ppermute | solution.py:20
  23.3 11.9 %collective-permute-start.4 = (bf16[32,4096]{1,0:T(8,128)(2,1)S(1)}, bf16[32,4096]{1,0:T(8,128)(2,1)S(1)}, u32[]{:S(2)}, u32[]{:S(2)}) collective-permute-start(bf16[32,4096]{1,0:T(8,128)(2,1)S(1)} %get-tuple-element.29), channel_id=1, source_target_pairs={{4,0},{8,4},{12,8},{16,12},{20,16},{24,20},{28,24},{5,1},{9,5},{13... | collective-permute-start | bytes 786440 | tf_op jit(solution)/shard_map/ppermute | solution.py:24
  27.3 4.1 %collective-permute-start.6 = (bf16[32,1280]{1,0:T(8,128)(2,1)S(1)}, bf16[32,1280]{1,0:T(8,128)(2,1)S(1)}, u32[]{:S(2)}, u32[]{:S(2)}) collective-permute-start(bf16[32,1280]{1,0:T(8,128)(2,1)S(1)} %get-tuple-element.30), channel_id=1, source_target_pairs={{0,1},{1,0},{2,3},{3,2},{4,5},{5,4},{6,7},{7,6},{8,9},{9,8},{10,11... | collective-permute-start | bytes 245768 | tf_op jit(solution)/shard_map/ppermute | solution.py:20
  28.9 5.0 %collective-permute-start.7 = (bf16[32,1280]{1,0:T(8,128)(2,1)S(1)}, bf16[32,1280]{1,0:T(8,128)(2,1)S(1)}, u32[]{:S(2)}, u32[]{:S(2)}) collective-permute-start(bf16[32,1280]{1,0:T(8,128)(2,1)S(1)} %get-tuple-element.31), channel_id=1, source_target_pairs={{0,2},{1,3},{2,0},{3,1},{4,6},{5,7},{6,4},{7,5},{8,10},{9,11},{10,... | collective-permute-start | bytes 245768 | tf_op jit(solution)/shard_map/ppermute | solution.py:20
  30.1 5.0 %collective-permute-start.8 = (bf16[32,1280]{1,0:T(8,128)(2,1)S(1)}, bf16[32,1280]{1,0:T(8,128)(2,1)S(1)}, u32[]{:S(2)}, u32[]{:S(2)}) collective-permute-start(bf16[32,1280]{1,0:T(8,128)(2,1)S(1)} %get-tuple-element.32), channel_id=1, source_target_pairs={{0,3},{1,2},{2,1},{3,0},{4,7},{5,6},{6,5},{7,4},{8,11},{9,10},{10,... | collective-permute-start | bytes 245768 | tf_op jit(solution)/shard_map/ppermute | solution.py:20
  30.2 16.9 %collective-permute-start.10 = (bf16[32,4096]{1,0:T(8,128)(2,1)S(1)}, bf16[32,4096]{1,0:T(8,128)(2,1)S(1)}, u32[]{:S(2)}, u32[]{:S(2)}) collective-permute-start(bf16[32,4096]{1,0:T(8,128)(2,1)S(1)} %get-tuple-element.34), channel_id=1, source_target_pairs={{0,16},{4,20},{8,24},{12,28},{16,0},{20,4},{24,8},{28,12},{1,17},{... | collective-permute-start | bytes 786440 | tf_op jit(solution)/shard_map/ppermute | solution.py:20
  36.1 18.4 %collective-permute-start.9 = (bf16[32,4096]{1,0:T(8,128)(2,1)S(1)}, bf16[32,4096]{1,0:T(8,128)(2,1)S(1)}, u32[]{:S(2)}, u32[]{:S(2)}) collective-permute-start(bf16[32,4096]{1,0:T(8,128)(2,1)S(1)} %get-tuple-element.33), channel_id=1, source_target_pairs={{4,0},{8,4},{12,8},{16,12},{20,16},{24,20},{28,24},{5,1},{9,5},{13... | collective-permute-start | bytes 786440 | tf_op jit(solution)/shard_map/ppermute | solution.py:24
  38.8 24.9 %collective-permute-start.15 = (bf16[32,4096]{1,0:T(8,128)(2,1)S(1)}, bf16[32,4096]{1,0:T(8,128)(2,1)S(1)}, u32[]{:S(2)}, u32[]{:S(2)}) collective-permute-start(bf16[32,4096]{1,0:T(8,128)(2,1)S(1)} %get-tuple-element.39), channel_id=1, source_target_pairs={{0,16},{4,20},{8,24},{12,28},{16,0},{20,4},{24,8},{28,12},{1,17},{... | collective-permute-start | bytes 786440 | tf_op jit(solution)/shard_map/ppermute | solution.py:20
  39.3 13.4 %collective-permute-start.11 = (bf16[32,1280]{1,0:T(8,128)(2,1)S(1)}, bf16[32,1280]{1,0:T(8,128)(2,1)S(1)}, u32[]{:S(2)}, u32[]{:S(2)}) collective-permute-start(bf16[32,1280]{1,0:T(8,128)(2,1)S(1)} %get-tuple-element.35), channel_id=1, source_target_pairs={{0,1},{1,0},{2,3},{3,2},{4,5},{5,4},{6,7},{7,6},{8,9},{9,8},{10,11... | collective-permute-start | bytes 245768 | tf_op jit(solution)/shard_map/ppermute | solution.py:20
  39.6 13.1 %collective-permute-start.12 = (bf16[32,1280]{1,0:T(8,128)(2,1)S(1)}, bf16[32,1280]{1,0:T(8,128)(2,1)S(1)}, u32[]{:S(2)}, u32[]{:S(2)}) collective-permute-start(bf16[32,1280]{1,0:T(8,128)(2,1)S(1)} %get-tuple-element.36), channel_id=1, source_target_pairs={{0,2},{1,3},{2,0},{3,1},{4,6},{5,7},{6,4},{7,5},{8,10},{9,11},{10,... | collective-permute-start | bytes 245768 | tf_op jit(solution)/shard_map/ppermute | solution.py:20
  47.0 7.5 %collective-permute-start.13 = (bf16[32,1280]{1,0:T(8,128)(2,1)S(1)}, bf16[32,1280]{1,0:T(8,128)(2,1)S(1)}, u32[]{:S(2)}, u32[]{:S(2)}) collective-permute-start(bf16[32,1280]{1,0:T(8,128)(2,1)S(1)} %get-tuple-element.37), channel_id=1, source_target_pairs={{0,3},{1,2},{2,1},{3,0},{4,7},{5,6},{6,5},{7,4},{8,11},{9,10},{10,... | collective-permute-start | bytes 245768 | tf_op jit(solution)/shard_map/ppermute | solution.py:20
  55.4 7.6 %collective-permute-start.16 = (bf16[32,1280]{1,0:T(8,128)(2,1)S(1)}, bf16[32,1280]{1,0:T(8,128)(2,1)S(1)}, u32[]{:S(2)}, u32[]{:S(2)}) collective-permute-start(bf16[32,1280]{1,0:T(8,128)(2,1)S(1)} %get-tuple-element.43), channel_id=1, source_target_pairs={{0,1},{1,0},{2,3},{3,2},{4,5},{5,4},{6,7},{7,6},{8,9},{9,8},{10,11... | collective-permute-start | bytes 245768 | tf_op jit(solution)/shard_map/ppermute | solution.py:20
  56.9 6.2 %collective-permute-start.17 = (bf16[32,1280]{1,0:T(8,128)(2,1)S(1)}, bf16[32,1280]{1,0:T(8,128)(2,1)S(1)}, u32[]{:S(2)}, u32[]{:S(2)}) collective-permute-start(bf16[32,1280]{1,0:T(8,128)(2,1)S(1)} %get-tuple-element.44), channel_id=1, source_target_pairs={{0,2},{1,3},{2,0},{3,1},{4,6},{5,7},{6,4},{7,5},{8,10},{9,11},{10,... | collective-permute-start | bytes 245768 | tf_op jit(solution)/shard_map/ppermute | solution.py:20
  58.1 5.0 %collective-permute-start.18 = (bf16[32,1280]{1,0:T(8,128)(2,1)S(1)}, bf16[32,1280]{1,0:T(8,128)(2,1)S(1)}, u32[]{:S(2)}, u32[]{:S(2)}) collective-permute-start(bf16[32,1280]{1,0:T(8,128)(2,1)S(1)} %get-tuple-element.45), channel_id=1, source_target_pairs={{0,3},{1,2},{2,1},{3,0},{4,7},{5,6},{6,5},{7,4},{8,11},{9,10},{10,... | collective-permute-start | bytes 245768 | tf_op jit(solution)/shard_map/ppermute | solution.py:20
  58.1 19.0 %collective-permute-start.14 = (bf16[32,4096]{1,0:T(8,128)(2,1)S(1)}, bf16[32,4096]{1,0:T(8,128)(2,1)S(1)}, u32[]{:S(2)}, u32[]{:S(2)}) collective-permute-start(bf16[32,4096]{1,0:T(8,128)(2,1)S(1)} %get-tuple-element.38), channel_id=1, source_target_pairs={{4,0},{8,4},{12,8},{16,12},{20,16},{24,20},{28,24},{5,1},{9,5},{13... | collective-permute-start | bytes 786440 | tf_op jit(solution)/shard_map/ppermute | solution.py:24
  64.6 12.5 %collective-permute-start.19 = (bf16[32,4096]{1,0:T(8,128)(2,1)S(1)}, bf16[32,4096]{1,0:T(8,128)(2,1)S(1)}, u32[]{:S(2)}, u32[]{:S(2)}) collective-permute-start(bf16[32,4096]{1,0:T(8,128)(2,1)S(1)} %get-tuple-element.48), channel_id=1, source_target_pairs={{4,0},{8,4},{12,8},{16,12},{20,16},{24,20},{28,24},{5,1},{9,5},{13... | collective-permute-start | bytes 786440 | tf_op jit(solution)/shard_map/ppermute | solution.py:24
  69.4 4.4 %collective-permute-start.20 = (bf16[32,1280]{1,0:T(8,128)(2,1)S(1)}, bf16[32,1280]{1,0:T(8,128)(2,1)S(1)}, u32[]{:S(2)}, u32[]{:S(2)}) collective-permute-start(bf16[32,1280]{1,0:T(8,128)(2,1)S(1)} %get-tuple-element.50), channel_id=1, source_target_pairs={{0,1},{1,0},{2,3},{3,2},{4,5},{5,4},{6,7},{7,6},{8,9},{9,8},{10,11... | collective-permute-start | bytes 245768 | tf_op jit(solution)/shard_map/ppermute | solution.py:20
  69.7 6.1 %collective-permute-start.21 = (bf16[32,1280]{1,0:T(8,128)(2,1)S(1)}, bf16[32,1280]{1,0:T(8,128)(2,1)S(1)}, u32[]{:S(2)}, u32[]{:S(2)}) collective-permute-start(bf16[32,1280]{1,0:T(8,128)(2,1)S(1)} %get-tuple-element.51), channel_id=1, source_target_pairs={{0,2},{1,3},{2,0},{3,1},{4,6},{5,7},{6,4},{7,5},{8,10},{9,11},{10,... | collective-permute-start | bytes 245768 | tf_op jit(solution)/shard_map/ppermute | solution.py:20
  69.9 5.9 %collective-permute-start.22 = (bf16[32,1280]{1,0:T(8,128)(2,1)S(1)}, bf16[32,1280]{1,0:T(8,128)(2,1)S(1)}, u32[]{:S(2)}, u32[]{:S(2)}) collective-permute-start(bf16[32,1280]{1,0:T(8,128)(2,1)S(1)} %get-tuple-element.52), channel_id=1, source_target_pairs={{0,3},{1,2},{2,1},{3,0},{4,7},{5,6},{6,5},{7,4},{8,11},{9,10},{10,... | collective-permute-start | bytes 245768 | tf_op jit(solution)/shard_map/ppermute | solution.py:20

commit v3 on v2

--- a/solution.py
+++ b/solution.py
@@ -8,7 +8,6 @@
 from jax.sharding import PartitionSpec as P
 
 SHARES = (2, 2, 2, 2)
-AHEAD = 2
 LANES = 512
 VMEM = pl.BlockSpec(memory_space=pltpu.VMEM)
 SMEM = pl.BlockSpec(memory_space=pltpu.SMEM)
@@ -39,15 +38,40 @@
     return 0.5 * x * (1.0 + th), slope
 
 
-def chunk_kernel(groups, start, following, waits, me_ref, saved_ref, cot_ref, dact_ref, down_ref, gain_ref, stash_ref, *refs):
+def copy_kernel(start, stash_ref, *refs):
+    out_ref, done = refs[-2:]
+    copy = pltpu.make_async_copy(stash_ref.at[pl.ds(start, out_ref.shape[0])], out_ref, done)
+    copy.start()
+    copy.wait()
+
+
+def rows_after(stash, start, rows, waits):
+    return pl.pallas_call(
+        functools.partial(copy_kernel, start),
+        out_shape=jax.ShapeDtypeStruct((rows, stash.shape[1]), stash.dtype),
+        in_specs=[ANY] * (1 + len(waits)),
+        out_specs=ANY,
+        scratch_shapes=[pltpu.SemaphoreType.DMA],
+    )(stash, *waits)
+
+
+def pass_kernel(value_ref, wait_ref, out_ref):
+    pass
+
+
+def after(value, wait):
+    return pl.pallas_call(
+        pass_kernel,
+        out_shape=jax.ShapeDtypeStruct(value.shape, value.dtype),
+        in_specs=[ANY, ANY],
+        out_specs=ANY,
+        input_output_aliases={0: 0},
+    )(value, wait)
+
+
+def chunk_kernel(groups, start, waits, me_ref, saved_ref, cot_ref, dact_ref, down_ref, gain_ref, *refs):
     outs = refs[waits:]
-    dx_ref, pack_refs = outs[0], outs[1 : 1 + groups]
-    rest = outs[1 + groups :]
-    normed_ref = rest[-2] if following else rest[-1]
-    copy = None
-    if following:
-        copy = pltpu.make_async_copy(stash_ref.at[pl.ds(*following)], rest[0], rest[-1])
-        copy.start()
+    dx_ref, pack_refs, normed_ref = outs[0], outs[1:-1], outs[-1]
     rows, features = saved_ref.shape
     width = features // groups
     rank = down_ref.shape[1]
@@ -76,38 +100,34 @@
         xf = saved_ref[:, at].astype(jnp.float32)
         held = cot_ref[pl.ds(start, rows), at].astype(jnp.float32)
         dx_ref[:, at] = (held + (dnorm - xf * pull) * inverse).astype(jnp.bfloat16)
-    if copy is not None:
-        copy.wait()
-
-
-def run_chunk(me, saved, cot, dact, down, gain, stash, start, following, waits, groups):
+
+
+def run_chunk(me, saved, cot, dact, down, gain, start, waits, groups):
     rows, features = saved.shape
     rank = down.shape[1]
     pack = jax.ShapeDtypeStruct((rows, features // groups + 2 * rank), jnp.bfloat16)
     outs = [jax.ShapeDtypeStruct((rows, features), jnp.bfloat16)] + [pack] * groups
-    specs = [VMEM] * len(outs)
-    scratch = [pltpu.VMEM((rows, features), jnp.bfloat16)]
-    if following:
-        outs.append(jax.ShapeDtypeStruct((following[1], features), jnp.bfloat16))
-        specs.append(ANY)
-        scratch.append(pltpu.SemaphoreType.DMA)
     got = pl.pallas_call(
-        functools.partial(chunk_kernel, groups, start, following, len(waits)),
+        functools.partial(chunk_kernel, groups, start, len(waits)),
         out_shape=outs,
-        in_specs=[SMEM] + [VMEM] * 5 + [ANY] * (1 + len(waits)),
-        out_specs=specs,
-        scratch_shapes=scratch,
+        in_specs=[SMEM] + [VMEM] * 5 + [ANY] * len(waits),
+        out_specs=[VMEM] * len(outs),
+        scratch_shapes=[pltpu.VMEM((rows, features), jnp.bfloat16)],
         compiler_params=PARAMS,
-    )(me, saved, cot, dact, down, gain, stash, *waits)
-    return got[0], got[1 : 1 + groups], got[1 + groups :]
+    )(me, saved, cot, dact, down, gain, *waits)
+    return got[0], got[1:]
 
 
 def sum_kernel(groups, spans, first, *refs):
     count = groups * len(spans)
     packs, cots = refs[:count], refs[count : count + groups]
     rest = refs[count + groups :]
-    olds, rest = ((), rest) if first else (rest[:2], rest[2:])
-    down_ref, up_ref, every, held = rest
+    if first:
+        parts, (down_ref, up_ref, joined, every, held) = rest[: len(spans)], rest[len(spans) :]
+        for (start, rows), part in zip(spans, parts):
+            joined[pl.ds(start, rows), :] = part[...]
+    else:
+        olds, (down_ref, up_ref, every, held) = rest[:2], rest[2:]
     width = held.shape[1]
     rank = up_ref.shape[0]
     at = 0
@@ -122,19 +142,23 @@
     up_ref[...] = up if first else up + olds[1][...]
 
 
-def run_sum(packs, cots, spans, olds, rank):
+def run_sum(packs, cots, spans, others, first, rank):
     groups = len(cots)
     width = cots[0].shape[1]
     depth = groups * sum(rows for _, rows in spans)
-    args = [packs[j][k] for k in range(groups) for j in range(len(spans))] + list(cots) + list(olds)
+    args = [packs[j][k] for k in range(groups) for j in range(len(spans))] + list(cots) + list(others)
+    outs = [
+        jax.ShapeDtypeStruct((width, rank), jnp.float32),
+        jax.ShapeDtypeStruct((rank, width), jnp.float32),
+    ]
+    if first:
+        rows = sum(part.shape[0] for part in others)
+        outs.append(jax.ShapeDtypeStruct((rows, others[0].shape[1]), others[0].dtype))
     return pl.pallas_call(
-        functools.partial(sum_kernel, groups, spans, not olds),
-        out_shape=[
-            jax.ShapeDtypeStruct((width, rank), jnp.float32),
-            jax.ShapeDtypeStruct((rank, width), jnp.float32),
-        ],
+        functools.partial(sum_kernel, groups, spans, first),
+        out_shape=outs,
         in_specs=[VMEM] * len(args),
-        out_specs=[VMEM, VMEM],
+        out_specs=[VMEM] * len(outs),
         scratch_shapes=[
             pltpu.VMEM((depth, width + 2 * rank), jnp.bfloat16),
             pltpu.VMEM((depth, width), jnp.bfloat16),
@@ -158,31 +182,33 @@
     def held(value):
         return exchanged(value, "pipe", sections // 2)
 
-    arrivals = [held(stash[start : start + rows]) for start, rows in spans[:AHEAD]]
+    def coming(i, *waits):
+        return held(rows_after(stash, *spans[i], waits))
+
+    arrivals = [held(stash[: sizes[0]])]
     cot_all = []
     for k in range(groups):
         part = lax.dynamic_slice_in_dim(cot, (me ^ k) * width, width, axis=1)
         cot_all.append(exchanged(part, "dp", k) if k else part)
     dact = last_dot(cot, upper)
+    arrivals.append(coming(1, cot_all[0]))
     index = jnp.reshape(me.astype(jnp.int32), (1,))
 
-    before, packs, partial = [], [], []
-    waits = list(cot_all[1:])
+    parts, packs, waits = [], [], cot_all[1:]
     for i, (start, rows) in enumerate(spans):
-        following = spans[i + AHEAD] if i + AHEAD < chunks else None
+        if i + 2 < chunks:
+            arrivals.append(coming(i + 2, arrivals[i], *parts[-1:]))
         if i == chunks - 1:
-            partial = run_sum(packs, cot_all, spans[:-1], [], rank)
-            waits = list(partial) + before[:-1]
-        dx, pack, coming = run_chunk(
-            index, arrivals[i], cot, dact, down, gain, stash, start, following, waits, groups
-        )
-        if following:
-            arrivals.append(held(coming[0]))
+            *partial, joined = run_sum(packs, cot_all, spans[:-1], parts, True, rank)
+            first = to_previous(after(joined, arrivals[i]), "pipe")
+            waits = partial
+        dx, pack = run_chunk(index, arrivals[i], cot, dact, down, gain, start, waits, groups)
         packs.append([exchanged(pack[k], "dp", k) if k else pack[k] for k in range(groups)])
-        before.append(to_previous(dx, "pipe"))
-        waits = list(packs[-1][1:]) + before[-1:]
-    down_grad, up_grad = run_sum(packs[-1:], cot_all, spans[-1:], partial, rank)
-    return (jnp.concatenate(before, axis=0)[None], down_grad[None], up_grad[None])
+        parts.append(dx)
+        waits = packs[-1][1:]
+    last = to_previous(parts[-1], "pipe")
+    down_grad, up_grad = run_sum(packs[-1:], cot_all, spans[-1:], partial, False, rank)
+    return (jnp.concatenate([first, last], axis=0)[None], down_grad[None], up_grad[None])
 
 
 def solution(mesh):

time: 78.9 us -> 96.5 us (1.22)
  Pallas kernels: 5.44 us -> 37.4 us
  waiting for transfers between devices: 31.6 us -> 12.7 us
  local copies, waits for them, and re-layouts: 1.32 us -> 11.8 us
  starting transfers between devices: 37.5 us -> 31.6 us
    pallas_call x6 -> x10, Pallas kernels: 5.44 us -> 37.4 us  [the longest x3 27.2 us: rows_after(): pl.pallas_call(functools.partial(copy_kernel, start), out_shape=jax.Shape...]
    ppermute x19, waiting for transfers between devices: 31.6 us -> 12.7 us  [exchanged(): lax.ppermute(x, axis, [(i, i ^ mask) for i in range(lax.axis_size(axis))])]
    unnamed x10 -> x52, local copies, waits for them, and re-layouts: 0.02 us -> 8.54 us
    ppermute x4 -> x2, starting transfers between devices: 16.3 us -> 10.1 us  [to_previous(): lax.ppermute(x, axis, [(i, i - 1) for i in range(1, lax.axis_size(axis))])]
    dynamic_slice x1, local copies, waits for them, and re-layouts: 0.08 us -> 2.17 us  [per_device(): part = lax.dynamic_slice_in_dim(cot, (me ^ k) * width, width, axis=1)]
  transfers between devices with their start and end apart: 23 -> 21, of which waited for: 9 -> 11; matrix products, arithmetic and copies ran while one was open for 1% -> 3% of each run, Pallas kernels for 7% -> 39%
where the time goes in v3:
time: 96.5 us; the launch traced here: 95.9 us
  Pallas kernels  37.4 us (39%)
  starting transfers between devices  31.6 us (33%)
  waiting for transfers between devices  12.7 us (13%)
  local copies, waits for them, and re-layouts  11.8 us (12%)
  other arithmetic  1.04 us (1%)
    pallas_call x3, Pallas kernels, rows_after(): pl.pallas_call(functools.partial(copy_kernel, start), out_shape=jax.Shape...  27.2 us
    ppermute x19, starting transfers between devices, exchanged(): lax.ppermute(x, axis, [(i, i ^ mask) for i in range(lax.axis_size(axis))])  21.5 us
    ppermute x19, waiting for transfers between devices, exchanged(): lax.ppermute(x, axis, [(i, i ^ mask) for i in range(lax.axis_size(axis))])  12.7 us
    ppermute x2, starting transfers between devices, to_previous(): lax.ppermute(x, axis, [(i, i - 1) for i in range(1, lax.axis_size(axis))])  10.1 us
    unnamed x52, local copies, waits for them, and re-layouts  8.54 us
    pallas_call x4, Pallas kernels, run_chunk(): pl.pallas_call(functools.partial(chunk_kernel, groups, start, len(waits))...  6.34 us
    pallas_call x2, Pallas kernels, run_sum(): pl.pallas_call(functools.partial(sum_kernel, groups, spans, first), out_s...  3.95 us
    dynamic_slice x1, local copies, waits for them, and re-layouts, per_device(): part = lax.dynamic_slice_in_dim(cot, (me ^ k) * width, width, axis=1)  2.17 us
  transfers between devices with their start and end apart: 21, of which 11 were waited for; matrix products, arithmetic and copies ran while one was open for 3% of the time, Pallas kernels for 39%

profile of v3, /device:TPU:1, one launch (start us, length us, event | category | flops | bytes accessed | tf_op | source)
XLA Modules:
  0.0 95.9 jit_solution(3450559936798267232)
XLA Ops:
  0.6 1.1 %slice_bitcast_fusion = bf16[32,4096]{1,0:T(8,128)(2,1)S(1)} fusion(bf16[1,128,4096]{2,1,0:T(8,128)(2,1)} %param.5), kind=kLoop, calls=%fused_computation.7 | loop fusion | bytes 524288 | tf_op jit(solution)/shard_map/slice | solution.py:188
  1.7 3.2 %collective-permute-start = (bf16[32,4096]{1,0:T(8,128)(2,1)S(1)}, bf16[32,4096]{1,0:T(8,128)(2,1)S(1)}, u32[]{:S(2)}, u32[]{:S(2)}) collective-permute-start(bf16[32,4096]{1,0:T(8,128)(2,1)S(1)} %slice_bitcast_fusion), channel_id=1, source_target_pairs={{0,16},{4,20},{8,24},{12,28},{16,0},{20,4},{24,8},{28,12},{1,17},{... | collective-permute-start | bytes 786440 | tf_op jit(solution)/shard_map/ppermute | solution.py:19
  4.9 2.2 %dynamic-slice_bitcast_fusion.1 = (bf16[128,1024]{1,0:T(8,128)(2,1)}, bf16[128,1024]{1,0:T(8,128)(2,1)}, bf16[128,1024]{1,0:T(8,128)(2,1)}, bf16[128,1024]{1,0:T(8,128)(2,1)}) fusion(bf16[1,128,4096]{2,1,0:T(8,128)(2,1)} %param.6, s32[]{:T(128)S(6)} %select_n.14, s32[]{:T(128)S(6)} %select_n.13, s32[]{:T(128)S(6)} %select_n.12, s32[]{:T(128)S(6)} %select_n.15), kind=kLoop, calls=%fused_computation.4 | loop fusion | bytes 2097168 | tf_op jit(solution)/shard_map/dynamic_slice | solution.py:191
  7.1 9.0 %shard_map.77 = bf16[32,4096]{1,0:T(8,128)(2,1)} custom-call(bf16[128,4096]{1,0:T(8,128)(2,1)} %bitcast.31, bf16[128,1024]{1,0:T(8,128)(2,1)} %get-tuple-element.56.refs_0_.refs_12_.refs_4_), custom_call_target="tpu_custom_call" | custom-call | tf_op jit(solution)/shard_map/pallas_call | solution.py:49
  16.3 2.2 %collective-permute-start.3 = (bf16[128,1024]{1,0:T(8,128)(2,1)}, bf16[128,1024]{1,0:T(8,128)(2,1)S(1)}, u32[]{:S(2)}, u32[]{:S(2)}) collective-permute-start(bf16[128,1024]{1,0:T(8,128)(2,1)} %get-tuple-element.53), channel_id=1, source_target_pairs={{0,3},{1,2},{2,1},{3,0},{4,7},{5,6},{6,5},{7,4},{8,11},{9,10},{10,... | collective-permute-start | bytes 786440 | tf_op jit(solution)/shard_map/ppermute | solution.py:19
  19.7 9.0 %shard_map.79 = bf16[32,4096]{1,0:T(8,128)(2,1)} custom-call(bf16[128,4096]{1,0:T(8,128)(2,1)} %bitcast.32, bf16[32,4096]{1,0:T(8,128)(2,1)} %copy-done.14), custom_call_target="tpu_custom_call" | custom-call | tf_op jit(solution)/shard_map/pallas_call | solution.py:49
  28.7 2.4 %collective-permute-start.8 = (bf16[32,4096]{1,0:T(8,128)(2,1)}, bf16[32,4096]{1,0:T(8,128)(2,1)}, u32[]{:S(2)}, u32[]{:S(2)}) collective-permute-start(bf16[32,4096]{1,0:T(8,128)(2,1)} %shard_map.79), channel_id=1, source_target_pairs={{0,16},{4,20},{8,24},{12,28},{16,0},{20,4},{24,8},{28,12},{1,17},{... | collective-permute-start | bytes 786440 | tf_op jit(solution)/shard_map/ppermute | solution.py:19
  35.7 9.1 %shard_map.82 = bf16[32,4096]{1,0:T(8,128)(2,1)} custom-call(bf16[128,4096]{1,0:T(8,128)(2,1)} %bitcast.33, bf16[32,4096]{1,0:T(8,128)(2,1)} %collective-permute-done.4.saved_ref.refs_0_, bf16[32,4096]{1,0:T(8,128)(2,1)} %copy-done.12), custom_call_target="tpu_custom_call" | custom-call | tf_op jit(solution)/shard_map/pallas_call | solution.py:49
  44.8 2.1 %collective-permute-start.15 = (bf16[32,4096]{1,0:T(8,128)(2,1)}, bf16[32,4096]{1,0:T(8,128)(2,1)}, u32[]{:S(2)}, u32[]{:S(2)}) collective-permute-start(bf16[32,4096]{1,0:T(8,128)(2,1)} %shard_map.82), channel_id=1, source_target_pairs={{0,16},{4,20},{8,24},{12,28},{16,0},{20,4},{24,8},{28,12},{1,17},{... | collective-permute-start | bytes 786440 | tf_op jit(solution)/shard_map/ppermute | solution.py:19
  46.9 1.2 %collective-permute-start.5 = (bf16[32,1280]{1,0:T(8,128)(2,1)S(1)}, bf16[32,1280]{1,0:T(8,128)(2,1)S(1)}, u32[]{:S(2)}, u32[]{:S(2)}) collective-permute-start(bf16[32,1280]{1,0:T(8,128)(2,1)S(1)} %copy-done.25), channel_id=1, source_target_pairs={{0,1},{1,0},{2,3},{3,2},{4,5},{5,4},{6,7},{7,6},{8,9},{9,8},{10,11... | collective-permute-start | bytes 245768 | tf_op jit(solution)/shard_map/ppermute | solution.py:19
  48.2 1.3 %collective-permute-start.7 = (bf16[32,1280]{1,0:T(8,128)(2,1)S(1)}, bf16[32,1280]{1,0:T(8,128)(2,1)S(1)}, u32[]{:S(2)}, u32[]{:S(2)}) collective-permute-start(bf16[32,1280]{1,0:T(8,128)(2,1)S(1)} %copy-done.21), channel_id=1, source_target_pairs={{0,3},{1,2},{2,1},{3,0},{4,7},{5,6},{6,5},{7,4},{8,11},{9,10},{10,... | collective-permute-start | bytes 245768 | tf_op jit(solution)/shard_map/ppermute | solution.py:19
  50.2 1.5 %collective-permute-done.6.refs_1_.refs_6_ = bf16[32,1280]{1,0:T(8,128)(2,1)S(1)} collective-permute-done((bf16[32,1280]{1,0:T(8,128)(2,1)S(1)}, bf16[32,1280]{1,0:T(8,128)(2,1)S(1)}, u32[]{:S(2)}, u32[]{:S(2)}) %collective-permute-start.6) | collective-permute-done | bytes 81952 | tf_op jit(solution)/shard_map/ppermute | solution.py:19
  51.7 1.4 %collective-permute-done.7.refs_2_.refs_9_ = bf16[32,1280]{1,0:T(8,128)(2,1)S(1)} collective-permute-done((bf16[32,1280]{1,0:T(8,128)(2,1)S(1)}, bf16[32,1280]{1,0:T(8,128)(2,1)S(1)}, u32[]{:S(2)}, u32[]{:S(2)}) %collective-permute-start.7) | collective-permute-done | bytes 81952 | tf_op jit(solution)/shard_map/ppermute | solution.py:19
  53.1 1.8 %shard_map.78 = (bf16[32,4096]{1,0:T(8,128)(2,1)S(1)}, bf16[32,1280]{1,0:T(8,128)(2,1)S(1)}, bf16[32,1280]{1,0:T(8,128)(2,1)S(1)}, bf16[32,1280]{1,0:T(8,128)(2,1)S(1)}, bf16[32,1280]{1,0:T(8,128)(2,1)S(1)}) custom-call(s32[1]{0:T(128)} %bitcast.me_ref, bf16[32,4096]{1,0:T(8,128)(2,1)} %collective-permute-done.4.saved_ref.refs_0_, ...), custom_call_target="tpu_custom_call" | custom-call | tf_op jit(solution)/shard_map/pallas_call | solution.py:110
  54.9 1.6 %collective-permute-start.9 = (bf16[32,1280]{1,0:T(8,128)(2,1)S(1)}, bf16[32,1280]{1,0:T(8,128)(2,1)S(1)}, u32[]{:S(2)}, u32[]{:S(2)}) collective-permute-start(bf16[32,1280]{1,0:T(8,128)(2,1)S(1)} %get-tuple-element.33), channel_id=1, source_target_pairs={{0,1},{1,0},{2,3},{3,2},{4,5},{5,4},{6,7},{7,6},{8,9},{9,8},{10,11... | collective-permute-start | bytes 245768 | tf_op jit(solution)/shard_map/ppermute | solution.py:19
  56.8 1.1 %collective-permute-start.11 = (bf16[32,1280]{1,0:T(8,128)(2,1)S(1)}, bf16[32,1280]{1,0:T(8,128)(2,1)S(1)}, u32[]{:S(2)}, u32[]{:S(2)}) collective-permute-start(bf16[32,1280]{1,0:T(8,128)(2,1)S(1)} %get-tuple-element.35), channel_id=1, source_target_pairs={{0,3},{1,2},{2,1},{3,0},{4,7},{5,6},{6,5},{7,4},{8,11},{9,10},{10,... | collective-permute-start | bytes 245768 | tf_op jit(solution)/shard_map/ppermute | solution.py:19
  58.8 1.2 %collective-permute-done.10.refs_1_.refs_7_ = bf16[32,1280]{1,0:T(8,128)(2,1)S(1)} collective-permute-done((bf16[32,1280]{1,0:T(8,128)(2,1)S(1)}, bf16[32,1280]{1,0:T(8,128)(2,1)S(1)}, u32[]{:S(2)}, u32[]{:S(2)}) %collective-permute-start.10) | collective-permute-done | bytes 81952 | tf_op jit(solution)/shard_map/ppermute | solution.py:19
  60.0 1.1 %collective-permute-done.11.refs_2_.refs_10_ = bf16[32,1280]{1,0:T(8,128)(2,1)S(1)} collective-permute-done((bf16[32,1280]{1,0:T(8,128)(2,1)S(1)}, bf16[32,1280]{1,0:T(8,128)(2,1)S(1)}, u32[]{:S(2)}, u32[]{:S(2)}) %collective-permute-start.11) | collective-permute-done | bytes 81952 | tf_op jit(solution)/shard_map/ppermute | solution.py:19
  61.2 1.8 %shard_map.80 = (bf16[32,4096]{1,0:T(8,128)(2,1)S(1)}, bf16[32,1280]{1,0:T(8,128)(2,1)S(1)}, bf16[32,1280]{1,0:T(8,128)(2,1)S(1)}, bf16[32,1280]{1,0:T(8,128)(2,1)S(1)}, bf16[32,1280]{1,0:T(8,128)(2,1)S(1)}) custom-call(s32[1]{0:T(128)} %bitcast.me_ref, bf16[32,4096]{1,0:T(8,128)(2,1)} %collective-permute-done.8.saved_ref, bf16[128,4096]{1,0:T(8,128)(2,1)S(1)} %bitcast.25, ...), custom_call_target="tpu_custom_call" | custom-call | tf_op jit(solution)/shard_map/pallas_call | solution.py:110
  64.3 1.3 %collective-permute-start.14 = (bf16[32,1280]{1,0:T(8,128)(2,1)S(1)}, bf16[32,1280]{1,0:T(8,128)(2,1)S(1)}, u32[]{:S(2)}, u32[]{:S(2)}) collective-permute-start(bf16[32,1280]{1,0:T(8,128)(2,1)S(1)} %get-tuple-element.39), channel_id=1, source_target_pairs={{0,3},{1,2},{2,1},{3,0},{4,7},{5,6},{6,5},{7,4},{8,11},{9,10},{10,... | collective-permute-start | bytes 245768 | tf_op jit(solution)/shard_map/ppermute | solution.py:19
  66.8 1.7 %collective-permute-done.14.refs_11_ = bf16[32,1280]{1,0:T(8,128)(2,1)S(1)} collective-permute-done((bf16[32,1280]{1,0:T(8,128)(2,1)S(1)}, bf16[32,1280]{1,0:T(8,128)(2,1)S(1)}, u32[]{:S(2)}, u32[]{:S(2)}) %collective-permute-start.14) | collective-permute-done | bytes 81952 | tf_op jit(solution)/shard_map/ppermute | solution.py:19
  68.6 1.6 %shard_map.81 = (f32[1024,128]{1,0:T(8,128)S(1)}, f32[128,1024]{1,0:T(8,128)S(1)}, bf16[96,4096]{1,0:T(8,128)(2,1)S(1)}) custom-call(bf16[32,1280]{1,0:T(8,128)(2,1)S(1)} %copy-done.19, bf16[32,1280]{1,0:T(8,128)(2,1)S(1)} %get-tuple-element.32.refs_1_, bf16[32,1280]{1,0:T(8,128)(2,1)S(1)} %get-tuple-element.36.refs_2_, ...), custom_call_target="tpu_custom_call" | custom-call | tf_op jit(solution)/shard_map/pallas_call | solution.py:157
  72.7 8.2 %collective-permute-start.16 = (bf16[96,4096]{1,0:T(8,128)(2,1)}, bf16[96,4096]{1,0:T(8,128)(2,1)S(1)}, u32[]{:S(2)}, u32[]{:S(2)}) collective-permute-start(bf16[96,4096]{1,0:T(8,128)(2,1)} %shard_map.83), channel_id=1, source_target_pairs={{4,0},{8,4},{12,8},{16,12},{20,16},{24,20},{28,24},{5,1},{9,5},{13... | collective-permute-start | bytes 2359304 | tf_op jit(solution)/shard_map/ppermute | solution.py:23
  80.9 1.0 %copy-done.8 = f32[1024,128]{1,0:T(8,128)S(1)} copy-done((f32[1024,128]{1,0:T(8,128)S(1)}, f32[1024,128]{1,0:T(8,128)}, u32[]{:S(2)}) %copy-start.8) | copy-done | bytes 524312
  81.9 1.0 %copy-done.11 = f32[128,1024]{1,0:T(8,128)S(1)} copy-done((f32[128,1024]{1,0:T(8,128)S(1)}, f32[128,1024]{1,0:T(8,128)}, u32[]{:S(2)}) %copy-start.11) | copy-done | bytes 524312
  83.0 1.9 %shard_map.84 = (bf16[32,4096]{1,0:T(8,128)(2,1)S(1)}, bf16[32,1280]{1,0:T(8,128)(2,1)S(1)}, bf16[32,1280]{1,0:T(8,128)(2,1)S(1)}, bf16[32,1280]{1,0:T(8,128)(2,1)S(1)}, bf16[32,1280]{1,0:T(8,128)(2,1)S(1)}) custom-call(s32[1]{0:T(128)} %bitcast.me_ref, bf16[32,4096]{1,0:T(8,128)(2,1)} %collective-permute-done.15.wait_ref.saved_ref, ...), custom_call_target="tpu_custom_call" | custom-call | tf_op jit(solution)/shard_map/pallas_call | solution.py:110
  84.8 1.9 %collective-permute-start.17 = (bf16[32,4096]{1,0:T(8,128)(2,1)S(1)}, bf16[32,4096]{1,0:T(8,128)(2,1)S(1)}, u32[]{:S(2)}, u32[]{:S(2)}) collective-permute-start(bf16[32,4096]{1,0:T(8,128)(2,1)S(1)} %get-tuple-element.46), channel_id=1, source_target_pairs={{4,0},{8,4},{12,8},{16,12},{20,16},{24,20},{28,24},{5,1},{9,5},{13... | collective-permute-start | bytes 786440 | tf_op jit(solution)/shard_map/ppermute | solution.py:23
  87.3 2.1 %collective-permute-start.20 = (bf16[32,1280]{1,0:T(8,128)(2,1)S(1)}, bf16[32,1280]{1,0:T(8,128)(2,1)S(1)}, u32[]{:S(2)}, u32[]{:S(2)}) collective-permute-start(bf16[32,1280]{1,0:T(8,128)(2,1)S(1)} %get-tuple-element.50), channel_id=1, source_target_pairs={{0,3},{1,2},{2,1},{3,0},{4,7},{5,6},{6,5},{7,4},{8,11},{9,10},{10,... | collective-permute-start | bytes 245768 | tf_op jit(solution)/shard_map/ppermute | solution.py:19
  89.5 1.0 %collective-permute-done.18.refs_1_ = bf16[32,1280]{1,0:T(8,128)(2,1)S(1)} collective-permute-done((bf16[32,1280]{1,0:T(8,128)(2,1)S(1)}, bf16[32,1280]{1,0:T(8,128)(2,1)S(1)}, u32[]{:S(2)}, u32[]{:S(2)}) %collective-permute-start.18) | collective-permute-done | bytes 81952 | tf_op jit(solution)/shard_map/ppermute | solution.py:19
  90.5 2.0 %collective-permute-done.19.refs_2_ = bf16[32,1280]{1,0:T(8,128)(2,1)S(1)} collective-permute-done((bf16[32,1280]{1,0:T(8,128)(2,1)S(1)}, bf16[32,1280]{1,0:T(8,128)(2,1)S(1)}, u32[]{:S(2)}, u32[]{:S(2)}) %collective-permute-start.19) | collective-permute-done | bytes 81952 | tf_op jit(solution)/shard_map/ppermute | solution.py:19
  92.5 2.3 %shard_map.85 = (f32[1024,128]{1,0:T(8,128)}, f32[128,1024]{1,0:T(8,128)}) custom-call(bf16[32,1280]{1,0:T(8,128)(2,1)S(1)} %get-tuple-element.47.refs_0_, bf16[32,1280]{1,0:T(8,128)(2,1)S(1)} %collective-permute-done.18.refs_1_, bf16[32,1280]{1,0:T(8,128)(2,1)S(1)} %collective-permute-done.19.refs_2_, bf16[32,1280]{1,0:T(8,128)(2,1)S(1)} %collective-permute-done.20.refs_3_, ...), custom_call_target="tpu_custom_call" | custom-call | tf_op jit(solution)/shard_map/pallas_call | solution.py:157
  94.9 1.0 %maximum_bitcast_fusion = bf16[1,128,4096]{2,1,0:T(8,128)(2,1)} fusion(bf16[32,4096]{1,0:T(8,128)(2,1)S(1)} %collective-permute-done.17, bf16[96,4096]{1,0:T(8,128)(2,1)S(1)} %collective-permute-done.16), kind=kLoop, calls=%fused_computation | loop fusion | flops 2097152 | bytes 2097152 | tf_op jit(solution)/shard_map/broadcast_in_dim | solution.py:211
  (76 shorter events, 13.3 us)
Async XLA Ops:
  0.6 30.5 %copy-start = (bf16[1,128,4096]{2,1,0:T(8,128)(2,1)S(1)}, bf16[1,128,4096]{2,1,0:T(8,128)(2,1)}, u32[]{:S(2)}) copy-start(bf16[1,128,4096]{2,1,0:T(8,128)(2,1)} %param.8) | copy-start | bytes 3145732
  1.7 17.2 %collective-permute-start = (bf16[32,4096]{1,0:T(8,128)(2,1)S(1)}, bf16[32,4096]{1,0:T(8,128)(2,1)S(1)}, u32[]{:S(2)}, u32[]{:S(2)}) collective-permute-start(bf16[32,4096]{1,0:T(8,128)(2,1)S(1)} %slice_bitcast_fusion), channel_id=1, source_target_pairs={{0,16},{4,20},{8,24},{12,28},{16,0},{20,4},{24,8},{28,12},{1,17},{... | collective-permute-start | bytes 786440 | tf_op jit(solution)/shard_map/ppermute | solution.py:19
  16.1 15.0 %copy-start.1 = (bf16[1,128,4096]{2,1,0:T(8,128)(2,1)S(1)}, bf16[1,128,4096]{2,1,0:T(8,128)(2,1)}, u32[]{:S(2)}) copy-start(bf16[1,128,4096]{2,1,0:T(8,128)(2,1)} %param.6) | copy-start | bytes 3145732
  16.1 19.6 %collective-permute-start.4 = (bf16[32,4096]{1,0:T(8,128)(2,1)}, bf16[32,4096]{1,0:T(8,128)(2,1)}, u32[]{:S(2)}, u32[]{:S(2)}) collective-permute-start(bf16[32,4096]{1,0:T(8,128)(2,1)} %shard_map.77), channel_id=1, source_target_pairs={{0,16},{4,20},{8,24},{12,28},{16,0},{20,4},{24,8},{28,12},{1,17},{... | collective-permute-start | bytes 786440 | tf_op jit(solution)/shard_map/ppermute | solution.py:19
  16.3 15.3 %collective-permute-start.3 = (bf16[128,1024]{1,0:T(8,128)(2,1)}, bf16[128,1024]{1,0:T(8,128)(2,1)S(1)}, u32[]{:S(2)}, u32[]{:S(2)}) collective-permute-start(bf16[128,1024]{1,0:T(8,128)(2,1)} %get-tuple-element.53), channel_id=1, source_target_pairs={{0,3},{1,2},{2,1},{3,0},{4,7},{5,6},{6,5},{7,4},{8,11},{9,10},{10,... | collective-permute-start | bytes 786440 | tf_op jit(solution)/shard_map/ppermute | solution.py:19
  18.5 13.1 %collective-permute-start.2 = (bf16[128,1024]{1,0:T(8,128)(2,1)}, bf16[128,1024]{1,0:T(8,128)(2,1)}, u32[]{:S(2)}, u32[]{:S(2)}) collective-permute-start(bf16[128,1024]{1,0:T(8,128)(2,1)} %get-tuple-element.54), channel_id=1, source_target_pairs={{0,2},{1,3},{2,0},{3,1},{4,6},{5,7},{6,4},{7,5},{8,10},{9,11},{10,... | collective-permute-start | bytes 786440 | tf_op jit(solution)/shard_map/ppermute | solution.py:19
  18.7 12.9 %collective-permute-start.1 = (bf16[128,1024]{1,0:T(8,128)(2,1)}, bf16[128,1024]{1,0:T(8,128)(2,1)}, u32[]{:S(2)}, u32[]{:S(2)}) collective-permute-start(bf16[128,1024]{1,0:T(8,128)(2,1)} %get-tuple-element.55), channel_id=1, source_target_pairs={{0,1},{1,0},{2,3},{3,2},{4,5},{5,4},{6,7},{7,6},{8,9},{9,8},{10,11... | collective-permute-start | bytes 786440 | tf_op jit(solution)/shard_map/ppermute | solution.py:19
  28.7 32.4 %collective-permute-start.8 = (bf16[32,4096]{1,0:T(8,128)(2,1)}, bf16[32,4096]{1,0:T(8,128)(2,1)}, u32[]{:S(2)}, u32[]{:S(2)}) collective-permute-start(bf16[32,4096]{1,0:T(8,128)(2,1)} %shard_map.79), channel_id=1, source_target_pairs={{0,16},{4,20},{8,24},{12,28},{16,0},{20,4},{24,8},{28,12},{1,17},{... | collective-permute-start | bytes 786440 | tf_op jit(solution)/shard_map/ppermute | solution.py:19
  35.7 11.2 %copy-start.25 = (bf16[32,1280]{1,0:T(8,128)(2,1)S(1)}, bf16[32,1280]{1,0:T(8,128)(2,1)}, u32[]{:S(2)}) copy-start(bf16[32,1280]{1,0:T(8,128)(2,1)} %copy-done.24) | copy-start | bytes 245764
  35.7 12.4 %copy-start.23 = (bf16[32,1280]{1,0:T(8,128)(2,1)S(1)}, bf16[32,1280]{1,0:T(8,128)(2,1)}, u32[]{:S(2)}) copy-start(bf16[32,1280]{1,0:T(8,128)(2,1)} %copy-done.22) | copy-start | bytes 245764
  35.7 12.5 %copy-start.21 = (bf16[32,1280]{1,0:T(8,128)(2,1)S(1)}, bf16[32,1280]{1,0:T(8,128)(2,1)}, u32[]{:S(2)}) copy-start(bf16[32,1280]{1,0:T(8,128)(2,1)} %copy-done.20) | copy-start | bytes 245764
  44.8 27.9 %collective-permute-start.15 = (bf16[32,4096]{1,0:T(8,128)(2,1)}, bf16[32,4096]{1,0:T(8,128)(2,1)}, u32[]{:S(2)}, u32[]{:S(2)}) collective-permute-start(bf16[32,4096]{1,0:T(8,128)(2,1)} %shard_map.82), channel_id=1, source_target_pairs={{0,16},{4,20},{8,24},{12,28},{16,0},{20,4},{24,8},{28,12},{1,17},{... | collective-permute-start | bytes 786440 | tf_op jit(solution)/shard_map/ppermute | solution.py:19
  46.9 3.3 %collective-permute-start.5 = (bf16[32,1280]{1,0:T(8,128)(2,1)S(1)}, bf16[32,1280]{1,0:T(8,128)(2,1)S(1)}, u32[]{:S(2)}, u32[]{:S(2)}) collective-permute-start(bf16[32,1280]{1,0:T(8,128)(2,1)S(1)} %copy-done.25), channel_id=1, source_target_pairs={{0,1},{1,0},{2,3},{3,2},{4,5},{5,4},{6,7},{7,6},{8,9},{9,8},{10,11... | collective-permute-start | bytes 245768 | tf_op jit(solution)/shard_map/ppermute | solution.py:19
  48.1 3.6 %collective-permute-start.6 = (bf16[32,1280]{1,0:T(8,128)(2,1)S(1)}, bf16[32,1280]{1,0:T(8,128)(2,1)S(1)}, u32[]{:S(2)}, u32[]{:S(2)}) collective-permute-start(bf16[32,1280]{1,0:T(8,128)(2,1)S(1)} %copy-done.23), channel_id=1, source_target_pairs={{0,2},{1,3},{2,0},{3,1},{4,6},{5,7},{6,4},{7,5},{8,10},{9,11},{10,... | collective-permute-start | bytes 245768 | tf_op jit(solution)/shard_map/ppermute | solution.py:19
  48.2 4.9 %collective-permute-start.7 = (bf16[32,1280]{1,0:T(8,128)(2,1)S(1)}, bf16[32,1280]{1,0:T(8,128)(2,1)S(1)}, u32[]{:S(2)}, u32[]{:S(2)}) collective-permute-start(bf16[32,1280]{1,0:T(8,128)(2,1)S(1)} %copy-done.21), channel_id=1, source_target_pairs={{0,3},{1,2},{2,1},{3,0},{4,7},{5,6},{6,5},{7,4},{8,11},{9,10},{10,... | collective-permute-start | bytes 245768 | tf_op jit(solution)/shard_map/ppermute | solution.py:19
  54.9 3.9 %collective-permute-start.9 = (bf16[32,1280]{1,0:T(8,128)(2,1)S(1)}, bf16[32,1280]{1,0:T(8,128)(2,1)S(1)}, u32[]{:S(2)}, u32[]{:S(2)}) collective-permute-start(bf16[32,1280]{1,0:T(8,128)(2,1)S(1)} %get-tuple-element.33), channel_id=1, source_target_pairs={{0,1},{1,0},{2,3},{3,2},{4,5},{5,4},{6,7},{7,6},{8,9},{9,8},{10,11... | collective-permute-start | bytes 245768 | tf_op jit(solution)/shard_map/ppermute | solution.py:19
  56.5 3.5 %collective-permute-start.10 = (bf16[32,1280]{1,0:T(8,128)(2,1)S(1)}, bf16[32,1280]{1,0:T(8,128)(2,1)S(1)}, u32[]{:S(2)}, u32[]{:S(2)}) collective-permute-start(bf16[32,1280]{1,0:T(8,128)(2,1)S(1)} %get-tuple-element.34), channel_id=1, source_target_pairs={{0,2},{1,3},{2,0},{3,1},{4,6},{5,7},{6,4},{7,5},{8,10},{9,11},{10,... | collective-permute-start | bytes 245768 | tf_op jit(solution)/shard_map/ppermute | solution.py:19
  56.8 11.8 %copy-start.3 = (bf16[128,1024]{1,0:T(8,128)(2,1)S(1)}, bf16[128,1024]{1,0:T(8,128)(2,1)}, u32[]{:S(2)}) copy-start(bf16[128,1024]{1,0:T(8,128)(2,1)} %get-tuple-element.56.refs_0_.refs_12_.refs_4_) | copy-start | bytes 786436
  56.8 11.8 %copy-start.5 = (bf16[128,1024]{1,0:T(8,128)(2,1)S(1)}, bf16[128,1024]{1,0:T(8,128)(2,1)}, u32[]{:S(2)}) copy-start(bf16[128,1024]{1,0:T(8,128)(2,1)} %copy-done.4) | copy-start | bytes 786436
  56.8 11.8 %copy-start.13 = (bf16[32,4096]{1,0:T(8,128)(2,1)S(1)}, bf16[32,4096]{1,0:T(8,128)(2,1)}, u32[]{:S(2)}) copy-start(bf16[32,4096]{1,0:T(8,128)(2,1)} %copy-done.12) | copy-start | bytes 786436
  56.8 11.8 %copy-start.19 = (bf16[32,1280]{1,0:T(8,128)(2,1)S(1)}, bf16[32,1280]{1,0:T(8,128)(2,1)}, u32[]{:S(2)}) copy-start(bf16[32,1280]{1,0:T(8,128)(2,1)} %copy-done.18) | copy-start | bytes 245764
  56.8 4.4 %collective-permute-start.11 = (bf16[32,1280]{1,0:T(8,128)(2,1)S(1)}, bf16[32,1280]{1,0:T(8,128)(2,1)S(1)}, u32[]{:S(2)}, u32[]{:S(2)}) collective-permute-start(bf16[32,1280]{1,0:T(8,128)(2,1)S(1)} %get-tuple-element.35), channel_id=1, source_target_pairs={{0,3},{1,2},{2,1},{3,0},{4,7},{5,6},{6,5},{7,4},{8,11},{9,10},{10,... | collective-permute-start | bytes 245768 | tf_op jit(solution)/shard_map/ppermute | solution.py:19
  63.0 3.4 %collective-permute-start.12 = (bf16[32,1280]{1,0:T(8,128)(2,1)S(1)}, bf16[32,1280]{1,0:T(8,128)(2,1)S(1)}, u32[]{:S(2)}, u32[]{:S(2)}) collective-permute-start(bf16[32,1280]{1,0:T(8,128)(2,1)S(1)} %get-tuple-element.37), channel_id=1, source_target_pairs={{0,1},{1,0},{2,3},{3,2},{4,5},{5,4},{6,7},{7,6},{8,9},{9,8},{10,11... | collective-permute-start | bytes 245768 | tf_op jit(solution)/shard_map/ppermute | solution.py:19
  63.5 3.3 %collective-permute-start.13 = (bf16[32,1280]{1,0:T(8,128)(2,1)S(1)}, bf16[32,1280]{1,0:T(8,128)(2,1)S(1)}, u32[]{:S(2)}, u32[]{:S(2)}) collective-permute-start(bf16[32,1280]{1,0:T(8,128)(2,1)S(1)} %get-tuple-element.38), channel_id=1, source_target_pairs={{0,2},{1,3},{2,0},{3,1},{4,6},{5,7},{6,4},{7,5},{8,10},{9,11},{10,... | collective-permute-start | bytes 245768 | tf_op jit(solution)/shard_map/ppermute | solution.py:19
  64.3 4.2 %collective-permute-start.14 = (bf16[32,1280]{1,0:T(8,128)(2,1)S(1)}, bf16[32,1280]{1,0:T(8,128)(2,1)S(1)}, u32[]{:S(2)}, u32[]{:S(2)}) collective-permute-start(bf16[32,1280]{1,0:T(8,128)(2,1)S(1)} %get-tuple-element.39), channel_id=1, source_target_pairs={{0,3},{1,2},{2,1},{3,0},{4,7},{5,6},{6,5},{7,4},{8,11},{9,10},{10,... | collective-permute-start | bytes 245768 | tf_op jit(solution)/shard_map/ppermute | solution.py:19
  72.7 22.2 %collective-permute-start.16 = (bf16[96,4096]{1,0:T(8,128)(2,1)}, bf16[96,4096]{1,0:T(8,128)(2,1)S(1)}, u32[]{:S(2)}, u32[]{:S(2)}) collective-permute-start(bf16[96,4096]{1,0:T(8,128)(2,1)} %shard_map.83), channel_id=1, source_target_pairs={{4,0},{8,4},{12,8},{16,12},{20,16},{24,20},{28,24},{5,1},{9,5},{13... | collective-permute-start | bytes 2359304 | tf_op jit(solution)/shard_map/ppermute | solution.py:23
  82.9 9.6 %copy-start.6 = (bf16[128,1024]{1,0:T(8,128)(2,1)S(1)}, bf16[128,1024]{1,0:T(8,128)(2,1)}, u32[]{:S(2)}) copy-start(bf16[128,1024]{1,0:T(8,128)(2,1)} %copy-done.4) | copy-start | bytes 786436
  82.9 9.6 %copy-start.9 = (f32[1024,128]{1,0:T(8,128)S(1)}, f32[1024,128]{1,0:T(8,128)}, u32[]{:S(2)}) copy-start(f32[1024,128]{1,0:T(8,128)} %copy-done.7) | copy-start | bytes 1572868
  84.8 10.0 %collective-permute-start.17 = (bf16[32,4096]{1,0:T(8,128)(2,1)S(1)}, bf16[32,4096]{1,0:T(8,128)(2,1)S(1)}, u32[]{:S(2)}, u32[]{:S(2)}) collective-permute-start(bf16[32,4096]{1,0:T(8,128)(2,1)S(1)} %get-tuple-element.46), channel_id=1, source_target_pairs={{4,0},{8,4},{12,8},{16,12},{20,16},{24,20},{28,24},{5,1},{9,5},{13... | collective-permute-start | bytes 786440 | tf_op jit(solution)/shard_map/ppermute | solution.py:23
  86.8 3.7 %collective-permute-start.18 = (bf16[32,1280]{1,0:T(8,128)(2,1)S(1)}, bf16[32,1280]{1,0:T(8,128)(2,1)S(1)}, u32[]{:S(2)}, u32[]{:S(2)}) collective-permute-start(bf16[32,1280]{1,0:T(8,128)(2,1)S(1)} %get-tuple-element.48), channel_id=1, source_target_pairs={{0,1},{1,0},{2,3},{3,2},{4,5},{5,4},{6,7},{7,6},{8,9},{9,8},{10,11... | collective-permute-start | bytes 245768 | tf_op jit(solution)/shard_map/ppermute | solution.py:19
  87.1 5.4 %collective-permute-start.19 = (bf16[32,1280]{1,0:T(8,128)(2,1)S(1)}, bf16[32,1280]{1,0:T(8,128)(2,1)S(1)}, u32[]{:S(2)}, u32[]{:S(2)}) collective-permute-start(bf16[32,1280]{1,0:T(8,128)(2,1)S(1)} %get-tuple-element.49), channel_id=1, source_target_pairs={{0,2},{1,3},{2,0},{3,1},{4,6},{5,7},{6,4},{7,5},{8,10},{9,11},{10,... | collective-permute-start | bytes 245768 | tf_op jit(solution)/shard_map/ppermute | solution.py:19
  87.3 5.2 %collective-permute-start.20 = (bf16[32,1280]{1,0:T(8,128)(2,1)S(1)}, bf16[32,1280]{1,0:T(8,128)(2,1)S(1)}, u32[]{:S(2)}, u32[]{:S(2)}) collective-permute-start(bf16[32,1280]{1,0:T(8,128)(2,1)S(1)} %get-tuple-element.50), channel_id=1, source_target_pairs={{0,3},{1,2},{2,1},{3,0},{4,7},{5,6},{6,5},{7,4},{8,11},{9,10},{10,... | collective-permute-start | bytes 245768 | tf_op jit(solution)/shard_map/ppermute | solution.py:19
  (15 other events, 18.1 us)

commit v4 on v3

--- a/solution.py
+++ b/solution.py
@@ -12,7 +12,8 @@
 VMEM = pl.BlockSpec(memory_space=pltpu.VMEM)
 SMEM = pl.BlockSpec(memory_space=pltpu.SMEM)
 ANY = pl.BlockSpec(memory_space=pl.ANY)
-PARAMS = pltpu.CompilerParams(vmem_limit_bytes=32 * 1024 * 1024)
+PARAMS = pltpu.CompilerParams(vmem_limit_bytes=16 * 1024 * 1024)
+SMALL = pltpu.CompilerParams(vmem_limit_bytes=4 * 1024 * 1024)
 
 
 def exchanged(x, axis, mask):
@@ -50,8 +51,9 @@
         functools.partial(copy_kernel, start),
         out_shape=jax.ShapeDtypeStruct((rows, stash.shape[1]), stash.dtype),
         in_specs=[ANY] * (1 + len(waits)),
-        out_specs=ANY,
+        out_specs=VMEM,
         scratch_shapes=[pltpu.SemaphoreType.DMA],
+        compiler_params=SMALL,
     )(stash, *waits)
 
 
@@ -66,6 +68,7 @@
         in_specs=[ANY, ANY],
         out_specs=ANY,
         input_output_aliases={0: 0},
+        compiler_params=SMALL,
     )(value, wait)
 
 

time: 96.5 us -> 82.5 us (0.85)
  Pallas kernels: 37.4 us -> 5.37 us
  waiting for transfers between devices: 12.7 us -> 40.7 us
  local copies, waits for them, and re-layouts: 11.8 us -> 3.25 us
    pallas_call x3, Pallas kernels: 27.2 us -> 0.09 us  [rows_after(): pl.pallas_call(functools.partial(copy_kernel, start), out_shape=jax.Shape...]
    ppermute x19, waiting for transfers between devices: 12.7 us -> 33.9 us  [exchanged(): lax.ppermute(x, axis, [(i, i ^ mask) for i in range(lax.axis_size(axis))])]
    unnamed x52 -> x10, local copies, waits for them, and re-layouts: 8.54 us -> 0.82 us
    ppermute x2, waiting for transfers between devices: 0.01 us -> 6.73 us  [to_previous(): lax.ppermute(x, axis, [(i, i - 1) for i in range(1, lax.axis_size(axis))])]
    ppermute x19, starting transfers between devices: 21.5 us -> 17 us  [exchanged(): lax.ppermute(x, axis, [(i, i ^ mask) for i in range(lax.axis_size(axis))])]
    ppermute x2, starting transfers between devices: 10.1 us -> 13.7 us  [to_previous(): lax.ppermute(x, axis, [(i, i - 1) for i in range(1, lax.axis_size(axis))])]
    pallas_call x4, Pallas kernels: 6.34 us -> 3.41 us  [run_chunk(): pl.pallas_call(functools.partial(chunk_kernel, groups, start, len(waits))...]
    pallas_call x2, Pallas kernels: 3.95 us -> 1.87 us  [run_sum(): pl.pallas_call(functools.partial(sum_kernel, groups, spans, first), out_s...]
  transfers between devices with their start and end apart: 21 -> 21, of which waited for: 11 -> 13; matrix products, arithmetic and copies ran while one was open for 3% -> 2% of each run, Pallas kernels for 39% -> 7%
where the time goes in v4:
time: 82.5 us; the launch traced here: 82.3 us
  waiting for transfers between devices  40.7 us (49%)
  starting transfers between devices  30.7 us (37%)
  Pallas kernels  5.37 us (7%)
  local copies, waits for them, and re-layouts  3.25 us (4%)
  other arithmetic  1.05 us (1%)
  between operations  0.87 us (1%)
    ppermute x19, waiting for transfers between devices, exchanged(): lax.ppermute(x, axis, [(i, i ^ mask) for i in range(lax.axis_size(axis))])  33.9 us
    ppermute x19, starting transfers between devices, exchanged(): lax.ppermute(x, axis, [(i, i ^ mask) for i in range(lax.axis_size(axis))])  17 us
    ppermute x2, starting transfers between devices, to_previous(): lax.ppermute(x, axis, [(i, i - 1) for i in range(1, lax.axis_size(axis))])  13.7 us
    ppermute x2, waiting for transfers between devices, to_previous(): lax.ppermute(x, axis, [(i, i - 1) for i in range(1, lax.axis_size(axis))])  6.73 us
    pallas_call x4, Pallas kernels, run_chunk(): pl.pallas_call(functools.partial(chunk_kernel, groups, start, len(waits))...  3.41 us
    pallas_call x2, Pallas kernels, run_sum(): pl.pallas_call(functools.partial(sum_kernel, groups, spans, first), out_s...  1.87 us
  transfers between devices with their start and end apart: 21, of which 13 were waited for; matrix products, arithmetic and copies ran while one was open for 2% of the time, Pallas kernels for 7%

profile of v4, /device:TPU:1, one launch (start us, length us, event | category | flops | bytes accessed | tf_op | source)
XLA Modules:
  0.0 82.3 jit_solution(16988328596074360156)
XLA Ops:
  0.6 1.1 %slice_bitcast_fusion = bf16[32,4096]{1,0:T(8,128)(2,1)S(1)} fusion(bf16[1,128,4096]{2,1,0:T(8,128)(2,1)} %param.5), kind=kLoop, calls=%fused_computation.7 | loop fusion | bytes 524288 | tf_op jit(solution)/shard_map/slice | solution.py:191
  1.7 3.2 %collective-permute-start = (bf16[32,4096]{1,0:T(8,128)(2,1)S(1)}, bf16[32,4096]{1,0:T(8,128)(2,1)S(1)}, u32[]{:S(2)}, u32[]{:S(2)}) collective-permute-start(bf16[32,4096]{1,0:T(8,128)(2,1)S(1)} %slice_bitcast_fusion), channel_id=1, source_target_pairs={{0,16},{4,20},{8,24},{12,28},{16,0},{20,4},{24,8},{28,12},{1,17},{... | collective-permute-start | bytes 786440 | tf_op jit(solution)/shard_map/ppermute | solution.py:20
  4.9 1.4 %dynamic-slice_bitcast_fusion.1 = (bf16[128,1024]{1,0:T(8,128)(2,1)S(1)}, bf16[128,1024]{1,0:T(8,128)(2,1)S(1)}, bf16[128,1024]{1,0:T(8,128)(2,1)S(1)}, bf16[128,1024]{1,0:T(8,128)(2,1)S(1)}) fusion(bf16[1,128,4096]{2,1,0:T(8,128)(2,1)} %param.6, s32[]{:T(128)S(6)} %select_n.14, s32[]{:T(128)S(6)} %select_n.13, s32[]{:T(128)S(6)} %select_n.12, s32[]{:T(128)S(6)} %select_n.15), kind=kLoop, calls=%fused_computation.4 | loop fusion | bytes 2097168 | tf_op jit(solution)/shard_map/dynamic_slice | solution.py:194
  6.6 2.2 %collective-permute-start.3 = (bf16[128,1024]{1,0:T(8,128)(2,1)S(1)}, bf16[128,1024]{1,0:T(8,128)(2,1)S(1)}, u32[]{:S(2)}, u32[]{:S(2)}) collective-permute-start(bf16[128,1024]{1,0:T(8,128)(2,1)S(1)} %get-tuple-element.53), channel_id=1, source_target_pairs={{0,3},{1,2},{2,1},{3,0},{4,7},{5,6},{6,5},{7,4},{8,11},{9,10},{10,... | collective-permute-start | bytes 786440 | tf_op jit(solution)/shard_map/ppermute | solution.py:20
  9.3 12.9 %collective-permute-done.saved_ref.refs_0_ = bf16[32,4096]{1,0:T(8,128)(2,1)S(1)} collective-permute-done((bf16[32,4096]{1,0:T(8,128)(2,1)S(1)}, bf16[32,4096]{1,0:T(8,128)(2,1)S(1)}, u32[]{:S(2)}, u32[]{:S(2)}) %collective-permute-start) | collective-permute-done | bytes 262176 | tf_op jit(solution)/shard_map/ppermute | solution.py:20
  22.3 0.4 fusion.dact_ref
  22.8 0.6 copy-done.2
  23.4 0.8 %shard_map.76 = (bf16[32,4096]{1,0:T(8,128)(2,1)S(1)}, bf16[32,1280]{1,0:T(8,128)(2,1)S(1)}, bf16[32,1280]{1,0:T(8,128)(2,1)S(1)}, bf16[32,1280]{1,0:T(8,128)(2,1)S(1)}, bf16[32,1280]{1,0:T(8,128)(2,1)S(1)}) custom-call(s32[1]{0:T(128)} %bitcast.me_ref, bf16[32,4096]{1,0:T(8,128)(2,1)S(1)} %collective-permute-done.saved_ref.refs_0_, ...), custom_call_target="tpu_custom_call" | custom-call | tf_op jit(solution)/shard_map/pallas_call | solution.py:113
  24.3 9.1 %collective-permute-done.4.saved_ref.refs_0_ = bf16[32,4096]{1,0:T(8,128)(2,1)S(1)} collective-permute-done((bf16[32,4096]{1,0:T(8,128)(2,1)S(1)}, bf16[32,4096]{1,0:T(8,128)(2,1)S(1)}, u32[]{:S(2)}, u32[]{:S(2)}) %collective-permute-start.4) | collective-permute-done | bytes 262176 | tf_op jit(solution)/shard_map/ppermute | solution.py:20
  33.7 2.6 %collective-permute-start.7 = (bf16[32,1280]{1,0:T(8,128)(2,1)S(1)}, bf16[32,1280]{1,0:T(8,128)(2,1)S(1)}, u32[]{:S(2)}, u32[]{:S(2)}) collective-permute-start(bf16[32,1280]{1,0:T(8,128)(2,1)S(1)} %get-tuple-element.31), channel_id=1, source_target_pairs={{0,3},{1,2},{2,1},{3,0},{4,7},{5,6},{6,5},{7,4},{8,11},{9,10},{10,... | collective-permute-start | bytes 245768 | tf_op jit(solution)/shard_map/ppermute | solution.py:20
  36.2 0.9 %collective-permute-done.5.refs_0_.refs_3_ = bf16[32,1280]{1,0:T(8,128)(2,1)S(1)} collective-permute-done((bf16[32,1280]{1,0:T(8,128)(2,1)S(1)}, bf16[32,1280]{1,0:T(8,128)(2,1)S(1)}, u32[]{:S(2)}, u32[]{:S(2)}) %collective-permute-start.5) | collective-permute-done | bytes 81952 | tf_op jit(solution)/shard_map/ppermute | solution.py:20
  37.3 1.1 %collective-permute-done.7.refs_2_.refs_9_ = bf16[32,1280]{1,0:T(8,128)(2,1)S(1)} collective-permute-done((bf16[32,1280]{1,0:T(8,128)(2,1)S(1)}, bf16[32,1280]{1,0:T(8,128)(2,1)S(1)}, u32[]{:S(2)}, u32[]{:S(2)}) %collective-permute-start.7) | collective-permute-done | bytes 81952 | tf_op jit(solution)/shard_map/ppermute | solution.py:20
  38.4 0.8 %shard_map.78 = (bf16[32,4096]{1,0:T(8,128)(2,1)S(1)}, bf16[32,1280]{1,0:T(8,128)(2,1)S(1)}, bf16[32,1280]{1,0:T(8,128)(2,1)S(1)}, bf16[32,1280]{1,0:T(8,128)(2,1)S(1)}, bf16[32,1280]{1,0:T(8,128)(2,1)S(1)}) custom-call(s32[1]{0:T(128)} %bitcast.me_ref, bf16[32,4096]{1,0:T(8,128)(2,1)S(1)} %collective-permute-done.4.saved_ref.refs_0_, ...), custom_call_target="tpu_custom_call" | custom-call | tf_op jit(solution)/shard_map/pallas_call | solution.py:113
  39.2 1.2 %collective-permute-start.9 = (bf16[32,1280]{1,0:T(8,128)(2,1)S(1)}, bf16[32,1280]{1,0:T(8,128)(2,1)S(1)}, u32[]{:S(2)}, u32[]{:S(2)}) collective-permute-start(bf16[32,1280]{1,0:T(8,128)(2,1)S(1)} %get-tuple-element.33), channel_id=1, source_target_pairs={{0,1},{1,0},{2,3},{3,2},{4,5},{5,4},{6,7},{7,6},{8,9},{9,8},{10,11... | collective-permute-start | bytes 245768 | tf_op jit(solution)/shard_map/ppermute | solution.py:20
  40.5 1.5 %collective-permute-start.10 = (bf16[32,1280]{1,0:T(8,128)(2,1)S(1)}, bf16[32,1280]{1,0:T(8,128)(2,1)S(1)}, u32[]{:S(2)}, u32[]{:S(2)}) collective-permute-start(bf16[32,1280]{1,0:T(8,128)(2,1)S(1)} %get-tuple-element.34), channel_id=1, source_target_pairs={{0,2},{1,3},{2,0},{3,1},{4,6},{5,7},{6,4},{7,5},{8,10},{9,11},{10,... | collective-permute-start | bytes 245768 | tf_op jit(solution)/shard_map/ppermute | solution.py:20
  41.9 1.7 %collective-permute-done.9.refs_0_.refs_4_ = bf16[32,1280]{1,0:T(8,128)(2,1)S(1)} collective-permute-done((bf16[32,1280]{1,0:T(8,128)(2,1)S(1)}, bf16[32,1280]{1,0:T(8,128)(2,1)S(1)}, u32[]{:S(2)}, u32[]{:S(2)}) %collective-permute-start.9) | collective-permute-done | bytes 81952 | tf_op jit(solution)/shard_map/ppermute | solution.py:20
  43.6 1.3 %collective-permute-done.10.refs_1_.refs_7_ = bf16[32,1280]{1,0:T(8,128)(2,1)S(1)} collective-permute-done((bf16[32,1280]{1,0:T(8,128)(2,1)S(1)}, bf16[32,1280]{1,0:T(8,128)(2,1)S(1)}, u32[]{:S(2)}, u32[]{:S(2)}) %collective-permute-start.10) | collective-permute-done | bytes 81952 | tf_op jit(solution)/shard_map/ppermute | solution.py:20
  44.9 1.5 %collective-permute-done.11.refs_2_.refs_10_ = bf16[32,1280]{1,0:T(8,128)(2,1)S(1)} collective-permute-done((bf16[32,1280]{1,0:T(8,128)(2,1)S(1)}, bf16[32,1280]{1,0:T(8,128)(2,1)S(1)}, u32[]{:S(2)}, u32[]{:S(2)}) %collective-permute-start.11) | collective-permute-done | bytes 81952 | tf_op jit(solution)/shard_map/ppermute | solution.py:20
  46.4 0.9 %shard_map.80 = (bf16[32,4096]{1,0:T(8,128)(2,1)S(1)}, bf16[32,1280]{1,0:T(8,128)(2,1)S(1)}, bf16[32,1280]{1,0:T(8,128)(2,1)S(1)}, bf16[32,1280]{1,0:T(8,128)(2,1)S(1)}, bf16[32,1280]{1,0:T(8,128)(2,1)S(1)}) custom-call(s32[1]{0:T(128)} %bitcast.me_ref, bf16[32,4096]{1,0:T(8,128)(2,1)S(1)} %collective-permute-done.8.saved_ref, ...), custom_call_target="tpu_custom_call" | custom-call | tf_op jit(solution)/shard_map/pallas_call | solution.py:113
  47.6 2.4 %collective-permute-start.14 = (bf16[32,1280]{1,0:T(8,128)(2,1)S(1)}, bf16[32,1280]{1,0:T(8,128)(2,1)S(1)}, u32[]{:S(2)}, u32[]{:S(2)}) collective-permute-start(bf16[32,1280]{1,0:T(8,128)(2,1)S(1)} %get-tuple-element.39), channel_id=1, source_target_pairs={{0,3},{1,2},{2,1},{3,0},{4,7},{5,6},{6,5},{7,4},{8,11},{9,10},{10,... | collective-permute-start | bytes 245768 | tf_op jit(solution)/shard_map/ppermute | solution.py:20
  50.0 1.3 %collective-permute-done.12.refs_5_ = bf16[32,1280]{1,0:T(8,128)(2,1)S(1)} collective-permute-done((bf16[32,1280]{1,0:T(8,128)(2,1)S(1)}, bf16[32,1280]{1,0:T(8,128)(2,1)S(1)}, u32[]{:S(2)}, u32[]{:S(2)}) %collective-permute-start.12) | collective-permute-done | bytes 81952 | tf_op jit(solution)/shard_map/ppermute | solution.py:20
  51.3 1.3 %collective-permute-done.13.refs_8_ = bf16[32,1280]{1,0:T(8,128)(2,1)S(1)} collective-permute-done((bf16[32,1280]{1,0:T(8,128)(2,1)S(1)}, bf16[32,1280]{1,0:T(8,128)(2,1)S(1)}, u32[]{:S(2)}, u32[]{:S(2)}) %collective-permute-start.13) | collective-permute-done | bytes 81952 | tf_op jit(solution)/shard_map/ppermute | solution.py:20
  52.6 0.6 shard_map.81
  53.2 11.8 %collective-permute-start.16 = (bf16[96,4096]{1,0:T(8,128)(2,1)S(1)}, bf16[96,4096]{1,0:T(8,128)(2,1)S(1)}, u32[]{:S(2)}, u32[]{:S(2)}) collective-permute-start(bf16[96,4096]{1,0:T(8,128)(2,1)S(1)} %shard_map.83), channel_id=1, source_target_pairs={{4,0},{8,4},{12,8},{16,12},{20,16},{24,20},{28,24},{5,1},{9,5},{13... | collective-permute-start | bytes 2359304 | tf_op jit(solution)/shard_map/ppermute | solution.py:24
  65.0 0.9 %shard_map.84 = (bf16[32,4096]{1,0:T(8,128)(2,1)S(1)}, bf16[32,1280]{1,0:T(8,128)(2,1)S(1)}, bf16[32,1280]{1,0:T(8,128)(2,1)S(1)}, bf16[32,1280]{1,0:T(8,128)(2,1)S(1)}, bf16[32,1280]{1,0:T(8,128)(2,1)S(1)}) custom-call(s32[1]{0:T(128)} %bitcast.me_ref, bf16[32,4096]{1,0:T(8,128)(2,1)S(1)} %collective-permute-done.15.wait_ref.saved_ref, ...), custom_call_target="tpu_custom_call" | custom-call | tf_op jit(solution)/shard_map/pallas_call | solution.py:113
  65.9 1.9 %collective-permute-start.17 = (bf16[32,4096]{1,0:T(8,128)(2,1)S(1)}, bf16[32,4096]{1,0:T(8,128)(2,1)S(1)}, u32[]{:S(2)}, u32[]{:S(2)}) collective-permute-start(bf16[32,4096]{1,0:T(8,128)(2,1)S(1)} %get-tuple-element.46), channel_id=1, source_target_pairs={{4,0},{8,4},{12,8},{16,12},{20,16},{24,20},{28,24},{5,1},{9,5},{13... | collective-permute-start | bytes 786440 | tf_op jit(solution)/shard_map/ppermute | solution.py:24
  68.3 2.2 %collective-permute-start.20 = (bf16[32,1280]{1,0:T(8,128)(2,1)S(1)}, bf16[32,1280]{1,0:T(8,128)(2,1)S(1)}, u32[]{:S(2)}, u32[]{:S(2)}) collective-permute-start(bf16[32,1280]{1,0:T(8,128)(2,1)S(1)} %get-tuple-element.50), channel_id=1, source_target_pairs={{0,3},{1,2},{2,1},{3,0},{4,7},{5,6},{6,5},{7,4},{8,11},{9,10},{10,... | collective-permute-start | bytes 245768 | tf_op jit(solution)/shard_map/ppermute | solution.py:20
  70.5 1.1 %collective-permute-done.18.refs_1_ = bf16[32,1280]{1,0:T(8,128)(2,1)S(1)} collective-permute-done((bf16[32,1280]{1,0:T(8,128)(2,1)S(1)}, bf16[32,1280]{1,0:T(8,128)(2,1)S(1)}, u32[]{:S(2)}, u32[]{:S(2)}) %collective-permute-start.18) | collective-permute-done | bytes 81952 | tf_op jit(solution)/shard_map/ppermute | solution.py:20
  71.6 1.6 %collective-permute-done.19.refs_2_ = bf16[32,1280]{1,0:T(8,128)(2,1)S(1)} collective-permute-done((bf16[32,1280]{1,0:T(8,128)(2,1)S(1)}, bf16[32,1280]{1,0:T(8,128)(2,1)S(1)}, u32[]{:S(2)}, u32[]{:S(2)}) %collective-permute-start.19) | collective-permute-done | bytes 81952 | tf_op jit(solution)/shard_map/ppermute | solution.py:20
  73.2 1.3 %shard_map.85 = (f32[1024,128]{1,0:T(8,128)}, f32[128,1024]{1,0:T(8,128)}) custom-call(bf16[32,1280]{1,0:T(8,128)(2,1)S(1)} %get-tuple-element.47.refs_0_, bf16[32,1280]{1,0:T(8,128)(2,1)S(1)} %collective-permute-done.18.refs_1_, bf16[32,1280]{1,0:T(8,128)(2,1)S(1)} %collective-permute-done.19.refs_2_, bf16[32,1280]{1,0:T(8,128)(2,1)S(1)} %collective-permute-done.20.refs_3_, ...), custom_call_target="tpu_custom_call" | custom-call | tf_op jit(solution)/shard_map/pallas_call | solution.py:160
  74.5 6.7 %collective-permute-done.17 = bf16[32,4096]{1,0:T(8,128)(2,1)S(1)} collective-permute-done((bf16[32,4096]{1,0:T(8,128)(2,1)S(1)}, bf16[32,4096]{1,0:T(8,128)(2,1)S(1)}, u32[]{:S(2)}, u32[]{:S(2)}) %collective-permute-start.17) | collective-permute-done | bytes 262176 | tf_op jit(solution)/shard_map/ppermute | solution.py:24
  81.3 1.1 %maximum_bitcast_fusion = bf16[1,128,4096]{2,1,0:T(8,128)(2,1)} fusion(bf16[32,4096]{1,0:T(8,128)(2,1)S(1)} %collective-permute-done.17, bf16[96,4096]{1,0:T(8,128)(2,1)S(1)} %collective-permute-done.16), kind=kLoop, calls=%fused_computation | loop fusion | flops 2097152 | bytes 2097152 | tf_op jit(solution)/shard_map/broadcast_in_dim | solution.py:214
  (34 shorter events, 2.1 us)
Async XLA Ops:
  0.6 21.7 %copy-start = (bf16[1,128,4096]{2,1,0:T(8,128)(2,1)S(1)}, bf16[1,128,4096]{2,1,0:T(8,128)(2,1)}, u32[]{:S(2)}) copy-start(bf16[1,128,4096]{2,1,0:T(8,128)(2,1)} %param.8) | copy-start | bytes 3145732
  1.7 20.5 %collective-permute-start = (bf16[32,4096]{1,0:T(8,128)(2,1)S(1)}, bf16[32,4096]{1,0:T(8,128)(2,1)S(1)}, u32[]{:S(2)}, u32[]{:S(2)}) collective-permute-start(bf16[32,4096]{1,0:T(8,128)(2,1)S(1)} %slice_bitcast_fusion), channel_id=1, source_target_pairs={{0,16},{4,20},{8,24},{12,28},{16,0},{20,4},{24,8},{28,12},{1,17},{... | collective-permute-start | bytes 786440 | tf_op jit(solution)/shard_map/ppermute | solution.py:20
  4.9 1.5 %copy-start.3 = (bf16[1,128,4096]{2,1,0:T(8,128)(2,1)S(1)}, bf16[1,128,4096]{2,1,0:T(8,128)(2,1)}, u32[]{:S(2)}) copy-start(bf16[1,128,4096]{2,1,0:T(8,128)(2,1)} %param.5) | copy-start | bytes 3145732
  6.5 15.8 %copy-start.1 = (bf16[1,128,4096]{2,1,0:T(8,128)(2,1)S(1)}, bf16[1,128,4096]{2,1,0:T(8,128)(2,1)}, u32[]{:S(2)}) copy-start(bf16[1,128,4096]{2,1,0:T(8,128)(2,1)} %param.6) | copy-start | bytes 3145732
  6.5 26.9 %collective-permute-start.4 = (bf16[32,4096]{1,0:T(8,128)(2,1)S(1)}, bf16[32,4096]{1,0:T(8,128)(2,1)S(1)}, u32[]{:S(2)}, u32[]{:S(2)}) collective-permute-start(bf16[32,4096]{1,0:T(8,128)(2,1)S(1)} %shard_map.77), channel_id=1, source_target_pairs={{0,16},{4,20},{8,24},{12,28},{16,0},{20,4},{24,8},{28,12},{1,17},{... | collective-permute-start | bytes 786440 | tf_op jit(solution)/shard_map/ppermute | solution.py:20
  6.6 16.2 %collective-permute-start.3 = (bf16[128,1024]{1,0:T(8,128)(2,1)S(1)}, bf16[128,1024]{1,0:T(8,128)(2,1)S(1)}, u32[]{:S(2)}, u32[]{:S(2)}) collective-permute-start(bf16[128,1024]{1,0:T(8,128)(2,1)S(1)} %get-tuple-element.53), channel_id=1, source_target_pairs={{0,3},{1,2},{2,1},{3,0},{4,7},{5,6},{6,5},{7,4},{8,11},{9,10},{10,... | collective-permute-start | bytes 786440 | tf_op jit(solution)/shard_map/ppermute | solution.py:20
  8.8 14.0 %collective-permute-start.2 = (bf16[128,1024]{1,0:T(8,128)(2,1)S(1)}, bf16[128,1024]{1,0:T(8,128)(2,1)S(1)}, u32[]{:S(2)}, u32[]{:S(2)}) collective-permute-start(bf16[128,1024]{1,0:T(8,128)(2,1)S(1)} %get-tuple-element.54), channel_id=1, source_target_pairs={{0,2},{1,3},{2,0},{3,1},{4,6},{5,7},{6,4},{7,5},{8,10},{9,11},{10,... | collective-permute-start | bytes 786440 | tf_op jit(solution)/shard_map/ppermute | solution.py:20
  9.0 13.8 %collective-permute-start.1 = (bf16[128,1024]{1,0:T(8,128)(2,1)S(1)}, bf16[128,1024]{1,0:T(8,128)(2,1)S(1)}, u32[]{:S(2)}, u32[]{:S(2)}) collective-permute-start(bf16[128,1024]{1,0:T(8,128)(2,1)S(1)} %get-tuple-element.55), channel_id=1, source_target_pairs={{0,1},{1,0},{2,3},{3,2},{4,5},{5,4},{6,7},{7,6},{8,9},{9,8},{10,11... | collective-permute-start | bytes 786440 | tf_op jit(solution)/shard_map/ppermute | solution.py:20
  22.2 1.2 %copy-start.2 = (bf16[1,4096,128]{2,1,0:T(8,128)(2,1)S(1)}, bf16[1,4096,128]{2,1,0:T(8,128)(2,1)}, u32[]{:S(2)}) copy-start(bf16[1,4096,128]{2,1,0:T(8,128)(2,1)} %param.7) | copy-start | bytes 3145732
  22.2 1.2 %copy-start.4 = (f32[1,4096]{1,0:T(1,128)S(1)}, f32[1,4096]{1,0:T(1,128)}, u32[]{:S(2)}) copy-start(f32[1,4096]{1,0:T(1,128)} %gain_ref.7) | copy-start | bytes 49156
  22.2 24.2 %collective-permute-start.8 = (bf16[32,4096]{1,0:T(8,128)(2,1)S(1)}, bf16[32,4096]{1,0:T(8,128)(2,1)S(1)}, u32[]{:S(2)}, u32[]{:S(2)}) collective-permute-start(bf16[32,4096]{1,0:T(8,128)(2,1)S(1)} %shard_map.79), channel_id=1, source_target_pairs={{0,16},{4,20},{8,24},{12,28},{16,0},{20,4},{24,8},{28,12},{1,17},{... | collective-permute-start | bytes 786440 | tf_op jit(solution)/shard_map/ppermute | solution.py:20
  33.4 19.7 %collective-permute-start.15 = (bf16[32,4096]{1,0:T(8,128)(2,1)S(1)}, bf16[32,4096]{1,0:T(8,128)(2,1)S(1)}, u32[]{:S(2)}, u32[]{:S(2)}) collective-permute-start(bf16[32,4096]{1,0:T(8,128)(2,1)S(1)} %shard_map.82), channel_id=1, source_target_pairs={{0,16},{4,20},{8,24},{12,28},{16,0},{20,4},{24,8},{28,12},{1,17},{... | collective-permute-start | bytes 786440 | tf_op jit(solution)/shard_map/ppermute | solution.py:20
  33.5 3.7 %collective-permute-start.5 = (bf16[32,1280]{1,0:T(8,128)(2,1)S(1)}, bf16[32,1280]{1,0:T(8,128)(2,1)S(1)}, u32[]{:S(2)}, u32[]{:S(2)}) collective-permute-start(bf16[32,1280]{1,0:T(8,128)(2,1)S(1)} %get-tuple-element.29), channel_id=1, source_target_pairs={{0,1},{1,0},{2,3},{3,2},{4,5},{5,4},{6,7},{7,6},{8,9},{9,8},{10,11... | collective-permute-start | bytes 245768 | tf_op jit(solution)/shard_map/ppermute | solution.py:20
  33.6 3.7 %collective-permute-start.6 = (bf16[32,1280]{1,0:T(8,128)(2,1)S(1)}, bf16[32,1280]{1,0:T(8,128)(2,1)S(1)}, u32[]{:S(2)}, u32[]{:S(2)}) collective-permute-start(bf16[32,1280]{1,0:T(8,128)(2,1)S(1)} %get-tuple-element.30), channel_id=1, source_target_pairs={{0,2},{1,3},{2,0},{3,1},{4,6},{5,7},{6,4},{7,5},{8,10},{9,11},{10,... | collective-permute-start | bytes 245768 | tf_op jit(solution)/shard_map/ppermute | solution.py:20
  33.7 4.7 %collective-permute-start.7 = (bf16[32,1280]{1,0:T(8,128)(2,1)S(1)}, bf16[32,1280]{1,0:T(8,128)(2,1)S(1)}, u32[]{:S(2)}, u32[]{:S(2)}) collective-permute-start(bf16[32,1280]{1,0:T(8,128)(2,1)S(1)} %get-tuple-element.31), channel_id=1, source_target_pairs={{0,3},{1,2},{2,1},{3,0},{4,7},{5,6},{6,5},{7,4},{8,11},{9,10},{10,... | collective-permute-start | bytes 245768 | tf_op jit(solution)/shard_map/ppermute | solution.py:20
  39.2 4.4 %collective-permute-start.9 = (bf16[32,1280]{1,0:T(8,128)(2,1)S(1)}, bf16[32,1280]{1,0:T(8,128)(2,1)S(1)}, u32[]{:S(2)}, u32[]{:S(2)}) collective-permute-start(bf16[32,1280]{1,0:T(8,128)(2,1)S(1)} %get-tuple-element.33), channel_id=1, source_target_pairs={{0,1},{1,0},{2,3},{3,2},{4,5},{5,4},{6,7},{7,6},{8,9},{9,8},{10,11... | collective-permute-start | bytes 245768 | tf_op jit(solution)/shard_map/ppermute | solution.py:20
  40.5 4.4 %collective-permute-start.10 = (bf16[32,1280]{1,0:T(8,128)(2,1)S(1)}, bf16[32,1280]{1,0:T(8,128)(2,1)S(1)}, u32[]{:S(2)}, u32[]{:S(2)}) collective-permute-start(bf16[32,1280]{1,0:T(8,128)(2,1)S(1)} %get-tuple-element.34), channel_id=1, source_target_pairs={{0,2},{1,3},{2,0},{3,1},{4,6},{5,7},{6,4},{7,5},{8,10},{9,11},{10,... | collective-permute-start | bytes 245768 | tf_op jit(solution)/shard_map/ppermute | solution.py:20
  41.9 4.5 %collective-permute-start.11 = (bf16[32,1280]{1,0:T(8,128)(2,1)S(1)}, bf16[32,1280]{1,0:T(8,128)(2,1)S(1)}, u32[]{:S(2)}, u32[]{:S(2)}) collective-permute-start(bf16[32,1280]{1,0:T(8,128)(2,1)S(1)} %get-tuple-element.35), channel_id=1, source_target_pairs={{0,3},{1,2},{2,1},{3,0},{4,7},{5,6},{6,5},{7,4},{8,11},{9,10},{10,... | collective-permute-start | bytes 245768 | tf_op jit(solution)/shard_map/ppermute | solution.py:20
  47.3 4.0 %collective-permute-start.12 = (bf16[32,1280]{1,0:T(8,128)(2,1)S(1)}, bf16[32,1280]{1,0:T(8,128)(2,1)S(1)}, u32[]{:S(2)}, u32[]{:S(2)}) collective-permute-start(bf16[32,1280]{1,0:T(8,128)(2,1)S(1)} %get-tuple-element.37), channel_id=1, source_target_pairs={{0,1},{1,0},{2,3},{3,2},{4,5},{5,4},{6,7},{7,6},{8,9},{9,8},{10,11... | collective-permute-start | bytes 245768 | tf_op jit(solution)/shard_map/ppermute | solution.py:20
  47.4 5.2 %collective-permute-start.13 = (bf16[32,1280]{1,0:T(8,128)(2,1)S(1)}, bf16[32,1280]{1,0:T(8,128)(2,1)S(1)}, u32[]{:S(2)}, u32[]{:S(2)}) collective-permute-start(bf16[32,1280]{1,0:T(8,128)(2,1)S(1)} %get-tuple-element.38), channel_id=1, source_target_pairs={{0,2},{1,3},{2,0},{3,1},{4,6},{5,7},{6,4},{7,5},{8,10},{9,11},{10,... | collective-permute-start | bytes 245768 | tf_op jit(solution)/shard_map/ppermute | solution.py:20
  47.6 5.0 %collective-permute-start.14 = (bf16[32,1280]{1,0:T(8,128)(2,1)S(1)}, bf16[32,1280]{1,0:T(8,128)(2,1)S(1)}, u32[]{:S(2)}, u32[]{:S(2)}) collective-permute-start(bf16[32,1280]{1,0:T(8,128)(2,1)S(1)} %get-tuple-element.39), channel_id=1, source_target_pairs={{0,3},{1,2},{2,1},{3,0},{4,7},{5,6},{6,5},{7,4},{8,11},{9,10},{10,... | collective-permute-start | bytes 245768 | tf_op jit(solution)/shard_map/ppermute | solution.py:20
  53.2 28.1 %collective-permute-start.16 = (bf16[96,4096]{1,0:T(8,128)(2,1)S(1)}, bf16[96,4096]{1,0:T(8,128)(2,1)S(1)}, u32[]{:S(2)}, u32[]{:S(2)}) collective-permute-start(bf16[96,4096]{1,0:T(8,128)(2,1)S(1)} %shard_map.83), channel_id=1, source_target_pairs={{4,0},{8,4},{12,8},{16,12},{20,16},{24,20},{28,24},{5,1},{9,5},{13... | collective-permute-start | bytes 2359304 | tf_op jit(solution)/shard_map/ppermute | solution.py:24
  65.9 15.4 %collective-permute-start.17 = (bf16[32,4096]{1,0:T(8,128)(2,1)S(1)}, bf16[32,4096]{1,0:T(8,128)(2,1)S(1)}, u32[]{:S(2)}, u32[]{:S(2)}) collective-permute-start(bf16[32,4096]{1,0:T(8,128)(2,1)S(1)} %get-tuple-element.46), channel_id=1, source_target_pairs={{4,0},{8,4},{12,8},{16,12},{20,16},{24,20},{28,24},{5,1},{9,5},{13... | collective-permute-start | bytes 786440 | tf_op jit(solution)/shard_map/ppermute | solution.py:24
  67.8 3.8 %collective-permute-start.18 = (bf16[32,1280]{1,0:T(8,128)(2,1)S(1)}, bf16[32,1280]{1,0:T(8,128)(2,1)S(1)}, u32[]{:S(2)}, u32[]{:S(2)}) collective-permute-start(bf16[32,1280]{1,0:T(8,128)(2,1)S(1)} %get-tuple-element.48), channel_id=1, source_target_pairs={{0,1},{1,0},{2,3},{3,2},{4,5},{5,4},{6,7},{7,6},{8,9},{9,8},{10,11... | collective-permute-start | bytes 245768 | tf_op jit(solution)/shard_map/ppermute | solution.py:20
  67.9 5.4 %collective-permute-start.19 = (bf16[32,1280]{1,0:T(8,128)(2,1)S(1)}, bf16[32,1280]{1,0:T(8,128)(2,1)S(1)}, u32[]{:S(2)}, u32[]{:S(2)}) collective-permute-start(bf16[32,1280]{1,0:T(8,128)(2,1)S(1)} %get-tuple-element.49), channel_id=1, source_target_pairs={{0,2},{1,3},{2,0},{3,1},{4,6},{5,7},{6,4},{7,5},{8,10},{9,11},{10,... | collective-permute-start | bytes 245768 | tf_op jit(solution)/shard_map/ppermute | solution.py:20
  68.3 5.0 %collective-permute-start.20 = (bf16[32,1280]{1,0:T(8,128)(2,1)S(1)}, bf16[32,1280]{1,0:T(8,128)(2,1)S(1)}, u32[]{:S(2)}, u32[]{:S(2)}) collective-permute-start(bf16[32,1280]{1,0:T(8,128)(2,1)S(1)} %get-tuple-element.50), channel_id=1, source_target_pairs={{0,3},{1,2},{2,1},{3,0},{4,7},{5,6},{6,5},{7,4},{8,11},{9,10},{10,... | collective-permute-start | bytes 245768 | tf_op jit(solution)/shard_map/ppermute | solution.py:20

commit v5 on v4

--- a/solution.py
+++ b/solution.py
@@ -7,7 +7,7 @@
 from jax.experimental.pallas import tpu as pltpu
 from jax.sharding import PartitionSpec as P
 
-SHARES = (2, 2, 2, 2)
+SHARES = (1, 2, 2, 3)
 LANES = 512
 VMEM = pl.BlockSpec(memory_space=pltpu.VMEM)
 SMEM = pl.BlockSpec(memory_space=pltpu.SMEM)
@@ -55,21 +55,6 @@
         scratch_shapes=[pltpu.SemaphoreType.DMA],
         compiler_params=SMALL,
     )(stash, *waits)
-
-
-def pass_kernel(value_ref, wait_ref, out_ref):
-    pass
-
-
-def after(value, wait):
-    return pl.pallas_call(
-        pass_kernel,
-        out_shape=jax.ShapeDtypeStruct(value.shape, value.dtype),
-        in_specs=[ANY, ANY],
-        out_specs=ANY,
-        input_output_aliases={0: 0},
-        compiler_params=SMALL,
-    )(value, wait)
 
 
 def chunk_kernel(groups, start, waits, me_ref, saved_ref, cot_ref, dact_ref, down_ref, gain_ref, *refs):
@@ -121,51 +106,100 @@
     return got[0], got[1:]
 
 
-def sum_kernel(groups, spans, first, *refs):
-    count = groups * len(spans)
-    packs, cots = refs[:count], refs[count : count + groups]
-    rest = refs[count + groups :]
-    if first:
-        parts, (down_ref, up_ref, joined, every, held) = rest[: len(spans)], rest[len(spans) :]
-        for (start, rows), part in zip(spans, parts):
-            joined[pl.ds(start, rows), :] = part[...]
-    else:
-        olds, (down_ref, up_ref, every, held) = rest[:2], rest[2:]
-    width = held.shape[1]
-    rank = up_ref.shape[0]
+def gather_rows(groups, spans, packs, cots, every, held):
     at = 0
     for k in range(groups):
         for j, (start, rows) in enumerate(spans):
             every[pl.ds(at, rows), :] = packs[k * len(spans) + j][...]
             held[pl.ds(at, rows), :] = cots[k][pl.ds(start, rows), :]
             at += rows
-    down = rows_dot(every[:, :width], every[:, width : width + rank])
-    up = rows_dot(every[:, width + rank :], held[...])
-    down_ref[...] = down if first else down + olds[0][...]
-    up_ref[...] = up if first else up + olds[1][...]
-
-
-def run_sum(packs, cots, spans, others, first, rank):
+
+
+def sum_kernel(groups, spans, *refs):
+    count = groups * len(spans)
+    packs, cots, parts = refs[:count], refs[count : count + groups], refs[count + groups : -5]
+    down_ref, up_ref, joined, every, held = refs[-5:]
+    width, rank = down_ref.shape
+    gather_rows(groups, spans, packs, cots, every, held)
+    down_ref[...] = rows_dot(every[:, :width], every[:, width : width + rank])
+    up_ref[...] = rows_dot(every[:, width + rank :], held[...])
+    for (start, rows), part in zip(spans, parts):
+        joined[pl.ds(start, rows), :] = part[...]
+
+
+def final_kernel(groups, spans, *refs):
+    packs, cots = refs[:groups], refs[groups : 2 * groups]
+    old_down, old_up, first, last = refs[2 * groups : 2 * groups + 4]
+    before_ref, down_ref, up_ref, every, held, down, up, done = refs[2 * groups + 4 :]
+    width, rank = down.shape
+    rows = first.shape[0]
+    copies = [
+        pltpu.make_async_copy(first, before_ref.at[pl.ds(0, rows)], done.at[0]),
+        pltpu.make_async_copy(last, before_ref.at[pl.ds(rows, last.shape[0])], done.at[1]),
+        pltpu.make_async_copy(down, down_ref, done.at[2]),
+        pltpu.make_async_copy(up, up_ref, done.at[3]),
+    ]
+    copies[0].start()
+    copies[1].start()
+    gather_rows(groups, spans, packs, cots, every, held)
+    down[...] = old_down[...] + rows_dot(every[:, :width], every[:, width : width + rank])
+    copies[2].start()
+    up[...] = old_up[...] + rows_dot(every[:, width + rank :], held[...])
+    copies[3].start()
+    for copy in copies:
+        copy.wait()
+
+
+def operands(packs, cots, spans):
     groups = len(cots)
     width = cots[0].shape[1]
     depth = groups * sum(rows for _, rows in spans)
-    args = [packs[j][k] for k in range(groups) for j in range(len(spans))] + list(cots) + list(others)
-    outs = [
-        jax.ShapeDtypeStruct((width, rank), jnp.float32),
-        jax.ShapeDtypeStruct((rank, width), jnp.float32),
+    args = [packs[j][k] for k in range(groups) for j in range(len(spans))] + list(cots)
+    scratch = [
+        pltpu.VMEM((depth, packs[0][0].shape[1]), jnp.bfloat16),
+        pltpu.VMEM((depth, width), jnp.bfloat16),
     ]
-    if first:
-        rows = sum(part.shape[0] for part in others)
-        outs.append(jax.ShapeDtypeStruct((rows, others[0].shape[1]), others[0].dtype))
+    return groups, width, args, scratch
+
+
+def run_sum(packs, cots, spans, parts, rank):
+    groups, width, args, scratch = operands(packs, cots, spans)
+    args += parts
+    rows = sum(part.shape[0] for part in parts)
     return pl.pallas_call(
-        functools.partial(sum_kernel, groups, spans, first),
-        out_shape=outs,
+        functools.partial(sum_kernel, groups, spans),
+        out_shape=[
+            jax.ShapeDtypeStruct((width, rank), jnp.float32),
+            jax.ShapeDtypeStruct((rank, width), jnp.float32),
+            jax.ShapeDtypeStruct((rows, parts[0].shape[1]), jnp.bfloat16),
+        ],
         in_specs=[VMEM] * len(args),
-        out_specs=[VMEM] * len(outs),
-        scratch_shapes=[
-            pltpu.VMEM((depth, width + 2 * rank), jnp.bfloat16),
-            pltpu.VMEM((depth, width), jnp.bfloat16),
+        out_specs=[VMEM] * 3,
+        scratch_shapes=scratch,
+        compiler_params=PARAMS,
+    )(*args)
+
+
+def run_final(packs, cots, spans, partial, first, last):
+    groups, width, args, scratch = operands(packs, cots, spans)
+    down, up = partial
+    args += [down, up, first, last]
+    before = jax.ShapeDtypeStruct((first.shape[0] + last.shape[0], first.shape[1]), jnp.bfloat16)
+    scratch += [
+        pltpu.VMEM(down.shape, jnp.float32),
+        pltpu.VMEM(up.shape, jnp.float32),
+        pltpu.SemaphoreType.DMA((4,)),
+    ]
+    return pl.pallas_call(
+        functools.partial(final_kernel, groups, spans),
+        out_shape=[
+            before,
+            jax.ShapeDtypeStruct(down.shape, jnp.float32),
+            jax.ShapeDtypeStruct(up.shape, jnp.float32),
         ],
+        in_specs=[VMEM] * len(args),
+        out_specs=[ANY] * 3,
+        scratch_shapes=scratch,
         compiler_params=PARAMS,
     )(*args)
 
@@ -185,33 +219,31 @@
     def held(value):
         return exchanged(value, "pipe", sections // 2)
 
-    def coming(i, *waits):
-        return held(rows_after(stash, *spans[i], waits))
-
-    arrivals = [held(stash[: sizes[0]])]
+    arrivals = [held(stash[start : start + rows]) for start, rows in spans[:2]]
     cot_all = []
     for k in range(groups):
         part = lax.dynamic_slice_in_dim(cot, (me ^ k) * width, width, axis=1)
         cot_all.append(exchanged(part, "dp", k) if k else part)
     dact = last_dot(cot, upper)
-    arrivals.append(coming(1, cot_all[0]))
     index = jnp.reshape(me.astype(jnp.int32), (1,))
 
     parts, packs, waits = [], [], cot_all[1:]
     for i, (start, rows) in enumerate(spans):
         if i + 2 < chunks:
-            arrivals.append(coming(i + 2, arrivals[i], *parts[-1:]))
+            coming = rows_after(stash, *spans[i + 2], [arrivals[i]] + waits * (i > 0))
+            arrivals.append(held(coming))
+            waits = waits + [coming]
         if i == chunks - 1:
-            *partial, joined = run_sum(packs, cot_all, spans[:-1], parts, True, rank)
-            first = to_previous(after(joined, arrivals[i]), "pipe")
+            *partial, joined = run_sum(packs, cot_all, spans[:-1], parts, rank)
+            first = to_previous(joined, "pipe")
             waits = partial
         dx, pack = run_chunk(index, arrivals[i], cot, dact, down, gain, start, waits, groups)
         packs.append([exchanged(pack[k], "dp", k) if k else pack[k] for k in range(groups)])
         parts.append(dx)
         waits = packs[-1][1:]
     last = to_previous(parts[-1], "pipe")
-    down_grad, up_grad = run_sum(packs[-1:], cot_all, spans[-1:], partial, False, rank)
-    return (jnp.concatenate([first, last], axis=0)[None], down_grad[None], up_grad[None])
+    before, down_grad, up_grad = run_final(packs[-1:], cot_all, spans[-1:], partial, first, last)
+    return (before[None], down_grad[None], up_grad[None])
 
 
 def solution(mesh):

time: 82.5 us -> 69.4 us (0.84)
  the two profiles are of different devices: /device:TPU:1 before, /device:TPU:17 now
where the time goes in v5:
time: 69.4 us; the launch traced here: 69.2 us
  starting transfers between devices  31.4 us (45%)
  waiting for transfers between devices  27.3 us (39%)
  Pallas kernels  5.79 us (8%)
  local copies, waits for them, and re-layouts  3.36 us (5%)
  between operations  0.8 us (1%)
    ppermute x19, waiting for transfers between devices, exchanged(): lax.ppermute(x, axis, [(i, i ^ mask) for i in range(lax.axis_size(axis))])  20.8 us
    ppermute x19, starting transfers between devices, exchanged(): lax.ppermute(x, axis, [(i, i ^ mask) for i in range(lax.axis_size(axis))])  19.7 us
    ppermute x2, starting transfers between devices, to_previous(): lax.ppermute(x, axis, [(i, i - 1) for i in range(1, lax.axis_size(axis))])  11.7 us
    ppermute x2, waiting for transfers between devices, to_previous(): lax.ppermute(x, axis, [(i, i - 1) for i in range(1, lax.axis_size(axis))])  6.48 us
    pallas_call x4, Pallas kernels, run_chunk(): pl.pallas_call(functools.partial(chunk_kernel, groups, start, len(waits))...  3.44 us
    slice x2, local copies, waits for them, and re-layouts, per_device(): arrivals = [held(stash[start:start + rows]) for start, rows in spans[:2]]  1.97 us
    pallas_call x1, Pallas kernels, run_final(): pl.pallas_call(functools.partial(final_kernel, groups, spans), out_shape=...  1.58 us
  transfers between devices with their start and end apart: 21, of which 15 were waited for; matrix products, arithmetic and copies ran while one was open for 4% of the time, Pallas kernels for 6%

profile of v5, /device:TPU:17, one launch (start us, length us, event | category | flops | bytes accessed | tf_op | source)
XLA Modules:
  0.0 69.2 jit_solution(10861787789070891676)
XLA Ops:
  0.6 1.0 %slice_bitcast_fusion.1 = bf16[16,4096]{1,0:T(8,128)(2,1)S(1)} fusion(bf16[1,128,4096]{2,1,0:T(8,128)(2,1)} %param.5), kind=kLoop, calls=%fused_computation.7 | loop fusion | bytes 262144 | tf_op jit(solution)/shard_map/slice | solution.py:222
  1.7 1.0 %slice_bitcast_fusion = bf16[32,4096]{1,0:T(8,128)(2,1)S(1)} fusion(bf16[1,128,4096]{2,1,0:T(8,128)(2,1)} %param.5), kind=kLoop, calls=%fused_computation.6 | loop fusion | bytes 524288 | tf_op jit(solution)/shard_map/slice | solution.py:222
  2.7 2.4 %collective-permute-start = (bf16[32,4096]{1,0:T(8,128)(2,1)S(1)}, bf16[32,4096]{1,0:T(8,128)(2,1)S(1)}, u32[]{:S(2)}, u32[]{:S(2)}) collective-permute-start(bf16[32,4096]{1,0:T(8,128)(2,1)S(1)} %slice_bitcast_fusion), channel_id=1, source_target_pairs={{0,16},{4,20},{8,24},{12,28},{16,0},{20,4},{24,8},{28,12},{1,17},{... | collective-permute-start | bytes 786440 | tf_op jit(solution)/shard_map/ppermute | solution.py:20
  5.1 1.4 %dynamic-slice_bitcast_fusion = (bf16[128,1024]{1,0:T(8,128)(2,1)S(1)}, bf16[128,1024]{1,0:T(8,128)(2,1)S(1)}, bf16[128,1024]{1,0:T(8,128)(2,1)S(1)}, bf16[128,1024]{1,0:T(8,128)(2,1)S(1)}) fusion(bf16[1,128,4096]{2,1,0:T(8,128)(2,1)} %param.6, s32[]{:T(128)S(6)} %select_n.15, s32[]{:T(128)S(6)} %select_n.13, s32[]{:T(128)S(6)} %select_n.12, s32[]{:T(128)S(6)} %select_n.14), kind=kLoop, calls=%fused_computation.2 | loop fusion | bytes 2097168 | tf_op jit(solution)/shard_map/dynamic_slice | solution.py:225
  6.5 1.3 %collective-permute-start.3 = (bf16[128,1024]{1,0:T(8,128)(2,1)S(1)}, bf16[128,1024]{1,0:T(8,128)(2,1)S(1)}, u32[]{:S(2)}, u32[]{:S(2)}) collective-permute-start(bf16[128,1024]{1,0:T(8,128)(2,1)S(1)} %get-tuple-element.56), channel_id=1, source_target_pairs={{0,2},{1,3},{2,0},{3,1},{4,6},{5,7},{6,4},{7,5},{8,10},{9,11},{10,... | collective-permute-start | bytes 786440 | tf_op jit(solution)/shard_map/ppermute | solution.py:20
  7.8 1.2 %collective-permute-start.2 = (bf16[128,1024]{1,0:T(8,128)(2,1)S(1)}, bf16[128,1024]{1,0:T(8,128)(2,1)S(1)}, u32[]{:S(2)}, u32[]{:S(2)}) collective-permute-start(bf16[128,1024]{1,0:T(8,128)(2,1)S(1)} %get-tuple-element.57), channel_id=1, source_target_pairs={{0,1},{1,0},{2,3},{3,2},{4,5},{5,4},{6,7},{7,6},{8,9},{9,8},{10,11... | collective-permute-start | bytes 786440 | tf_op jit(solution)/shard_map/ppermute | solution.py:20
  9.2 3.3 %collective-permute-done.1.refs_0_.saved_ref = bf16[16,4096]{1,0:T(8,128)(2,1)S(1)} collective-permute-done((bf16[16,4096]{1,0:T(8,128)(2,1)S(1)}, bf16[16,4096]{1,0:T(8,128)(2,1)S(1)}, u32[]{:S(2)}, u32[]{:S(2)}) %collective-permute-start.1) | collective-permute-done | bytes 131104 | tf_op jit(solution)/shard_map/ppermute | solution.py:20
  12.5 3.3 %collective-permute-start.9 = (bf16[32,4096]{1,0:T(8,128)(2,1)S(1)}, bf16[32,4096]{1,0:T(8,128)(2,1)S(1)}, u32[]{:S(2)}, u32[]{:S(2)}) collective-permute-start(bf16[32,4096]{1,0:T(8,128)(2,1)S(1)} %shard_map.76.refs_3_), channel_id=1, source_target_pairs={{0,16},{4,20},{8,24},{12,28},{16,0},{20,4},{24,8},{28,12},{1,17},{... | collective-permute-start | bytes 786440 | tf_op jit(solution)/shard_map/ppermute | solution.py:20
  16.4 3.2 %collective-permute-done.4.refs_2_.refs_15_.refs_7_ = bf16[128,1024]{1,0:T(8,128)(2,1)S(1)} collective-permute-done((bf16[128,1024]{1,0:T(8,128)(2,1)S(1)}, bf16[128,1024]{1,0:T(8,128)(2,1)S(1)}, u32[]{:S(2)}, u32[]{:S(2)}) %collective-permute-start.4) | collective-permute-done | bytes 262176 | tf_op jit(solution)/shard_map/ppermute | solution.py:20
  19.6 0.7 %shard_map.77 = (bf16[16,4096]{1,0:T(8,128)(2,1)S(1)}, bf16[16,1280]{1,0:T(8,128)(2,1)S(1)}, bf16[16,1280]{1,0:T(8,128)(2,1)S(1)}, bf16[16,1280]{1,0:T(8,128)(2,1)S(1)}, bf16[16,1280]{1,0:T(8,128)(2,1)S(1)}) custom-call(s32[1]{0:T(128)} %bitcast.me_ref, bf16[16,4096]{1,0:T(8,128)(2,1)S(1)} %collective-permute-done.1.refs_0_.saved_ref, ...), custom_call_target="tpu_custom_call" | custom-call | tf_op jit(solution)/shard_map/pallas_call | solution.py:98
  20.4 1.3 %collective-permute-start.5 = (bf16[16,1280]{1,0:T(8,128)(2,1)S(1)}, bf16[16,1280]{1,0:T(8,128)(2,1)S(1)}, u32[]{:S(2)}, u32[]{:S(2)}) collective-permute-start(bf16[16,1280]{1,0:T(8,128)(2,1)S(1)} %get-tuple-element.29), channel_id=1, source_target_pairs={{0,1},{1,0},{2,3},{3,2},{4,5},{5,4},{6,7},{7,6},{8,9},{9,8},{10,11... | collective-permute-start | bytes 122888 | tf_op jit(solution)/shard_map/ppermute | solution.py:20
  21.7 1.2 %collective-permute-start.6 = (bf16[16,1280]{1,0:T(8,128)(2,1)S(1)}, bf16[16,1280]{1,0:T(8,128)(2,1)S(1)}, u32[]{:S(2)}, u32[]{:S(2)}) collective-permute-start(bf16[16,1280]{1,0:T(8,128)(2,1)S(1)} %get-tuple-element.30), channel_id=1, source_target_pairs={{0,2},{1,3},{2,0},{3,1},{4,6},{5,7},{6,4},{7,5},{8,10},{9,11},{10,... | collective-permute-start | bytes 122888 | tf_op jit(solution)/shard_map/ppermute | solution.py:20
  23.3 1.2 %collective-permute-done.6.refs_2_.refs_1_.refs_6_ = bf16[16,1280]{1,0:T(8,128)(2,1)S(1)} collective-permute-done((bf16[16,1280]{1,0:T(8,128)(2,1)S(1)}, bf16[16,1280]{1,0:T(8,128)(2,1)S(1)}, u32[]{:S(2)}, u32[]{:S(2)}) %collective-permute-start.6) | collective-permute-done | bytes 40992 | tf_op jit(solution)/shard_map/ppermute | solution.py:20
  24.5 2.1 %collective-permute-done.7.refs_3_.refs_2_.refs_9_ = bf16[16,1280]{1,0:T(8,128)(2,1)S(1)} collective-permute-done((bf16[16,1280]{1,0:T(8,128)(2,1)S(1)}, bf16[16,1280]{1,0:T(8,128)(2,1)S(1)}, u32[]{:S(2)}, u32[]{:S(2)}) %collective-permute-start.7) | collective-permute-done | bytes 40992 | tf_op jit(solution)/shard_map/ppermute | solution.py:20
  26.9 0.9 %shard_map.79 = (bf16[32,4096]{1,0:T(8,128)(2,1)S(1)}, bf16[32,1280]{1,0:T(8,128)(2,1)S(1)}, bf16[32,1280]{1,0:T(8,128)(2,1)S(1)}, bf16[32,1280]{1,0:T(8,128)(2,1)S(1)}, bf16[32,1280]{1,0:T(8,128)(2,1)S(1)}) custom-call(s32[1]{0:T(128)} %bitcast.me_ref, bf16[32,4096]{1,0:T(8,128)(2,1)S(1)} %collective-permute-done.refs_0_.saved_ref, ...), custom_call_target="tpu_custom_call" | custom-call | tf_op jit(solution)/shard_map/pallas_call | solution.py:98
  28.3 2.2 %collective-permute-start.12 = (bf16[32,1280]{1,0:T(8,128)(2,1)S(1)}, bf16[32,1280]{1,0:T(8,128)(2,1)S(1)}, u32[]{:S(2)}, u32[]{:S(2)}) collective-permute-start(bf16[32,1280]{1,0:T(8,128)(2,1)S(1)} %get-tuple-element.36), channel_id=1, source_target_pairs={{0,3},{1,2},{2,1},{3,0},{4,7},{5,6},{6,5},{7,4},{8,11},{9,10},{10,... | collective-permute-start | bytes 245768 | tf_op jit(solution)/shard_map/ppermute | solution.py:20
  31.4 1.1 %collective-permute-done.12.refs_2_.refs_10_ = bf16[32,1280]{1,0:T(8,128)(2,1)S(1)} collective-permute-done((bf16[32,1280]{1,0:T(8,128)(2,1)S(1)}, bf16[32,1280]{1,0:T(8,128)(2,1)S(1)}, u32[]{:S(2)}, u32[]{:S(2)}) %collective-permute-start.12) | collective-permute-done | bytes 81952 | tf_op jit(solution)/shard_map/ppermute | solution.py:20
  32.5 0.9 %shard_map.80 = (bf16[32,4096]{1,0:T(8,128)(2,1)S(1)}, bf16[32,1280]{1,0:T(8,128)(2,1)S(1)}, bf16[32,1280]{1,0:T(8,128)(2,1)S(1)}, bf16[32,1280]{1,0:T(8,128)(2,1)S(1)}, bf16[32,1280]{1,0:T(8,128)(2,1)S(1)}) custom-call(s32[1]{0:T(128)} %bitcast.me_ref, bf16[32,4096]{1,0:T(8,128)(2,1)S(1)} %collective-permute-done.9.saved_ref, ...), custom_call_target="tpu_custom_call" | custom-call | tf_op jit(solution)/shard_map/pallas_call | solution.py:98
  33.4 1.3 %collective-permute-start.13 = (bf16[32,1280]{1,0:T(8,128)(2,1)S(1)}, bf16[32,1280]{1,0:T(8,128)(2,1)S(1)}, u32[]{:S(2)}, u32[]{:S(2)}) collective-permute-start(bf16[32,1280]{1,0:T(8,128)(2,1)S(1)} %get-tuple-element.38), channel_id=1, source_target_pairs={{0,1},{1,0},{2,3},{3,2},{4,5},{5,4},{6,7},{7,6},{8,9},{9,8},{10,11... | collective-permute-start | bytes 245768 | tf_op jit(solution)/shard_map/ppermute | solution.py:20
  34.6 1.2 %collective-permute-start.14 = (bf16[32,1280]{1,0:T(8,128)(2,1)S(1)}, bf16[32,1280]{1,0:T(8,128)(2,1)S(1)}, u32[]{:S(2)}, u32[]{:S(2)}) collective-permute-start(bf16[32,1280]{1,0:T(8,128)(2,1)S(1)} %get-tuple-element.39), channel_id=1, source_target_pairs={{0,2},{1,3},{2,0},{3,1},{4,6},{5,7},{6,4},{7,5},{8,10},{9,11},{10,... | collective-permute-start | bytes 245768 | tf_op jit(solution)/shard_map/ppermute | solution.py:20
  36.1 0.6 collective-permute-done.13.refs_5_
  36.7 2.1 %collective-permute-done.14.refs_8_ = bf16[32,1280]{1,0:T(8,128)(2,1)S(1)} collective-permute-done((bf16[32,1280]{1,0:T(8,128)(2,1)S(1)}, bf16[32,1280]{1,0:T(8,128)(2,1)S(1)}, u32[]{:S(2)}, u32[]{:S(2)}) %collective-permute-start.14) | collective-permute-done | bytes 81952 | tf_op jit(solution)/shard_map/ppermute | solution.py:20
  38.8 1.6 %collective-permute-done.15.refs_11_ = bf16[32,1280]{1,0:T(8,128)(2,1)S(1)} collective-permute-done((bf16[32,1280]{1,0:T(8,128)(2,1)S(1)}, bf16[32,1280]{1,0:T(8,128)(2,1)S(1)}, u32[]{:S(2)}, u32[]{:S(2)}) %collective-permute-start.15) | collective-permute-done | bytes 81952 | tf_op jit(solution)/shard_map/ppermute | solution.py:20
  40.9 9.8 %collective-permute-start.19 = (bf16[80,4096]{1,0:T(8,128)(2,1)S(1)}, bf16[80,4096]{1,0:T(8,128)(2,1)S(1)}, u32[]{:S(2)}, u32[]{:S(2)}) collective-permute-start(bf16[80,4096]{1,0:T(8,128)(2,1)S(1)} %get-tuple-element.50), channel_id=1, source_target_pairs={{4,0},{8,4},{12,8},{16,12},{20,16},{24,20},{28,24},{5,1},{9,5},{13... | collective-permute-start | bytes 1966088 | tf_op jit(solution)/shard_map/ppermute | solution.py:24
  50.7 0.9 %shard_map.82 = (bf16[48,4096]{1,0:T(8,128)(2,1)S(1)}, bf16[48,1280]{1,0:T(8,128)(2,1)S(1)}, bf16[48,1280]{1,0:T(8,128)(2,1)S(1)}, bf16[48,1280]{1,0:T(8,128)(2,1)S(1)}, bf16[48,1280]{1,0:T(8,128)(2,1)S(1)}) custom-call(s32[1]{0:T(128)} %bitcast.me_ref, bf16[48,4096]{1,0:T(8,128)(2,1)S(1)} %collective-permute-done.8.saved_ref, ...), custom_call_target="tpu_custom_call" | custom-call | tf_op jit(solution)/shard_map/pallas_call | solution.py:98
  51.7 1.9 %collective-permute-start.20 = (bf16[48,4096]{1,0:T(8,128)(2,1)S(1)}, bf16[48,4096]{1,0:T(8,128)(2,1)S(1)}, u32[]{:S(2)}, u32[]{:S(2)}) collective-permute-start(bf16[48,4096]{1,0:T(8,128)(2,1)S(1)} %get-tuple-element.51), channel_id=1, source_target_pairs={{4,0},{8,4},{12,8},{16,12},{20,16},{24,20},{28,24},{5,1},{9,5},{13... | collective-permute-start | bytes 1179656 | tf_op jit(solution)/shard_map/ppermute | solution.py:24
  53.7 0.7 %collective-permute-start.17 = (bf16[48,1280]{1,0:T(8,128)(2,1)S(1)}, bf16[48,1280]{1,0:T(8,128)(2,1)S(1)}, u32[]{:S(2)}, u32[]{:S(2)}) collective-permute-start(bf16[48,1280]{1,0:T(8,128)(2,1)S(1)} %get-tuple-element.48), channel_id=1, source_target_pairs={{0,2},{1,3},{2,0},{3,1},{4,6},{5,7},{6,4},{7,5},{8,10},{9,11},{10,... | collective-permute-start | bytes 368648 | tf_op jit(solution)/shard_map/ppermute | solution.py:20
  54.4 1.9 %collective-permute-start.18 = (bf16[48,1280]{1,0:T(8,128)(2,1)S(1)}, bf16[48,1280]{1,0:T(8,128)(2,1)S(1)}, u32[]{:S(2)}, u32[]{:S(2)}) collective-permute-start(bf16[48,1280]{1,0:T(8,128)(2,1)S(1)} %get-tuple-element.49), channel_id=1, source_target_pairs={{0,3},{1,2},{2,1},{3,0},{4,7},{5,6},{6,5},{7,4},{8,11},{9,10},{10,... | collective-permute-start | bytes 368648 | tf_op jit(solution)/shard_map/ppermute | solution.py:20
  56.3 1.7 %collective-permute-done.16.refs_1_ = bf16[48,1280]{1,0:T(8,128)(2,1)S(1)} collective-permute-done((bf16[48,1280]{1,0:T(8,128)(2,1)S(1)}, bf16[48,1280]{1,0:T(8,128)(2,1)S(1)}, u32[]{:S(2)}, u32[]{:S(2)}) %collective-permute-start.16) | collective-permute-done | bytes 122912 | tf_op jit(solution)/shard_map/ppermute | solution.py:20
  58.1 3.1 %collective-permute-done.18.refs_3_ = bf16[48,1280]{1,0:T(8,128)(2,1)S(1)} collective-permute-done((bf16[48,1280]{1,0:T(8,128)(2,1)S(1)}, bf16[48,1280]{1,0:T(8,128)(2,1)S(1)}, u32[]{:S(2)}, u32[]{:S(2)}) %collective-permute-start.18) | collective-permute-done | bytes 122912 | tf_op jit(solution)/shard_map/ppermute | solution.py:20
  61.2 6.5 %collective-permute-done.20.refs_11_ = bf16[48,4096]{1,0:T(8,128)(2,1)S(1)} collective-permute-done((bf16[48,4096]{1,0:T(8,128)(2,1)S(1)}, bf16[48,4096]{1,0:T(8,128)(2,1)S(1)}, u32[]{:S(2)}, u32[]{:S(2)}) %collective-permute-start.20) | collective-permute-done | bytes 393248 | tf_op jit(solution)/shard_map/ppermute | solution.py:24
  67.6 1.6 %shard_map.83 = (bf16[128,4096]{1,0:T(8,128)(2,1)}, f32[1024,128]{1,0:T(8,128)}, f32[128,1024]{1,0:T(8,128)}) custom-call(bf16[48,1280]{1,0:T(8,128)(2,1)S(1)} %get-tuple-element.46.refs_0_, bf16[48,1280]{1,0:T(8,128)(2,1)S(1)} %collective-permute-done.16.refs_1_, bf16[48,1280]{1,0:T(8,128)(2,1)S(1)} %collective-permute-done.17.refs_2_, ...), custom_call_target="tpu_custom_call" | custom-call | tf_op jit(solution)/shard_map/pallas_call | solution.py:193
  (32 shorter events, 3.8 us)
Async XLA Ops:
  0.6 15.2 %copy-start = (bf16[1,128,4096]{2,1,0:T(8,128)(2,1)S(1)}, bf16[1,128,4096]{2,1,0:T(8,128)(2,1)}, u32[]{:S(2)}) copy-start(bf16[1,128,4096]{2,1,0:T(8,128)(2,1)} %param.8) | copy-start | bytes 3145732
  1.7 10.8 %collective-permute-start.1 = (bf16[16,4096]{1,0:T(8,128)(2,1)S(1)}, bf16[16,4096]{1,0:T(8,128)(2,1)S(1)}, u32[]{:S(2)}, u32[]{:S(2)}) collective-permute-start(bf16[16,4096]{1,0:T(8,128)(2,1)S(1)} %slice_bitcast_fusion.1), channel_id=1, source_target_pairs={{0,16},{4,20},{8,24},{12,28},{16,0},{20,4},{24,8},{28,12},{1,17},{... | collective-permute-start | bytes 393224 | tf_op jit(solution)/shard_map/ppermute | solution.py:20
  2.7 20.4 %collective-permute-start = (bf16[32,4096]{1,0:T(8,128)(2,1)S(1)}, bf16[32,4096]{1,0:T(8,128)(2,1)S(1)}, u32[]{:S(2)}, u32[]{:S(2)}) collective-permute-start(bf16[32,4096]{1,0:T(8,128)(2,1)S(1)} %slice_bitcast_fusion), channel_id=1, source_target_pairs={{0,16},{4,20},{8,24},{12,28},{16,0},{20,4},{24,8},{28,12},{1,17},{... | collective-permute-start | bytes 786440 | tf_op jit(solution)/shard_map/ppermute | solution.py:20
  5.1 7.4 %copy-start.3 = (bf16[1,128,4096]{2,1,0:T(8,128)(2,1)S(1)}, bf16[1,128,4096]{2,1,0:T(8,128)(2,1)}, u32[]{:S(2)}) copy-start(bf16[1,128,4096]{2,1,0:T(8,128)(2,1)} %param.5) | copy-start | bytes 3145732
  6.5 9.4 %copy-start.1 = (bf16[1,128,4096]{2,1,0:T(8,128)(2,1)S(1)}, bf16[1,128,4096]{2,1,0:T(8,128)(2,1)}, u32[]{:S(2)}) copy-start(bf16[1,128,4096]{2,1,0:T(8,128)(2,1)} %param.6) | copy-start | bytes 3145732
  6.5 9.9 %collective-permute-start.3 = (bf16[128,1024]{1,0:T(8,128)(2,1)S(1)}, bf16[128,1024]{1,0:T(8,128)(2,1)S(1)}, u32[]{:S(2)}, u32[]{:S(2)}) collective-permute-start(bf16[128,1024]{1,0:T(8,128)(2,1)S(1)} %get-tuple-element.56), channel_id=1, source_target_pairs={{0,2},{1,3},{2,0},{3,1},{4,6},{5,7},{6,4},{7,5},{8,10},{9,11},{10,... | collective-permute-start | bytes 786440 | tf_op jit(solution)/shard_map/ppermute | solution.py:20
  7.8 8.6 %collective-permute-start.2 = (bf16[128,1024]{1,0:T(8,128)(2,1)S(1)}, bf16[128,1024]{1,0:T(8,128)(2,1)S(1)}, u32[]{:S(2)}, u32[]{:S(2)}) collective-permute-start(bf16[128,1024]{1,0:T(8,128)(2,1)S(1)} %get-tuple-element.57), channel_id=1, source_target_pairs={{0,1},{1,0},{2,3},{3,2},{4,5},{5,4},{6,7},{7,6},{8,9},{9,8},{10,11... | collective-permute-start | bytes 786440 | tf_op jit(solution)/shard_map/ppermute | solution.py:20
  9.0 10.6 %collective-permute-start.4 = (bf16[128,1024]{1,0:T(8,128)(2,1)S(1)}, bf16[128,1024]{1,0:T(8,128)(2,1)S(1)}, u32[]{:S(2)}, u32[]{:S(2)}) collective-permute-start(bf16[128,1024]{1,0:T(8,128)(2,1)S(1)} %get-tuple-element.58), channel_id=1, source_target_pairs={{0,3},{1,2},{2,1},{3,0},{4,7},{5,6},{6,5},{7,4},{8,11},{9,10},{10,... | collective-permute-start | bytes 786440 | tf_op jit(solution)/shard_map/ppermute | solution.py:20
  12.5 7.1 %copy-start.2 = (bf16[1,4096,128]{2,1,0:T(8,128)(2,1)S(1)}, bf16[1,4096,128]{2,1,0:T(8,128)(2,1)}, u32[]{:S(2)}) copy-start(bf16[1,4096,128]{2,1,0:T(8,128)(2,1)} %param.7) | copy-start | bytes 3145732
  12.5 20.0 %collective-permute-start.9 = (bf16[32,4096]{1,0:T(8,128)(2,1)S(1)}, bf16[32,4096]{1,0:T(8,128)(2,1)S(1)}, u32[]{:S(2)}, u32[]{:S(2)}) collective-permute-start(bf16[32,4096]{1,0:T(8,128)(2,1)S(1)} %shard_map.76.refs_3_), channel_id=1, source_target_pairs={{0,16},{4,20},{8,24},{12,28},{16,0},{20,4},{24,8},{28,12},{1,17},{... | collective-permute-start | bytes 786440 | tf_op jit(solution)/shard_map/ppermute | solution.py:20
  15.9 3.8 %copy-start.4 = (f32[1,4096]{1,0:T(1,128)S(1)}, f32[1,4096]{1,0:T(1,128)}, u32[]{:S(2)}) copy-start(f32[1,4096]{1,0:T(1,128)} %gain_ref.7) | copy-start | bytes 49156
  20.4 2.9 %collective-permute-start.5 = (bf16[16,1280]{1,0:T(8,128)(2,1)S(1)}, bf16[16,1280]{1,0:T(8,128)(2,1)S(1)}, u32[]{:S(2)}, u32[]{:S(2)}) collective-permute-start(bf16[16,1280]{1,0:T(8,128)(2,1)S(1)} %get-tuple-element.29), channel_id=1, source_target_pairs={{0,1},{1,0},{2,3},{3,2},{4,5},{5,4},{6,7},{7,6},{8,9},{9,8},{10,11... | collective-permute-start | bytes 122888 | tf_op jit(solution)/shard_map/ppermute | solution.py:20
  21.7 2.9 %collective-permute-start.6 = (bf16[16,1280]{1,0:T(8,128)(2,1)S(1)}, bf16[16,1280]{1,0:T(8,128)(2,1)S(1)}, u32[]{:S(2)}, u32[]{:S(2)}) collective-permute-start(bf16[16,1280]{1,0:T(8,128)(2,1)S(1)} %get-tuple-element.30), channel_id=1, source_target_pairs={{0,2},{1,3},{2,0},{3,1},{4,6},{5,7},{6,4},{7,5},{8,10},{9,11},{10,... | collective-permute-start | bytes 122888 | tf_op jit(solution)/shard_map/ppermute | solution.py:20
  22.9 3.8 %collective-permute-start.7 = (bf16[16,1280]{1,0:T(8,128)(2,1)S(1)}, bf16[16,1280]{1,0:T(8,128)(2,1)S(1)}, u32[]{:S(2)}, u32[]{:S(2)}) collective-permute-start(bf16[16,1280]{1,0:T(8,128)(2,1)S(1)} %get-tuple-element.31), channel_id=1, source_target_pairs={{0,3},{1,2},{2,1},{3,0},{4,7},{5,6},{6,5},{7,4},{8,11},{9,10},{10,... | collective-permute-start | bytes 122888 | tf_op jit(solution)/shard_map/ppermute | solution.py:20
  27.8 3.4 %collective-permute-start.10 = (bf16[32,1280]{1,0:T(8,128)(2,1)S(1)}, bf16[32,1280]{1,0:T(8,128)(2,1)S(1)}, u32[]{:S(2)}, u32[]{:S(2)}) collective-permute-start(bf16[32,1280]{1,0:T(8,128)(2,1)S(1)} %get-tuple-element.34), channel_id=1, source_target_pairs={{0,1},{1,0},{2,3},{3,2},{4,5},{5,4},{6,7},{7,6},{8,9},{9,8},{10,11... | collective-permute-start | bytes 245768 | tf_op jit(solution)/shard_map/ppermute | solution.py:20
  28.1 3.3 %collective-permute-start.11 = (bf16[32,1280]{1,0:T(8,128)(2,1)S(1)}, bf16[32,1280]{1,0:T(8,128)(2,1)S(1)}, u32[]{:S(2)}, u32[]{:S(2)}) collective-permute-start(bf16[32,1280]{1,0:T(8,128)(2,1)S(1)} %get-tuple-element.35), channel_id=1, source_target_pairs={{0,2},{1,3},{2,0},{3,1},{4,6},{5,7},{6,4},{7,5},{8,10},{9,11},{10,... | collective-permute-start | bytes 245768 | tf_op jit(solution)/shard_map/ppermute | solution.py:20
  28.3 4.2 %collective-permute-start.12 = (bf16[32,1280]{1,0:T(8,128)(2,1)S(1)}, bf16[32,1280]{1,0:T(8,128)(2,1)S(1)}, u32[]{:S(2)}, u32[]{:S(2)}) collective-permute-start(bf16[32,1280]{1,0:T(8,128)(2,1)S(1)} %get-tuple-element.36), channel_id=1, source_target_pairs={{0,3},{1,2},{2,1},{3,0},{4,7},{5,6},{6,5},{7,4},{8,11},{9,10},{10,... | collective-permute-start | bytes 245768 | tf_op jit(solution)/shard_map/ppermute | solution.py:20
  30.5 20.3 %collective-permute-start.8 = (bf16[48,4096]{1,0:T(8,128)(2,1)S(1)}, bf16[48,4096]{1,0:T(8,128)(2,1)S(1)}, u32[]{:S(2)}, u32[]{:S(2)}) collective-permute-start(bf16[48,4096]{1,0:T(8,128)(2,1)S(1)} %shard_map.78.refs_3_), channel_id=1, source_target_pairs={{0,16},{4,20},{8,24},{12,28},{16,0},{20,4},{24,8},{28,12},{1,17},{... | collective-permute-start | bytes 1179656 | tf_op jit(solution)/shard_map/ppermute | solution.py:20
  33.4 3.4 %collective-permute-start.13 = (bf16[32,1280]{1,0:T(8,128)(2,1)S(1)}, bf16[32,1280]{1,0:T(8,128)(2,1)S(1)}, u32[]{:S(2)}, u32[]{:S(2)}) collective-permute-start(bf16[32,1280]{1,0:T(8,128)(2,1)S(1)} %get-tuple-element.38), channel_id=1, source_target_pairs={{0,1},{1,0},{2,3},{3,2},{4,5},{5,4},{6,7},{7,6},{8,9},{9,8},{10,11... | collective-permute-start | bytes 245768 | tf_op jit(solution)/shard_map/ppermute | solution.py:20
  34.6 4.2 %collective-permute-start.14 = (bf16[32,1280]{1,0:T(8,128)(2,1)S(1)}, bf16[32,1280]{1,0:T(8,128)(2,1)S(1)}, u32[]{:S(2)}, u32[]{:S(2)}) collective-permute-start(bf16[32,1280]{1,0:T(8,128)(2,1)S(1)} %get-tuple-element.39), channel_id=1, source_target_pairs={{0,2},{1,3},{2,0},{3,1},{4,6},{5,7},{6,4},{7,5},{8,10},{9,11},{10,... | collective-permute-start | bytes 245768 | tf_op jit(solution)/shard_map/ppermute | solution.py:20
  35.9 4.5 %collective-permute-start.15 = (bf16[32,1280]{1,0:T(8,128)(2,1)S(1)}, bf16[32,1280]{1,0:T(8,128)(2,1)S(1)}, u32[]{:S(2)}, u32[]{:S(2)}) collective-permute-start(bf16[32,1280]{1,0:T(8,128)(2,1)S(1)} %get-tuple-element.40), channel_id=1, source_target_pairs={{0,3},{1,2},{2,1},{3,0},{4,7},{5,6},{6,5},{7,4},{8,11},{9,10},{10,... | collective-permute-start | bytes 245768 | tf_op jit(solution)/shard_map/ppermute | solution.py:20
  40.9 26.7 %collective-permute-start.19 = (bf16[80,4096]{1,0:T(8,128)(2,1)S(1)}, bf16[80,4096]{1,0:T(8,128)(2,1)S(1)}, u32[]{:S(2)}, u32[]{:S(2)}) collective-permute-start(bf16[80,4096]{1,0:T(8,128)(2,1)S(1)} %get-tuple-element.50), channel_id=1, source_target_pairs={{4,0},{8,4},{12,8},{16,12},{20,16},{24,20},{28,24},{5,1},{9,5},{13... | collective-permute-start | bytes 1966088 | tf_op jit(solution)/shard_map/ppermute | solution.py:24
  51.7 15.9 %collective-permute-start.20 = (bf16[48,4096]{1,0:T(8,128)(2,1)S(1)}, bf16[48,4096]{1,0:T(8,128)(2,1)S(1)}, u32[]{:S(2)}, u32[]{:S(2)}) collective-permute-start(bf16[48,4096]{1,0:T(8,128)(2,1)S(1)} %get-tuple-element.51), channel_id=1, source_target_pairs={{4,0},{8,4},{12,8},{16,12},{20,16},{24,20},{28,24},{5,1},{9,5},{13... | collective-permute-start | bytes 1179656 | tf_op jit(solution)/shard_map/ppermute | solution.py:24
  53.6 4.4 %collective-permute-start.16 = (bf16[48,1280]{1,0:T(8,128)(2,1)S(1)}, bf16[48,1280]{1,0:T(8,128)(2,1)S(1)}, u32[]{:S(2)}, u32[]{:S(2)}) collective-permute-start(bf16[48,1280]{1,0:T(8,128)(2,1)S(1)} %get-tuple-element.47), channel_id=1, source_target_pairs={{0,1},{1,0},{2,3},{3,2},{4,5},{5,4},{6,7},{7,6},{8,9},{9,8},{10,11... | collective-permute-start | bytes 368648 | tf_op jit(solution)/shard_map/ppermute | solution.py:20
  53.7 4.4 %collective-permute-start.17 = (bf16[48,1280]{1,0:T(8,128)(2,1)S(1)}, bf16[48,1280]{1,0:T(8,128)(2,1)S(1)}, u32[]{:S(2)}, u32[]{:S(2)}) collective-permute-start(bf16[48,1280]{1,0:T(8,128)(2,1)S(1)} %get-tuple-element.48), channel_id=1, source_target_pairs={{0,2},{1,3},{2,0},{3,1},{4,6},{5,7},{6,4},{7,5},{8,10},{9,11},{10,... | collective-permute-start | bytes 368648 | tf_op jit(solution)/shard_map/ppermute | solution.py:20
  54.4 6.8 %collective-permute-start.18 = (bf16[48,1280]{1,0:T(8,128)(2,1)S(1)}, bf16[48,1280]{1,0:T(8,128)(2,1)S(1)}, u32[]{:S(2)}, u32[]{:S(2)}) collective-permute-start(bf16[48,1280]{1,0:T(8,128)(2,1)S(1)} %get-tuple-element.49), channel_id=1, source_target_pairs={{0,3},{1,2},{2,1},{3,0},{4,7},{5,6},{6,5},{7,4},{8,11},{9,10},{10,... | collective-permute-start | bytes 368648 | tf_op jit(solution)/shard_map/ppermute | solution.py:20

commit v6 on v5

--- a/solution.py
+++ b/solution.py
@@ -57,10 +57,16 @@
     )(stash, *waits)
 
 
-def chunk_kernel(groups, start, waits, me_ref, saved_ref, cot_ref, dact_ref, down_ref, gain_ref, *refs):
-    outs = refs[waits:]
+def chunk_kernel(start, joins, waits, me_ref, saved_ref, cot_ref, dact_ref, down_ref, gain_ref, *refs):
+    outs = refs[joins + waits :]
     dx_ref, pack_refs, normed_ref = outs[0], outs[1:-1], outs[-1]
+    groups = len(pack_refs)
     rows, features = saved_ref.shape
+    ahead = dx_ref.shape[0] - rows
+    at = 0
+    for part in refs[:joins]:
+        dx_ref[pl.ds(at, part.shape[0]), :] = part[...]
+        at += part.shape[0]
     width = features // groups
     rank = down_ref.shape[1]
     lanes = [pl.ds(f, LANES) for f in range(0, features, LANES)]
@@ -87,22 +93,23 @@
         dnorm = last_dot(dpre, down_ref[at, :]) * gain_ref[:, at]
         xf = saved_ref[:, at].astype(jnp.float32)
         held = cot_ref[pl.ds(start, rows), at].astype(jnp.float32)
-        dx_ref[:, at] = (held + (dnorm - xf * pull) * inverse).astype(jnp.bfloat16)
-
-
-def run_chunk(me, saved, cot, dact, down, gain, start, waits, groups):
+        dx_ref[pl.ds(ahead, rows), at] = (held + (dnorm - xf * pull) * inverse).astype(jnp.bfloat16)
+
+
+def run_chunk(me, saved, cot, dact, down, gain, start, joins, waits, groups):
     rows, features = saved.shape
     rank = down.shape[1]
     pack = jax.ShapeDtypeStruct((rows, features // groups + 2 * rank), jnp.bfloat16)
-    outs = [jax.ShapeDtypeStruct((rows, features), jnp.bfloat16)] + [pack] * groups
+    ahead = sum(part.shape[0] for part in joins)
+    outs = [jax.ShapeDtypeStruct((ahead + rows, features), jnp.bfloat16)] + [pack] * groups
     got = pl.pallas_call(
-        functools.partial(chunk_kernel, groups, start, len(waits)),
+        functools.partial(chunk_kernel, start, len(joins), len(waits)),
         out_shape=outs,
-        in_specs=[SMEM] + [VMEM] * 5 + [ANY] * len(waits),
+        in_specs=[SMEM] + [VMEM] * (5 + len(joins)) + [ANY] * len(waits),
         out_specs=[VMEM] * len(outs),
         scratch_shapes=[pltpu.VMEM((rows, features), jnp.bfloat16)],
         compiler_params=PARAMS,
-    )(me, saved, cot, dact, down, gain, *waits)
+    )(me, saved, cot, dact, down, gain, *joins, *waits)
     return got[0], got[1:]
 
 
@@ -117,14 +124,12 @@
 
 def sum_kernel(groups, spans, *refs):
     count = groups * len(spans)
-    packs, cots, parts = refs[:count], refs[count : count + groups], refs[count + groups : -5]
-    down_ref, up_ref, joined, every, held = refs[-5:]
+    packs, cots = refs[:count], refs[count : count + groups]
+    down_ref, up_ref, every, held = refs[-4:]
     width, rank = down_ref.shape
     gather_rows(groups, spans, packs, cots, every, held)
     down_ref[...] = rows_dot(every[:, :width], every[:, width : width + rank])
     up_ref[...] = rows_dot(every[:, width + rank :], held[...])
-    for (start, rows), part in zip(spans, parts):
-        joined[pl.ds(start, rows), :] = part[...]
 
 
 def final_kernel(groups, spans, *refs):
@@ -162,22 +167,19 @@
     return groups, width, args, scratch
 
 
-def run_sum(packs, cots, spans, parts, rank):
+def run_sum(packs, cots, spans, waits, rank):
     groups, width, args, scratch = operands(packs, cots, spans)
-    args += parts
-    rows = sum(part.shape[0] for part in parts)
     return pl.pallas_call(
         functools.partial(sum_kernel, groups, spans),
         out_shape=[
             jax.ShapeDtypeStruct((width, rank), jnp.float32),
             jax.ShapeDtypeStruct((rank, width), jnp.float32),
-            jax.ShapeDtypeStruct((rows, parts[0].shape[1]), jnp.bfloat16),
         ],
-        in_specs=[VMEM] * len(args),
-        out_specs=[VMEM] * 3,
+        in_specs=[VMEM] * len(args) + [ANY] * len(waits),
+        out_specs=[VMEM] * 2,
         scratch_shapes=scratch,
         compiler_params=PARAMS,
-    )(*args)
+    )(*args, *waits)
 
 
 def run_final(packs, cots, spans, partial, first, last):
@@ -233,15 +235,13 @@
             coming = rows_after(stash, *spans[i + 2], [arrivals[i]] + waits * (i > 0))
             arrivals.append(held(coming))
             waits = waits + [coming]
-        if i == chunks - 1:
-            *partial, joined = run_sum(packs, cot_all, spans[:-1], parts, rank)
-            first = to_previous(joined, "pipe")
-            waits = partial
-        dx, pack = run_chunk(index, arrivals[i], cot, dact, down, gain, start, waits, groups)
+        joins = parts if i == chunks - 2 else []
+        dx, pack = run_chunk(index, arrivals[i], cot, dact, down, gain, start, joins, waits, groups)
         packs.append([exchanged(pack[k], "dp", k) if k else pack[k] for k in range(groups)])
         parts.append(dx)
         waits = packs[-1][1:]
-    last = to_previous(parts[-1], "pipe")
+    partial = run_sum(packs[:-1], cot_all, spans[:-1], [pack[0]], rank)
+    first, last = [to_previous(dx, "pipe") for dx in parts[-2:]]
     before, down_grad, up_grad = run_final(packs[-1:], cot_all, spans[-1:], partial, first, last)
     return (before[None], down_grad[None], up_grad[None])
 

time: 69.4 us -> 68.6 us (0.988)
  the two profiles are of different devices: /device:TPU:17 before, /device:TPU:1 now
where the time goes in v6:
time: 68.6 us; the launch traced here: 68 us
  starting transfers between devices  31.6 us (46%)
  waiting for transfers between devices  25.9 us (38%)
  Pallas kernels  5.76 us (8%)
  local copies, waits for them, and re-layouts  3.37 us (5%)
  between operations  0.84 us (1%)
    ppermute x19, waiting for transfers between devices, exchanged(): lax.ppermute(x, axis, [(i, i ^ mask) for i in range(lax.axis_size(axis))])  25.9 us
    ppermute x19, starting transfers between devices, exchanged(): lax.ppermute(x, axis, [(i, i ^ mask) for i in range(lax.axis_size(axis))])  19.2 us
    ppermute x2, starting transfers between devices, to_previous(): lax.ppermute(x, axis, [(i, i - 1) for i in range(1, lax.axis_size(axis))])  12.4 us
    pallas_call x4, Pallas kernels, run_chunk(): pl.pallas_call(functools.partial(chunk_kernel, start, len(joins), len(wai...  3.41 us
    slice x2, local copies, waits for them, and re-layouts, per_device(): arrivals = [held(stash[start:start + rows]) for start, rows in spans[:2]]  1.97 us
    pallas_call x1, Pallas kernels, run_final(): pl.pallas_call(functools.partial(final_kernel, groups, spans), out_shape=...  1.58 us
  transfers between devices with their start and end apart: 21, of which 12 were waited for; matrix products, arithmetic and copies ran while one was open for 4% of the time, Pallas kernels for 6%

profile of v6, /device:TPU:1, one launch (start us, length us, event | category | flops | bytes accessed | tf_op | source)
XLA Modules:
  0.0 68.0 jit_solution(16088991328617286526)
XLA Ops:
  0.6 1.0 %slice_bitcast_fusion.1 = bf16[16,4096]{1,0:T(8,128)(2,1)S(1)} fusion(bf16[1,128,4096]{2,1,0:T(8,128)(2,1)} %param.5), kind=kLoop, calls=%fused_computation.7 | loop fusion | bytes 262144 | tf_op jit(solution)/shard_map/slice | solution.py:224
  1.7 3.2 %collective-permute-start.1 = (bf16[16,4096]{1,0:T(8,128)(2,1)S(1)}, bf16[16,4096]{1,0:T(8,128)(2,1)S(1)}, u32[]{:S(2)}, u32[]{:S(2)}) collective-permute-start(bf16[16,4096]{1,0:T(8,128)(2,1)S(1)} %slice_bitcast_fusion.1), channel_id=1, source_target_pairs={{0,16},{4,20},{8,24},{12,28},{16,0},{20,4},{24,8},{28,12},{1,17},{... | collective-permute-start | bytes 393224 | tf_op jit(solution)/shard_map/ppermute | solution.py:20
  4.9 1.0 %slice_bitcast_fusion = bf16[32,4096]{1,0:T(8,128)(2,1)S(1)} fusion(bf16[1,128,4096]{2,1,0:T(8,128)(2,1)} %param.5), kind=kLoop, calls=%fused_computation.6 | loop fusion | bytes 524288 | tf_op jit(solution)/shard_map/slice | solution.py:224
  5.9 1.4 %dynamic-slice_bitcast_fusion = (bf16[128,1024]{1,0:T(8,128)(2,1)S(1)}, bf16[128,1024]{1,0:T(8,128)(2,1)S(1)}, bf16[128,1024]{1,0:T(8,128)(2,1)S(1)}, bf16[128,1024]{1,0:T(8,128)(2,1)S(1)}) fusion(bf16[1,128,4096]{2,1,0:T(8,128)(2,1)} %param.6, s32[]{:T(128)S(6)} %select_n.15, s32[]{:T(128)S(6)} %select_n.13, s32[]{:T(128)S(6)} %select_n.12, s32[]{:T(128)S(6)} %select_n.14), kind=kLoop, calls=%fused_computation.2 | loop fusion | bytes 2097168 | tf_op jit(solution)/shard_map/dynamic_slice | solution.py:227
  7.3 1.3 %collective-permute-start.3 = (bf16[128,1024]{1,0:T(8,128)(2,1)S(1)}, bf16[128,1024]{1,0:T(8,128)(2,1)S(1)}, u32[]{:S(2)}, u32[]{:S(2)}) collective-permute-start(bf16[128,1024]{1,0:T(8,128)(2,1)S(1)} %get-tuple-element.54), channel_id=1, source_target_pairs={{0,2},{1,3},{2,0},{3,1},{4,6},{5,7},{6,4},{7,5},{8,10},{9,11},{10,... | collective-permute-start | bytes 786440 | tf_op jit(solution)/shard_map/ppermute | solution.py:20
  8.6 1.2 %collective-permute-start.2 = (bf16[128,1024]{1,0:T(8,128)(2,1)S(1)}, bf16[128,1024]{1,0:T(8,128)(2,1)S(1)}, u32[]{:S(2)}, u32[]{:S(2)}) collective-permute-start(bf16[128,1024]{1,0:T(8,128)(2,1)S(1)} %get-tuple-element.55), channel_id=1, source_target_pairs={{0,1},{1,0},{2,3},{3,2},{4,5},{5,4},{6,7},{7,6},{8,9},{9,8},{10,11... | collective-permute-start | bytes 786440 | tf_op jit(solution)/shard_map/ppermute | solution.py:20
  10.0 6.5 %collective-permute-done.1.refs_0_.saved_ref = bf16[16,4096]{1,0:T(8,128)(2,1)S(1)} collective-permute-done((bf16[16,4096]{1,0:T(8,128)(2,1)S(1)}, bf16[16,4096]{1,0:T(8,128)(2,1)S(1)}, u32[]{:S(2)}, u32[]{:S(2)}) %collective-permute-start.1) | collective-permute-done | bytes 131104 | tf_op jit(solution)/shard_map/ppermute | solution.py:20
  17.2 3.5 %collective-permute-done.4.refs_2_.refs_15_.refs_7_ = bf16[128,1024]{1,0:T(8,128)(2,1)S(1)} collective-permute-done((bf16[128,1024]{1,0:T(8,128)(2,1)S(1)}, bf16[128,1024]{1,0:T(8,128)(2,1)S(1)}, u32[]{:S(2)}, u32[]{:S(2)}) %collective-permute-start.4) | collective-permute-done | bytes 262176 | tf_op jit(solution)/shard_map/ppermute | solution.py:20
  20.8 0.7 %shard_map.77 = (bf16[16,4096]{1,0:T(8,128)(2,1)S(1)}, bf16[16,1280]{1,0:T(8,128)(2,1)S(1)}, bf16[16,1280]{1,0:T(8,128)(2,1)S(1)}, bf16[16,1280]{1,0:T(8,128)(2,1)S(1)}, bf16[16,1280]{1,0:T(8,128)(2,1)S(1)}) custom-call(s32[1]{0:T(128)} %bitcast.me_ref, bf16[16,4096]{1,0:T(8,128)(2,1)S(1)} %collective-permute-done.1.refs_0_.saved_ref, ...), custom_call_target="tpu_custom_call" | custom-call | tf_op jit(solution)/shard_map/pallas_call | solution.py:105
  21.5 1.0 %collective-permute-start.5 = (bf16[16,1280]{1,0:T(8,128)(2,1)S(1)}, bf16[16,1280]{1,0:T(8,128)(2,1)S(1)}, u32[]{:S(2)}, u32[]{:S(2)}) collective-permute-start(bf16[16,1280]{1,0:T(8,128)(2,1)S(1)} %get-tuple-element.28), channel_id=1, source_target_pairs={{0,1},{1,0},{2,3},{3,2},{4,5},{5,4},{6,7},{7,6},{8,9},{9,8},{10,11... | collective-permute-start | bytes 122888 | tf_op jit(solution)/shard_map/ppermute | solution.py:20
  22.5 1.2 %collective-permute-start.6 = (bf16[16,1280]{1,0:T(8,128)(2,1)S(1)}, bf16[16,1280]{1,0:T(8,128)(2,1)S(1)}, u32[]{:S(2)}, u32[]{:S(2)}) collective-permute-start(bf16[16,1280]{1,0:T(8,128)(2,1)S(1)} %get-tuple-element.29), channel_id=1, source_target_pairs={{0,2},{1,3},{2,0},{3,1},{4,6},{5,7},{6,4},{7,5},{8,10},{9,11},{10,... | collective-permute-start | bytes 122888 | tf_op jit(solution)/shard_map/ppermute | solution.py:20
  24.2 3.5 %collective-permute-done.refs_0_.saved_ref = bf16[32,4096]{1,0:T(8,128)(2,1)S(1)} collective-permute-done((bf16[32,4096]{1,0:T(8,128)(2,1)S(1)}, bf16[32,4096]{1,0:T(8,128)(2,1)S(1)}, u32[]{:S(2)}, u32[]{:S(2)}) %collective-permute-start) | collective-permute-done | bytes 262176 | tf_op jit(solution)/shard_map/ppermute | solution.py:20
  28.0 2.1 %collective-permute-start.8 = (bf16[48,4096]{1,0:T(8,128)(2,1)S(1)}, bf16[48,4096]{1,0:T(8,128)(2,1)S(1)}, u32[]{:S(2)}, u32[]{:S(2)}) collective-permute-start(bf16[48,4096]{1,0:T(8,128)(2,1)S(1)} %shard_map.78.refs_3_), channel_id=1, source_target_pairs={{0,16},{4,20},{8,24},{12,28},{16,0},{20,4},{24,8},{28,12},{1,17},{... | collective-permute-start | bytes 1179656 | tf_op jit(solution)/shard_map/ppermute | solution.py:20
  30.1 0.9 %shard_map.79 = (bf16[32,4096]{1,0:T(8,128)(2,1)S(1)}, bf16[32,1280]{1,0:T(8,128)(2,1)S(1)}, bf16[32,1280]{1,0:T(8,128)(2,1)S(1)}, bf16[32,1280]{1,0:T(8,128)(2,1)S(1)}, bf16[32,1280]{1,0:T(8,128)(2,1)S(1)}) custom-call(s32[1]{0:T(128)} %bitcast.me_ref, bf16[32,4096]{1,0:T(8,128)(2,1)S(1)} %collective-permute-done.refs_0_.saved_ref, ...), custom_call_target="tpu_custom_call" | custom-call | tf_op jit(solution)/shard_map/pallas_call | solution.py:105
  31.5 2.2 %collective-permute-start.12 = (bf16[32,1280]{1,0:T(8,128)(2,1)S(1)}, bf16[32,1280]{1,0:T(8,128)(2,1)S(1)}, u32[]{:S(2)}, u32[]{:S(2)}) collective-permute-start(bf16[32,1280]{1,0:T(8,128)(2,1)S(1)} %get-tuple-element.35), channel_id=1, source_target_pairs={{0,3},{1,2},{2,1},{3,0},{4,7},{5,6},{6,5},{7,4},{8,11},{9,10},{10,... | collective-permute-start | bytes 245768 | tf_op jit(solution)/shard_map/ppermute | solution.py:20
  33.7 0.9 %collective-permute-done.10.refs_2_.refs_4_ = bf16[32,1280]{1,0:T(8,128)(2,1)S(1)} collective-permute-done((bf16[32,1280]{1,0:T(8,128)(2,1)S(1)}, bf16[32,1280]{1,0:T(8,128)(2,1)S(1)}, u32[]{:S(2)}, u32[]{:S(2)}) %collective-permute-start.10) | collective-permute-done | bytes 81952 | tf_op jit(solution)/shard_map/ppermute | solution.py:20
  34.9 1.1 %collective-permute-done.12.refs_4_.refs_10_ = bf16[32,1280]{1,0:T(8,128)(2,1)S(1)} collective-permute-done((bf16[32,1280]{1,0:T(8,128)(2,1)S(1)}, bf16[32,1280]{1,0:T(8,128)(2,1)S(1)}, u32[]{:S(2)}, u32[]{:S(2)}) %collective-permute-start.12) | collective-permute-done | bytes 81952 | tf_op jit(solution)/shard_map/ppermute | solution.py:20
  36.0 0.9 %shard_map.80 = (bf16[80,4096]{1,0:T(8,128)(2,1)S(1)}, bf16[32,1280]{1,0:T(8,128)(2,1)S(1)}, bf16[32,1280]{1,0:T(8,128)(2,1)S(1)}, bf16[32,1280]{1,0:T(8,128)(2,1)S(1)}, bf16[32,1280]{1,0:T(8,128)(2,1)S(1)}) custom-call(s32[1]{0:T(128)} %bitcast.me_ref, bf16[32,4096]{1,0:T(8,128)(2,1)S(1)} %collective-permute-done.9.saved_ref, ...), custom_call_target="tpu_custom_call" | custom-call | tf_op jit(solution)/shard_map/pallas_call | solution.py:105
  36.8 9.8 %collective-permute-start.19 = (bf16[80,4096]{1,0:T(8,128)(2,1)S(1)}, bf16[80,4096]{1,0:T(8,128)(2,1)S(1)}, u32[]{:S(2)}, u32[]{:S(2)}) collective-permute-start(bf16[80,4096]{1,0:T(8,128)(2,1)S(1)} %get-tuple-element.48), channel_id=1, source_target_pairs={{4,0},{8,4},{12,8},{16,12},{20,16},{24,20},{28,24},{5,1},{9,5},{13... | collective-permute-start | bytes 1966088 | tf_op jit(solution)/shard_map/ppermute | solution.py:24
  46.6 1.6 %collective-permute-start.13 = (bf16[32,1280]{1,0:T(8,128)(2,1)S(1)}, bf16[32,1280]{1,0:T(8,128)(2,1)S(1)}, u32[]{:S(2)}, u32[]{:S(2)}) collective-permute-start(bf16[32,1280]{1,0:T(8,128)(2,1)S(1)} %get-tuple-element.36), channel_id=1, source_target_pairs={{0,1},{1,0},{2,3},{3,2},{4,5},{5,4},{6,7},{7,6},{8,9},{9,8},{10,11... | collective-permute-start | bytes 245768 | tf_op jit(solution)/shard_map/ppermute | solution.py:20
  48.3 1.2 %collective-permute-start.14 = (bf16[32,1280]{1,0:T(8,128)(2,1)S(1)}, bf16[32,1280]{1,0:T(8,128)(2,1)S(1)}, u32[]{:S(2)}, u32[]{:S(2)}) collective-permute-start(bf16[32,1280]{1,0:T(8,128)(2,1)S(1)} %get-tuple-element.37), channel_id=1, source_target_pairs={{0,2},{1,3},{2,0},{3,1},{4,6},{5,7},{6,4},{7,5},{8,10},{9,11},{10,... | collective-permute-start | bytes 245768 | tf_op jit(solution)/shard_map/ppermute | solution.py:20
  49.5 1.5 %collective-permute-done.13.refs_0_.refs_5_ = bf16[32,1280]{1,0:T(8,128)(2,1)S(1)} collective-permute-done((bf16[32,1280]{1,0:T(8,128)(2,1)S(1)}, bf16[32,1280]{1,0:T(8,128)(2,1)S(1)}, u32[]{:S(2)}, u32[]{:S(2)}) %collective-permute-start.13) | collective-permute-done | bytes 81952 | tf_op jit(solution)/shard_map/ppermute | solution.py:20
  51.0 2.2 %collective-permute-done.14.refs_1_.refs_8_ = bf16[32,1280]{1,0:T(8,128)(2,1)S(1)} collective-permute-done((bf16[32,1280]{1,0:T(8,128)(2,1)S(1)}, bf16[32,1280]{1,0:T(8,128)(2,1)S(1)}, u32[]{:S(2)}, u32[]{:S(2)}) %collective-permute-start.14) | collective-permute-done | bytes 81952 | tf_op jit(solution)/shard_map/ppermute | solution.py:20
  53.2 1.3 %collective-permute-done.15.refs_2_.refs_11_ = bf16[32,1280]{1,0:T(8,128)(2,1)S(1)} collective-permute-done((bf16[32,1280]{1,0:T(8,128)(2,1)S(1)}, bf16[32,1280]{1,0:T(8,128)(2,1)S(1)}, u32[]{:S(2)}, u32[]{:S(2)}) %collective-permute-start.15) | collective-permute-done | bytes 81952 | tf_op jit(solution)/shard_map/ppermute | solution.py:20
  54.5 0.9 %shard_map.81 = (bf16[48,4096]{1,0:T(8,128)(2,1)S(1)}, bf16[48,1280]{1,0:T(8,128)(2,1)S(1)}, bf16[48,1280]{1,0:T(8,128)(2,1)S(1)}, bf16[48,1280]{1,0:T(8,128)(2,1)S(1)}, bf16[48,1280]{1,0:T(8,128)(2,1)S(1)}) custom-call(s32[1]{0:T(128)} %bitcast.me_ref, bf16[48,4096]{1,0:T(8,128)(2,1)S(1)} %collective-permute-done.8.saved_ref, ...), custom_call_target="tpu_custom_call" | custom-call | tf_op jit(solution)/shard_map/pallas_call | solution.py:105
  55.5 2.6 %collective-permute-start.20 = (bf16[48,4096]{1,0:T(8,128)(2,1)S(1)}, bf16[48,4096]{1,0:T(8,128)(2,1)S(1)}, u32[]{:S(2)}, u32[]{:S(2)}) collective-permute-start(bf16[48,4096]{1,0:T(8,128)(2,1)S(1)} %get-tuple-element.49), channel_id=1, source_target_pairs={{4,0},{8,4},{12,8},{16,12},{20,16},{24,20},{28,24},{5,1},{9,5},{13... | collective-permute-start | bytes 1179656 | tf_op jit(solution)/shard_map/ppermute | solution.py:24
  58.6 0.7 %collective-permute-start.17 = (bf16[48,1280]{1,0:T(8,128)(2,1)S(1)}, bf16[48,1280]{1,0:T(8,128)(2,1)S(1)}, u32[]{:S(2)}, u32[]{:S(2)}) collective-permute-start(bf16[48,1280]{1,0:T(8,128)(2,1)S(1)} %get-tuple-element.41), channel_id=1, source_target_pairs={{0,2},{1,3},{2,0},{3,1},{4,6},{5,7},{6,4},{7,5},{8,10},{9,11},{10,... | collective-permute-start | bytes 368648 | tf_op jit(solution)/shard_map/ppermute | solution.py:20
  59.3 1.5 %collective-permute-start.18 = (bf16[48,1280]{1,0:T(8,128)(2,1)S(1)}, bf16[48,1280]{1,0:T(8,128)(2,1)S(1)}, u32[]{:S(2)}, u32[]{:S(2)}) collective-permute-start(bf16[48,1280]{1,0:T(8,128)(2,1)S(1)} %get-tuple-element.42), channel_id=1, source_target_pairs={{0,3},{1,2},{2,1},{3,0},{4,7},{5,6},{6,5},{7,4},{8,11},{9,10},{10,... | collective-permute-start | bytes 368648 | tf_op jit(solution)/shard_map/ppermute | solution.py:20
  60.8 0.5 shard_map.82
  61.4 2.1 %collective-permute-done.16.refs_1_ = bf16[48,1280]{1,0:T(8,128)(2,1)S(1)} collective-permute-done((bf16[48,1280]{1,0:T(8,128)(2,1)S(1)}, bf16[48,1280]{1,0:T(8,128)(2,1)S(1)}, u32[]{:S(2)}, u32[]{:S(2)}) %collective-permute-start.16) | collective-permute-done | bytes 122912 | tf_op jit(solution)/shard_map/ppermute | solution.py:20
  63.8 2.6 %collective-permute-done.18.refs_3_ = bf16[48,1280]{1,0:T(8,128)(2,1)S(1)} collective-permute-done((bf16[48,1280]{1,0:T(8,128)(2,1)S(1)}, bf16[48,1280]{1,0:T(8,128)(2,1)S(1)}, u32[]{:S(2)}, u32[]{:S(2)}) %collective-permute-start.18) | collective-permute-done | bytes 122912 | tf_op jit(solution)/shard_map/ppermute | solution.py:20
  66.4 1.6 %shard_map.83 = (bf16[128,4096]{1,0:T(8,128)(2,1)}, f32[1024,128]{1,0:T(8,128)}, f32[128,1024]{1,0:T(8,128)}) custom-call(bf16[48,1280]{1,0:T(8,128)(2,1)S(1)} %get-tuple-element.39.refs_16_.refs_0_, bf16[48,1280]{1,0:T(8,128)(2,1)S(1)} %collective-permute-done.16.refs_1_, bf16[48,1280]{1,0:T(8,128)(2,1)S(1)} %collective-permute-done.17.refs_2_, ...), custom_call_target="tpu_custom_call" | custom-call | tf_op jit(solution)/shard_map/pallas_call | solution.py:195
  (32 shorter events, 3.3 us)
Async XLA Ops:
  0.6 16.0 %copy-start = (bf16[1,128,4096]{2,1,0:T(8,128)(2,1)S(1)}, bf16[1,128,4096]{2,1,0:T(8,128)(2,1)}, u32[]{:S(2)}) copy-start(bf16[1,128,4096]{2,1,0:T(8,128)(2,1)} %param.8) | copy-start | bytes 3145732
  1.7 14.9 %collective-permute-start.1 = (bf16[16,4096]{1,0:T(8,128)(2,1)S(1)}, bf16[16,4096]{1,0:T(8,128)(2,1)S(1)}, u32[]{:S(2)}, u32[]{:S(2)}) collective-permute-start(bf16[16,4096]{1,0:T(8,128)(2,1)S(1)} %slice_bitcast_fusion.1), channel_id=1, source_target_pairs={{0,16},{4,20},{8,24},{12,28},{16,0},{20,4},{24,8},{28,12},{1,17},{... | collective-permute-start | bytes 393224 | tf_op jit(solution)/shard_map/ppermute | solution.py:20
  5.8 21.9 %collective-permute-start = (bf16[32,4096]{1,0:T(8,128)(2,1)S(1)}, bf16[32,4096]{1,0:T(8,128)(2,1)S(1)}, u32[]{:S(2)}, u32[]{:S(2)}) collective-permute-start(bf16[32,4096]{1,0:T(8,128)(2,1)S(1)} %slice_bitcast_fusion), channel_id=1, source_target_pairs={{0,16},{4,20},{8,24},{12,28},{16,0},{20,4},{24,8},{28,12},{1,17},{... | collective-permute-start | bytes 786440 | tf_op jit(solution)/shard_map/ppermute | solution.py:20
  5.9 10.6 %copy-start.3 = (bf16[1,128,4096]{2,1,0:T(8,128)(2,1)S(1)}, bf16[1,128,4096]{2,1,0:T(8,128)(2,1)}, u32[]{:S(2)}) copy-start(bf16[1,128,4096]{2,1,0:T(8,128)(2,1)} %param.5) | copy-start | bytes 3145732
  7.3 9.3 %copy-start.1 = (bf16[1,128,4096]{2,1,0:T(8,128)(2,1)S(1)}, bf16[1,128,4096]{2,1,0:T(8,128)(2,1)}, u32[]{:S(2)}) copy-start(bf16[1,128,4096]{2,1,0:T(8,128)(2,1)} %param.6) | copy-start | bytes 3145732
  7.3 9.9 %collective-permute-start.3 = (bf16[128,1024]{1,0:T(8,128)(2,1)S(1)}, bf16[128,1024]{1,0:T(8,128)(2,1)S(1)}, u32[]{:S(2)}, u32[]{:S(2)}) collective-permute-start(bf16[128,1024]{1,0:T(8,128)(2,1)S(1)} %get-tuple-element.54), channel_id=1, source_target_pairs={{0,2},{1,3},{2,0},{3,1},{4,6},{5,7},{6,4},{7,5},{8,10},{9,11},{10,... | collective-permute-start | bytes 786440 | tf_op jit(solution)/shard_map/ppermute | solution.py:20
  8.6 8.6 %collective-permute-start.2 = (bf16[128,1024]{1,0:T(8,128)(2,1)S(1)}, bf16[128,1024]{1,0:T(8,128)(2,1)S(1)}, u32[]{:S(2)}, u32[]{:S(2)}) collective-permute-start(bf16[128,1024]{1,0:T(8,128)(2,1)S(1)} %get-tuple-element.55), channel_id=1, source_target_pairs={{0,1},{1,0},{2,3},{3,2},{4,5},{5,4},{6,7},{7,6},{8,9},{9,8},{10,11... | collective-permute-start | bytes 786440 | tf_op jit(solution)/shard_map/ppermute | solution.py:20
  9.8 10.9 %collective-permute-start.4 = (bf16[128,1024]{1,0:T(8,128)(2,1)S(1)}, bf16[128,1024]{1,0:T(8,128)(2,1)S(1)}, u32[]{:S(2)}, u32[]{:S(2)}) collective-permute-start(bf16[128,1024]{1,0:T(8,128)(2,1)S(1)} %get-tuple-element.56), channel_id=1, source_target_pairs={{0,3},{1,2},{2,1},{3,0},{4,7},{5,6},{6,5},{7,4},{8,11},{9,10},{10,... | collective-permute-start | bytes 786440 | tf_op jit(solution)/shard_map/ppermute | solution.py:20
  16.5 4.2 %copy-start.2 = (bf16[1,4096,128]{2,1,0:T(8,128)(2,1)S(1)}, bf16[1,4096,128]{2,1,0:T(8,128)(2,1)}, u32[]{:S(2)}) copy-start(bf16[1,4096,128]{2,1,0:T(8,128)(2,1)} %param.7) | copy-start | bytes 3145732
  16.6 19.4 %collective-permute-start.9 = (bf16[32,4096]{1,0:T(8,128)(2,1)S(1)}, bf16[32,4096]{1,0:T(8,128)(2,1)S(1)}, u32[]{:S(2)}, u32[]{:S(2)}) collective-permute-start(bf16[32,4096]{1,0:T(8,128)(2,1)S(1)} %shard_map.76.refs_3_), channel_id=1, source_target_pairs={{0,16},{4,20},{8,24},{12,28},{16,0},{20,4},{24,8},{28,12},{1,17},{... | collective-permute-start | bytes 786440 | tf_op jit(solution)/shard_map/ppermute | solution.py:20
  16.7 4.1 %copy-start.4 = (f32[1,4096]{1,0:T(1,128)S(1)}, f32[1,4096]{1,0:T(1,128)}, u32[]{:S(2)}) copy-start(f32[1,4096]{1,0:T(1,128)} %gain_ref.7) | copy-start | bytes 49156
  21.5 6.3 %collective-permute-start.5 = (bf16[16,1280]{1,0:T(8,128)(2,1)S(1)}, bf16[16,1280]{1,0:T(8,128)(2,1)S(1)}, u32[]{:S(2)}, u32[]{:S(2)}) collective-permute-start(bf16[16,1280]{1,0:T(8,128)(2,1)S(1)} %get-tuple-element.28), channel_id=1, source_target_pairs={{0,1},{1,0},{2,3},{3,2},{4,5},{5,4},{6,7},{7,6},{8,9},{9,8},{10,11... | collective-permute-start | bytes 122888 | tf_op jit(solution)/shard_map/ppermute | solution.py:20
  22.5 5.3 %collective-permute-start.6 = (bf16[16,1280]{1,0:T(8,128)(2,1)S(1)}, bf16[16,1280]{1,0:T(8,128)(2,1)S(1)}, u32[]{:S(2)}, u32[]{:S(2)}) collective-permute-start(bf16[16,1280]{1,0:T(8,128)(2,1)S(1)} %get-tuple-element.29), channel_id=1, source_target_pairs={{0,2},{1,3},{2,0},{3,1},{4,6},{5,7},{6,4},{7,5},{8,10},{9,11},{10,... | collective-permute-start | bytes 122888 | tf_op jit(solution)/shard_map/ppermute | solution.py:20
  23.7 4.0 %collective-permute-start.7 = (bf16[16,1280]{1,0:T(8,128)(2,1)S(1)}, bf16[16,1280]{1,0:T(8,128)(2,1)S(1)}, u32[]{:S(2)}, u32[]{:S(2)}) collective-permute-start(bf16[16,1280]{1,0:T(8,128)(2,1)S(1)} %get-tuple-element.30), channel_id=1, source_target_pairs={{0,3},{1,2},{2,1},{3,0},{4,7},{5,6},{6,5},{7,4},{8,11},{9,10},{10,... | collective-permute-start | bytes 122888 | tf_op jit(solution)/shard_map/ppermute | solution.py:20
  28.0 26.6 %collective-permute-start.8 = (bf16[48,4096]{1,0:T(8,128)(2,1)S(1)}, bf16[48,4096]{1,0:T(8,128)(2,1)S(1)}, u32[]{:S(2)}, u32[]{:S(2)}) collective-permute-start(bf16[48,4096]{1,0:T(8,128)(2,1)S(1)} %shard_map.78.refs_3_), channel_id=1, source_target_pairs={{0,16},{4,20},{8,24},{12,28},{16,0},{20,4},{24,8},{28,12},{1,17},{... | collective-permute-start | bytes 1179656 | tf_op jit(solution)/shard_map/ppermute | solution.py:20
  30.9 3.7 %collective-permute-start.10 = (bf16[32,1280]{1,0:T(8,128)(2,1)S(1)}, bf16[32,1280]{1,0:T(8,128)(2,1)S(1)}, u32[]{:S(2)}, u32[]{:S(2)}) collective-permute-start(bf16[32,1280]{1,0:T(8,128)(2,1)S(1)} %get-tuple-element.33), channel_id=1, source_target_pairs={{0,1},{1,0},{2,3},{3,2},{4,5},{5,4},{6,7},{7,6},{8,9},{9,8},{10,11... | collective-permute-start | bytes 245768 | tf_op jit(solution)/shard_map/ppermute | solution.py:20
  31.3 3.6 %collective-permute-start.11 = (bf16[32,1280]{1,0:T(8,128)(2,1)S(1)}, bf16[32,1280]{1,0:T(8,128)(2,1)S(1)}, u32[]{:S(2)}, u32[]{:S(2)}) collective-permute-start(bf16[32,1280]{1,0:T(8,128)(2,1)S(1)} %get-tuple-element.34), channel_id=1, source_target_pairs={{0,2},{1,3},{2,0},{3,1},{4,6},{5,7},{6,4},{7,5},{8,10},{9,11},{10,... | collective-permute-start | bytes 245768 | tf_op jit(solution)/shard_map/ppermute | solution.py:20
  31.5 4.5 %collective-permute-start.12 = (bf16[32,1280]{1,0:T(8,128)(2,1)S(1)}, bf16[32,1280]{1,0:T(8,128)(2,1)S(1)}, u32[]{:S(2)}, u32[]{:S(2)}) collective-permute-start(bf16[32,1280]{1,0:T(8,128)(2,1)S(1)} %get-tuple-element.35), channel_id=1, source_target_pairs={{0,3},{1,2},{2,1},{3,0},{4,7},{5,6},{6,5},{7,4},{8,11},{9,10},{10,... | collective-permute-start | bytes 245768 | tf_op jit(solution)/shard_map/ppermute | solution.py:20
  36.8 29.6 %collective-permute-start.19 = (bf16[80,4096]{1,0:T(8,128)(2,1)S(1)}, bf16[80,4096]{1,0:T(8,128)(2,1)S(1)}, u32[]{:S(2)}, u32[]{:S(2)}) collective-permute-start(bf16[80,4096]{1,0:T(8,128)(2,1)S(1)} %get-tuple-element.48), channel_id=1, source_target_pairs={{4,0},{8,4},{12,8},{16,12},{20,16},{24,20},{28,24},{5,1},{9,5},{13... | collective-permute-start | bytes 1966088 | tf_op jit(solution)/shard_map/ppermute | solution.py:24
  46.6 4.4 %collective-permute-start.13 = (bf16[32,1280]{1,0:T(8,128)(2,1)S(1)}, bf16[32,1280]{1,0:T(8,128)(2,1)S(1)}, u32[]{:S(2)}, u32[]{:S(2)}) collective-permute-start(bf16[32,1280]{1,0:T(8,128)(2,1)S(1)} %get-tuple-element.36), channel_id=1, source_target_pairs={{0,1},{1,0},{2,3},{3,2},{4,5},{5,4},{6,7},{7,6},{8,9},{9,8},{10,11... | collective-permute-start | bytes 245768 | tf_op jit(solution)/shard_map/ppermute | solution.py:20
  48.3 5.0 %collective-permute-start.14 = (bf16[32,1280]{1,0:T(8,128)(2,1)S(1)}, bf16[32,1280]{1,0:T(8,128)(2,1)S(1)}, u32[]{:S(2)}, u32[]{:S(2)}) collective-permute-start(bf16[32,1280]{1,0:T(8,128)(2,1)S(1)} %get-tuple-element.37), channel_id=1, source_target_pairs={{0,2},{1,3},{2,0},{3,1},{4,6},{5,7},{6,4},{7,5},{8,10},{9,11},{10,... | collective-permute-start | bytes 245768 | tf_op jit(solution)/shard_map/ppermute | solution.py:20
  49.5 5.0 %collective-permute-start.15 = (bf16[32,1280]{1,0:T(8,128)(2,1)S(1)}, bf16[32,1280]{1,0:T(8,128)(2,1)S(1)}, u32[]{:S(2)}, u32[]{:S(2)}) collective-permute-start(bf16[32,1280]{1,0:T(8,128)(2,1)S(1)} %get-tuple-element.38), channel_id=1, source_target_pairs={{0,3},{1,2},{2,1},{3,0},{4,7},{5,6},{6,5},{7,4},{8,11},{9,10},{10,... | collective-permute-start | bytes 245768 | tf_op jit(solution)/shard_map/ppermute | solution.py:20
  55.5 10.9 %collective-permute-start.20 = (bf16[48,4096]{1,0:T(8,128)(2,1)S(1)}, bf16[48,4096]{1,0:T(8,128)(2,1)S(1)}, u32[]{:S(2)}, u32[]{:S(2)}) collective-permute-start(bf16[48,4096]{1,0:T(8,128)(2,1)S(1)} %get-tuple-element.49), channel_id=1, source_target_pairs={{4,0},{8,4},{12,8},{16,12},{20,16},{24,20},{28,24},{5,1},{9,5},{13... | collective-permute-start | bytes 1179656 | tf_op jit(solution)/shard_map/ppermute | solution.py:24
  58.1 5.4 %collective-permute-start.16 = (bf16[48,1280]{1,0:T(8,128)(2,1)S(1)}, bf16[48,1280]{1,0:T(8,128)(2,1)S(1)}, u32[]{:S(2)}, u32[]{:S(2)}) collective-permute-start(bf16[48,1280]{1,0:T(8,128)(2,1)S(1)} %get-tuple-element.40), channel_id=1, source_target_pairs={{0,1},{1,0},{2,3},{3,2},{4,5},{5,4},{6,7},{7,6},{8,9},{9,8},{10,11... | collective-permute-start | bytes 368648 | tf_op jit(solution)/shard_map/ppermute | solution.py:20
  58.6 5.2 %collective-permute-start.17 = (bf16[48,1280]{1,0:T(8,128)(2,1)S(1)}, bf16[48,1280]{1,0:T(8,128)(2,1)S(1)}, u32[]{:S(2)}, u32[]{:S(2)}) collective-permute-start(bf16[48,1280]{1,0:T(8,128)(2,1)S(1)} %get-tuple-element.41), channel_id=1, source_target_pairs={{0,2},{1,3},{2,0},{3,1},{4,6},{5,7},{6,4},{7,5},{8,10},{9,11},{10,... | collective-permute-start | bytes 368648 | tf_op jit(solution)/shard_map/ppermute | solution.py:20
  59.3 7.1 %collective-permute-start.18 = (bf16[48,1280]{1,0:T(8,128)(2,1)S(1)}, bf16[48,1280]{1,0:T(8,128)(2,1)S(1)}, u32[]{:S(2)}, u32[]{:S(2)}) collective-permute-start(bf16[48,1280]{1,0:T(8,128)(2,1)S(1)} %get-tuple-element.42), channel_id=1, source_target_pairs={{0,3},{1,2},{2,1},{3,0},{4,7},{5,6},{6,5},{7,4},{8,11},{9,10},{10,... | collective-permute-start | bytes 368648 | tf_op jit(solution)/shard_map/ppermute | solution.py:20

commit v7 on v5

--- a/solution.py
+++ b/solution.py
@@ -7,7 +7,7 @@
 from jax.experimental.pallas import tpu as pltpu
 from jax.sharding import PartitionSpec as P
 
-SHARES = (1, 2, 2, 3)
+SHARES = (3, 2, 3)
 LANES = 512
 VMEM = pl.BlockSpec(memory_space=pltpu.VMEM)
 SMEM = pl.BlockSpec(memory_space=pltpu.SMEM)
@@ -57,9 +57,13 @@
     )(stash, *waits)
 
 
-def chunk_kernel(groups, start, waits, me_ref, saved_ref, cot_ref, dact_ref, down_ref, gain_ref, *refs):
-    outs = refs[waits:]
-    dx_ref, pack_refs, normed_ref = outs[0], outs[1:-1], outs[-1]
+def chunk_kernel(start, pieces, groups, me_ref, cot_ref, dact_ref, down_ref, gain_ref, *refs):
+    saved_ref, normed_ref = refs[-2:]
+    dx_ref, pack_refs = refs[-3 - groups], refs[-2 - groups : -2]
+    at = 0
+    for piece in refs[:pieces]:
+        saved_ref[pl.ds(at, piece.shape[0]), :] = piece[...]
+        at += piece.shape[0]
     rows, features = saved_ref.shape
     width = features // groups
     rank = down_ref.shape[1]
@@ -91,43 +95,39 @@
 
 
 def run_chunk(me, saved, cot, dact, down, gain, start, waits, groups):
-    rows, features = saved.shape
+    features = cot.shape[1]
+    rows = sum(piece.shape[0] for piece in saved)
     rank = down.shape[1]
     pack = jax.ShapeDtypeStruct((rows, features // groups + 2 * rank), jnp.bfloat16)
     outs = [jax.ShapeDtypeStruct((rows, features), jnp.bfloat16)] + [pack] * groups
     got = pl.pallas_call(
-        functools.partial(chunk_kernel, groups, start, len(waits)),
+        functools.partial(chunk_kernel, start, len(saved), groups),
         out_shape=outs,
-        in_specs=[SMEM] + [VMEM] * 5 + [ANY] * len(waits),
+        in_specs=[SMEM] + [VMEM] * (4 + len(saved)) + [ANY] * len(waits),
         out_specs=[VMEM] * len(outs),
-        scratch_shapes=[pltpu.VMEM((rows, features), jnp.bfloat16)],
+        scratch_shapes=[pltpu.VMEM((rows, features), jnp.bfloat16)] * 2,
         compiler_params=PARAMS,
-    )(me, saved, cot, dact, down, gain, *waits)
+    )(me, cot, dact, down, gain, *saved, *waits)
     return got[0], got[1:]
 
 
-def gather_rows(groups, spans, packs, cots, every, held):
-    at = 0
-    for k in range(groups):
-        for j, (start, rows) in enumerate(spans):
-            every[pl.ds(at, rows), :] = packs[k * len(spans) + j][...]
-            held[pl.ds(at, rows), :] = cots[k][pl.ds(start, rows), :]
-            at += rows
-
-
-def sum_kernel(groups, spans, *refs):
-    count = groups * len(spans)
-    packs, cots, parts = refs[:count], refs[count : count + groups], refs[count + groups : -5]
-    down_ref, up_ref, joined, every, held = refs[-5:]
+def gather_rows(start, packs, cots, every, held):
+    rows = packs[0].shape[0]
+    for k, (pack, part) in enumerate(zip(packs, cots)):
+        every[pl.ds(k * rows, rows), :] = pack[...]
+        held[pl.ds(k * rows, rows), :] = part[pl.ds(start, rows), :]
+
+
+def sum_kernel(start, groups, *refs):
+    packs, cots = refs[:groups], refs[groups : 2 * groups]
+    down_ref, up_ref, every, held = refs[-4:]
     width, rank = down_ref.shape
-    gather_rows(groups, spans, packs, cots, every, held)
+    gather_rows(start, packs, cots, every, held)
     down_ref[...] = rows_dot(every[:, :width], every[:, width : width + rank])
     up_ref[...] = rows_dot(every[:, width + rank :], held[...])
-    for (start, rows), part in zip(spans, parts):
-        joined[pl.ds(start, rows), :] = part[...]
-
-
-def final_kernel(groups, spans, *refs):
+
+
+def final_kernel(start, groups, *refs):
     packs, cots = refs[:groups], refs[groups : 2 * groups]
     old_down, old_up, first, last = refs[2 * groups : 2 * groups + 4]
     before_ref, down_ref, up_ref, every, held, down, up, done = refs[2 * groups + 4 :]
@@ -141,7 +141,7 @@
     ]
     copies[0].start()
     copies[1].start()
-    gather_rows(groups, spans, packs, cots, every, held)
+    gather_rows(start, packs, cots, every, held)
     down[...] = old_down[...] + rows_dot(every[:, :width], every[:, width : width + rank])
     copies[2].start()
     up[...] = old_up[...] + rows_dot(every[:, width + rank :], held[...])
@@ -150,58 +150,46 @@
         copy.wait()
 
 
-def operands(packs, cots, spans):
-    groups = len(cots)
-    width = cots[0].shape[1]
-    depth = groups * sum(rows for _, rows in spans)
-    args = [packs[j][k] for k in range(groups) for j in range(len(spans))] + list(cots)
-    scratch = [
-        pltpu.VMEM((depth, packs[0][0].shape[1]), jnp.bfloat16),
-        pltpu.VMEM((depth, width), jnp.bfloat16),
+def gathered(packs, cots):
+    depth = len(packs) * packs[0].shape[0]
+    return [
+        pltpu.VMEM((depth, packs[0].shape[1]), jnp.bfloat16),
+        pltpu.VMEM((depth, cots[0].shape[1]), jnp.bfloat16),
     ]
-    return groups, width, args, scratch
-
-
-def run_sum(packs, cots, spans, parts, rank):
-    groups, width, args, scratch = operands(packs, cots, spans)
-    args += parts
-    rows = sum(part.shape[0] for part in parts)
+
+
+def run_sum(start, packs, cots, waits, rank):
+    groups, width = len(cots), cots[0].shape[1]
     return pl.pallas_call(
-        functools.partial(sum_kernel, groups, spans),
+        functools.partial(sum_kernel, start, groups),
         out_shape=[
             jax.ShapeDtypeStruct((width, rank), jnp.float32),
             jax.ShapeDtypeStruct((rank, width), jnp.float32),
-            jax.ShapeDtypeStruct((rows, parts[0].shape[1]), jnp.bfloat16),
         ],
-        in_specs=[VMEM] * len(args),
-        out_specs=[VMEM] * 3,
-        scratch_shapes=scratch,
+        in_specs=[VMEM] * (2 * groups) + [ANY] * len(waits),
+        out_specs=[VMEM] * 2,
+        scratch_shapes=gathered(packs, cots),
         compiler_params=PARAMS,
-    )(*args)
-
-
-def run_final(packs, cots, spans, partial, first, last):
-    groups, width, args, scratch = operands(packs, cots, spans)
-    down, up = partial
-    args += [down, up, first, last]
+    )(*packs, *cots, *waits)
+
+
+def run_final(start, packs, cots, partial, first, last):
+    groups = len(cots)
+    down, up = [jax.ShapeDtypeStruct(value.shape, jnp.float32) for value in partial]
     before = jax.ShapeDtypeStruct((first.shape[0] + last.shape[0], first.shape[1]), jnp.bfloat16)
-    scratch += [
-        pltpu.VMEM(down.shape, jnp.float32),
-        pltpu.VMEM(up.shape, jnp.float32),
-        pltpu.SemaphoreType.DMA((4,)),
-    ]
     return pl.pallas_call(
-        functools.partial(final_kernel, groups, spans),
-        out_shape=[
-            before,
-            jax.ShapeDtypeStruct(down.shape, jnp.float32),
-            jax.ShapeDtypeStruct(up.shape, jnp.float32),
+        functools.partial(final_kernel, start, groups),
+        out_shape=[before, down, up],
+        in_specs=[VMEM] * (2 * groups + 4),
+        out_specs=[ANY] * 3,
+        scratch_shapes=gathered(packs, cots)
+        + [
+            pltpu.VMEM(down.shape, jnp.float32),
+            pltpu.VMEM(up.shape, jnp.float32),
+            pltpu.SemaphoreType.DMA((4,)),
         ],
-        in_specs=[VMEM] * len(args),
-        out_specs=[ANY] * 3,
-        scratch_shapes=scratch,
         compiler_params=PARAMS,
-    )(*args)
+    )(*packs, *cots, *partial, first, last)
 
 
 def per_device(stash_held, grad_in, w_down, w_up, gain):
@@ -214,7 +202,6 @@
     width = features // groups
     sizes = [tokens * share // sum(SHARES) for share in SHARES]
     spans = [(sum(sizes[:i]), size) for i, size in enumerate(sizes)]
-    chunks = len(spans)
 
     def held(value):
         return exchanged(value, "pipe", sections // 2)
@@ -227,22 +214,22 @@
     dact = last_dot(cot, upper)
     index = jnp.reshape(me.astype(jnp.int32), (1,))
 
-    parts, packs, waits = [], [], cot_all[1:]
-    for i, (start, rows) in enumerate(spans):
-        if i + 2 < chunks:
-            coming = rows_after(stash, *spans[i + 2], [arrivals[i]] + waits * (i > 0))
-            arrivals.append(held(coming))
-            waits = waits + [coming]
-        if i == chunks - 1:
-            *partial, joined = run_sum(packs, cot_all, spans[:-1], parts, rank)
-            first = to_previous(joined, "pipe")
-            waits = partial
-        dx, pack = run_chunk(index, arrivals[i], cot, dact, down, gain, start, waits, groups)
-        packs.append([exchanged(pack[k], "dp", k) if k else pack[k] for k in range(groups)])
-        parts.append(dx)
-        waits = packs[-1][1:]
-    last = to_previous(parts[-1], "pipe")
-    before, down_grad, up_grad = run_final(packs[-1:], cot_all, spans[-1:], partial, first, last)
+    coming = rows_after(stash, *spans[2], [arrivals[1]])
+    arrivals.append(held(coming))
+
+    def swapped(packs):
+        return [exchanged(pack, "dp", k) if k else pack for k, pack in enumerate(packs)]
+
+    late = spans[2][0]
+    dx, pack = run_chunk(
+        index, arrivals[:2], cot, dact, down, gain, 0, cot_all[1:] + [coming], groups
+    )
+    first = to_previous(dx, "pipe")
+    packs = swapped(pack)
+    dx, pack = run_chunk(index, arrivals[2:], cot, dact, down, gain, late, packs[1:], groups)
+    last = to_previous(dx, "pipe")
+    partial = run_sum(0, packs, cot_all, [pack[0]], rank)
+    before, down_grad, up_grad = run_final(late, swapped(pack), cot_all, partial, first, last)
     return (before[None], down_grad[None], up_grad[None])
 
 

time: 69.4 us -> 74.3 us (1.071)
  the two profiles are of different devices: /device:TPU:17 before, /device:TPU:1 now
where the time goes in v7:
time: 74.3 us; the launch traced here: 73.8 us
  waiting for transfers between devices  47.7 us (64%)
  starting transfers between devices  18.1 us (24%)
  Pallas kernels  4.46 us (6%)
  local copies, waits for them, and re-layouts  2.27 us (3%)
  between operations  0.82 us (1%)
    ppermute x12, waiting for transfers between devices, exchanged(): lax.ppermute(x, axis, [(i, i ^ mask) for i in range(lax.axis_size(axis))])  47.7 us
    ppermute x12, starting transfers between devices, exchanged(): lax.ppermute(x, axis, [(i, i ^ mask) for i in range(lax.axis_size(axis))])  11.7 us
    ppermute x2, starting transfers between devices, to_previous(): lax.ppermute(x, axis, [(i, i - 1) for i in range(1, lax.axis_size(axis))])  6.39 us
    pallas_call x2, Pallas kernels, run_chunk(): pl.pallas_call(functools.partial(chunk_kernel, start, len(saved), groups)...  2.14 us
    slice x2, local copies, waits for them, and re-layouts, per_device(): arrivals = [held(stash[start:start + rows]) for start, rows in spans[:2]]  2.14 us
    pallas_call x1, Pallas kernels, run_final(): pl.pallas_call(functools.partial(final_kernel, start, groups), out_shape=...  1.58 us
  transfers between devices with their start and end apart: 14, of which 7 were waited for; matrix products, arithmetic and copies ran while one was open for 2% of the time, Pallas kernels for 4%

profile of v7, /device:TPU:1, one launch (start us, length us, event | category | flops | bytes accessed | tf_op | source)
XLA Modules:
  0.0 73.8 jit_solution(4868650721780247798)
XLA Ops:
  0.6 0.0 copy-start
  0.7 1.1 %slice_bitcast_fusion.1 = bf16[32,4096]{1,0:T(8,128)(2,1)S(1)} fusion(bf16[1,128,4096]{2,1,0:T(8,128)(2,1)} %param.5), kind=kLoop, calls=%fused_computation.7 | loop fusion | bytes 524288 | tf_op jit(solution)/shard_map/slice | solution.py:209
  1.8 3.2 %collective-permute-start = (bf16[32,4096]{1,0:T(8,128)(2,1)S(1)}, bf16[32,4096]{1,0:T(8,128)(2,1)S(1)}, u32[]{:S(2)}, u32[]{:S(2)}) collective-permute-start(bf16[32,4096]{1,0:T(8,128)(2,1)S(1)} %slice_bitcast_fusion.1), channel_id=1, source_target_pairs={{0,16},{4,20},{8,24},{12,28},{16,0},{20,4},{24,8},{28,12},{1,17},{... | collective-permute-start | bytes 786440 | tf_op jit(solution)/shard_map/ppermute | solution.py:20
  5.0 1.0 %slice_bitcast_fusion = bf16[48,4096]{1,0:T(8,128)(2,1)S(1)} fusion(bf16[1,128,4096]{2,1,0:T(8,128)(2,1)} %param.5), kind=kLoop, calls=%fused_computation.2 | loop fusion | bytes 786432 | tf_op jit(solution)/shard_map/slice | solution.py:209
  6.0 0.1 collective-permute-start.2
  6.1 0.0 copy-start.3
  6.1 0.1 dynamic-slice_bitcast_fusion
  6.2 1.3 %collective-permute-start.4 = (bf16[128,1024]{1,0:T(8,128)(2,1)S(1)}, bf16[128,1024]{1,0:T(8,128)(2,1)S(1)}, u32[]{:S(2)}, u32[]{:S(2)}) collective-permute-start(bf16[128,1024]{1,0:T(8,128)(2,1)S(1)} %get-tuple-element.34), channel_id=1, source_target_pairs={{0,2},{1,3},{2,0},{3,1},{4,6},{5,7},{6,4},{7,5},{8,10},{9,11},{10,... | collective-permute-start | bytes 786440 | tf_op jit(solution)/shard_map/ppermute | solution.py:20
  7.5 1.2 %collective-permute-start.3 = (bf16[128,1024]{1,0:T(8,128)(2,1)S(1)}, bf16[128,1024]{1,0:T(8,128)(2,1)S(1)}, u32[]{:S(2)}, u32[]{:S(2)}) collective-permute-start(bf16[128,1024]{1,0:T(8,128)(2,1)S(1)} %get-tuple-element.35), channel_id=1, source_target_pairs={{0,1},{1,0},{2,3},{3,2},{4,5},{5,4},{6,7},{7,6},{8,9},{9,8},{10,11... | collective-permute-start | bytes 786440 | tf_op jit(solution)/shard_map/ppermute | solution.py:20
  8.8 0.2 collective-permute-start.5
  9.0 16.1 %collective-permute-done.refs_0_.refs_1_ = bf16[32,4096]{1,0:T(8,128)(2,1)S(1)} collective-permute-done((bf16[32,4096]{1,0:T(8,128)(2,1)S(1)}, bf16[32,4096]{1,0:T(8,128)(2,1)S(1)}, u32[]{:S(2)}, u32[]{:S(2)}) %collective-permute-start) | collective-permute-done | bytes 262176 | tf_op jit(solution)/shard_map/ppermute | solution.py:20
  25.1 0.2 shard_map.76.refs_5_
  25.3 0.1 collective-permute-start.1
  25.4 0.4 fusion.dact_ref
  25.8 16.1 %collective-permute-done.2.refs_0_ = bf16[48,4096]{1,0:T(8,128)(2,1)S(1)} collective-permute-done((bf16[48,4096]{1,0:T(8,128)(2,1)S(1)}, bf16[48,4096]{1,0:T(8,128)(2,1)S(1)}, u32[]{:S(2)}, u32[]{:S(2)}) %collective-permute-start.2) | collective-permute-done | bytes 393248 | tf_op jit(solution)/shard_map/ppermute | solution.py:20
  41.9 1.2 %shard_map.77 = (bf16[80,4096]{1,0:T(8,128)(2,1)S(1)}, bf16[80,1280]{1,0:T(8,128)(2,1)S(1)}, bf16[80,1280]{1,0:T(8,128)(2,1)S(1)}, bf16[80,1280]{1,0:T(8,128)(2,1)S(1)}, bf16[80,1280]{1,0:T(8,128)(2,1)S(1)}) custom-call(s32[1]{0:T(128)} %bitcast.me_ref, bf16[128,4096]{1,0:T(8,128)(2,1)S(1)} %bitcast.24, f32[128,128]{1,0:T(8,128)S(1)} %fusion.dact_ref, ...), custom_call_target="tpu_custom_call" | custom-call | tf_op jit(solution)/shard_map/pallas_call | solution.py:103
  43.1 4.0 %collective-permute-start.12 = (bf16[80,4096]{1,0:T(8,128)(2,1)S(1)}, bf16[80,4096]{1,0:T(8,128)(2,1)S(1)}, u32[]{:S(2)}, u32[]{:S(2)}) collective-permute-start(bf16[80,4096]{1,0:T(8,128)(2,1)S(1)} %get-tuple-element.28), channel_id=1, source_target_pairs={{4,0},{8,4},{12,8},{16,12},{20,16},{24,20},{28,24},{5,1},{9,5},{13... | collective-permute-start | bytes 1966088 | tf_op jit(solution)/shard_map/ppermute | solution.py:24
  47.0 1.6 %collective-permute-start.6 = (bf16[80,1280]{1,0:T(8,128)(2,1)S(1)}, bf16[80,1280]{1,0:T(8,128)(2,1)S(1)}, u32[]{:S(2)}, u32[]{:S(2)}) collective-permute-start(bf16[80,1280]{1,0:T(8,128)(2,1)S(1)} %get-tuple-element.18), channel_id=1, source_target_pairs={{0,1},{1,0},{2,3},{3,2},{4,5},{5,4},{6,7},{7,6},{8,9},{9,8},{10,11... | collective-permute-start | bytes 614408 | tf_op jit(solution)/shard_map/ppermute | solution.py:20
  48.7 1.2 %collective-permute-start.7 = (bf16[80,1280]{1,0:T(8,128)(2,1)S(1)}, bf16[80,1280]{1,0:T(8,128)(2,1)S(1)}, u32[]{:S(2)}, u32[]{:S(2)}) collective-permute-start(bf16[80,1280]{1,0:T(8,128)(2,1)S(1)} %get-tuple-element.19), channel_id=1, source_target_pairs={{0,2},{1,3},{2,0},{3,1},{4,6},{5,7},{6,4},{7,5},{8,10},{9,11},{10,... | collective-permute-start | bytes 614408 | tf_op jit(solution)/shard_map/ppermute | solution.py:20
  49.9 0.0 collective-permute-start.8
  50.0 4.4 %collective-permute-done.6.refs_1_ = bf16[80,1280]{1,0:T(8,128)(2,1)S(1)} collective-permute-done((bf16[80,1280]{1,0:T(8,128)(2,1)S(1)}, bf16[80,1280]{1,0:T(8,128)(2,1)S(1)}, u32[]{:S(2)}, u32[]{:S(2)}) %collective-permute-start.6) | collective-permute-done | bytes 204832 | tf_op jit(solution)/shard_map/ppermute | solution.py:20
  54.3 5.7 %collective-permute-done.7.refs_2_ = bf16[80,1280]{1,0:T(8,128)(2,1)S(1)} collective-permute-done((bf16[80,1280]{1,0:T(8,128)(2,1)S(1)}, bf16[80,1280]{1,0:T(8,128)(2,1)S(1)}, u32[]{:S(2)}, u32[]{:S(2)}) %collective-permute-start.7) | collective-permute-done | bytes 204832 | tf_op jit(solution)/shard_map/ppermute | solution.py:20
  60.1 1.0 %shard_map.78 = (bf16[48,4096]{1,0:T(8,128)(2,1)S(1)}, bf16[48,1280]{1,0:T(8,128)(2,1)S(1)}, bf16[48,1280]{1,0:T(8,128)(2,1)S(1)}, bf16[48,1280]{1,0:T(8,128)(2,1)S(1)}, bf16[48,1280]{1,0:T(8,128)(2,1)S(1)}) custom-call(s32[1]{0:T(128)} %bitcast.me_ref, bf16[128,4096]{1,0:T(8,128)(2,1)S(1)} %bitcast.25, f32[128,128]{1,0:T(8,128)S(1)} %fusion.dact_ref, ...), custom_call_target="tpu_custom_call" | custom-call | tf_op jit(solution)/shard_map/pallas_call | solution.py:103
  61.0 2.4 %collective-permute-start.13 = (bf16[48,4096]{1,0:T(8,128)(2,1)S(1)}, bf16[48,4096]{1,0:T(8,128)(2,1)S(1)}, u32[]{:S(2)}, u32[]{:S(2)}) collective-permute-start(bf16[48,4096]{1,0:T(8,128)(2,1)S(1)} %get-tuple-element.29), channel_id=1, source_target_pairs={{4,0},{8,4},{12,8},{16,12},{20,16},{24,20},{28,24},{5,1},{9,5},{13... | collective-permute-start | bytes 1179656 | tf_op jit(solution)/shard_map/ppermute | solution.py:24
  63.5 0.7 collective-permute-start.9
  64.2 0.8 %collective-permute-start.10 = (bf16[48,1280]{1,0:T(8,128)(2,1)S(1)}, bf16[48,1280]{1,0:T(8,128)(2,1)S(1)}, u32[]{:S(2)}, u32[]{:S(2)}) collective-permute-start(bf16[48,1280]{1,0:T(8,128)(2,1)S(1)} %get-tuple-element.23), channel_id=1, source_target_pairs={{0,2},{1,3},{2,0},{3,1},{4,6},{5,7},{6,4},{7,5},{8,10},{9,11},{10,... | collective-permute-start | bytes 368648 | tf_op jit(solution)/shard_map/ppermute | solution.py:20
  65.0 1.2 %collective-permute-start.11 = (bf16[48,1280]{1,0:T(8,128)(2,1)S(1)}, bf16[48,1280]{1,0:T(8,128)(2,1)S(1)}, u32[]{:S(2)}, u32[]{:S(2)}) collective-permute-start(bf16[48,1280]{1,0:T(8,128)(2,1)S(1)} %get-tuple-element.24), channel_id=1, source_target_pairs={{0,3},{1,2},{2,1},{3,0},{4,7},{5,6},{6,5},{7,4},{8,11},{9,10},{10,... | collective-permute-start | bytes 368648 | tf_op jit(solution)/shard_map/ppermute | solution.py:20
  66.2 0.5 shard_map.79
  66.8 2.1 %collective-permute-done.9.refs_1_ = bf16[48,1280]{1,0:T(8,128)(2,1)S(1)} collective-permute-done((bf16[48,1280]{1,0:T(8,128)(2,1)S(1)}, bf16[48,1280]{1,0:T(8,128)(2,1)S(1)}, u32[]{:S(2)}, u32[]{:S(2)}) %collective-permute-start.9) | collective-permute-done | bytes 122912 | tf_op jit(solution)/shard_map/ppermute | solution.py:20
  68.9 0.5 collective-permute-done.10.refs_2_
  69.4 2.8 %collective-permute-done.11.refs_3_ = bf16[48,1280]{1,0:T(8,128)(2,1)S(1)} collective-permute-done((bf16[48,1280]{1,0:T(8,128)(2,1)S(1)}, bf16[48,1280]{1,0:T(8,128)(2,1)S(1)}, u32[]{:S(2)}, u32[]{:S(2)}) %collective-permute-start.11) | collective-permute-done | bytes 122912 | tf_op jit(solution)/shard_map/ppermute | solution.py:20
  72.2 1.6 %shard_map.80 = (bf16[128,4096]{1,0:T(8,128)(2,1)}, f32[1024,128]{1,0:T(8,128)}, f32[128,1024]{1,0:T(8,128)}) custom-call(bf16[48,1280]{1,0:T(8,128)(2,1)S(1)} %get-tuple-element.21.refs_8_.refs_0_, bf16[48,1280]{1,0:T(8,128)(2,1)S(1)} %collective-permute-done.9.refs_1_, bf16[48,1280]{1,0:T(8,128)(2,1)S(1)} %collective-permute-done.10.refs_2_, ...), custom_call_target="tpu_custom_call" | custom-call | tf_op jit(solution)/shard_map/pallas_call | solution.py:180
  (15 shorter events, 0.0 us)
Async XLA Ops:
  0.6 24.7 %copy-start = (bf16[1,128,4096]{2,1,0:T(8,128)(2,1)S(1)}, bf16[1,128,4096]{2,1,0:T(8,128)(2,1)}, u32[]{:S(2)}) copy-start(bf16[1,128,4096]{2,1,0:T(8,128)(2,1)} %param.8) | copy-start | bytes 3145732
  0.6 5.5 %copy-start.1 = (bf16[1,128,4096]{2,1,0:T(8,128)(2,1)S(1)}, bf16[1,128,4096]{2,1,0:T(8,128)(2,1)}, u32[]{:S(2)}) copy-start(bf16[1,128,4096]{2,1,0:T(8,128)(2,1)} %param.6) | copy-start | bytes 3145732
  1.8 23.3 %collective-permute-start = (bf16[32,4096]{1,0:T(8,128)(2,1)S(1)}, bf16[32,4096]{1,0:T(8,128)(2,1)S(1)}, u32[]{:S(2)}, u32[]{:S(2)}) collective-permute-start(bf16[32,4096]{1,0:T(8,128)(2,1)S(1)} %slice_bitcast_fusion.1), channel_id=1, source_target_pairs={{0,16},{4,20},{8,24},{12,28},{16,0},{20,4},{24,8},{28,12},{1,17},{... | collective-permute-start | bytes 786440 | tf_op jit(solution)/shard_map/ppermute | solution.py:20
  6.0 35.9 %collective-permute-start.2 = (bf16[48,4096]{1,0:T(8,128)(2,1)S(1)}, bf16[48,4096]{1,0:T(8,128)(2,1)S(1)}, u32[]{:S(2)}, u32[]{:S(2)}) collective-permute-start(bf16[48,4096]{1,0:T(8,128)(2,1)S(1)} %slice_bitcast_fusion), channel_id=1, source_target_pairs={{0,16},{4,20},{8,24},{12,28},{16,0},{20,4},{24,8},{28,12},{1,17},{... | collective-permute-start | bytes 1179656 | tf_op jit(solution)/shard_map/ppermute | solution.py:20
  6.1 18.9 %copy-start.3 = (bf16[1,128,4096]{2,1,0:T(8,128)(2,1)S(1)}, bf16[1,128,4096]{2,1,0:T(8,128)(2,1)}, u32[]{:S(2)}) copy-start(bf16[1,128,4096]{2,1,0:T(8,128)(2,1)} %param.5) | copy-start | bytes 3145732
  6.2 19.6 %collective-permute-start.4 = (bf16[128,1024]{1,0:T(8,128)(2,1)S(1)}, bf16[128,1024]{1,0:T(8,128)(2,1)S(1)}, u32[]{:S(2)}, u32[]{:S(2)}) collective-permute-start(bf16[128,1024]{1,0:T(8,128)(2,1)S(1)} %get-tuple-element.34), channel_id=1, source_target_pairs={{0,2},{1,3},{2,0},{3,1},{4,6},{5,7},{6,4},{7,5},{8,10},{9,11},{10,... | collective-permute-start | bytes 786440 | tf_op jit(solution)/shard_map/ppermute | solution.py:20
  7.5 18.3 %collective-permute-start.3 = (bf16[128,1024]{1,0:T(8,128)(2,1)S(1)}, bf16[128,1024]{1,0:T(8,128)(2,1)S(1)}, u32[]{:S(2)}, u32[]{:S(2)}) collective-permute-start(bf16[128,1024]{1,0:T(8,128)(2,1)S(1)} %get-tuple-element.35), channel_id=1, source_target_pairs={{0,1},{1,0},{2,3},{3,2},{4,5},{5,4},{6,7},{7,6},{8,9},{9,8},{10,11... | collective-permute-start | bytes 786440 | tf_op jit(solution)/shard_map/ppermute | solution.py:20
  8.8 17.1 %collective-permute-start.5 = (bf16[128,1024]{1,0:T(8,128)(2,1)S(1)}, bf16[128,1024]{1,0:T(8,128)(2,1)S(1)}, u32[]{:S(2)}, u32[]{:S(2)}) collective-permute-start(bf16[128,1024]{1,0:T(8,128)(2,1)S(1)} %get-tuple-element.36), channel_id=1, source_target_pairs={{0,3},{1,2},{2,1},{3,0},{4,7},{5,6},{6,5},{7,4},{8,11},{9,10},{10,... | collective-permute-start | bytes 786440 | tf_op jit(solution)/shard_map/ppermute | solution.py:20
  25.3 16.7 %copy-start.2 = (bf16[1,4096,128]{2,1,0:T(8,128)(2,1)S(1)}, bf16[1,4096,128]{2,1,0:T(8,128)(2,1)}, u32[]{:S(2)}) copy-start(bf16[1,4096,128]{2,1,0:T(8,128)(2,1)} %param.7) | copy-start | bytes 3145732
  25.3 34.8 %collective-permute-start.1 = (bf16[48,4096]{1,0:T(8,128)(2,1)S(1)}, bf16[48,4096]{1,0:T(8,128)(2,1)S(1)}, u32[]{:S(2)}, u32[]{:S(2)}) collective-permute-start(bf16[48,4096]{1,0:T(8,128)(2,1)S(1)} %shard_map.76.refs_5_), channel_id=1, source_target_pairs={{0,16},{4,20},{8,24},{12,28},{16,0},{20,4},{24,8},{28,12},{1,17},{... | collective-permute-start | bytes 1179656 | tf_op jit(solution)/shard_map/ppermute | solution.py:20
  25.4 16.6 %copy-start.4 = (f32[1,4096]{1,0:T(1,128)S(1)}, f32[1,4096]{1,0:T(1,128)}, u32[]{:S(2)}) copy-start(f32[1,4096]{1,0:T(1,128)} %gain_ref.3) | copy-start | bytes 49156
  43.1 29.1 %collective-permute-start.12 = (bf16[80,4096]{1,0:T(8,128)(2,1)S(1)}, bf16[80,4096]{1,0:T(8,128)(2,1)S(1)}, u32[]{:S(2)}, u32[]{:S(2)}) collective-permute-start(bf16[80,4096]{1,0:T(8,128)(2,1)S(1)} %get-tuple-element.28), channel_id=1, source_target_pairs={{4,0},{8,4},{12,8},{16,12},{20,16},{24,20},{28,24},{5,1},{9,5},{13... | collective-permute-start | bytes 1966088 | tf_op jit(solution)/shard_map/ppermute | solution.py:24
  47.0 7.3 %collective-permute-start.6 = (bf16[80,1280]{1,0:T(8,128)(2,1)S(1)}, bf16[80,1280]{1,0:T(8,128)(2,1)S(1)}, u32[]{:S(2)}, u32[]{:S(2)}) collective-permute-start(bf16[80,1280]{1,0:T(8,128)(2,1)S(1)} %get-tuple-element.18), channel_id=1, source_target_pairs={{0,1},{1,0},{2,3},{3,2},{4,5},{5,4},{6,7},{7,6},{8,9},{9,8},{10,11... | collective-permute-start | bytes 614408 | tf_op jit(solution)/shard_map/ppermute | solution.py:20
  48.7 11.4 %collective-permute-start.7 = (bf16[80,1280]{1,0:T(8,128)(2,1)S(1)}, bf16[80,1280]{1,0:T(8,128)(2,1)S(1)}, u32[]{:S(2)}, u32[]{:S(2)}) collective-permute-start(bf16[80,1280]{1,0:T(8,128)(2,1)S(1)} %get-tuple-element.19), channel_id=1, source_target_pairs={{0,2},{1,3},{2,0},{3,1},{4,6},{5,7},{6,4},{7,5},{8,10},{9,11},{10,... | collective-permute-start | bytes 614408 | tf_op jit(solution)/shard_map/ppermute | solution.py:20
  49.9 10.1 %collective-permute-start.8 = (bf16[80,1280]{1,0:T(8,128)(2,1)S(1)}, bf16[80,1280]{1,0:T(8,128)(2,1)S(1)}, u32[]{:S(2)}, u32[]{:S(2)}) collective-permute-start(bf16[80,1280]{1,0:T(8,128)(2,1)S(1)} %get-tuple-element.20), channel_id=1, source_target_pairs={{0,3},{1,2},{2,1},{3,0},{4,7},{5,6},{6,5},{7,4},{8,11},{9,10},{10,... | collective-permute-start | bytes 614408 | tf_op jit(solution)/shard_map/ppermute | solution.py:20
  61.0 11.1 %collective-permute-start.13 = (bf16[48,4096]{1,0:T(8,128)(2,1)S(1)}, bf16[48,4096]{1,0:T(8,128)(2,1)S(1)}, u32[]{:S(2)}, u32[]{:S(2)}) collective-permute-start(bf16[48,4096]{1,0:T(8,128)(2,1)S(1)} %get-tuple-element.29), channel_id=1, source_target_pairs={{4,0},{8,4},{12,8},{16,12},{20,16},{24,20},{28,24},{5,1},{9,5},{13... | collective-permute-start | bytes 1179656 | tf_op jit(solution)/shard_map/ppermute | solution.py:24
  63.5 5.4 %collective-permute-start.9 = (bf16[48,1280]{1,0:T(8,128)(2,1)S(1)}, bf16[48,1280]{1,0:T(8,128)(2,1)S(1)}, u32[]{:S(2)}, u32[]{:S(2)}) collective-permute-start(bf16[48,1280]{1,0:T(8,128)(2,1)S(1)} %get-tuple-element.22), channel_id=1, source_target_pairs={{0,1},{1,0},{2,3},{3,2},{4,5},{5,4},{6,7},{7,6},{8,9},{9,8},{10,11... | collective-permute-start | bytes 368648 | tf_op jit(solution)/shard_map/ppermute | solution.py:20
  64.2 5.2 %collective-permute-start.10 = (bf16[48,1280]{1,0:T(8,128)(2,1)S(1)}, bf16[48,1280]{1,0:T(8,128)(2,1)S(1)}, u32[]{:S(2)}, u32[]{:S(2)}) collective-permute-start(bf16[48,1280]{1,0:T(8,128)(2,1)S(1)} %get-tuple-element.23), channel_id=1, source_target_pairs={{0,2},{1,3},{2,0},{3,1},{4,6},{5,7},{6,4},{7,5},{8,10},{9,11},{10,... | collective-permute-start | bytes 368648 | tf_op jit(solution)/shard_map/ppermute | solution.py:20
  65.0 7.1 %collective-permute-start.11 = (bf16[48,1280]{1,0:T(8,128)(2,1)S(1)}, bf16[48,1280]{1,0:T(8,128)(2,1)S(1)}, u32[]{:S(2)}, u32[]{:S(2)}) collective-permute-start(bf16[48,1280]{1,0:T(8,128)(2,1)S(1)} %get-tuple-element.24), channel_id=1, source_target_pairs={{0,3},{1,2},{2,1},{3,0},{4,7},{5,6},{6,5},{7,4},{8,11},{9,10},{10,... | collective-permute-start | bytes 368648 | tf_op jit(solution)/shard_map/ppermute | solution.py:20

commit v8 on v6

--- a/solution.py
+++ b/solution.py
@@ -7,12 +7,14 @@
 from jax.experimental.pallas import tpu as pltpu
 from jax.sharding import PartitionSpec as P
 
-SHARES = (1, 2, 2, 3)
+SHARES = (3, 2, 3)
 LANES = 512
 VMEM = pl.BlockSpec(memory_space=pltpu.VMEM)
 SMEM = pl.BlockSpec(memory_space=pltpu.SMEM)
 ANY = pl.BlockSpec(memory_space=pl.ANY)
 PARAMS = pltpu.CompilerParams(vmem_limit_bytes=16 * 1024 * 1024)
+SUMCOST = pl.CostEstimate(flops=30 * 10**8, bytes_accessed=10**6, transcendentals=0)
+COSTS = [pl.CostEstimate(flops=f, bytes_accessed=1, transcendentals=0) for f in (0 * 10**8, 0 * 10**8, 80 * 10**8)]
 SMALL = pltpu.CompilerParams(vmem_limit_bytes=4 * 1024 * 1024)
 
 
@@ -96,7 +98,7 @@
         dx_ref[pl.ds(ahead, rows), at] = (held + (dnorm - xf * pull) * inverse).astype(jnp.bfloat16)
 
 
-def run_chunk(me, saved, cot, dact, down, gain, start, joins, waits, groups):
+def run_chunk(me, saved, cot, dact, down, gain, start, joins, waits, groups, cost):
     rows, features = saved.shape
     rank = down.shape[1]
     pack = jax.ShapeDtypeStruct((rows, features // groups + 2 * rank), jnp.bfloat16)
@@ -108,6 +110,7 @@
         in_specs=[SMEM] + [VMEM] * (5 + len(joins)) + [ANY] * len(waits),
         out_specs=[VMEM] * len(outs),
         scratch_shapes=[pltpu.VMEM((rows, features), jnp.bfloat16)],
+        cost_estimate=cost,
         compiler_params=PARAMS,
     )(me, saved, cot, dact, down, gain, *joins, *waits)
     return got[0], got[1:]
@@ -134,25 +137,40 @@
 
 def final_kernel(groups, spans, *refs):
     packs, cots = refs[:groups], refs[groups : 2 * groups]
-    old_down, old_up, first, last = refs[2 * groups : 2 * groups + 4]
-    before_ref, down_ref, up_ref, every, held, down, up, done = refs[2 * groups + 4 :]
+    old_down, old_up, first = refs[2 * groups : 2 * groups + 3]
+    before_ref, down_ref, up_ref, every, held, down, up, done = refs[2 * groups + 3 :]
     width, rank = down.shape
-    rows = first.shape[0]
     copies = [
-        pltpu.make_async_copy(first, before_ref.at[pl.ds(0, rows)], done.at[0]),
-        pltpu.make_async_copy(last, before_ref.at[pl.ds(rows, last.shape[0])], done.at[1]),
-        pltpu.make_async_copy(down, down_ref, done.at[2]),
-        pltpu.make_async_copy(up, up_ref, done.at[3]),
+        pltpu.make_async_copy(first, before_ref.at[pl.ds(0, first.shape[0])], done.at[0]),
+        pltpu.make_async_copy(down, down_ref, done.at[1]),
+        pltpu.make_async_copy(up, up_ref, done.at[2]),
     ]
     copies[0].start()
-    copies[1].start()
     gather_rows(groups, spans, packs, cots, every, held)
     down[...] = old_down[...] + rows_dot(every[:, :width], every[:, width : width + rank])
+    copies[1].start()
+    up[...] = old_up[...] + rows_dot(every[:, width + rank :], held[...])
     copies[2].start()
-    up[...] = old_up[...] + rows_dot(every[:, width + rank :], held[...])
-    copies[3].start()
     for copy in copies:
         copy.wait()
+
+
+def join_kernel(start, before_ref, last, out_ref, done):
+    copy = pltpu.make_async_copy(last, out_ref.at[pl.ds(start, last.shape[0])], done)
+    copy.start()
+    copy.wait()
+
+
+def run_join(before, last):
+    return pl.pallas_call(
+        functools.partial(join_kernel, before.shape[0] - last.shape[0]),
+        out_shape=jax.ShapeDtypeStruct(before.shape, before.dtype),
+        in_specs=[ANY, VMEM],
+        out_specs=ANY,
+        scratch_shapes=[pltpu.SemaphoreType.DMA],
+        input_output_aliases={0: 0},
+        compiler_params=SMALL,
+    )(before, last)
 
 
 def operands(packs, cots, spans):
@@ -182,28 +200,23 @@
     )(*args, *waits)
 
 
-def run_final(packs, cots, spans, partial, first, last):
+def run_final(packs, cots, spans, partial, first, tokens):
     groups, width, args, scratch = operands(packs, cots, spans)
-    down, up = partial
-    args += [down, up, first, last]
-    before = jax.ShapeDtypeStruct((first.shape[0] + last.shape[0], first.shape[1]), jnp.bfloat16)
+    down, up = [jax.ShapeDtypeStruct(value.shape, jnp.float32) for value in partial]
     scratch += [
         pltpu.VMEM(down.shape, jnp.float32),
         pltpu.VMEM(up.shape, jnp.float32),
-        pltpu.SemaphoreType.DMA((4,)),
+        pltpu.SemaphoreType.DMA((3,)),
     ]
     return pl.pallas_call(
         functools.partial(final_kernel, groups, spans),
-        out_shape=[
-            before,
-            jax.ShapeDtypeStruct(down.shape, jnp.float32),
-            jax.ShapeDtypeStruct(up.shape, jnp.float32),
-        ],
-        in_specs=[VMEM] * len(args),
+        out_shape=[jax.ShapeDtypeStruct((tokens, first.shape[1]), first.dtype), down, up],
+        in_specs=[VMEM] * (len(args) + 3),
         out_specs=[ANY] * 3,
         scratch_shapes=scratch,
         compiler_params=PARAMS,
-    )(*args)
+        cost_estimate=SUMCOST,
+    )(*args, *partial, first)
 
 
 def per_device(stash_held, grad_in, w_down, w_up, gain):
@@ -236,13 +249,16 @@
             arrivals.append(held(coming))
             waits = waits + [coming]
         joins = parts if i == chunks - 2 else []
-        dx, pack = run_chunk(index, arrivals[i], cot, dact, down, gain, start, joins, waits, groups)
+        dx, pack = run_chunk(index, arrivals[i], cot, dact, down, gain, start, joins, waits, groups, COSTS[i])
         packs.append([exchanged(pack[k], "dp", k) if k else pack[k] for k in range(groups)])
         parts.append(dx)
         waits = packs[-1][1:]
+    first, last = [to_previous(dx, "pipe") for dx in parts[-2:]]
     partial = run_sum(packs[:-1], cot_all, spans[:-1], [pack[0]], rank)
-    first, last = [to_previous(dx, "pipe") for dx in parts[-2:]]
-    before, down_grad, up_grad = run_final(packs[-1:], cot_all, spans[-1:], partial, first, last)
+    before, down_grad, up_grad = run_final(
+        packs[-1:], cot_all, spans[-1:], partial, first, tokens
+    )
+    before = run_join(before, last)
     return (before[None], down_grad[None], up_grad[None])
 
 

time: 68.6 us -> 65.8 us (0.959)
  starting transfers between devices: 31.6 us -> 28.8 us
  waiting for transfers between devices: 25.9 us -> 26.8 us
    ppermute x19 -> x15, starting transfers between devices: 19.2 us -> 14.4 us  [exchanged(): lax.ppermute(x, axis, [(i, i ^ mask) for i in range(lax.axis_size(axis))])]
    ppermute x2, waiting for transfers between devices: 0.01 us -> 2.66 us  [to_previous(): lax.ppermute(x, axis, [(i, i - 1) for i in range(1, lax.axis_size(axis))])]
    ppermute x2, starting transfers between devices: 12.4 us -> 14.5 us  [to_previous(): lax.ppermute(x, axis, [(i, i - 1) for i in range(1, lax.axis_size(axis))])]
    ppermute x19 -> x15, waiting for transfers between devices: 25.9 us -> 24.1 us  [exchanged(): lax.ppermute(x, axis, [(i, i ^ mask) for i in range(lax.axis_size(axis))])]
    dynamic_slice x1, local copies, waits for them, and re-layouts: 1.36 us -> 0.09 us  [per_device(): part = lax.dynamic_slice_in_dim(cot, (me ^ k) * width, width, axis=1)]
    pallas_call x0 -> x1, Pallas kernels: none -> 0.75 us  [run_join(): pl.pallas_call(functools.partial(join_kernel, before.shape[0] - last.shap...]
    pallas_call x4 -> x3, Pallas kernels: 3.41 us -> 2.74 us  [run_chunk(): pl.pallas_call(functools.partial(chunk_kernel, start, len(joins), len(wai...]
  transfers between devices with their start and end apart: 21 -> 17, of which waited for: 12 -> 6; matrix products, arithmetic and copies ran while one was open for 4% -> 2% of each run, Pallas kernels for 6% -> 7%
where the time goes in v8:
time: 65.8 us; the launch traced here: 65.5 us
  starting transfers between devices  28.8 us (44%)
  waiting for transfers between devices  26.8 us (41%)
  Pallas kernels  5.67 us (9%)
  local copies, waits for them, and re-layouts  2.9 us (4%)
  between operations  0.9 us (1%)
    ppermute x15, waiting for transfers between devices, exchanged(): lax.ppermute(x, axis, [(i, i ^ mask) for i in range(lax.axis_size(axis))])  24.1 us
    ppermute x2, starting transfers between devices, to_previous(): lax.ppermute(x, axis, [(i, i - 1) for i in range(1, lax.axis_size(axis))])  14.5 us
    ppermute x15, starting transfers between devices, exchanged(): lax.ppermute(x, axis, [(i, i ^ mask) for i in range(lax.axis_size(axis))])  14.4 us
    pallas_call x3, Pallas kernels, run_chunk(): pl.pallas_call(functools.partial(chunk_kernel, start, len(joins), len(wai...  2.74 us
    ppermute x2, waiting for transfers between devices, to_previous(): lax.ppermute(x, axis, [(i, i - 1) for i in range(1, lax.axis_size(axis))])  2.66 us
    slice x2, local copies, waits for them, and re-layouts, per_device(): arrivals = [held(stash[start:start + rows]) for start, rows in spans[:2]]  2.14 us
    pallas_call x1, Pallas kernels, run_final(): pl.pallas_call(functools.partial(final_kernel, groups, spans), out_shape=...  1.42 us
  transfers between devices with their start and end apart: 17, of which 6 were waited for; matrix products, arithmetic and copies ran while one was open for 2% of the time, Pallas kernels for 7%

profile of v8, /device:TPU:1, one launch (start us, length us, event | category | flops | bytes accessed | tf_op | source)
XLA Modules:
  0.0 65.5 jit_solution(9122397156936803884)
XLA Ops:
  0.7 1.2 %slice_bitcast_fusion = bf16[48,4096]{1,0:T(8,128)(2,1)S(1)} fusion(bf16[1,128,4096]{2,1,0:T(8,128)(2,1)} %param.5), kind=kLoop, calls=%fused_computation.2 | loop fusion | bytes 786432 | tf_op jit(solution)/shard_map/slice | solution.py:237
  1.8 3.2 %collective-permute-start = (bf16[48,4096]{1,0:T(8,128)(2,1)S(1)}, bf16[48,4096]{1,0:T(8,128)(2,1)S(1)}, u32[]{:S(2)}, u32[]{:S(2)}) collective-permute-start(bf16[48,4096]{1,0:T(8,128)(2,1)S(1)} %slice_bitcast_fusion), channel_id=1, source_target_pairs={{0,16},{4,20},{8,24},{12,28},{16,0},{20,4},{24,8},{28,12},{1,17},{... | collective-permute-start | bytes 1179656 | tf_op jit(solution)/shard_map/ppermute | solution.py:22
  5.0 1.0 %slice_bitcast_fusion.1 = bf16[32,4096]{1,0:T(8,128)(2,1)S(1)} fusion(bf16[1,128,4096]{2,1,0:T(8,128)(2,1)} %param.5), kind=kLoop, calls=%fused_computation.7 | loop fusion | bytes 524288 | tf_op jit(solution)/shard_map/slice | solution.py:237
  6.0 0.1 collective-permute-start.2
  6.1 0.1 dynamic-slice_bitcast_fusion
  6.2 1.3 %collective-permute-start.4 = (bf16[128,1024]{1,0:T(8,128)(2,1)S(1)}, bf16[128,1024]{1,0:T(8,128)(2,1)S(1)}, u32[]{:S(2)}, u32[]{:S(2)}) collective-permute-start(bf16[128,1024]{1,0:T(8,128)(2,1)S(1)} %get-tuple-element.44), channel_id=1, source_target_pairs={{0,2},{1,3},{2,0},{3,1},{4,6},{5,7},{6,4},{7,5},{8,10},{9,11},{10,... | collective-permute-start | bytes 786440 | tf_op jit(solution)/shard_map/ppermute | solution.py:22
  7.5 1.2 %collective-permute-start.3 = (bf16[128,1024]{1,0:T(8,128)(2,1)S(1)}, bf16[128,1024]{1,0:T(8,128)(2,1)S(1)}, u32[]{:S(2)}, u32[]{:S(2)}) collective-permute-start(bf16[128,1024]{1,0:T(8,128)(2,1)S(1)} %get-tuple-element.45), channel_id=1, source_target_pairs={{0,1},{1,0},{2,3},{3,2},{4,5},{5,4},{6,7},{7,6},{8,9},{9,8},{10,11... | collective-permute-start | bytes 786440 | tf_op jit(solution)/shard_map/ppermute | solution.py:22
  8.7 0.2 collective-permute-start.5
  8.9 19.0 %collective-permute-done.refs_0_.saved_ref = bf16[48,4096]{1,0:T(8,128)(2,1)S(1)} collective-permute-done((bf16[48,4096]{1,0:T(8,128)(2,1)S(1)}, bf16[48,4096]{1,0:T(8,128)(2,1)S(1)}, u32[]{:S(2)}, u32[]{:S(2)}) %collective-permute-start) | collective-permute-done | bytes 393248 | tf_op jit(solution)/shard_map/ppermute | solution.py:22
  27.9 0.2 shard_map.76.refs_3_
  28.2 0.4 fusion.dact_ref
  28.7 0.6 copy-done.2
  29.4 0.9 %shard_map.77 = (bf16[48,4096]{1,0:T(8,128)(2,1)S(1)}, bf16[48,1280]{1,0:T(8,128)(2,1)S(1)}, bf16[48,1280]{1,0:T(8,128)(2,1)S(1)}, bf16[48,1280]{1,0:T(8,128)(2,1)S(1)}, bf16[48,1280]{1,0:T(8,128)(2,1)S(1)}) custom-call(s32[1]{0:T(128)} %bitcast.me_ref, bf16[48,4096]{1,0:T(8,128)(2,1)S(1)} %collective-permute-done.refs_0_.saved_ref, ...), custom_call_target="tpu_custom_call" | custom-call | bytes 1 | tf_op jit(solution)/shard_map/pallas_call | solution.py:107
  30.3 1.0 %collective-permute-start.6 = (bf16[48,1280]{1,0:T(8,128)(2,1)S(1)}, bf16[48,1280]{1,0:T(8,128)(2,1)S(1)}, u32[]{:S(2)}, u32[]{:S(2)}) collective-permute-start(bf16[48,1280]{1,0:T(8,128)(2,1)S(1)} %get-tuple-element.24), channel_id=1, source_target_pairs={{0,1},{1,0},{2,3},{3,2},{4,5},{5,4},{6,7},{7,6},{8,9},{9,8},{10,11... | collective-permute-start | bytes 368648 | tf_op jit(solution)/shard_map/ppermute | solution.py:22
  31.3 1.2 %collective-permute-start.7 = (bf16[48,1280]{1,0:T(8,128)(2,1)S(1)}, bf16[48,1280]{1,0:T(8,128)(2,1)S(1)}, u32[]{:S(2)}, u32[]{:S(2)}) collective-permute-start(bf16[48,1280]{1,0:T(8,128)(2,1)S(1)} %get-tuple-element.25), channel_id=1, source_target_pairs={{0,2},{1,3},{2,0},{3,1},{4,6},{5,7},{6,4},{7,5},{8,10},{9,11},{10,... | collective-permute-start | bytes 368648 | tf_op jit(solution)/shard_map/ppermute | solution.py:22
  32.6 0.4 collective-permute-start.8
  33.0 0.5 collective-permute-done.2.saved_ref
  33.5 0.8 %collective-permute-done.6.refs_1_.refs_2_ = bf16[48,1280]{1,0:T(8,128)(2,1)S(1)} collective-permute-done((bf16[48,1280]{1,0:T(8,128)(2,1)S(1)}, bf16[48,1280]{1,0:T(8,128)(2,1)S(1)}, u32[]{:S(2)}, u32[]{:S(2)}) %collective-permute-start.6) | collective-permute-done | bytes 122912 | tf_op jit(solution)/shard_map/ppermute | solution.py:22
  34.4 1.0 %collective-permute-done.7.refs_2_.refs_4_ = bf16[48,1280]{1,0:T(8,128)(2,1)S(1)} collective-permute-done((bf16[48,1280]{1,0:T(8,128)(2,1)S(1)}, bf16[48,1280]{1,0:T(8,128)(2,1)S(1)}, u32[]{:S(2)}, u32[]{:S(2)}) %collective-permute-start.7) | collective-permute-done | bytes 122912 | tf_op jit(solution)/shard_map/ppermute | solution.py:22
  35.3 2.8 %collective-permute-done.8.refs_3_.refs_6_ = bf16[48,1280]{1,0:T(8,128)(2,1)S(1)} collective-permute-done((bf16[48,1280]{1,0:T(8,128)(2,1)S(1)}, bf16[48,1280]{1,0:T(8,128)(2,1)S(1)}, u32[]{:S(2)}, u32[]{:S(2)}) %collective-permute-start.8) | collective-permute-done | bytes 122912 | tf_op jit(solution)/shard_map/ppermute | solution.py:22
  38.1 0.9 %shard_map.78 = (bf16[80,4096]{1,0:T(8,128)(2,1)S(1)}, bf16[32,1280]{1,0:T(8,128)(2,1)S(1)}, bf16[32,1280]{1,0:T(8,128)(2,1)S(1)}, bf16[32,1280]{1,0:T(8,128)(2,1)S(1)}, bf16[32,1280]{1,0:T(8,128)(2,1)S(1)}) custom-call(s32[1]{0:T(128)} %bitcast.me_ref, bf16[32,4096]{1,0:T(8,128)(2,1)S(1)} %collective-permute-done.2.saved_ref, ...), custom_call_target="tpu_custom_call" | custom-call | bytes 1 | tf_op jit(solution)/shard_map/pallas_call | solution.py:107
  39.1 0.7 %collective-permute-start.10 = (bf16[32,1280]{1,0:T(8,128)(2,1)S(1)}, bf16[32,1280]{1,0:T(8,128)(2,1)S(1)}, u32[]{:S(2)}, u32[]{:S(2)}) collective-permute-start(bf16[32,1280]{1,0:T(8,128)(2,1)S(1)} %get-tuple-element.28), channel_id=1, source_target_pairs={{0,2},{1,3},{2,0},{3,1},{4,6},{5,7},{6,4},{7,5},{8,10},{9,11},{10,... | collective-permute-start | bytes 245768 | tf_op jit(solution)/shard_map/ppermute | solution.py:22
  39.8 1.9 %collective-permute-start.11 = (bf16[32,1280]{1,0:T(8,128)(2,1)S(1)}, bf16[32,1280]{1,0:T(8,128)(2,1)S(1)}, u32[]{:S(2)}, u32[]{:S(2)}) collective-permute-start(bf16[32,1280]{1,0:T(8,128)(2,1)S(1)} %get-tuple-element.29), channel_id=1, source_target_pairs={{0,3},{1,2},{2,1},{3,0},{4,7},{5,6},{6,5},{7,4},{8,11},{9,10},{10,... | collective-permute-start | bytes 245768 | tf_op jit(solution)/shard_map/ppermute | solution.py:22
  41.7 8.6 %collective-permute-start.15 = (bf16[80,4096]{1,0:T(8,128)(2,1)S(1)}, bf16[80,4096]{1,0:T(8,128)(2,1)S(1)}, u32[]{:S(2)}, u32[]{:S(2)}) collective-permute-start(bf16[80,4096]{1,0:T(8,128)(2,1)S(1)} %get-tuple-element.38), channel_id=1, source_target_pairs={{4,0},{8,4},{12,8},{16,12},{20,16},{24,20},{28,24},{5,1},{9,5},{13... | collective-permute-start | bytes 1966088 | tf_op jit(solution)/shard_map/ppermute | solution.py:26
  50.4 0.9 %shard_map.79 = (bf16[48,4096]{1,0:T(8,128)(2,1)S(1)}, bf16[48,1280]{1,0:T(8,128)(2,1)S(1)}, bf16[48,1280]{1,0:T(8,128)(2,1)S(1)}, bf16[48,1280]{1,0:T(8,128)(2,1)S(1)}, bf16[48,1280]{1,0:T(8,128)(2,1)S(1)}) custom-call(s32[1]{0:T(128)} %bitcast.me_ref, bf16[48,4096]{1,0:T(8,128)(2,1)S(1)} %collective-permute-done.1.saved_ref, ...), custom_call_target="tpu_custom_call" | custom-call | flops 8000000000 | bytes 1 | tf_op jit(solution)/shard_map/pallas_call | solution.py:107
  51.4 1.6 %collective-permute-start.12 = (bf16[48,1280]{1,0:T(8,128)(2,1)S(1)}, bf16[48,1280]{1,0:T(8,128)(2,1)S(1)}, u32[]{:S(2)}, u32[]{:S(2)}) collective-permute-start(bf16[48,1280]{1,0:T(8,128)(2,1)S(1)} %get-tuple-element.31), channel_id=1, source_target_pairs={{0,1},{1,0},{2,3},{3,2},{4,5},{5,4},{6,7},{7,6},{8,9},{9,8},{10,11... | collective-permute-start | bytes 368648 | tf_op jit(solution)/shard_map/ppermute | solution.py:22
  53.0 1.2 %collective-permute-start.13 = (bf16[48,1280]{1,0:T(8,128)(2,1)S(1)}, bf16[48,1280]{1,0:T(8,128)(2,1)S(1)}, u32[]{:S(2)}, u32[]{:S(2)}) collective-permute-start(bf16[48,1280]{1,0:T(8,128)(2,1)S(1)} %get-tuple-element.32), channel_id=1, source_target_pairs={{0,2},{1,3},{2,0},{3,1},{4,6},{5,7},{6,4},{7,5},{8,10},{9,11},{10,... | collective-permute-start | bytes 368648 | tf_op jit(solution)/shard_map/ppermute | solution.py:22
  54.3 5.8 %collective-permute-start.16 = (bf16[48,4096]{1,0:T(8,128)(2,1)S(1)}, bf16[48,4096]{1,0:T(8,128)(2,1)S(1)}, u32[]{:S(2)}, u32[]{:S(2)}) collective-permute-start(bf16[48,4096]{1,0:T(8,128)(2,1)S(1)} %get-tuple-element.40), channel_id=1, source_target_pairs={{4,0},{8,4},{12,8},{16,12},{20,16},{24,20},{28,24},{5,1},{9,5},{13... | collective-permute-start | bytes 1179656 | tf_op jit(solution)/shard_map/ppermute | solution.py:26
  60.1 0.6 shard_map.80
  60.7 1.4 %shard_map.81 = (bf16[128,4096]{1,0:T(8,128)(2,1)}, f32[1024,128]{1,0:T(8,128)}, f32[128,1024]{1,0:T(8,128)}) custom-call(bf16[48,1280]{1,0:T(8,128)(2,1)S(1)} %get-tuple-element.30.refs_12_.refs_0_, bf16[48,1280]{1,0:T(8,128)(2,1)S(1)} %collective-permute-done.12.refs_1_, bf16[48,1280]{1,0:T(8,128)(2,1)S(1)} %collective-permute-done.13.refs_2_, ...), custom_call_target="tpu_custom_call" | custom-call | flops 3000000000 | bytes 1000000 | tf_op jit(solution)/shard_map/pallas_call | solution.py:211
  62.1 2.7 %collective-permute-done.16.last = bf16[48,4096]{1,0:T(8,128)(2,1)S(1)} collective-permute-done((bf16[48,4096]{1,0:T(8,128)(2,1)S(1)}, bf16[48,4096]{1,0:T(8,128)(2,1)S(1)}, u32[]{:S(2)}, u32[]{:S(2)}) %collective-permute-start.16) | collective-permute-done | bytes 393248 | tf_op jit(solution)/shard_map/ppermute | solution.py:26
  64.8 0.8 %shard_map.82 = bf16[128,4096]{1,0:T(8,128)(2,1)} custom-call(bf16[128,4096]{1,0:T(8,128)(2,1)} %get-tuple-element.39.before_ref, bf16[48,4096]{1,0:T(8,128)(2,1)S(1)} %collective-permute-done.16.last), custom_call_target="tpu_custom_call", output_to_operand_aliasing={{}: (0, {})} | custom-call | tf_op jit(solution)/shard_map/pallas_call | solution.py:165
  (23 shorter events, 0.2 us)
Async XLA Ops:
  0.6 27.6 %copy-start = (bf16[1,128,4096]{2,1,0:T(8,128)(2,1)S(1)}, bf16[1,128,4096]{2,1,0:T(8,128)(2,1)}, u32[]{:S(2)}) copy-start(bf16[1,128,4096]{2,1,0:T(8,128)(2,1)} %param.8) | copy-start | bytes 3145732
  0.6 5.5 %copy-start.1 = (bf16[1,128,4096]{2,1,0:T(8,128)(2,1)S(1)}, bf16[1,128,4096]{2,1,0:T(8,128)(2,1)}, u32[]{:S(2)}) copy-start(bf16[1,128,4096]{2,1,0:T(8,128)(2,1)} %param.6) | copy-start | bytes 3145732
  1.8 26.1 %collective-permute-start = (bf16[48,4096]{1,0:T(8,128)(2,1)S(1)}, bf16[48,4096]{1,0:T(8,128)(2,1)S(1)}, u32[]{:S(2)}, u32[]{:S(2)}) collective-permute-start(bf16[48,4096]{1,0:T(8,128)(2,1)S(1)} %slice_bitcast_fusion), channel_id=1, source_target_pairs={{0,16},{4,20},{8,24},{12,28},{16,0},{20,4},{24,8},{28,12},{1,17},{... | collective-permute-start | bytes 1179656 | tf_op jit(solution)/shard_map/ppermute | solution.py:22
  6.0 27.5 %collective-permute-start.2 = (bf16[32,4096]{1,0:T(8,128)(2,1)S(1)}, bf16[32,4096]{1,0:T(8,128)(2,1)S(1)}, u32[]{:S(2)}, u32[]{:S(2)}) collective-permute-start(bf16[32,4096]{1,0:T(8,128)(2,1)S(1)} %slice_bitcast_fusion.1), channel_id=1, source_target_pairs={{0,16},{4,20},{8,24},{12,28},{16,0},{20,4},{24,8},{28,12},{1,17},{... | collective-permute-start | bytes 786440 | tf_op jit(solution)/shard_map/ppermute | solution.py:22
  6.1 21.8 %copy-start.3 = (bf16[1,128,4096]{2,1,0:T(8,128)(2,1)S(1)}, bf16[1,128,4096]{2,1,0:T(8,128)(2,1)}, u32[]{:S(2)}) copy-start(bf16[1,128,4096]{2,1,0:T(8,128)(2,1)} %param.5) | copy-start | bytes 3145732
  6.2 22.4 %collective-permute-start.4 = (bf16[128,1024]{1,0:T(8,128)(2,1)S(1)}, bf16[128,1024]{1,0:T(8,128)(2,1)S(1)}, u32[]{:S(2)}, u32[]{:S(2)}) collective-permute-start(bf16[128,1024]{1,0:T(8,128)(2,1)S(1)} %get-tuple-element.44), channel_id=1, source_target_pairs={{0,2},{1,3},{2,0},{3,1},{4,6},{5,7},{6,4},{7,5},{8,10},{9,11},{10,... | collective-permute-start | bytes 786440 | tf_op jit(solution)/shard_map/ppermute | solution.py:22
  7.5 21.2 %collective-permute-start.3 = (bf16[128,1024]{1,0:T(8,128)(2,1)S(1)}, bf16[128,1024]{1,0:T(8,128)(2,1)S(1)}, u32[]{:S(2)}, u32[]{:S(2)}) collective-permute-start(bf16[128,1024]{1,0:T(8,128)(2,1)S(1)} %get-tuple-element.45), channel_id=1, source_target_pairs={{0,1},{1,0},{2,3},{3,2},{4,5},{5,4},{6,7},{7,6},{8,9},{9,8},{10,11... | collective-permute-start | bytes 786440 | tf_op jit(solution)/shard_map/ppermute | solution.py:22
  8.7 19.9 %collective-permute-start.5 = (bf16[128,1024]{1,0:T(8,128)(2,1)S(1)}, bf16[128,1024]{1,0:T(8,128)(2,1)S(1)}, u32[]{:S(2)}, u32[]{:S(2)}) collective-permute-start(bf16[128,1024]{1,0:T(8,128)(2,1)S(1)} %get-tuple-element.46), channel_id=1, source_target_pairs={{0,3},{1,2},{2,1},{3,0},{4,7},{5,6},{6,5},{7,4},{8,11},{9,10},{10,... | collective-permute-start | bytes 786440 | tf_op jit(solution)/shard_map/ppermute | solution.py:22
  28.1 1.2 %copy-start.2 = (bf16[1,4096,128]{2,1,0:T(8,128)(2,1)S(1)}, bf16[1,4096,128]{2,1,0:T(8,128)(2,1)}, u32[]{:S(2)}) copy-start(bf16[1,4096,128]{2,1,0:T(8,128)(2,1)} %param.7) | copy-start | bytes 3145732
  28.1 22.3 %collective-permute-start.1 = (bf16[48,4096]{1,0:T(8,128)(2,1)S(1)}, bf16[48,4096]{1,0:T(8,128)(2,1)S(1)}, u32[]{:S(2)}, u32[]{:S(2)}) collective-permute-start(bf16[48,4096]{1,0:T(8,128)(2,1)S(1)} %shard_map.76.refs_3_), channel_id=1, source_target_pairs={{0,16},{4,20},{8,24},{12,28},{16,0},{20,4},{24,8},{28,12},{1,17},{... | collective-permute-start | bytes 1179656 | tf_op jit(solution)/shard_map/ppermute | solution.py:22
  28.2 1.1 %copy-start.4 = (f32[1,4096]{1,0:T(1,128)S(1)}, f32[1,4096]{1,0:T(1,128)}, u32[]{:S(2)}) copy-start(f32[1,4096]{1,0:T(1,128)} %gain_ref.5) | copy-start | bytes 49156
  30.3 4.1 %collective-permute-start.6 = (bf16[48,1280]{1,0:T(8,128)(2,1)S(1)}, bf16[48,1280]{1,0:T(8,128)(2,1)S(1)}, u32[]{:S(2)}, u32[]{:S(2)}) collective-permute-start(bf16[48,1280]{1,0:T(8,128)(2,1)S(1)} %get-tuple-element.24), channel_id=1, source_target_pairs={{0,1},{1,0},{2,3},{3,2},{4,5},{5,4},{6,7},{7,6},{8,9},{9,8},{10,11... | collective-permute-start | bytes 368648 | tf_op jit(solution)/shard_map/ppermute | solution.py:22
  31.3 4.0 %collective-permute-start.7 = (bf16[48,1280]{1,0:T(8,128)(2,1)S(1)}, bf16[48,1280]{1,0:T(8,128)(2,1)S(1)}, u32[]{:S(2)}, u32[]{:S(2)}) collective-permute-start(bf16[48,1280]{1,0:T(8,128)(2,1)S(1)} %get-tuple-element.25), channel_id=1, source_target_pairs={{0,2},{1,3},{2,0},{3,1},{4,6},{5,7},{6,4},{7,5},{8,10},{9,11},{10,... | collective-permute-start | bytes 368648 | tf_op jit(solution)/shard_map/ppermute | solution.py:22
  32.6 5.6 %collective-permute-start.8 = (bf16[48,1280]{1,0:T(8,128)(2,1)S(1)}, bf16[48,1280]{1,0:T(8,128)(2,1)S(1)}, u32[]{:S(2)}, u32[]{:S(2)}) collective-permute-start(bf16[48,1280]{1,0:T(8,128)(2,1)S(1)} %get-tuple-element.26), channel_id=1, source_target_pairs={{0,3},{1,2},{2,1},{3,0},{4,7},{5,6},{6,5},{7,4},{8,11},{9,10},{10,... | collective-permute-start | bytes 368648 | tf_op jit(solution)/shard_map/ppermute | solution.py:22
  39.0 11.4 %collective-permute-start.9 = (bf16[32,1280]{1,0:T(8,128)(2,1)S(1)}, bf16[32,1280]{1,0:T(8,128)(2,1)S(1)}, u32[]{:S(2)}, u32[]{:S(2)}) collective-permute-start(bf16[32,1280]{1,0:T(8,128)(2,1)S(1)} %get-tuple-element.27), channel_id=1, source_target_pairs={{0,1},{1,0},{2,3},{3,2},{4,5},{5,4},{6,7},{7,6},{8,9},{9,8},{10,11... | collective-permute-start | bytes 245768 | tf_op jit(solution)/shard_map/ppermute | solution.py:22
  39.1 11.3 %collective-permute-start.10 = (bf16[32,1280]{1,0:T(8,128)(2,1)S(1)}, bf16[32,1280]{1,0:T(8,128)(2,1)S(1)}, u32[]{:S(2)}, u32[]{:S(2)}) collective-permute-start(bf16[32,1280]{1,0:T(8,128)(2,1)S(1)} %get-tuple-element.28), channel_id=1, source_target_pairs={{0,2},{1,3},{2,0},{3,1},{4,6},{5,7},{6,4},{7,5},{8,10},{9,11},{10,... | collective-permute-start | bytes 245768 | tf_op jit(solution)/shard_map/ppermute | solution.py:22
  39.8 10.6 %collective-permute-start.11 = (bf16[32,1280]{1,0:T(8,128)(2,1)S(1)}, bf16[32,1280]{1,0:T(8,128)(2,1)S(1)}, u32[]{:S(2)}, u32[]{:S(2)}) collective-permute-start(bf16[32,1280]{1,0:T(8,128)(2,1)S(1)} %get-tuple-element.29), channel_id=1, source_target_pairs={{0,3},{1,2},{2,1},{3,0},{4,7},{5,6},{6,5},{7,4},{8,11},{9,10},{10,... | collective-permute-start | bytes 245768 | tf_op jit(solution)/shard_map/ppermute | solution.py:22
  41.7 19.0 %collective-permute-start.15 = (bf16[80,4096]{1,0:T(8,128)(2,1)S(1)}, bf16[80,4096]{1,0:T(8,128)(2,1)S(1)}, u32[]{:S(2)}, u32[]{:S(2)}) collective-permute-start(bf16[80,4096]{1,0:T(8,128)(2,1)S(1)} %get-tuple-element.38), channel_id=1, source_target_pairs={{4,0},{8,4},{12,8},{16,12},{20,16},{24,20},{28,24},{5,1},{9,5},{13... | collective-permute-start | bytes 1966088 | tf_op jit(solution)/shard_map/ppermute | solution.py:26
  51.4 9.3 %collective-permute-start.12 = (bf16[48,1280]{1,0:T(8,128)(2,1)S(1)}, bf16[48,1280]{1,0:T(8,128)(2,1)S(1)}, u32[]{:S(2)}, u32[]{:S(2)}) collective-permute-start(bf16[48,1280]{1,0:T(8,128)(2,1)S(1)} %get-tuple-element.31), channel_id=1, source_target_pairs={{0,1},{1,0},{2,3},{3,2},{4,5},{5,4},{6,7},{7,6},{8,9},{9,8},{10,11... | collective-permute-start | bytes 368648 | tf_op jit(solution)/shard_map/ppermute | solution.py:22
  53.0 7.7 %collective-permute-start.13 = (bf16[48,1280]{1,0:T(8,128)(2,1)S(1)}, bf16[48,1280]{1,0:T(8,128)(2,1)S(1)}, u32[]{:S(2)}, u32[]{:S(2)}) collective-permute-start(bf16[48,1280]{1,0:T(8,128)(2,1)S(1)} %get-tuple-element.32), channel_id=1, source_target_pairs={{0,2},{1,3},{2,0},{3,1},{4,6},{5,7},{6,4},{7,5},{8,10},{9,11},{10,... | collective-permute-start | bytes 368648 | tf_op jit(solution)/shard_map/ppermute | solution.py:22
  54.2 6.4 %collective-permute-start.14 = (bf16[48,1280]{1,0:T(8,128)(2,1)S(1)}, bf16[48,1280]{1,0:T(8,128)(2,1)S(1)}, u32[]{:S(2)}, u32[]{:S(2)}) collective-permute-start(bf16[48,1280]{1,0:T(8,128)(2,1)S(1)} %get-tuple-element.33), channel_id=1, source_target_pairs={{0,3},{1,2},{2,1},{3,0},{4,7},{5,6},{6,5},{7,4},{8,11},{9,10},{10,... | collective-permute-start | bytes 368648 | tf_op jit(solution)/shard_map/ppermute | solution.py:22
  54.3 10.5 %collective-permute-start.16 = (bf16[48,4096]{1,0:T(8,128)(2,1)S(1)}, bf16[48,4096]{1,0:T(8,128)(2,1)S(1)}, u32[]{:S(2)}, u32[]{:S(2)}) collective-permute-start(bf16[48,4096]{1,0:T(8,128)(2,1)S(1)} %get-tuple-element.40), channel_id=1, source_target_pairs={{4,0},{8,4},{12,8},{16,12},{20,16},{24,20},{28,24},{5,1},{9,5},{13... | collective-permute-start | bytes 1179656 | tf_op jit(solution)/shard_map/ppermute | solution.py:26

commit v9 on v8

--- a/solution.py
+++ b/solution.py
@@ -7,14 +7,14 @@
 from jax.experimental.pallas import tpu as pltpu
 from jax.sharding import PartitionSpec as P
 
-SHARES = (3, 2, 3)
+SHARES = (1, 3, 1, 3)
 LANES = 512
 VMEM = pl.BlockSpec(memory_space=pltpu.VMEM)
 SMEM = pl.BlockSpec(memory_space=pltpu.SMEM)
 ANY = pl.BlockSpec(memory_space=pl.ANY)
 PARAMS = pltpu.CompilerParams(vmem_limit_bytes=16 * 1024 * 1024)
 SUMCOST = pl.CostEstimate(flops=30 * 10**8, bytes_accessed=10**6, transcendentals=0)
-COSTS = [pl.CostEstimate(flops=f, bytes_accessed=1, transcendentals=0) for f in (0 * 10**8, 0 * 10**8, 80 * 10**8)]
+COSTS = [pl.CostEstimate(flops=f, bytes_accessed=1, transcendentals=0) for f in (0 * 10**8, 0 * 10**8, 60 * 10**8, 90 * 10**8)]
 SMALL = pltpu.CompilerParams(vmem_limit_bytes=4 * 1024 * 1024)
 
 

time: 65.8 us -> 64.7 us (0.983)
  waiting for transfers between devices: 26.8 us -> 18.8 us
  starting transfers between devices: 28.8 us -> 35.2 us
  Pallas kernels: 5.67 us -> 6.47 us
    ppermute x15 -> x19, waiting for transfers between devices: 24.1 us -> 16.2 us  [exchanged(): lax.ppermute(x, axis, [(i, i ^ mask) for i in range(lax.axis_size(axis))])]
    ppermute x15 -> x19, starting transfers between devices: 14.4 us -> 19.2 us  [exchanged(): lax.ppermute(x, axis, [(i, i ^ mask) for i in range(lax.axis_size(axis))])]
    ppermute x2, starting transfers between devices: 14.5 us -> 16 us  [to_previous(): lax.ppermute(x, axis, [(i, i - 1) for i in range(1, lax.axis_size(axis))])]
    pallas_call x3 -> x4, Pallas kernels: 2.74 us -> 3.38 us  [run_chunk(): pl.pallas_call(functools.partial(chunk_kernel, start, len(joins), len(wai...]
  transfers between devices with their start and end apart: 17 -> 21, of which waited for: 6 -> 7; matrix products, arithmetic and copies ran while one was open for 2% -> 2% of each run, Pallas kernels for 7% -> 9%
where the time goes in v9:
time: 64.7 us; the launch traced here: 64.4 us
  starting transfers between devices  35.2 us (54%)
  waiting for transfers between devices  18.8 us (29%)
  Pallas kernels  6.47 us (10%)
  local copies, waits for them, and re-layouts  2.69 us (4%)
  between operations  0.88 us (1%)
    ppermute x19, starting transfers between devices, exchanged(): lax.ppermute(x, axis, [(i, i ^ mask) for i in range(lax.axis_size(axis))])  19.2 us
    ppermute x19, waiting for transfers between devices, exchanged(): lax.ppermute(x, axis, [(i, i ^ mask) for i in range(lax.axis_size(axis))])  16.2 us
    ppermute x2, starting transfers between devices, to_previous(): lax.ppermute(x, axis, [(i, i - 1) for i in range(1, lax.axis_size(axis))])  16 us
    pallas_call x4, Pallas kernels, run_chunk(): pl.pallas_call(functools.partial(chunk_kernel, start, len(joins), len(wai...  3.38 us
    ppermute x2, waiting for transfers between devices, to_previous(): lax.ppermute(x, axis, [(i, i - 1) for i in range(1, lax.axis_size(axis))])  2.61 us
    slice x2, local copies, waits for them, and re-layouts, per_device(): arrivals = [held(stash[start:start + rows]) for start, rows in spans[:2]]  2.08 us
    pallas_call x1, Pallas kernels, run_final(): pl.pallas_call(functools.partial(final_kernel, groups, spans), out_shape=...  1.42 us
  transfers between devices with their start and end apart: 21, of which 7 were waited for; matrix products, arithmetic and copies ran while one was open for 2% of the time, Pallas kernels for 9%

profile of v9, /device:TPU:1, one launch (start us, length us, event | category | flops | bytes accessed | tf_op | source)
XLA Modules:
  0.0 64.4 jit_solution(7341294387755541431)
XLA Ops:
  0.7 1.1 %slice_bitcast_fusion.1 = bf16[16,4096]{1,0:T(8,128)(2,1)S(1)} fusion(bf16[1,128,4096]{2,1,0:T(8,128)(2,1)} %param.5), kind=kLoop, calls=%fused_computation.7 | loop fusion | bytes 262144 | tf_op jit(solution)/shard_map/slice | solution.py:237
  1.7 3.2 %collective-permute-start.1 = (bf16[16,4096]{1,0:T(8,128)(2,1)S(1)}, bf16[16,4096]{1,0:T(8,128)(2,1)S(1)}, u32[]{:S(2)}, u32[]{:S(2)}) collective-permute-start(bf16[16,4096]{1,0:T(8,128)(2,1)S(1)} %slice_bitcast_fusion.1), channel_id=1, source_target_pairs={{0,16},{4,20},{8,24},{12,28},{16,0},{20,4},{24,8},{28,12},{1,17},{... | collective-permute-start | bytes 393224 | tf_op jit(solution)/shard_map/ppermute | solution.py:22
  4.9 1.0 %slice_bitcast_fusion = bf16[48,4096]{1,0:T(8,128)(2,1)S(1)} fusion(bf16[1,128,4096]{2,1,0:T(8,128)(2,1)} %param.5), kind=kLoop, calls=%fused_computation.2 | loop fusion | bytes 786432 | tf_op jit(solution)/shard_map/slice | solution.py:237
  6.2 1.3 %collective-permute-start.3 = (bf16[128,1024]{1,0:T(8,128)(2,1)S(1)}, bf16[128,1024]{1,0:T(8,128)(2,1)S(1)}, u32[]{:S(2)}, u32[]{:S(2)}) collective-permute-start(bf16[128,1024]{1,0:T(8,128)(2,1)S(1)} %get-tuple-element.54), channel_id=1, source_target_pairs={{0,2},{1,3},{2,0},{3,1},{4,6},{5,7},{6,4},{7,5},{8,10},{9,11},{10,... | collective-permute-start | bytes 786440 | tf_op jit(solution)/shard_map/ppermute | solution.py:22
  7.5 1.2 %collective-permute-start.2 = (bf16[128,1024]{1,0:T(8,128)(2,1)S(1)}, bf16[128,1024]{1,0:T(8,128)(2,1)S(1)}, u32[]{:S(2)}, u32[]{:S(2)}) collective-permute-start(bf16[128,1024]{1,0:T(8,128)(2,1)S(1)} %get-tuple-element.55), channel_id=1, source_target_pairs={{0,1},{1,0},{2,3},{3,2},{4,5},{5,4},{6,7},{7,6},{8,9},{9,8},{10,11... | collective-permute-start | bytes 786440 | tf_op jit(solution)/shard_map/ppermute | solution.py:22
  9.3 10.1 %collective-permute-done.1.refs_0_.saved_ref = bf16[16,4096]{1,0:T(8,128)(2,1)S(1)} collective-permute-done((bf16[16,4096]{1,0:T(8,128)(2,1)S(1)}, bf16[16,4096]{1,0:T(8,128)(2,1)S(1)}, u32[]{:S(2)}, u32[]{:S(2)}) %collective-permute-start.1) | collective-permute-done | bytes 131104 | tf_op jit(solution)/shard_map/ppermute | solution.py:22
  19.6 0.5 copy-done.4
  20.1 0.7 %shard_map.77 = (bf16[16,4096]{1,0:T(8,128)(2,1)S(1)}, bf16[16,1280]{1,0:T(8,128)(2,1)S(1)}, bf16[16,1280]{1,0:T(8,128)(2,1)S(1)}, bf16[16,1280]{1,0:T(8,128)(2,1)S(1)}, bf16[16,1280]{1,0:T(8,128)(2,1)S(1)}) custom-call(s32[1]{0:T(128)} %bitcast.me_ref, bf16[16,4096]{1,0:T(8,128)(2,1)S(1)} %collective-permute-done.1.refs_0_.saved_ref, ...), custom_call_target="tpu_custom_call" | custom-call | bytes 1 | tf_op jit(solution)/shard_map/pallas_call | solution.py:107
  21.3 1.2 %collective-permute-start.6 = (bf16[16,1280]{1,0:T(8,128)(2,1)S(1)}, bf16[16,1280]{1,0:T(8,128)(2,1)S(1)}, u32[]{:S(2)}, u32[]{:S(2)}) collective-permute-start(bf16[16,1280]{1,0:T(8,128)(2,1)S(1)} %get-tuple-element.29), channel_id=1, source_target_pairs={{0,2},{1,3},{2,0},{3,1},{4,6},{5,7},{6,4},{7,5},{8,10},{9,11},{10,... | collective-permute-start | bytes 122888 | tf_op jit(solution)/shard_map/ppermute | solution.py:22
  22.6 1.0 %collective-permute-start.7 = (bf16[16,1280]{1,0:T(8,128)(2,1)S(1)}, bf16[16,1280]{1,0:T(8,128)(2,1)S(1)}, u32[]{:S(2)}, u32[]{:S(2)}) collective-permute-start(bf16[16,1280]{1,0:T(8,128)(2,1)S(1)} %get-tuple-element.30), channel_id=1, source_target_pairs={{0,3},{1,2},{2,1},{3,0},{4,7},{5,6},{6,5},{7,4},{8,11},{9,10},{10,... | collective-permute-start | bytes 122888 | tf_op jit(solution)/shard_map/ppermute | solution.py:22
  23.6 1.5 %collective-permute-start.9 = (bf16[16,4096]{1,0:T(8,128)(2,1)S(1)}, bf16[16,4096]{1,0:T(8,128)(2,1)S(1)}, u32[]{:S(2)}, u32[]{:S(2)}) collective-permute-start(bf16[16,4096]{1,0:T(8,128)(2,1)S(1)} %shard_map.76.refs_3_), channel_id=1, source_target_pairs={{0,16},{4,20},{8,24},{12,28},{16,0},{20,4},{24,8},{28,12},{1,17},{... | collective-permute-start | bytes 393224 | tf_op jit(solution)/shard_map/ppermute | solution.py:22
  25.1 1.5 %collective-permute-done.7.refs_3_.refs_2_.refs_9_ = bf16[16,1280]{1,0:T(8,128)(2,1)S(1)} collective-permute-done((bf16[16,1280]{1,0:T(8,128)(2,1)S(1)}, bf16[16,1280]{1,0:T(8,128)(2,1)S(1)}, u32[]{:S(2)}, u32[]{:S(2)}) %collective-permute-start.7) | collective-permute-done | bytes 40992 | tf_op jit(solution)/shard_map/ppermute | solution.py:22
  26.6 1.2 %collective-permute-done.refs_0_.saved_ref = bf16[48,4096]{1,0:T(8,128)(2,1)S(1)} collective-permute-done((bf16[48,4096]{1,0:T(8,128)(2,1)S(1)}, bf16[48,4096]{1,0:T(8,128)(2,1)S(1)}, u32[]{:S(2)}, u32[]{:S(2)}) %collective-permute-start) | collective-permute-done | bytes 393248 | tf_op jit(solution)/shard_map/ppermute | solution.py:22
  28.0 0.9 %shard_map.79 = (bf16[48,4096]{1,0:T(8,128)(2,1)S(1)}, bf16[48,1280]{1,0:T(8,128)(2,1)S(1)}, bf16[48,1280]{1,0:T(8,128)(2,1)S(1)}, bf16[48,1280]{1,0:T(8,128)(2,1)S(1)}, bf16[48,1280]{1,0:T(8,128)(2,1)S(1)}) custom-call(s32[1]{0:T(128)} %bitcast.me_ref, bf16[48,4096]{1,0:T(8,128)(2,1)S(1)} %collective-permute-done.refs_0_.saved_ref, ...), custom_call_target="tpu_custom_call" | custom-call | bytes 1 | tf_op jit(solution)/shard_map/pallas_call | solution.py:107
  29.0 1.0 %collective-permute-start.10 = (bf16[48,1280]{1,0:T(8,128)(2,1)S(1)}, bf16[48,1280]{1,0:T(8,128)(2,1)S(1)}, u32[]{:S(2)}, u32[]{:S(2)}) collective-permute-start(bf16[48,1280]{1,0:T(8,128)(2,1)S(1)} %get-tuple-element.33), channel_id=1, source_target_pairs={{0,1},{1,0},{2,3},{3,2},{4,5},{5,4},{6,7},{7,6},{8,9},{9,8},{10,11... | collective-permute-start | bytes 368648 | tf_op jit(solution)/shard_map/ppermute | solution.py:22
  30.0 1.2 %collective-permute-start.11 = (bf16[48,1280]{1,0:T(8,128)(2,1)S(1)}, bf16[48,1280]{1,0:T(8,128)(2,1)S(1)}, u32[]{:S(2)}, u32[]{:S(2)}) collective-permute-start(bf16[48,1280]{1,0:T(8,128)(2,1)S(1)} %get-tuple-element.34), channel_id=1, source_target_pairs={{0,2},{1,3},{2,0},{3,1},{4,6},{5,7},{6,4},{7,5},{8,10},{9,11},{10,... | collective-permute-start | bytes 368648 | tf_op jit(solution)/shard_map/ppermute | solution.py:22
  31.7 0.8 %collective-permute-start.8 = (bf16[48,4096]{1,0:T(8,128)(2,1)S(1)}, bf16[48,4096]{1,0:T(8,128)(2,1)S(1)}, u32[]{:S(2)}, u32[]{:S(2)}) collective-permute-start(bf16[48,4096]{1,0:T(8,128)(2,1)S(1)} %shard_map.78.refs_3_), channel_id=1, source_target_pairs={{0,16},{4,20},{8,24},{12,28},{16,0},{20,4},{24,8},{28,12},{1,17},{... | collective-permute-start | bytes 1179656 | tf_op jit(solution)/shard_map/ppermute | solution.py:22
  32.5 0.9 %collective-permute-done.9.saved_ref = bf16[16,4096]{1,0:T(8,128)(2,1)S(1)} collective-permute-done((bf16[16,4096]{1,0:T(8,128)(2,1)S(1)}, bf16[16,4096]{1,0:T(8,128)(2,1)S(1)}, u32[]{:S(2)}, u32[]{:S(2)}) %collective-permute-start.9) | collective-permute-done | bytes 131104 | tf_op jit(solution)/shard_map/ppermute | solution.py:22
  33.4 0.6 collective-permute-done.11.refs_3_.refs_7_
  34.0 1.8 %collective-permute-done.12.refs_4_.refs_10_ = bf16[48,1280]{1,0:T(8,128)(2,1)S(1)} collective-permute-done((bf16[48,1280]{1,0:T(8,128)(2,1)S(1)}, bf16[48,1280]{1,0:T(8,128)(2,1)S(1)}, u32[]{:S(2)}, u32[]{:S(2)}) %collective-permute-start.12) | collective-permute-done | bytes 122912 | tf_op jit(solution)/shard_map/ppermute | solution.py:22
  35.9 0.8 %shard_map.80 = (bf16[80,4096]{1,0:T(8,128)(2,1)S(1)}, bf16[16,1280]{1,0:T(8,128)(2,1)S(1)}, bf16[16,1280]{1,0:T(8,128)(2,1)S(1)}, bf16[16,1280]{1,0:T(8,128)(2,1)S(1)}, bf16[16,1280]{1,0:T(8,128)(2,1)S(1)}) custom-call(s32[1]{0:T(128)} %bitcast.me_ref, bf16[16,4096]{1,0:T(8,128)(2,1)S(1)} %collective-permute-done.9.saved_ref, ...), custom_call_target="tpu_custom_call" | custom-call | flops 6000000000 | bytes 1 | tf_op jit(solution)/shard_map/pallas_call | solution.py:107
  36.9 0.6 collective-permute-start.14
  37.6 1.7 %collective-permute-start.15 = (bf16[16,1280]{1,0:T(8,128)(2,1)S(1)}, bf16[16,1280]{1,0:T(8,128)(2,1)S(1)}, u32[]{:S(2)}, u32[]{:S(2)}) collective-permute-start(bf16[16,1280]{1,0:T(8,128)(2,1)S(1)} %get-tuple-element.38), channel_id=1, source_target_pairs={{0,3},{1,2},{2,1},{3,0},{4,7},{5,6},{6,5},{7,4},{8,11},{9,10},{10,... | collective-permute-start | bytes 122888 | tf_op jit(solution)/shard_map/ppermute | solution.py:22
  39.3 10.2 %collective-permute-start.19 = (bf16[80,4096]{1,0:T(8,128)(2,1)S(1)}, bf16[80,4096]{1,0:T(8,128)(2,1)S(1)}, u32[]{:S(2)}, u32[]{:S(2)}) collective-permute-start(bf16[80,4096]{1,0:T(8,128)(2,1)S(1)} %get-tuple-element.48), channel_id=1, source_target_pairs={{4,0},{8,4},{12,8},{16,12},{20,16},{24,20},{28,24},{5,1},{9,5},{13... | collective-permute-start | bytes 1966088 | tf_op jit(solution)/shard_map/ppermute | solution.py:26
  49.6 0.9 %shard_map.81 = (bf16[48,4096]{1,0:T(8,128)(2,1)S(1)}, bf16[48,1280]{1,0:T(8,128)(2,1)S(1)}, bf16[48,1280]{1,0:T(8,128)(2,1)S(1)}, bf16[48,1280]{1,0:T(8,128)(2,1)S(1)}, bf16[48,1280]{1,0:T(8,128)(2,1)S(1)}) custom-call(s32[1]{0:T(128)} %bitcast.me_ref, bf16[48,4096]{1,0:T(8,128)(2,1)S(1)} %collective-permute-done.8.saved_ref, ...), custom_call_target="tpu_custom_call" | custom-call | flops 8999999488 | bytes 1 | tf_op jit(solution)/shard_map/pallas_call | solution.py:107
  51.0 0.9 %collective-permute-start.17 = (bf16[48,1280]{1,0:T(8,128)(2,1)S(1)}, bf16[48,1280]{1,0:T(8,128)(2,1)S(1)}, u32[]{:S(2)}, u32[]{:S(2)}) collective-permute-start(bf16[48,1280]{1,0:T(8,128)(2,1)S(1)} %get-tuple-element.41), channel_id=1, source_target_pairs={{0,2},{1,3},{2,0},{3,1},{4,6},{5,7},{6,4},{7,5},{8,10},{9,11},{10,... | collective-permute-start | bytes 368648 | tf_op jit(solution)/shard_map/ppermute | solution.py:22
  51.9 1.4 %collective-permute-start.18 = (bf16[48,1280]{1,0:T(8,128)(2,1)S(1)}, bf16[48,1280]{1,0:T(8,128)(2,1)S(1)}, u32[]{:S(2)}, u32[]{:S(2)}) collective-permute-start(bf16[48,1280]{1,0:T(8,128)(2,1)S(1)} %get-tuple-element.42), channel_id=1, source_target_pairs={{0,3},{1,2},{2,1},{3,0},{4,7},{5,6},{6,5},{7,4},{8,11},{9,10},{10,... | collective-permute-start | bytes 368648 | tf_op jit(solution)/shard_map/ppermute | solution.py:22
  53.3 5.8 %collective-permute-start.20 = (bf16[48,4096]{1,0:T(8,128)(2,1)S(1)}, bf16[48,4096]{1,0:T(8,128)(2,1)S(1)}, u32[]{:S(2)}, u32[]{:S(2)}) collective-permute-start(bf16[48,4096]{1,0:T(8,128)(2,1)S(1)} %get-tuple-element.50), channel_id=1, source_target_pairs={{4,0},{8,4},{12,8},{16,12},{20,16},{24,20},{28,24},{5,1},{9,5},{13... | collective-permute-start | bytes 1179656 | tf_op jit(solution)/shard_map/ppermute | solution.py:26
  59.0 0.6 shard_map.82
  59.6 1.4 %shard_map.83 = (bf16[128,4096]{1,0:T(8,128)(2,1)}, f32[1024,128]{1,0:T(8,128)}, f32[128,1024]{1,0:T(8,128)}) custom-call(bf16[48,1280]{1,0:T(8,128)(2,1)S(1)} %get-tuple-element.39.refs_16_.refs_0_, bf16[48,1280]{1,0:T(8,128)(2,1)S(1)} %collective-permute-done.16.refs_1_, bf16[48,1280]{1,0:T(8,128)(2,1)S(1)} %collective-permute-done.17.refs_2_, ...), custom_call_target="tpu_custom_call" | custom-call | flops 3000000000 | bytes 1000000 | tf_op jit(solution)/shard_map/pallas_call | solution.py:211
  61.1 2.6 %collective-permute-done.20.last = bf16[48,4096]{1,0:T(8,128)(2,1)S(1)} collective-permute-done((bf16[48,4096]{1,0:T(8,128)(2,1)S(1)}, bf16[48,4096]{1,0:T(8,128)(2,1)S(1)}, u32[]{:S(2)}, u32[]{:S(2)}) %collective-permute-start.20) | collective-permute-done | bytes 393248 | tf_op jit(solution)/shard_map/ppermute | solution.py:26
  63.7 0.8 %shard_map.84 = bf16[128,4096]{1,0:T(8,128)(2,1)} custom-call(bf16[128,4096]{1,0:T(8,128)(2,1)} %get-tuple-element.49.before_ref, bf16[48,4096]{1,0:T(8,128)(2,1)S(1)} %collective-permute-done.20.last), custom_call_target="tpu_custom_call", output_to_operand_aliasing={{}: (0, {})} | custom-call | tf_op jit(solution)/shard_map/pallas_call | solution.py:165
  (33 shorter events, 2.9 us)
Async XLA Ops:
  0.6 8.2 %copy-start = (bf16[1,128,4096]{2,1,0:T(8,128)(2,1)S(1)}, bf16[1,128,4096]{2,1,0:T(8,128)(2,1)}, u32[]{:S(2)}) copy-start(bf16[1,128,4096]{2,1,0:T(8,128)(2,1)} %param.8) | copy-start | bytes 3145732
  0.6 5.4 %copy-start.1 = (bf16[1,128,4096]{2,1,0:T(8,128)(2,1)S(1)}, bf16[1,128,4096]{2,1,0:T(8,128)(2,1)}, u32[]{:S(2)}) copy-start(bf16[1,128,4096]{2,1,0:T(8,128)(2,1)} %param.6) | copy-start | bytes 3145732
  1.7 17.7 %collective-permute-start.1 = (bf16[16,4096]{1,0:T(8,128)(2,1)S(1)}, bf16[16,4096]{1,0:T(8,128)(2,1)S(1)}, u32[]{:S(2)}, u32[]{:S(2)}) collective-permute-start(bf16[16,4096]{1,0:T(8,128)(2,1)S(1)} %slice_bitcast_fusion.1), channel_id=1, source_target_pairs={{0,16},{4,20},{8,24},{12,28},{16,0},{20,4},{24,8},{28,12},{1,17},{... | collective-permute-start | bytes 393224 | tf_op jit(solution)/shard_map/ppermute | solution.py:22
  5.9 21.9 %collective-permute-start = (bf16[48,4096]{1,0:T(8,128)(2,1)S(1)}, bf16[48,4096]{1,0:T(8,128)(2,1)S(1)}, u32[]{:S(2)}, u32[]{:S(2)}) collective-permute-start(bf16[48,4096]{1,0:T(8,128)(2,1)S(1)} %slice_bitcast_fusion), channel_id=1, source_target_pairs={{0,16},{4,20},{8,24},{12,28},{16,0},{20,4},{24,8},{28,12},{1,17},{... | collective-permute-start | bytes 1179656 | tf_op jit(solution)/shard_map/ppermute | solution.py:22
  6.2 13.4 %collective-permute-start.3 = (bf16[128,1024]{1,0:T(8,128)(2,1)S(1)}, bf16[128,1024]{1,0:T(8,128)(2,1)S(1)}, u32[]{:S(2)}, u32[]{:S(2)}) collective-permute-start(bf16[128,1024]{1,0:T(8,128)(2,1)S(1)} %get-tuple-element.54), channel_id=1, source_target_pairs={{0,2},{1,3},{2,0},{3,1},{4,6},{5,7},{6,4},{7,5},{8,10},{9,11},{10,... | collective-permute-start | bytes 786440 | tf_op jit(solution)/shard_map/ppermute | solution.py:22
  7.5 12.1 %collective-permute-start.2 = (bf16[128,1024]{1,0:T(8,128)(2,1)S(1)}, bf16[128,1024]{1,0:T(8,128)(2,1)S(1)}, u32[]{:S(2)}, u32[]{:S(2)}) collective-permute-start(bf16[128,1024]{1,0:T(8,128)(2,1)S(1)} %get-tuple-element.55), channel_id=1, source_target_pairs={{0,1},{1,0},{2,3},{3,2},{4,5},{5,4},{6,7},{7,6},{8,9},{9,8},{10,11... | collective-permute-start | bytes 786440 | tf_op jit(solution)/shard_map/ppermute | solution.py:22
  8.7 10.7 %copy-start.2 = (bf16[1,128,4096]{2,1,0:T(8,128)(2,1)S(1)}, bf16[1,128,4096]{2,1,0:T(8,128)(2,1)}, u32[]{:S(2)}) copy-start(bf16[1,128,4096]{2,1,0:T(8,128)(2,1)} %param.5) | copy-start | bytes 3145732
  8.7 10.9 %collective-permute-start.4 = (bf16[128,1024]{1,0:T(8,128)(2,1)S(1)}, bf16[128,1024]{1,0:T(8,128)(2,1)S(1)}, u32[]{:S(2)}, u32[]{:S(2)}) collective-permute-start(bf16[128,1024]{1,0:T(8,128)(2,1)S(1)} %get-tuple-element.56), channel_id=1, source_target_pairs={{0,3},{1,2},{2,1},{3,0},{4,7},{5,6},{6,5},{7,4},{8,11},{9,10},{10,... | collective-permute-start | bytes 786440 | tf_op jit(solution)/shard_map/ppermute | solution.py:22
  9.3 10.3 %copy-start.3 = (bf16[1,4096,128]{2,1,0:T(8,128)(2,1)S(1)}, bf16[1,4096,128]{2,1,0:T(8,128)(2,1)}, u32[]{:S(2)}) copy-start(bf16[1,4096,128]{2,1,0:T(8,128)(2,1)} %param.7) | copy-start | bytes 3145732
  19.4 0.7 %copy-start.4 = (f32[1,4096]{1,0:T(1,128)S(1)}, f32[1,4096]{1,0:T(1,128)}, u32[]{:S(2)}) copy-start(f32[1,4096]{1,0:T(1,128)} %gain_ref.7) | copy-start | bytes 49156
  20.8 4.2 %collective-permute-start.5 = (bf16[16,1280]{1,0:T(8,128)(2,1)S(1)}, bf16[16,1280]{1,0:T(8,128)(2,1)S(1)}, u32[]{:S(2)}, u32[]{:S(2)}) collective-permute-start(bf16[16,1280]{1,0:T(8,128)(2,1)S(1)} %get-tuple-element.28), channel_id=1, source_target_pairs={{0,1},{1,0},{2,3},{3,2},{4,5},{5,4},{6,7},{7,6},{8,9},{9,8},{10,11... | collective-permute-start | bytes 122888 | tf_op jit(solution)/shard_map/ppermute | solution.py:22
  21.3 3.8 %collective-permute-start.6 = (bf16[16,1280]{1,0:T(8,128)(2,1)S(1)}, bf16[16,1280]{1,0:T(8,128)(2,1)S(1)}, u32[]{:S(2)}, u32[]{:S(2)}) collective-permute-start(bf16[16,1280]{1,0:T(8,128)(2,1)S(1)} %get-tuple-element.29), channel_id=1, source_target_pairs={{0,2},{1,3},{2,0},{3,1},{4,6},{5,7},{6,4},{7,5},{8,10},{9,11},{10,... | collective-permute-start | bytes 122888 | tf_op jit(solution)/shard_map/ppermute | solution.py:22
  22.6 4.0 %collective-permute-start.7 = (bf16[16,1280]{1,0:T(8,128)(2,1)S(1)}, bf16[16,1280]{1,0:T(8,128)(2,1)S(1)}, u32[]{:S(2)}, u32[]{:S(2)}) collective-permute-start(bf16[16,1280]{1,0:T(8,128)(2,1)S(1)} %get-tuple-element.30), channel_id=1, source_target_pairs={{0,3},{1,2},{2,1},{3,0},{4,7},{5,6},{6,5},{7,4},{8,11},{9,10},{10,... | collective-permute-start | bytes 122888 | tf_op jit(solution)/shard_map/ppermute | solution.py:22
  23.6 9.9 %collective-permute-start.9 = (bf16[16,4096]{1,0:T(8,128)(2,1)S(1)}, bf16[16,4096]{1,0:T(8,128)(2,1)S(1)}, u32[]{:S(2)}, u32[]{:S(2)}) collective-permute-start(bf16[16,4096]{1,0:T(8,128)(2,1)S(1)} %shard_map.76.refs_3_), channel_id=1, source_target_pairs={{0,16},{4,20},{8,24},{12,28},{16,0},{20,4},{24,8},{28,12},{1,17},{... | collective-permute-start | bytes 393224 | tf_op jit(solution)/shard_map/ppermute | solution.py:22
  29.0 4.5 %collective-permute-start.10 = (bf16[48,1280]{1,0:T(8,128)(2,1)S(1)}, bf16[48,1280]{1,0:T(8,128)(2,1)S(1)}, u32[]{:S(2)}, u32[]{:S(2)}) collective-permute-start(bf16[48,1280]{1,0:T(8,128)(2,1)S(1)} %get-tuple-element.33), channel_id=1, source_target_pairs={{0,1},{1,0},{2,3},{3,2},{4,5},{5,4},{6,7},{7,6},{8,9},{9,8},{10,11... | collective-permute-start | bytes 368648 | tf_op jit(solution)/shard_map/ppermute | solution.py:22
  30.0 4.0 %collective-permute-start.11 = (bf16[48,1280]{1,0:T(8,128)(2,1)S(1)}, bf16[48,1280]{1,0:T(8,128)(2,1)S(1)}, u32[]{:S(2)}, u32[]{:S(2)}) collective-permute-start(bf16[48,1280]{1,0:T(8,128)(2,1)S(1)} %get-tuple-element.34), channel_id=1, source_target_pairs={{0,2},{1,3},{2,0},{3,1},{4,6},{5,7},{6,4},{7,5},{8,10},{9,11},{10,... | collective-permute-start | bytes 368648 | tf_op jit(solution)/shard_map/ppermute | solution.py:22
  31.2 4.6 %collective-permute-start.12 = (bf16[48,1280]{1,0:T(8,128)(2,1)S(1)}, bf16[48,1280]{1,0:T(8,128)(2,1)S(1)}, u32[]{:S(2)}, u32[]{:S(2)}) collective-permute-start(bf16[48,1280]{1,0:T(8,128)(2,1)S(1)} %get-tuple-element.35), channel_id=1, source_target_pairs={{0,3},{1,2},{2,1},{3,0},{4,7},{5,6},{6,5},{7,4},{8,11},{9,10},{10,... | collective-permute-start | bytes 368648 | tf_op jit(solution)/shard_map/ppermute | solution.py:22
  31.7 17.9 %collective-permute-start.8 = (bf16[48,4096]{1,0:T(8,128)(2,1)S(1)}, bf16[48,4096]{1,0:T(8,128)(2,1)S(1)}, u32[]{:S(2)}, u32[]{:S(2)}) collective-permute-start(bf16[48,4096]{1,0:T(8,128)(2,1)S(1)} %shard_map.78.refs_3_), channel_id=1, source_target_pairs={{0,16},{4,20},{8,24},{12,28},{16,0},{20,4},{24,8},{28,12},{1,17},{... | collective-permute-start | bytes 1179656 | tf_op jit(solution)/shard_map/ppermute | solution.py:22
  36.6 12.9 %collective-permute-start.13 = (bf16[16,1280]{1,0:T(8,128)(2,1)S(1)}, bf16[16,1280]{1,0:T(8,128)(2,1)S(1)}, u32[]{:S(2)}, u32[]{:S(2)}) collective-permute-start(bf16[16,1280]{1,0:T(8,128)(2,1)S(1)} %get-tuple-element.36), channel_id=1, source_target_pairs={{0,1},{1,0},{2,3},{3,2},{4,5},{5,4},{6,7},{7,6},{8,9},{9,8},{10,11... | collective-permute-start | bytes 122888 | tf_op jit(solution)/shard_map/ppermute | solution.py:22
  36.9 12.6 %collective-permute-start.14 = (bf16[16,1280]{1,0:T(8,128)(2,1)S(1)}, bf16[16,1280]{1,0:T(8,128)(2,1)S(1)}, u32[]{:S(2)}, u32[]{:S(2)}) collective-permute-start(bf16[16,1280]{1,0:T(8,128)(2,1)S(1)} %get-tuple-element.37), channel_id=1, source_target_pairs={{0,2},{1,3},{2,0},{3,1},{4,6},{5,7},{6,4},{7,5},{8,10},{9,11},{10,... | collective-permute-start | bytes 122888 | tf_op jit(solution)/shard_map/ppermute | solution.py:22
  37.6 12.0 %collective-permute-start.15 = (bf16[16,1280]{1,0:T(8,128)(2,1)S(1)}, bf16[16,1280]{1,0:T(8,128)(2,1)S(1)}, u32[]{:S(2)}, u32[]{:S(2)}) collective-permute-start(bf16[16,1280]{1,0:T(8,128)(2,1)S(1)} %get-tuple-element.38), channel_id=1, source_target_pairs={{0,3},{1,2},{2,1},{3,0},{4,7},{5,6},{6,5},{7,4},{8,11},{9,10},{10,... | collective-permute-start | bytes 122888 | tf_op jit(solution)/shard_map/ppermute | solution.py:22
  39.3 20.3 %collective-permute-start.19 = (bf16[80,4096]{1,0:T(8,128)(2,1)S(1)}, bf16[80,4096]{1,0:T(8,128)(2,1)S(1)}, u32[]{:S(2)}, u32[]{:S(2)}) collective-permute-start(bf16[80,4096]{1,0:T(8,128)(2,1)S(1)} %get-tuple-element.48), channel_id=1, source_target_pairs={{4,0},{8,4},{12,8},{16,12},{20,16},{24,20},{28,24},{5,1},{9,5},{13... | collective-permute-start | bytes 1966088 | tf_op jit(solution)/shard_map/ppermute | solution.py:26
  50.5 9.1 %collective-permute-start.16 = (bf16[48,1280]{1,0:T(8,128)(2,1)S(1)}, bf16[48,1280]{1,0:T(8,128)(2,1)S(1)}, u32[]{:S(2)}, u32[]{:S(2)}) collective-permute-start(bf16[48,1280]{1,0:T(8,128)(2,1)S(1)} %get-tuple-element.40), channel_id=1, source_target_pairs={{0,1},{1,0},{2,3},{3,2},{4,5},{5,4},{6,7},{7,6},{8,9},{9,8},{10,11... | collective-permute-start | bytes 368648 | tf_op jit(solution)/shard_map/ppermute | solution.py:22
  51.0 8.6 %collective-permute-start.17 = (bf16[48,1280]{1,0:T(8,128)(2,1)S(1)}, bf16[48,1280]{1,0:T(8,128)(2,1)S(1)}, u32[]{:S(2)}, u32[]{:S(2)}) collective-permute-start(bf16[48,1280]{1,0:T(8,128)(2,1)S(1)} %get-tuple-element.41), channel_id=1, source_target_pairs={{0,2},{1,3},{2,0},{3,1},{4,6},{5,7},{6,4},{7,5},{8,10},{9,11},{10,... | collective-permute-start | bytes 368648 | tf_op jit(solution)/shard_map/ppermute | solution.py:22
  51.9 7.7 %collective-permute-start.18 = (bf16[48,1280]{1,0:T(8,128)(2,1)S(1)}, bf16[48,1280]{1,0:T(8,128)(2,1)S(1)}, u32[]{:S(2)}, u32[]{:S(2)}) collective-permute-start(bf16[48,1280]{1,0:T(8,128)(2,1)S(1)} %get-tuple-element.42), channel_id=1, source_target_pairs={{0,3},{1,2},{2,1},{3,0},{4,7},{5,6},{6,5},{7,4},{8,11},{9,10},{10,... | collective-permute-start | bytes 368648 | tf_op jit(solution)/shard_map/ppermute | solution.py:22
  53.3 10.4 %collective-permute-start.20 = (bf16[48,4096]{1,0:T(8,128)(2,1)S(1)}, bf16[48,4096]{1,0:T(8,128)(2,1)S(1)}, u32[]{:S(2)}, u32[]{:S(2)}) collective-permute-start(bf16[48,4096]{1,0:T(8,128)(2,1)S(1)} %get-tuple-element.50), channel_id=1, source_target_pairs={{4,0},{8,4},{12,8},{16,12},{20,16},{24,20},{28,24},{5,1},{9,5},{13... | collective-permute-start | bytes 1179656 | tf_op jit(solution)/shard_map/ppermute | solution.py:26

commit v10 on v9

--- a/solution.py
+++ b/solution.py
@@ -131,6 +131,11 @@
     down_ref, up_ref, every, held = refs[-4:]
     width, rank = down_ref.shape
     gather_rows(groups, spans, packs, cots, every, held)
+    own = refs[count + groups]
+    rows = own.shape[0]
+    rest = pl.ds(every.shape[0] - rows, rows)
+    every[rest, :] = own[...]
+    held[rest, :] = cots[0][pl.ds(cots[0].shape[0] - rows, rows), :]
     down_ref[...] = rows_dot(every[:, :width], every[:, width : width + rank])
     up_ref[...] = rows_dot(every[:, width + rank :], held[...])
 
@@ -173,10 +178,10 @@
     )(before, last)
 
 
-def operands(packs, cots, spans):
+def operands(packs, cots, spans, more=0):
     groups = len(cots)
     width = cots[0].shape[1]
-    depth = groups * sum(rows for _, rows in spans)
+    depth = groups * sum(rows for _, rows in spans) + more
     args = [packs[j][k] for k in range(groups) for j in range(len(spans))] + list(cots)
     scratch = [
         pltpu.VMEM((depth, packs[0][0].shape[1]), jnp.bfloat16),
@@ -185,19 +190,19 @@
     return groups, width, args, scratch
 
 
-def run_sum(packs, cots, spans, waits, rank):
-    groups, width, args, scratch = operands(packs, cots, spans)
+def run_sum(packs, cots, spans, own, rank):
+    groups, width, args, scratch = operands(packs, cots, spans, own.shape[0])
     return pl.pallas_call(
         functools.partial(sum_kernel, groups, spans),
         out_shape=[
             jax.ShapeDtypeStruct((width, rank), jnp.float32),
             jax.ShapeDtypeStruct((rank, width), jnp.float32),
         ],
-        in_specs=[VMEM] * len(args) + [ANY] * len(waits),
+        in_specs=[VMEM] * (len(args) + 1),
         out_specs=[VMEM] * 2,
         scratch_shapes=scratch,
         compiler_params=PARAMS,
-    )(*args, *waits)
+    )(*args, own)
 
 
 def run_final(packs, cots, spans, partial, first, tokens):
@@ -245,7 +250,7 @@
     parts, packs, waits = [], [], cot_all[1:]
     for i, (start, rows) in enumerate(spans):
         if i + 2 < chunks:
-            coming = rows_after(stash, *spans[i + 2], [arrivals[i]] + waits * (i > 0))
+            coming = rows_after(stash, *spans[i + 2], [arrivals[i]] + waits[:1] * (i > 0))
             arrivals.append(held(coming))
             waits = waits + [coming]
         joins = parts if i == chunks - 2 else []
@@ -254,9 +259,9 @@
         parts.append(dx)
         waits = packs[-1][1:]
     first, last = [to_previous(dx, "pipe") for dx in parts[-2:]]
-    partial = run_sum(packs[:-1], cot_all, spans[:-1], [pack[0]], rank)
+    partial = run_sum(packs[:-1], cot_all, spans[:-1], pack[0], rank)
     before, down_grad, up_grad = run_final(
-        packs[-1:], cot_all, spans[-1:], partial, first, tokens
+        [packs[-1][1:]], cot_all[1:], spans[-1:], partial, first, tokens
     )
     before = run_join(before, last)
     return (before[None], down_grad[None], up_grad[None])

time: 64.7 us -> 64.7 us (level)
  transfers between devices with their start and end apart: 21 -> 21, of which waited for: 7 -> 6; matrix products, arithmetic and copies ran while one was open for 2% -> 2% of each run, Pallas kernels for 9% -> 9%
where the time goes in v10:
time: 64.7 us; the launch traced here: 64.4 us
  starting transfers between devices  34.9 us (54%)
  waiting for transfers between devices  19 us (29%)
  Pallas kernels  6.53 us (10%)
  local copies, waits for them, and re-layouts  2.69 us (4%)
  between operations  0.9 us (1%)
    ppermute x19, starting transfers between devices, exchanged(): lax.ppermute(x, axis, [(i, i ^ mask) for i in range(lax.axis_size(axis))])  18.9 us
    ppermute x19, waiting for transfers between devices, exchanged(): lax.ppermute(x, axis, [(i, i ^ mask) for i in range(lax.axis_size(axis))])  16.4 us
    ppermute x2, starting transfers between devices, to_previous(): lax.ppermute(x, axis, [(i, i - 1) for i in range(1, lax.axis_size(axis))])  16 us
    pallas_call x4, Pallas kernels, run_chunk(): pl.pallas_call(functools.partial(chunk_kernel, start, len(joins), len(wai...  3.39 us
    ppermute x2, waiting for transfers between devices, to_previous(): lax.ppermute(x, axis, [(i, i - 1) for i in range(1, lax.axis_size(axis))])  2.53 us
    slice x2, local copies, waits for them, and re-layouts, per_device(): arrivals = [held(stash[start:start + rows]) for start, rows in spans[:2]]  2.08 us
    pallas_call x1, Pallas kernels, run_final(): pl.pallas_call(functools.partial(final_kernel, groups, spans), out_shape=...  1.47 us
  transfers between devices with their start and end apart: 21, of which 6 were waited for; matrix products, arithmetic and copies ran while one was open for 2% of the time, Pallas kernels for 9%

profile of v10, /device:TPU:1, one launch (start us, length us, event | category | flops | bytes accessed | tf_op | source)
XLA Modules:
  0.0 64.4 jit_solution(14329824727950688790)
XLA Ops:
  0.7 1.1 %slice_bitcast_fusion.1 = bf16[16,4096]{1,0:T(8,128)(2,1)S(1)} fusion(bf16[1,128,4096]{2,1,0:T(8,128)(2,1)} %param.5), kind=kLoop, calls=%fused_computation.7 | loop fusion | bytes 262144 | tf_op jit(solution)/shard_map/slice | solution.py:242
  1.7 3.2 %collective-permute-start.1 = (bf16[16,4096]{1,0:T(8,128)(2,1)S(1)}, bf16[16,4096]{1,0:T(8,128)(2,1)S(1)}, u32[]{:S(2)}, u32[]{:S(2)}) collective-permute-start(bf16[16,4096]{1,0:T(8,128)(2,1)S(1)} %slice_bitcast_fusion.1), channel_id=1, source_target_pairs={{0,16},{4,20},{8,24},{12,28},{16,0},{20,4},{24,8},{28,12},{1,17},{... | collective-permute-start | bytes 393224 | tf_op jit(solution)/shard_map/ppermute | solution.py:22
  4.9 1.0 %slice_bitcast_fusion = bf16[48,4096]{1,0:T(8,128)(2,1)S(1)} fusion(bf16[1,128,4096]{2,1,0:T(8,128)(2,1)} %param.5), kind=kLoop, calls=%fused_computation.2 | loop fusion | bytes 786432 | tf_op jit(solution)/shard_map/slice | solution.py:242
  6.2 1.3 %collective-permute-start.3 = (bf16[128,1024]{1,0:T(8,128)(2,1)S(1)}, bf16[128,1024]{1,0:T(8,128)(2,1)S(1)}, u32[]{:S(2)}, u32[]{:S(2)}) collective-permute-start(bf16[128,1024]{1,0:T(8,128)(2,1)S(1)} %get-tuple-element.54), channel_id=1, source_target_pairs={{0,2},{1,3},{2,0},{3,1},{4,6},{5,7},{6,4},{7,5},{8,10},{9,11},{10,... | collective-permute-start | bytes 786440 | tf_op jit(solution)/shard_map/ppermute | solution.py:22
  7.5 1.2 %collective-permute-start.2 = (bf16[128,1024]{1,0:T(8,128)(2,1)S(1)}, bf16[128,1024]{1,0:T(8,128)(2,1)S(1)}, u32[]{:S(2)}, u32[]{:S(2)}) collective-permute-start(bf16[128,1024]{1,0:T(8,128)(2,1)S(1)} %get-tuple-element.55), channel_id=1, source_target_pairs={{0,1},{1,0},{2,3},{3,2},{4,5},{5,4},{6,7},{7,6},{8,9},{9,8},{10,11... | collective-permute-start | bytes 786440 | tf_op jit(solution)/shard_map/ppermute | solution.py:22
  9.3 10.1 %collective-permute-done.1.refs_0_.saved_ref = bf16[16,4096]{1,0:T(8,128)(2,1)S(1)} collective-permute-done((bf16[16,4096]{1,0:T(8,128)(2,1)S(1)}, bf16[16,4096]{1,0:T(8,128)(2,1)S(1)}, u32[]{:S(2)}, u32[]{:S(2)}) %collective-permute-start.1) | collective-permute-done | bytes 131104 | tf_op jit(solution)/shard_map/ppermute | solution.py:22
  19.6 0.5 copy-done.4
  20.1 0.7 %shard_map.77 = (bf16[16,4096]{1,0:T(8,128)(2,1)S(1)}, bf16[16,1280]{1,0:T(8,128)(2,1)S(1)}, bf16[16,1280]{1,0:T(8,128)(2,1)S(1)}, bf16[16,1280]{1,0:T(8,128)(2,1)S(1)}, bf16[16,1280]{1,0:T(8,128)(2,1)S(1)}) custom-call(s32[1]{0:T(128)} %bitcast.me_ref, bf16[16,4096]{1,0:T(8,128)(2,1)S(1)} %collective-permute-done.1.refs_0_.saved_ref, ...), custom_call_target="tpu_custom_call" | custom-call | bytes 1 | tf_op jit(solution)/shard_map/pallas_call | solution.py:107
  20.8 0.5 collective-permute-start.5
  21.3 1.2 %collective-permute-start.8 = (bf16[16,1280]{1,0:T(8,128)(2,1)S(1)}, bf16[16,1280]{1,0:T(8,128)(2,1)S(1)}, u32[]{:S(2)}, u32[]{:S(2)}) collective-permute-start(bf16[16,1280]{1,0:T(8,128)(2,1)S(1)} %get-tuple-element.30), channel_id=1, source_target_pairs={{0,2},{1,3},{2,0},{3,1},{4,6},{5,7},{6,4},{7,5},{8,10},{9,11},{10,... | collective-permute-start | bytes 122888 | tf_op jit(solution)/shard_map/ppermute | solution.py:22
  22.6 1.0 %collective-permute-start.9 = (bf16[16,1280]{1,0:T(8,128)(2,1)S(1)}, bf16[16,1280]{1,0:T(8,128)(2,1)S(1)}, u32[]{:S(2)}, u32[]{:S(2)}) collective-permute-start(bf16[16,1280]{1,0:T(8,128)(2,1)S(1)} %get-tuple-element.31), channel_id=1, source_target_pairs={{0,3},{1,2},{2,1},{3,0},{4,7},{5,6},{6,5},{7,4},{8,11},{9,10},{10,... | collective-permute-start | bytes 122888 | tf_op jit(solution)/shard_map/ppermute | solution.py:22
  23.6 1.5 %collective-permute-start.7 = (bf16[16,4096]{1,0:T(8,128)(2,1)S(1)}, bf16[16,4096]{1,0:T(8,128)(2,1)S(1)}, u32[]{:S(2)}, u32[]{:S(2)}) collective-permute-start(bf16[16,4096]{1,0:T(8,128)(2,1)S(1)} %shard_map.76.refs_3_), channel_id=1, source_target_pairs={{0,16},{4,20},{8,24},{12,28},{16,0},{20,4},{24,8},{28,12},{1,17},{... | collective-permute-start | bytes 393224 | tf_op jit(solution)/shard_map/ppermute | solution.py:22
  25.1 2.7 %collective-permute-done.refs_0_.saved_ref = bf16[48,4096]{1,0:T(8,128)(2,1)S(1)} collective-permute-done((bf16[48,4096]{1,0:T(8,128)(2,1)S(1)}, bf16[48,4096]{1,0:T(8,128)(2,1)S(1)}, u32[]{:S(2)}, u32[]{:S(2)}) %collective-permute-start) | collective-permute-done | bytes 393248 | tf_op jit(solution)/shard_map/ppermute | solution.py:22
  28.0 0.9 %shard_map.79 = (bf16[48,4096]{1,0:T(8,128)(2,1)S(1)}, bf16[48,1280]{1,0:T(8,128)(2,1)S(1)}, bf16[48,1280]{1,0:T(8,128)(2,1)S(1)}, bf16[48,1280]{1,0:T(8,128)(2,1)S(1)}, bf16[48,1280]{1,0:T(8,128)(2,1)S(1)}) custom-call(s32[1]{0:T(128)} %bitcast.me_ref, bf16[48,4096]{1,0:T(8,128)(2,1)S(1)} %collective-permute-done.refs_0_.saved_ref, ...), custom_call_target="tpu_custom_call" | custom-call | bytes 1 | tf_op jit(solution)/shard_map/pallas_call | solution.py:107
  29.0 1.0 %collective-permute-start.10 = (bf16[48,1280]{1,0:T(8,128)(2,1)S(1)}, bf16[48,1280]{1,0:T(8,128)(2,1)S(1)}, u32[]{:S(2)}, u32[]{:S(2)}) collective-permute-start(bf16[48,1280]{1,0:T(8,128)(2,1)S(1)} %get-tuple-element.33), channel_id=1, source_target_pairs={{0,1},{1,0},{2,3},{3,2},{4,5},{5,4},{6,7},{7,6},{8,9},{9,8},{10,11... | collective-permute-start | bytes 368648 | tf_op jit(solution)/shard_map/ppermute | solution.py:22
  30.0 1.2 %collective-permute-start.11 = (bf16[48,1280]{1,0:T(8,128)(2,1)S(1)}, bf16[48,1280]{1,0:T(8,128)(2,1)S(1)}, u32[]{:S(2)}, u32[]{:S(2)}) collective-permute-start(bf16[48,1280]{1,0:T(8,128)(2,1)S(1)} %get-tuple-element.34), channel_id=1, source_target_pairs={{0,2},{1,3},{2,0},{3,1},{4,6},{5,7},{6,4},{7,5},{8,10},{9,11},{10,... | collective-permute-start | bytes 368648 | tf_op jit(solution)/shard_map/ppermute | solution.py:22
  31.7 0.6 collective-permute-start.6
  32.3 1.1 %collective-permute-done.7.saved_ref = bf16[16,4096]{1,0:T(8,128)(2,1)S(1)} collective-permute-done((bf16[16,4096]{1,0:T(8,128)(2,1)S(1)}, bf16[16,4096]{1,0:T(8,128)(2,1)S(1)}, u32[]{:S(2)}, u32[]{:S(2)}) %collective-permute-start.7) | collective-permute-done | bytes 131104 | tf_op jit(solution)/shard_map/ppermute | solution.py:22
  33.4 0.6 collective-permute-done.11.refs_3_.refs_7_
  34.0 1.8 %collective-permute-done.12.refs_4_.refs_10_ = bf16[48,1280]{1,0:T(8,128)(2,1)S(1)} collective-permute-done((bf16[48,1280]{1,0:T(8,128)(2,1)S(1)}, bf16[48,1280]{1,0:T(8,128)(2,1)S(1)}, u32[]{:S(2)}, u32[]{:S(2)}) %collective-permute-start.12) | collective-permute-done | bytes 122912 | tf_op jit(solution)/shard_map/ppermute | solution.py:22
  35.9 0.8 %shard_map.80 = (bf16[80,4096]{1,0:T(8,128)(2,1)S(1)}, bf16[16,1280]{1,0:T(8,128)(2,1)S(1)}, bf16[16,1280]{1,0:T(8,128)(2,1)S(1)}, bf16[16,1280]{1,0:T(8,128)(2,1)S(1)}, bf16[16,1280]{1,0:T(8,128)(2,1)S(1)}) custom-call(s32[1]{0:T(128)} %bitcast.me_ref, bf16[16,4096]{1,0:T(8,128)(2,1)S(1)} %collective-permute-done.7.saved_ref, ...), custom_call_target="tpu_custom_call" | custom-call | flops 6000000000 | bytes 1 | tf_op jit(solution)/shard_map/pallas_call | solution.py:107
  37.0 0.6 collective-permute-start.14
  37.6 1.8 %collective-permute-start.15 = (bf16[16,1280]{1,0:T(8,128)(2,1)S(1)}, bf16[16,1280]{1,0:T(8,128)(2,1)S(1)}, u32[]{:S(2)}, u32[]{:S(2)}) collective-permute-start(bf16[16,1280]{1,0:T(8,128)(2,1)S(1)} %get-tuple-element.38), channel_id=1, source_target_pairs={{0,3},{1,2},{2,1},{3,0},{4,7},{5,6},{6,5},{7,4},{8,11},{9,10},{10,... | collective-permute-start | bytes 122888 | tf_op jit(solution)/shard_map/ppermute | solution.py:22
  39.4 10.2 %collective-permute-start.19 = (bf16[80,4096]{1,0:T(8,128)(2,1)S(1)}, bf16[80,4096]{1,0:T(8,128)(2,1)S(1)}, u32[]{:S(2)}, u32[]{:S(2)}) collective-permute-start(bf16[80,4096]{1,0:T(8,128)(2,1)S(1)} %get-tuple-element.48), channel_id=1, source_target_pairs={{4,0},{8,4},{12,8},{16,12},{20,16},{24,20},{28,24},{5,1},{9,5},{13... | collective-permute-start | bytes 1966088 | tf_op jit(solution)/shard_map/ppermute | solution.py:26
  49.6 0.9 %shard_map.81 = (bf16[48,4096]{1,0:T(8,128)(2,1)S(1)}, bf16[48,1280]{1,0:T(8,128)(2,1)S(1)}, bf16[48,1280]{1,0:T(8,128)(2,1)S(1)}, bf16[48,1280]{1,0:T(8,128)(2,1)S(1)}, bf16[48,1280]{1,0:T(8,128)(2,1)S(1)}) custom-call(s32[1]{0:T(128)} %bitcast.me_ref, bf16[48,4096]{1,0:T(8,128)(2,1)S(1)} %collective-permute-done.6.saved_ref, ...), custom_call_target="tpu_custom_call" | custom-call | flops 8999999488 | bytes 1 | tf_op jit(solution)/shard_map/pallas_call | solution.py:107
  51.0 0.9 %collective-permute-start.17 = (bf16[48,1280]{1,0:T(8,128)(2,1)S(1)}, bf16[48,1280]{1,0:T(8,128)(2,1)S(1)}, u32[]{:S(2)}, u32[]{:S(2)}) collective-permute-start(bf16[48,1280]{1,0:T(8,128)(2,1)S(1)} %get-tuple-element.40), channel_id=1, source_target_pairs={{0,2},{1,3},{2,0},{3,1},{4,6},{5,7},{6,4},{7,5},{8,10},{9,11},{10,... | collective-permute-start | bytes 368648 | tf_op jit(solution)/shard_map/ppermute | solution.py:22
  51.9 1.3 %collective-permute-start.18 = (bf16[48,1280]{1,0:T(8,128)(2,1)S(1)}, bf16[48,1280]{1,0:T(8,128)(2,1)S(1)}, u32[]{:S(2)}, u32[]{:S(2)}) collective-permute-start(bf16[48,1280]{1,0:T(8,128)(2,1)S(1)} %get-tuple-element.41), channel_id=1, source_target_pairs={{0,3},{1,2},{2,1},{3,0},{4,7},{5,6},{6,5},{7,4},{8,11},{9,10},{10,... | collective-permute-start | bytes 368648 | tf_op jit(solution)/shard_map/ppermute | solution.py:22
  53.3 5.8 %collective-permute-start.20 = (bf16[48,4096]{1,0:T(8,128)(2,1)S(1)}, bf16[48,4096]{1,0:T(8,128)(2,1)S(1)}, u32[]{:S(2)}, u32[]{:S(2)}) collective-permute-start(bf16[48,4096]{1,0:T(8,128)(2,1)S(1)} %get-tuple-element.50), channel_id=1, source_target_pairs={{4,0},{8,4},{12,8},{16,12},{20,16},{24,20},{28,24},{5,1},{9,5},{13... | collective-permute-start | bytes 1179656 | tf_op jit(solution)/shard_map/ppermute | solution.py:26
  59.1 0.6 shard_map.82
  59.7 1.5 %shard_map.83 = (bf16[128,4096]{1,0:T(8,128)(2,1)}, f32[1024,128]{1,0:T(8,128)}, f32[128,1024]{1,0:T(8,128)}) custom-call(bf16[48,1280]{1,0:T(8,128)(2,1)S(1)} %collective-permute-done.16.refs_0_, bf16[48,1280]{1,0:T(8,128)(2,1)S(1)} %collective-permute-done.17.refs_1_, bf16[48,1280]{1,0:T(8,128)(2,1)S(1)} %collective-permute-done.18.refs_2_, ...), custom_call_target="tpu_custom_call" | custom-call | flops 3000000000 | bytes 1000000 | tf_op jit(solution)/shard_map/pallas_call | solution.py:216
  61.1 2.5 %collective-permute-done.20.last = bf16[48,4096]{1,0:T(8,128)(2,1)S(1)} collective-permute-done((bf16[48,4096]{1,0:T(8,128)(2,1)S(1)}, bf16[48,4096]{1,0:T(8,128)(2,1)S(1)}, u32[]{:S(2)}, u32[]{:S(2)}) %collective-permute-start.20) | collective-permute-done | bytes 393248 | tf_op jit(solution)/shard_map/ppermute | solution.py:26
  63.7 0.8 %shard_map.84 = bf16[128,4096]{1,0:T(8,128)(2,1)} custom-call(bf16[128,4096]{1,0:T(8,128)(2,1)} %get-tuple-element.49.before_ref, bf16[48,4096]{1,0:T(8,128)(2,1)S(1)} %collective-permute-done.20.last), custom_call_target="tpu_custom_call", output_to_operand_aliasing={{}: (0, {})} | custom-call | tf_op jit(solution)/shard_map/pallas_call | solution.py:170
  (33 shorter events, 2.4 us)
Async XLA Ops:
  0.6 8.2 %copy-start = (bf16[1,128,4096]{2,1,0:T(8,128)(2,1)S(1)}, bf16[1,128,4096]{2,1,0:T(8,128)(2,1)}, u32[]{:S(2)}) copy-start(bf16[1,128,4096]{2,1,0:T(8,128)(2,1)} %param.8) | copy-start | bytes 3145732
  0.6 5.4 %copy-start.1 = (bf16[1,128,4096]{2,1,0:T(8,128)(2,1)S(1)}, bf16[1,128,4096]{2,1,0:T(8,128)(2,1)}, u32[]{:S(2)}) copy-start(bf16[1,128,4096]{2,1,0:T(8,128)(2,1)} %param.6) | copy-start | bytes 3145732
  1.7 17.7 %collective-permute-start.1 = (bf16[16,4096]{1,0:T(8,128)(2,1)S(1)}, bf16[16,4096]{1,0:T(8,128)(2,1)S(1)}, u32[]{:S(2)}, u32[]{:S(2)}) collective-permute-start(bf16[16,4096]{1,0:T(8,128)(2,1)S(1)} %slice_bitcast_fusion.1), channel_id=1, source_target_pairs={{0,16},{4,20},{8,24},{12,28},{16,0},{20,4},{24,8},{28,12},{1,17},{... | collective-permute-start | bytes 393224 | tf_op jit(solution)/shard_map/ppermute | solution.py:22
  5.9 21.9 %collective-permute-start = (bf16[48,4096]{1,0:T(8,128)(2,1)S(1)}, bf16[48,4096]{1,0:T(8,128)(2,1)S(1)}, u32[]{:S(2)}, u32[]{:S(2)}) collective-permute-start(bf16[48,4096]{1,0:T(8,128)(2,1)S(1)} %slice_bitcast_fusion), channel_id=1, source_target_pairs={{0,16},{4,20},{8,24},{12,28},{16,0},{20,4},{24,8},{28,12},{1,17},{... | collective-permute-start | bytes 1179656 | tf_op jit(solution)/shard_map/ppermute | solution.py:22
  6.2 13.4 %collective-permute-start.3 = (bf16[128,1024]{1,0:T(8,128)(2,1)S(1)}, bf16[128,1024]{1,0:T(8,128)(2,1)S(1)}, u32[]{:S(2)}, u32[]{:S(2)}) collective-permute-start(bf16[128,1024]{1,0:T(8,128)(2,1)S(1)} %get-tuple-element.54), channel_id=1, source_target_pairs={{0,2},{1,3},{2,0},{3,1},{4,6},{5,7},{6,4},{7,5},{8,10},{9,11},{10,... | collective-permute-start | bytes 786440 | tf_op jit(solution)/shard_map/ppermute | solution.py:22
  7.5 12.1 %collective-permute-start.2 = (bf16[128,1024]{1,0:T(8,128)(2,1)S(1)}, bf16[128,1024]{1,0:T(8,128)(2,1)S(1)}, u32[]{:S(2)}, u32[]{:S(2)}) collective-permute-start(bf16[128,1024]{1,0:T(8,128)(2,1)S(1)} %get-tuple-element.55), channel_id=1, source_target_pairs={{0,1},{1,0},{2,3},{3,2},{4,5},{5,4},{6,7},{7,6},{8,9},{9,8},{10,11... | collective-permute-start | bytes 786440 | tf_op jit(solution)/shard_map/ppermute | solution.py:22
  8.7 10.7 %copy-start.2 = (bf16[1,128,4096]{2,1,0:T(8,128)(2,1)S(1)}, bf16[1,128,4096]{2,1,0:T(8,128)(2,1)}, u32[]{:S(2)}) copy-start(bf16[1,128,4096]{2,1,0:T(8,128)(2,1)} %param.5) | copy-start | bytes 3145732
  8.7 10.9 %collective-permute-start.4 = (bf16[128,1024]{1,0:T(8,128)(2,1)S(1)}, bf16[128,1024]{1,0:T(8,128)(2,1)S(1)}, u32[]{:S(2)}, u32[]{:S(2)}) collective-permute-start(bf16[128,1024]{1,0:T(8,128)(2,1)S(1)} %get-tuple-element.56), channel_id=1, source_target_pairs={{0,3},{1,2},{2,1},{3,0},{4,7},{5,6},{6,5},{7,4},{8,11},{9,10},{10,... | collective-permute-start | bytes 786440 | tf_op jit(solution)/shard_map/ppermute | solution.py:22
  9.3 10.3 %copy-start.3 = (bf16[1,4096,128]{2,1,0:T(8,128)(2,1)S(1)}, bf16[1,4096,128]{2,1,0:T(8,128)(2,1)}, u32[]{:S(2)}) copy-start(bf16[1,4096,128]{2,1,0:T(8,128)(2,1)} %param.7) | copy-start | bytes 3145732
  19.4 0.7 %copy-start.4 = (f32[1,4096]{1,0:T(1,128)S(1)}, f32[1,4096]{1,0:T(1,128)}, u32[]{:S(2)}) copy-start(f32[1,4096]{1,0:T(1,128)} %gain_ref.7) | copy-start | bytes 49156
  20.8 4.2 %collective-permute-start.5 = (bf16[16,1280]{1,0:T(8,128)(2,1)S(1)}, bf16[16,1280]{1,0:T(8,128)(2,1)S(1)}, u32[]{:S(2)}, u32[]{:S(2)}) collective-permute-start(bf16[16,1280]{1,0:T(8,128)(2,1)S(1)} %get-tuple-element.28), channel_id=1, source_target_pairs={{0,1},{1,0},{2,3},{3,2},{4,5},{5,4},{6,7},{7,6},{8,9},{9,8},{10,11... | collective-permute-start | bytes 122888 | tf_op jit(solution)/shard_map/ppermute | solution.py:22
  21.3 6.7 %collective-permute-start.8 = (bf16[16,1280]{1,0:T(8,128)(2,1)S(1)}, bf16[16,1280]{1,0:T(8,128)(2,1)S(1)}, u32[]{:S(2)}, u32[]{:S(2)}) collective-permute-start(bf16[16,1280]{1,0:T(8,128)(2,1)S(1)} %get-tuple-element.30), channel_id=1, source_target_pairs={{0,2},{1,3},{2,0},{3,1},{4,6},{5,7},{6,4},{7,5},{8,10},{9,11},{10,... | collective-permute-start | bytes 122888 | tf_op jit(solution)/shard_map/ppermute | solution.py:22
  22.6 5.5 %collective-permute-start.9 = (bf16[16,1280]{1,0:T(8,128)(2,1)S(1)}, bf16[16,1280]{1,0:T(8,128)(2,1)S(1)}, u32[]{:S(2)}, u32[]{:S(2)}) collective-permute-start(bf16[16,1280]{1,0:T(8,128)(2,1)S(1)} %get-tuple-element.31), channel_id=1, source_target_pairs={{0,3},{1,2},{2,1},{3,0},{4,7},{5,6},{6,5},{7,4},{8,11},{9,10},{10,... | collective-permute-start | bytes 122888 | tf_op jit(solution)/shard_map/ppermute | solution.py:22
  23.6 9.9 %collective-permute-start.7 = (bf16[16,4096]{1,0:T(8,128)(2,1)S(1)}, bf16[16,4096]{1,0:T(8,128)(2,1)S(1)}, u32[]{:S(2)}, u32[]{:S(2)}) collective-permute-start(bf16[16,4096]{1,0:T(8,128)(2,1)S(1)} %shard_map.76.refs_3_), channel_id=1, source_target_pairs={{0,16},{4,20},{8,24},{12,28},{16,0},{20,4},{24,8},{28,12},{1,17},{... | collective-permute-start | bytes 393224 | tf_op jit(solution)/shard_map/ppermute | solution.py:22
  29.0 4.4 %collective-permute-start.10 = (bf16[48,1280]{1,0:T(8,128)(2,1)S(1)}, bf16[48,1280]{1,0:T(8,128)(2,1)S(1)}, u32[]{:S(2)}, u32[]{:S(2)}) collective-permute-start(bf16[48,1280]{1,0:T(8,128)(2,1)S(1)} %get-tuple-element.33), channel_id=1, source_target_pairs={{0,1},{1,0},{2,3},{3,2},{4,5},{5,4},{6,7},{7,6},{8,9},{9,8},{10,11... | collective-permute-start | bytes 368648 | tf_op jit(solution)/shard_map/ppermute | solution.py:22
  30.0 4.0 %collective-permute-start.11 = (bf16[48,1280]{1,0:T(8,128)(2,1)S(1)}, bf16[48,1280]{1,0:T(8,128)(2,1)S(1)}, u32[]{:S(2)}, u32[]{:S(2)}) collective-permute-start(bf16[48,1280]{1,0:T(8,128)(2,1)S(1)} %get-tuple-element.34), channel_id=1, source_target_pairs={{0,2},{1,3},{2,0},{3,1},{4,6},{5,7},{6,4},{7,5},{8,10},{9,11},{10,... | collective-permute-start | bytes 368648 | tf_op jit(solution)/shard_map/ppermute | solution.py:22
  31.3 4.6 %collective-permute-start.12 = (bf16[48,1280]{1,0:T(8,128)(2,1)S(1)}, bf16[48,1280]{1,0:T(8,128)(2,1)S(1)}, u32[]{:S(2)}, u32[]{:S(2)}) collective-permute-start(bf16[48,1280]{1,0:T(8,128)(2,1)S(1)} %get-tuple-element.35), channel_id=1, source_target_pairs={{0,3},{1,2},{2,1},{3,0},{4,7},{5,6},{6,5},{7,4},{8,11},{9,10},{10,... | collective-permute-start | bytes 368648 | tf_op jit(solution)/shard_map/ppermute | solution.py:22
  31.7 17.9 %collective-permute-start.6 = (bf16[48,4096]{1,0:T(8,128)(2,1)S(1)}, bf16[48,4096]{1,0:T(8,128)(2,1)S(1)}, u32[]{:S(2)}, u32[]{:S(2)}) collective-permute-start(bf16[48,4096]{1,0:T(8,128)(2,1)S(1)} %shard_map.78.refs_3_), channel_id=1, source_target_pairs={{0,16},{4,20},{8,24},{12,28},{16,0},{20,4},{24,8},{28,12},{1,17},{... | collective-permute-start | bytes 1179656 | tf_op jit(solution)/shard_map/ppermute | solution.py:22
  36.7 12.9 %collective-permute-start.13 = (bf16[16,1280]{1,0:T(8,128)(2,1)S(1)}, bf16[16,1280]{1,0:T(8,128)(2,1)S(1)}, u32[]{:S(2)}, u32[]{:S(2)}) collective-permute-start(bf16[16,1280]{1,0:T(8,128)(2,1)S(1)} %get-tuple-element.36), channel_id=1, source_target_pairs={{0,1},{1,0},{2,3},{3,2},{4,5},{5,4},{6,7},{7,6},{8,9},{9,8},{10,11... | collective-permute-start | bytes 122888 | tf_op jit(solution)/shard_map/ppermute | solution.py:22
  37.0 12.6 %collective-permute-start.14 = (bf16[16,1280]{1,0:T(8,128)(2,1)S(1)}, bf16[16,1280]{1,0:T(8,128)(2,1)S(1)}, u32[]{:S(2)}, u32[]{:S(2)}) collective-permute-start(bf16[16,1280]{1,0:T(8,128)(2,1)S(1)} %get-tuple-element.37), channel_id=1, source_target_pairs={{0,2},{1,3},{2,0},{3,1},{4,6},{5,7},{6,4},{7,5},{8,10},{9,11},{10,... | collective-permute-start | bytes 122888 | tf_op jit(solution)/shard_map/ppermute | solution.py:22
  37.6 12.0 %collective-permute-start.15 = (bf16[16,1280]{1,0:T(8,128)(2,1)S(1)}, bf16[16,1280]{1,0:T(8,128)(2,1)S(1)}, u32[]{:S(2)}, u32[]{:S(2)}) collective-permute-start(bf16[16,1280]{1,0:T(8,128)(2,1)S(1)} %get-tuple-element.38), channel_id=1, source_target_pairs={{0,3},{1,2},{2,1},{3,0},{4,7},{5,6},{6,5},{7,4},{8,11},{9,10},{10,... | collective-permute-start | bytes 122888 | tf_op jit(solution)/shard_map/ppermute | solution.py:22
  39.4 20.3 %collective-permute-start.19 = (bf16[80,4096]{1,0:T(8,128)(2,1)S(1)}, bf16[80,4096]{1,0:T(8,128)(2,1)S(1)}, u32[]{:S(2)}, u32[]{:S(2)}) collective-permute-start(bf16[80,4096]{1,0:T(8,128)(2,1)S(1)} %get-tuple-element.48), channel_id=1, source_target_pairs={{4,0},{8,4},{12,8},{16,12},{20,16},{24,20},{28,24},{5,1},{9,5},{13... | collective-permute-start | bytes 1966088 | tf_op jit(solution)/shard_map/ppermute | solution.py:26
  50.5 9.1 %collective-permute-start.16 = (bf16[48,1280]{1,0:T(8,128)(2,1)S(1)}, bf16[48,1280]{1,0:T(8,128)(2,1)S(1)}, u32[]{:S(2)}, u32[]{:S(2)}) collective-permute-start(bf16[48,1280]{1,0:T(8,128)(2,1)S(1)} %get-tuple-element.39), channel_id=1, source_target_pairs={{0,1},{1,0},{2,3},{3,2},{4,5},{5,4},{6,7},{7,6},{8,9},{9,8},{10,11... | collective-permute-start | bytes 368648 | tf_op jit(solution)/shard_map/ppermute | solution.py:22
  51.0 8.6 %collective-permute-start.17 = (bf16[48,1280]{1,0:T(8,128)(2,1)S(1)}, bf16[48,1280]{1,0:T(8,128)(2,1)S(1)}, u32[]{:S(2)}, u32[]{:S(2)}) collective-permute-start(bf16[48,1280]{1,0:T(8,128)(2,1)S(1)} %get-tuple-element.40), channel_id=1, source_target_pairs={{0,2},{1,3},{2,0},{3,1},{4,6},{5,7},{6,4},{7,5},{8,10},{9,11},{10,... | collective-permute-start | bytes 368648 | tf_op jit(solution)/shard_map/ppermute | solution.py:22
  51.9 7.7 %collective-permute-start.18 = (bf16[48,1280]{1,0:T(8,128)(2,1)S(1)}, bf16[48,1280]{1,0:T(8,128)(2,1)S(1)}, u32[]{:S(2)}, u32[]{:S(2)}) collective-permute-start(bf16[48,1280]{1,0:T(8,128)(2,1)S(1)} %get-tuple-element.41), channel_id=1, source_target_pairs={{0,3},{1,2},{2,1},{3,0},{4,7},{5,6},{6,5},{7,4},{8,11},{9,10},{10,... | collective-permute-start | bytes 368648 | tf_op jit(solution)/shard_map/ppermute | solution.py:22
  53.3 10.4 %collective-permute-start.20 = (bf16[48,4096]{1,0:T(8,128)(2,1)S(1)}, bf16[48,4096]{1,0:T(8,128)(2,1)S(1)}, u32[]{:S(2)}, u32[]{:S(2)}) collective-permute-start(bf16[48,4096]{1,0:T(8,128)(2,1)S(1)} %get-tuple-element.50), channel_id=1, source_target_pairs={{4,0},{8,4},{12,8},{16,12},{20,16},{24,20},{28,24},{5,1},{9,5},{13... | collective-permute-start | bytes 1179656 | tf_op jit(solution)/shard_map/ppermute | solution.py:26

commit v11 on v9

--- a/solution.py
+++ b/solution.py
@@ -165,7 +165,7 @@
     return pl.pallas_call(
         functools.partial(join_kernel, before.shape[0] - last.shape[0]),
         out_shape=jax.ShapeDtypeStruct(before.shape, before.dtype),
-        in_specs=[ANY, VMEM],
+        in_specs=[ANY, ANY],
         out_specs=ANY,
         scratch_shapes=[pltpu.SemaphoreType.DMA],
         input_output_aliases={0: 0},
@@ -245,7 +245,7 @@
     parts, packs, waits = [], [], cot_all[1:]
     for i, (start, rows) in enumerate(spans):
         if i + 2 < chunks:
-            coming = rows_after(stash, *spans[i + 2], [arrivals[i]] + waits * (i > 0))
+            coming = rows_after(stash, *spans[i + 2], [arrivals[i]] + waits[:1] * (i > 0))
             arrivals.append(held(coming))
             waits = waits + [coming]
         joins = parts if i == chunks - 2 else []

time: 64.7 us -> 64.7 us (level)
  transfers between devices with their start and end apart: 21 -> 21, of which waited for: 7 -> 6; matrix products, arithmetic and copies ran while one was open for 2% -> 2% of each run, Pallas kernels for 9% -> 9%
where the time goes in v11:
time: 64.7 us; the launch traced here: 64.4 us
  starting transfers between devices  34.9 us (54%)
  waiting for transfers between devices  19 us (29%)
  Pallas kernels  6.47 us (10%)
  local copies, waits for them, and re-layouts  2.69 us (4%)
  between operations  0.9 us (1%)
    ppermute x19, starting transfers between devices, exchanged(): lax.ppermute(x, axis, [(i, i ^ mask) for i in range(lax.axis_size(axis))])  18.9 us
    ppermute x19, waiting for transfers between devices, exchanged(): lax.ppermute(x, axis, [(i, i ^ mask) for i in range(lax.axis_size(axis))])  16.4 us
    ppermute x2, starting transfers between devices, to_previous(): lax.ppermute(x, axis, [(i, i - 1) for i in range(1, lax.axis_size(axis))])  16 us
    pallas_call x4, Pallas kernels, run_chunk(): pl.pallas_call(functools.partial(chunk_kernel, start, len(joins), len(wai...  3.38 us
    ppermute x2, waiting for transfers between devices, to_previous(): lax.ppermute(x, axis, [(i, i - 1) for i in range(1, lax.axis_size(axis))])  2.59 us
    slice x2, local copies, waits for them, and re-layouts, per_device(): arrivals = [held(stash[start:start + rows]) for start, rows in spans[:2]]  2.08 us
    pallas_call x1, Pallas kernels, run_final(): pl.pallas_call(functools.partial(final_kernel, groups, spans), out_shape=...  1.42 us
  transfers between devices with their start and end apart: 21, of which 6 were waited for; matrix products, arithmetic and copies ran while one was open for 2% of the time, Pallas kernels for 9%

profile of v11, /device:TPU:1, one launch (start us, length us, event | category | flops | bytes accessed | tf_op | source)
XLA Modules:
  0.0 64.4 jit_solution(13392372399598466624)
XLA Ops:
  0.7 1.1 %slice_bitcast_fusion.1 = bf16[16,4096]{1,0:T(8,128)(2,1)S(1)} fusion(bf16[1,128,4096]{2,1,0:T(8,128)(2,1)} %param.5), kind=kLoop, calls=%fused_computation.7 | loop fusion | bytes 262144 | tf_op jit(solution)/shard_map/slice | solution.py:237
  1.7 3.2 %collective-permute-start.1 = (bf16[16,4096]{1,0:T(8,128)(2,1)S(1)}, bf16[16,4096]{1,0:T(8,128)(2,1)S(1)}, u32[]{:S(2)}, u32[]{:S(2)}) collective-permute-start(bf16[16,4096]{1,0:T(8,128)(2,1)S(1)} %slice_bitcast_fusion.1), channel_id=1, source_target_pairs={{0,16},{4,20},{8,24},{12,28},{16,0},{20,4},{24,8},{28,12},{1,17},{... | collective-permute-start | bytes 393224 | tf_op jit(solution)/shard_map/ppermute | solution.py:22
  4.9 1.0 %slice_bitcast_fusion = bf16[48,4096]{1,0:T(8,128)(2,1)S(1)} fusion(bf16[1,128,4096]{2,1,0:T(8,128)(2,1)} %param.5), kind=kLoop, calls=%fused_computation.2 | loop fusion | bytes 786432 | tf_op jit(solution)/shard_map/slice | solution.py:237
  6.2 1.3 %collective-permute-start.3 = (bf16[128,1024]{1,0:T(8,128)(2,1)S(1)}, bf16[128,1024]{1,0:T(8,128)(2,1)S(1)}, u32[]{:S(2)}, u32[]{:S(2)}) collective-permute-start(bf16[128,1024]{1,0:T(8,128)(2,1)S(1)} %get-tuple-element.54), channel_id=1, source_target_pairs={{0,2},{1,3},{2,0},{3,1},{4,6},{5,7},{6,4},{7,5},{8,10},{9,11},{10,... | collective-permute-start | bytes 786440 | tf_op jit(solution)/shard_map/ppermute | solution.py:22
  7.5 1.2 %collective-permute-start.2 = (bf16[128,1024]{1,0:T(8,128)(2,1)S(1)}, bf16[128,1024]{1,0:T(8,128)(2,1)S(1)}, u32[]{:S(2)}, u32[]{:S(2)}) collective-permute-start(bf16[128,1024]{1,0:T(8,128)(2,1)S(1)} %get-tuple-element.55), channel_id=1, source_target_pairs={{0,1},{1,0},{2,3},{3,2},{4,5},{5,4},{6,7},{7,6},{8,9},{9,8},{10,11... | collective-permute-start | bytes 786440 | tf_op jit(solution)/shard_map/ppermute | solution.py:22
  9.3 10.1 %collective-permute-done.1.refs_0_.saved_ref = bf16[16,4096]{1,0:T(8,128)(2,1)S(1)} collective-permute-done((bf16[16,4096]{1,0:T(8,128)(2,1)S(1)}, bf16[16,4096]{1,0:T(8,128)(2,1)S(1)}, u32[]{:S(2)}, u32[]{:S(2)}) %collective-permute-start.1) | collective-permute-done | bytes 131104 | tf_op jit(solution)/shard_map/ppermute | solution.py:22
  19.6 0.5 copy-done.4
  20.1 0.7 %shard_map.77 = (bf16[16,4096]{1,0:T(8,128)(2,1)S(1)}, bf16[16,1280]{1,0:T(8,128)(2,1)S(1)}, bf16[16,1280]{1,0:T(8,128)(2,1)S(1)}, bf16[16,1280]{1,0:T(8,128)(2,1)S(1)}, bf16[16,1280]{1,0:T(8,128)(2,1)S(1)}) custom-call(s32[1]{0:T(128)} %bitcast.me_ref, bf16[16,4096]{1,0:T(8,128)(2,1)S(1)} %collective-permute-done.1.refs_0_.saved_ref, ...), custom_call_target="tpu_custom_call" | custom-call | bytes 1 | tf_op jit(solution)/shard_map/pallas_call | solution.py:107
  21.3 1.2 %collective-permute-start.8 = (bf16[16,1280]{1,0:T(8,128)(2,1)S(1)}, bf16[16,1280]{1,0:T(8,128)(2,1)S(1)}, u32[]{:S(2)}, u32[]{:S(2)}) collective-permute-start(bf16[16,1280]{1,0:T(8,128)(2,1)S(1)} %get-tuple-element.30), channel_id=1, source_target_pairs={{0,2},{1,3},{2,0},{3,1},{4,6},{5,7},{6,4},{7,5},{8,10},{9,11},{10,... | collective-permute-start | bytes 122888 | tf_op jit(solution)/shard_map/ppermute | solution.py:22
  22.6 1.0 %collective-permute-start.9 = (bf16[16,1280]{1,0:T(8,128)(2,1)S(1)}, bf16[16,1280]{1,0:T(8,128)(2,1)S(1)}, u32[]{:S(2)}, u32[]{:S(2)}) collective-permute-start(bf16[16,1280]{1,0:T(8,128)(2,1)S(1)} %get-tuple-element.31), channel_id=1, source_target_pairs={{0,3},{1,2},{2,1},{3,0},{4,7},{5,6},{6,5},{7,4},{8,11},{9,10},{10,... | collective-permute-start | bytes 122888 | tf_op jit(solution)/shard_map/ppermute | solution.py:22
  23.6 1.5 %collective-permute-start.7 = (bf16[16,4096]{1,0:T(8,128)(2,1)S(1)}, bf16[16,4096]{1,0:T(8,128)(2,1)S(1)}, u32[]{:S(2)}, u32[]{:S(2)}) collective-permute-start(bf16[16,4096]{1,0:T(8,128)(2,1)S(1)} %shard_map.76.refs_3_), channel_id=1, source_target_pairs={{0,16},{4,20},{8,24},{12,28},{16,0},{20,4},{24,8},{28,12},{1,17},{... | collective-permute-start | bytes 393224 | tf_op jit(solution)/shard_map/ppermute | solution.py:22
  25.1 2.7 %collective-permute-done.refs_0_.saved_ref = bf16[48,4096]{1,0:T(8,128)(2,1)S(1)} collective-permute-done((bf16[48,4096]{1,0:T(8,128)(2,1)S(1)}, bf16[48,4096]{1,0:T(8,128)(2,1)S(1)}, u32[]{:S(2)}, u32[]{:S(2)}) %collective-permute-start) | collective-permute-done | bytes 393248 | tf_op jit(solution)/shard_map/ppermute | solution.py:22
  28.0 0.9 %shard_map.79 = (bf16[48,4096]{1,0:T(8,128)(2,1)S(1)}, bf16[48,1280]{1,0:T(8,128)(2,1)S(1)}, bf16[48,1280]{1,0:T(8,128)(2,1)S(1)}, bf16[48,1280]{1,0:T(8,128)(2,1)S(1)}, bf16[48,1280]{1,0:T(8,128)(2,1)S(1)}) custom-call(s32[1]{0:T(128)} %bitcast.me_ref, bf16[48,4096]{1,0:T(8,128)(2,1)S(1)} %collective-permute-done.refs_0_.saved_ref, ...), custom_call_target="tpu_custom_call" | custom-call | bytes 1 | tf_op jit(solution)/shard_map/pallas_call | solution.py:107
  29.0 1.0 %collective-permute-start.10 = (bf16[48,1280]{1,0:T(8,128)(2,1)S(1)}, bf16[48,1280]{1,0:T(8,128)(2,1)S(1)}, u32[]{:S(2)}, u32[]{:S(2)}) collective-permute-start(bf16[48,1280]{1,0:T(8,128)(2,1)S(1)} %get-tuple-element.33), channel_id=1, source_target_pairs={{0,1},{1,0},{2,3},{3,2},{4,5},{5,4},{6,7},{7,6},{8,9},{9,8},{10,11... | collective-permute-start | bytes 368648 | tf_op jit(solution)/shard_map/ppermute | solution.py:22
  30.0 1.2 %collective-permute-start.11 = (bf16[48,1280]{1,0:T(8,128)(2,1)S(1)}, bf16[48,1280]{1,0:T(8,128)(2,1)S(1)}, u32[]{:S(2)}, u32[]{:S(2)}) collective-permute-start(bf16[48,1280]{1,0:T(8,128)(2,1)S(1)} %get-tuple-element.34), channel_id=1, source_target_pairs={{0,2},{1,3},{2,0},{3,1},{4,6},{5,7},{6,4},{7,5},{8,10},{9,11},{10,... | collective-permute-start | bytes 368648 | tf_op jit(solution)/shard_map/ppermute | solution.py:22
  31.7 0.6 collective-permute-start.6
  32.3 1.1 %collective-permute-done.7.saved_ref = bf16[16,4096]{1,0:T(8,128)(2,1)S(1)} collective-permute-done((bf16[16,4096]{1,0:T(8,128)(2,1)S(1)}, bf16[16,4096]{1,0:T(8,128)(2,1)S(1)}, u32[]{:S(2)}, u32[]{:S(2)}) %collective-permute-start.7) | collective-permute-done | bytes 131104 | tf_op jit(solution)/shard_map/ppermute | solution.py:22
  33.4 0.6 collective-permute-done.11.refs_3_.refs_7_
  34.0 1.8 %collective-permute-done.12.refs_4_.refs_10_ = bf16[48,1280]{1,0:T(8,128)(2,1)S(1)} collective-permute-done((bf16[48,1280]{1,0:T(8,128)(2,1)S(1)}, bf16[48,1280]{1,0:T(8,128)(2,1)S(1)}, u32[]{:S(2)}, u32[]{:S(2)}) %collective-permute-start.12) | collective-permute-done | bytes 122912 | tf_op jit(solution)/shard_map/ppermute | solution.py:22
  35.9 0.8 %shard_map.80 = (bf16[80,4096]{1,0:T(8,128)(2,1)S(1)}, bf16[16,1280]{1,0:T(8,128)(2,1)S(1)}, bf16[16,1280]{1,0:T(8,128)(2,1)S(1)}, bf16[16,1280]{1,0:T(8,128)(2,1)S(1)}, bf16[16,1280]{1,0:T(8,128)(2,1)S(1)}) custom-call(s32[1]{0:T(128)} %bitcast.me_ref, bf16[16,4096]{1,0:T(8,128)(2,1)S(1)} %collective-permute-done.7.saved_ref, ...), custom_call_target="tpu_custom_call" | custom-call | flops 6000000000 | bytes 1 | tf_op jit(solution)/shard_map/pallas_call | solution.py:107
  37.0 0.6 collective-permute-start.14
  37.6 1.8 %collective-permute-start.15 = (bf16[16,1280]{1,0:T(8,128)(2,1)S(1)}, bf16[16,1280]{1,0:T(8,128)(2,1)S(1)}, u32[]{:S(2)}, u32[]{:S(2)}) collective-permute-start(bf16[16,1280]{1,0:T(8,128)(2,1)S(1)} %get-tuple-element.38), channel_id=1, source_target_pairs={{0,3},{1,2},{2,1},{3,0},{4,7},{5,6},{6,5},{7,4},{8,11},{9,10},{10,... | collective-permute-start | bytes 122888 | tf_op jit(solution)/shard_map/ppermute | solution.py:22
  39.4 10.2 %collective-permute-start.19 = (bf16[80,4096]{1,0:T(8,128)(2,1)S(1)}, bf16[80,4096]{1,0:T(8,128)(2,1)S(1)}, u32[]{:S(2)}, u32[]{:S(2)}) collective-permute-start(bf16[80,4096]{1,0:T(8,128)(2,1)S(1)} %get-tuple-element.48), channel_id=1, source_target_pairs={{4,0},{8,4},{12,8},{16,12},{20,16},{24,20},{28,24},{5,1},{9,5},{13... | collective-permute-start | bytes 1966088 | tf_op jit(solution)/shard_map/ppermute | solution.py:26
  49.6 0.9 %shard_map.81 = (bf16[48,4096]{1,0:T(8,128)(2,1)S(1)}, bf16[48,1280]{1,0:T(8,128)(2,1)S(1)}, bf16[48,1280]{1,0:T(8,128)(2,1)S(1)}, bf16[48,1280]{1,0:T(8,128)(2,1)S(1)}, bf16[48,1280]{1,0:T(8,128)(2,1)S(1)}) custom-call(s32[1]{0:T(128)} %bitcast.me_ref, bf16[48,4096]{1,0:T(8,128)(2,1)S(1)} %collective-permute-done.6.saved_ref, ...), custom_call_target="tpu_custom_call" | custom-call | flops 8999999488 | bytes 1 | tf_op jit(solution)/shard_map/pallas_call | solution.py:107
  50.5 0.5 collective-permute-start.16
  51.0 0.9 %collective-permute-start.17 = (bf16[48,1280]{1,0:T(8,128)(2,1)S(1)}, bf16[48,1280]{1,0:T(8,128)(2,1)S(1)}, u32[]{:S(2)}, u32[]{:S(2)}) collective-permute-start(bf16[48,1280]{1,0:T(8,128)(2,1)S(1)} %get-tuple-element.41), channel_id=1, source_target_pairs={{0,2},{1,3},{2,0},{3,1},{4,6},{5,7},{6,4},{7,5},{8,10},{9,11},{10,... | collective-permute-start | bytes 368648 | tf_op jit(solution)/shard_map/ppermute | solution.py:22
  51.9 1.3 %collective-permute-start.18 = (bf16[48,1280]{1,0:T(8,128)(2,1)S(1)}, bf16[48,1280]{1,0:T(8,128)(2,1)S(1)}, u32[]{:S(2)}, u32[]{:S(2)}) collective-permute-start(bf16[48,1280]{1,0:T(8,128)(2,1)S(1)} %get-tuple-element.42), channel_id=1, source_target_pairs={{0,3},{1,2},{2,1},{3,0},{4,7},{5,6},{6,5},{7,4},{8,11},{9,10},{10,... | collective-permute-start | bytes 368648 | tf_op jit(solution)/shard_map/ppermute | solution.py:22
  53.3 5.8 %collective-permute-start.20 = (bf16[48,4096]{1,0:T(8,128)(2,1)S(1)}, bf16[48,4096]{1,0:T(8,128)(2,1)S(1)}, u32[]{:S(2)}, u32[]{:S(2)}) collective-permute-start(bf16[48,4096]{1,0:T(8,128)(2,1)S(1)} %get-tuple-element.50), channel_id=1, source_target_pairs={{4,0},{8,4},{12,8},{16,12},{20,16},{24,20},{28,24},{5,1},{9,5},{13... | collective-permute-start | bytes 1179656 | tf_op jit(solution)/shard_map/ppermute | solution.py:26
  59.1 0.6 shard_map.82
  59.7 1.4 %shard_map.83 = (bf16[128,4096]{1,0:T(8,128)(2,1)}, f32[1024,128]{1,0:T(8,128)}, f32[128,1024]{1,0:T(8,128)}) custom-call(bf16[48,1280]{1,0:T(8,128)(2,1)S(1)} %get-tuple-element.39.refs_16_.refs_0_, bf16[48,1280]{1,0:T(8,128)(2,1)S(1)} %collective-permute-done.16.refs_1_, bf16[48,1280]{1,0:T(8,128)(2,1)S(1)} %collective-permute-done.17.refs_2_, ...), custom_call_target="tpu_custom_call" | custom-call | flops 3000000000 | bytes 1000000 | tf_op jit(solution)/shard_map/pallas_call | solution.py:211
  61.1 2.6 %collective-permute-done.20.last = bf16[48,4096]{1,0:T(8,128)(2,1)S(1)} collective-permute-done((bf16[48,4096]{1,0:T(8,128)(2,1)S(1)}, bf16[48,4096]{1,0:T(8,128)(2,1)S(1)}, u32[]{:S(2)}, u32[]{:S(2)}) %collective-permute-start.20) | collective-permute-done | bytes 393248 | tf_op jit(solution)/shard_map/ppermute | solution.py:26
  63.7 0.8 %shard_map.84 = bf16[128,4096]{1,0:T(8,128)(2,1)} custom-call(bf16[128,4096]{1,0:T(8,128)(2,1)} %get-tuple-element.49.before_ref, bf16[48,4096]{1,0:T(8,128)(2,1)S(1)} %collective-permute-done.20.last), custom_call_target="tpu_custom_call", output_to_operand_aliasing={{}: (0, {})} | custom-call | tf_op jit(solution)/shard_map/pallas_call | solution.py:165
  (33 shorter events, 2.5 us)
Async XLA Ops:
  0.6 8.2 %copy-start = (bf16[1,128,4096]{2,1,0:T(8,128)(2,1)S(1)}, bf16[1,128,4096]{2,1,0:T(8,128)(2,1)}, u32[]{:S(2)}) copy-start(bf16[1,128,4096]{2,1,0:T(8,128)(2,1)} %param.8) | copy-start | bytes 3145732
  0.6 5.4 %copy-start.1 = (bf16[1,128,4096]{2,1,0:T(8,128)(2,1)S(1)}, bf16[1,128,4096]{2,1,0:T(8,128)(2,1)}, u32[]{:S(2)}) copy-start(bf16[1,128,4096]{2,1,0:T(8,128)(2,1)} %param.6) | copy-start | bytes 3145732
  1.7 17.7 %collective-permute-start.1 = (bf16[16,4096]{1,0:T(8,128)(2,1)S(1)}, bf16[16,4096]{1,0:T(8,128)(2,1)S(1)}, u32[]{:S(2)}, u32[]{:S(2)}) collective-permute-start(bf16[16,4096]{1,0:T(8,128)(2,1)S(1)} %slice_bitcast_fusion.1), channel_id=1, source_target_pairs={{0,16},{4,20},{8,24},{12,28},{16,0},{20,4},{24,8},{28,12},{1,17},{... | collective-permute-start | bytes 393224 | tf_op jit(solution)/shard_map/ppermute | solution.py:22
  5.9 21.9 %collective-permute-start = (bf16[48,4096]{1,0:T(8,128)(2,1)S(1)}, bf16[48,4096]{1,0:T(8,128)(2,1)S(1)}, u32[]{:S(2)}, u32[]{:S(2)}) collective-permute-start(bf16[48,4096]{1,0:T(8,128)(2,1)S(1)} %slice_bitcast_fusion), channel_id=1, source_target_pairs={{0,16},{4,20},{8,24},{12,28},{16,0},{20,4},{24,8},{28,12},{1,17},{... | collective-permute-start | bytes 1179656 | tf_op jit(solution)/shard_map/ppermute | solution.py:22
  6.2 13.4 %collective-permute-start.3 = (bf16[128,1024]{1,0:T(8,128)(2,1)S(1)}, bf16[128,1024]{1,0:T(8,128)(2,1)S(1)}, u32[]{:S(2)}, u32[]{:S(2)}) collective-permute-start(bf16[128,1024]{1,0:T(8,128)(2,1)S(1)} %get-tuple-element.54), channel_id=1, source_target_pairs={{0,2},{1,3},{2,0},{3,1},{4,6},{5,7},{6,4},{7,5},{8,10},{9,11},{10,... | collective-permute-start | bytes 786440 | tf_op jit(solution)/shard_map/ppermute | solution.py:22
  7.5 12.1 %collective-permute-start.2 = (bf16[128,1024]{1,0:T(8,128)(2,1)S(1)}, bf16[128,1024]{1,0:T(8,128)(2,1)S(1)}, u32[]{:S(2)}, u32[]{:S(2)}) collective-permute-start(bf16[128,1024]{1,0:T(8,128)(2,1)S(1)} %get-tuple-element.55), channel_id=1, source_target_pairs={{0,1},{1,0},{2,3},{3,2},{4,5},{5,4},{6,7},{7,6},{8,9},{9,8},{10,11... | collective-permute-start | bytes 786440 | tf_op jit(solution)/shard_map/ppermute | solution.py:22
  8.7 10.7 %copy-start.2 = (bf16[1,128,4096]{2,1,0:T(8,128)(2,1)S(1)}, bf16[1,128,4096]{2,1,0:T(8,128)(2,1)}, u32[]{:S(2)}) copy-start(bf16[1,128,4096]{2,1,0:T(8,128)(2,1)} %param.5) | copy-start | bytes 3145732
  8.7 10.9 %collective-permute-start.4 = (bf16[128,1024]{1,0:T(8,128)(2,1)S(1)}, bf16[128,1024]{1,0:T(8,128)(2,1)S(1)}, u32[]{:S(2)}, u32[]{:S(2)}) collective-permute-start(bf16[128,1024]{1,0:T(8,128)(2,1)S(1)} %get-tuple-element.56), channel_id=1, source_target_pairs={{0,3},{1,2},{2,1},{3,0},{4,7},{5,6},{6,5},{7,4},{8,11},{9,10},{10,... | collective-permute-start | bytes 786440 | tf_op jit(solution)/shard_map/ppermute | solution.py:22
  9.3 10.3 %copy-start.3 = (bf16[1,4096,128]{2,1,0:T(8,128)(2,1)S(1)}, bf16[1,4096,128]{2,1,0:T(8,128)(2,1)}, u32[]{:S(2)}) copy-start(bf16[1,4096,128]{2,1,0:T(8,128)(2,1)} %param.7) | copy-start | bytes 3145732
  19.4 0.7 %copy-start.4 = (f32[1,4096]{1,0:T(1,128)S(1)}, f32[1,4096]{1,0:T(1,128)}, u32[]{:S(2)}) copy-start(f32[1,4096]{1,0:T(1,128)} %gain_ref.7) | copy-start | bytes 49156
  20.8 4.2 %collective-permute-start.5 = (bf16[16,1280]{1,0:T(8,128)(2,1)S(1)}, bf16[16,1280]{1,0:T(8,128)(2,1)S(1)}, u32[]{:S(2)}, u32[]{:S(2)}) collective-permute-start(bf16[16,1280]{1,0:T(8,128)(2,1)S(1)} %get-tuple-element.28), channel_id=1, source_target_pairs={{0,1},{1,0},{2,3},{3,2},{4,5},{5,4},{6,7},{7,6},{8,9},{9,8},{10,11... | collective-permute-start | bytes 122888 | tf_op jit(solution)/shard_map/ppermute | solution.py:22
  21.3 6.7 %collective-permute-start.8 = (bf16[16,1280]{1,0:T(8,128)(2,1)S(1)}, bf16[16,1280]{1,0:T(8,128)(2,1)S(1)}, u32[]{:S(2)}, u32[]{:S(2)}) collective-permute-start(bf16[16,1280]{1,0:T(8,128)(2,1)S(1)} %get-tuple-element.30), channel_id=1, source_target_pairs={{0,2},{1,3},{2,0},{3,1},{4,6},{5,7},{6,4},{7,5},{8,10},{9,11},{10,... | collective-permute-start | bytes 122888 | tf_op jit(solution)/shard_map/ppermute | solution.py:22
  22.6 5.5 %collective-permute-start.9 = (bf16[16,1280]{1,0:T(8,128)(2,1)S(1)}, bf16[16,1280]{1,0:T(8,128)(2,1)S(1)}, u32[]{:S(2)}, u32[]{:S(2)}) collective-permute-start(bf16[16,1280]{1,0:T(8,128)(2,1)S(1)} %get-tuple-element.31), channel_id=1, source_target_pairs={{0,3},{1,2},{2,1},{3,0},{4,7},{5,6},{6,5},{7,4},{8,11},{9,10},{10,... | collective-permute-start | bytes 122888 | tf_op jit(solution)/shard_map/ppermute | solution.py:22
  23.6 9.9 %collective-permute-start.7 = (bf16[16,4096]{1,0:T(8,128)(2,1)S(1)}, bf16[16,4096]{1,0:T(8,128)(2,1)S(1)}, u32[]{:S(2)}, u32[]{:S(2)}) collective-permute-start(bf16[16,4096]{1,0:T(8,128)(2,1)S(1)} %shard_map.76.refs_3_), channel_id=1, source_target_pairs={{0,16},{4,20},{8,24},{12,28},{16,0},{20,4},{24,8},{28,12},{1,17},{... | collective-permute-start | bytes 393224 | tf_op jit(solution)/shard_map/ppermute | solution.py:22
  29.0 4.4 %collective-permute-start.10 = (bf16[48,1280]{1,0:T(8,128)(2,1)S(1)}, bf16[48,1280]{1,0:T(8,128)(2,1)S(1)}, u32[]{:S(2)}, u32[]{:S(2)}) collective-permute-start(bf16[48,1280]{1,0:T(8,128)(2,1)S(1)} %get-tuple-element.33), channel_id=1, source_target_pairs={{0,1},{1,0},{2,3},{3,2},{4,5},{5,4},{6,7},{7,6},{8,9},{9,8},{10,11... | collective-permute-start | bytes 368648 | tf_op jit(solution)/shard_map/ppermute | solution.py:22
  30.0 4.0 %collective-permute-start.11 = (bf16[48,1280]{1,0:T(8,128)(2,1)S(1)}, bf16[48,1280]{1,0:T(8,128)(2,1)S(1)}, u32[]{:S(2)}, u32[]{:S(2)}) collective-permute-start(bf16[48,1280]{1,0:T(8,128)(2,1)S(1)} %get-tuple-element.34), channel_id=1, source_target_pairs={{0,2},{1,3},{2,0},{3,1},{4,6},{5,7},{6,4},{7,5},{8,10},{9,11},{10,... | collective-permute-start | bytes 368648 | tf_op jit(solution)/shard_map/ppermute | solution.py:22
  31.3 4.6 %collective-permute-start.12 = (bf16[48,1280]{1,0:T(8,128)(2,1)S(1)}, bf16[48,1280]{1,0:T(8,128)(2,1)S(1)}, u32[]{:S(2)}, u32[]{:S(2)}) collective-permute-start(bf16[48,1280]{1,0:T(8,128)(2,1)S(1)} %get-tuple-element.35), channel_id=1, source_target_pairs={{0,3},{1,2},{2,1},{3,0},{4,7},{5,6},{6,5},{7,4},{8,11},{9,10},{10,... | collective-permute-start | bytes 368648 | tf_op jit(solution)/shard_map/ppermute | solution.py:22
  31.7 17.9 %collective-permute-start.6 = (bf16[48,4096]{1,0:T(8,128)(2,1)S(1)}, bf16[48,4096]{1,0:T(8,128)(2,1)S(1)}, u32[]{:S(2)}, u32[]{:S(2)}) collective-permute-start(bf16[48,4096]{1,0:T(8,128)(2,1)S(1)} %shard_map.78.refs_3_), channel_id=1, source_target_pairs={{0,16},{4,20},{8,24},{12,28},{16,0},{20,4},{24,8},{28,12},{1,17},{... | collective-permute-start | bytes 1179656 | tf_op jit(solution)/shard_map/ppermute | solution.py:22
  36.6 12.9 %collective-permute-start.13 = (bf16[16,1280]{1,0:T(8,128)(2,1)S(1)}, bf16[16,1280]{1,0:T(8,128)(2,1)S(1)}, u32[]{:S(2)}, u32[]{:S(2)}) collective-permute-start(bf16[16,1280]{1,0:T(8,128)(2,1)S(1)} %get-tuple-element.36), channel_id=1, source_target_pairs={{0,1},{1,0},{2,3},{3,2},{4,5},{5,4},{6,7},{7,6},{8,9},{9,8},{10,11... | collective-permute-start | bytes 122888 | tf_op jit(solution)/shard_map/ppermute | solution.py:22
  37.0 12.6 %collective-permute-start.14 = (bf16[16,1280]{1,0:T(8,128)(2,1)S(1)}, bf16[16,1280]{1,0:T(8,128)(2,1)S(1)}, u32[]{:S(2)}, u32[]{:S(2)}) collective-permute-start(bf16[16,1280]{1,0:T(8,128)(2,1)S(1)} %get-tuple-element.37), channel_id=1, source_target_pairs={{0,2},{1,3},{2,0},{3,1},{4,6},{5,7},{6,4},{7,5},{8,10},{9,11},{10,... | collective-permute-start | bytes 122888 | tf_op jit(solution)/shard_map/ppermute | solution.py:22
  37.6 12.0 %collective-permute-start.15 = (bf16[16,1280]{1,0:T(8,128)(2,1)S(1)}, bf16[16,1280]{1,0:T(8,128)(2,1)S(1)}, u32[]{:S(2)}, u32[]{:S(2)}) collective-permute-start(bf16[16,1280]{1,0:T(8,128)(2,1)S(1)} %get-tuple-element.38), channel_id=1, source_target_pairs={{0,3},{1,2},{2,1},{3,0},{4,7},{5,6},{6,5},{7,4},{8,11},{9,10},{10,... | collective-permute-start | bytes 122888 | tf_op jit(solution)/shard_map/ppermute | solution.py:22
  39.4 20.3 %collective-permute-start.19 = (bf16[80,4096]{1,0:T(8,128)(2,1)S(1)}, bf16[80,4096]{1,0:T(8,128)(2,1)S(1)}, u32[]{:S(2)}, u32[]{:S(2)}) collective-permute-start(bf16[80,4096]{1,0:T(8,128)(2,1)S(1)} %get-tuple-element.48), channel_id=1, source_target_pairs={{4,0},{8,4},{12,8},{16,12},{20,16},{24,20},{28,24},{5,1},{9,5},{13... | collective-permute-start | bytes 1966088 | tf_op jit(solution)/shard_map/ppermute | solution.py:26
  50.5 9.1 %collective-permute-start.16 = (bf16[48,1280]{1,0:T(8,128)(2,1)S(1)}, bf16[48,1280]{1,0:T(8,128)(2,1)S(1)}, u32[]{:S(2)}, u32[]{:S(2)}) collective-permute-start(bf16[48,1280]{1,0:T(8,128)(2,1)S(1)} %get-tuple-element.40), channel_id=1, source_target_pairs={{0,1},{1,0},{2,3},{3,2},{4,5},{5,4},{6,7},{7,6},{8,9},{9,8},{10,11... | collective-permute-start | bytes 368648 | tf_op jit(solution)/shard_map/ppermute | solution.py:22
  51.0 8.6 %collective-permute-start.17 = (bf16[48,1280]{1,0:T(8,128)(2,1)S(1)}, bf16[48,1280]{1,0:T(8,128)(2,1)S(1)}, u32[]{:S(2)}, u32[]{:S(2)}) collective-permute-start(bf16[48,1280]{1,0:T(8,128)(2,1)S(1)} %get-tuple-element.41), channel_id=1, source_target_pairs={{0,2},{1,3},{2,0},{3,1},{4,6},{5,7},{6,4},{7,5},{8,10},{9,11},{10,... | collective-permute-start | bytes 368648 | tf_op jit(solution)/shard_map/ppermute | solution.py:22
  51.9 7.7 %collective-permute-start.18 = (bf16[48,1280]{1,0:T(8,128)(2,1)S(1)}, bf16[48,1280]{1,0:T(8,128)(2,1)S(1)}, u32[]{:S(2)}, u32[]{:S(2)}) collective-permute-start(bf16[48,1280]{1,0:T(8,128)(2,1)S(1)} %get-tuple-element.42), channel_id=1, source_target_pairs={{0,3},{1,2},{2,1},{3,0},{4,7},{5,6},{6,5},{7,4},{8,11},{9,10},{10,... | collective-permute-start | bytes 368648 | tf_op jit(solution)/shard_map/ppermute | solution.py:22
  53.3 10.4 %collective-permute-start.20 = (bf16[48,4096]{1,0:T(8,128)(2,1)S(1)}, bf16[48,4096]{1,0:T(8,128)(2,1)S(1)}, u32[]{:S(2)}, u32[]{:S(2)}) collective-permute-start(bf16[48,4096]{1,0:T(8,128)(2,1)S(1)} %get-tuple-element.50), channel_id=1, source_target_pairs={{4,0},{8,4},{12,8},{16,12},{20,16},{24,20},{28,24},{5,1},{9,5},{13... | collective-permute-start | bytes 1179656 | tf_op jit(solution)/shard_map/ppermute | solution.py:26
